TPU v7x, 32 devices: a whole 2x2x4 slice. The times are simulated.
32 devices in a mesh: seq: 8 (over y, x, core), head: 4 (over z).
Axes of the slice: x: 2, y: 2, z: 4, core: 2. Of those that a mesh axis runs over, the one named last changes fastest.
Arguments:
- signal: bfloat16 [1024, 8192], P('seq', 'head'), may hold values from -6 to 6
- gate_input: bfloat16 [1024, 8192], P('seq', 'head'), may hold values from -6 to 6
- state_in: bfloat16 [1024, 128], P('seq'), may hold values from -1.796875 to 1.796875
- state_out: bfloat16 [1024, 128], P('seq'), may hold values from -1.796875 to 1.796875
- step_size: float32 [128, 1024], P('head', 'seq'), may hold values from 0 to 2, as said below
- log_decay: float32 [128, 1024], P('head', 'seq'), may hold values from -4 to 0, as said below
- skip_gain: float32 [128], P('head'), may hold values from 0.5 to 1.5
- norm_gain: float32 [8192], P('head'), may hold values from 0.1 to 1.9
- out_weight: bfloat16 [8192, 4096], P('head', 'seq'), may hold values from -0.09375 to 0.09375
Outputs:
- mixed: bfloat16 [1024, 4096], P('seq', 'head')
Inputs may be any that keep to these rules, and one draw needn't show every extreme that they name: step_size is positive. log_decay is negative.
All inputs are finite; a program needn't handle non-finite values.
Results may differ from a plain program's by a relative error of at most 0.025.
Values may be sent and summed in bfloat16 or wider, within the bound.
No kernel may reach another device: no remote copies, remote signals or barrier semaphores. Data moves between devices by JAX's collectives and lax.ppermute only.
A program may use at most 64 MiB of HBM per device.

v0:
```python
import jax
import jax.numpy as jnp
from jax import lax
from jax.sharding import PartitionSpec as P

HIGH = lax.Precision.HIGHEST


def entering_2(value, axis, join, neutral):
    place = lax.axis_index(axis)
    gathered = jax.tree.map(
        lambda a, kind: lax.all_gather(a.astype(kind), axis), value, (jnp.bfloat16, jnp.bfloat16)
    )
    state = jax.tree.map(lambda a, e: jnp.zeros_like(a) + jnp.asarray(e, a.dtype), value, neutral)

    def one(turn, state):
        return join(
            state,
            jax.tree.map(
                lambda a, own: lax.dynamic_index_in_dim(a, turn, 0, False).astype(own.dtype),
                gathered,
                value,
            ),
        )

    return lax.fori_loop(0, place, one, state)


def ssd_block(state, inputs):
    signal_part, keys_part, queries_part, decay_part, step_sizes_local = inputs
    signal_f = signal_part.astype(jnp.float32)
    keys_f = keys_part.astype(jnp.float32)
    queries_f = queries_part.astype(jnp.float32)
    running = jnp.cumsum(decay_part, axis=1)
    width = decay_part.shape[1]
    lower = (jnp.arange(width)[:, None] >= jnp.arange(width)[None, :])[None]
    spread = running[:, :, None] - running[:, None, :]
    factors = jnp.where(lower, jnp.exp(jnp.where(lower, spread, 0.0)), 0.0)
    scores = jnp.dot(queries_f, keys_f.T, precision=HIGH)
    weights = factors * scores[None] * step_sizes_local[:, None, :]
    inside = jnp.einsum("hij,jhp->ihp", weights, signal_f, precision=HIGH)
    carried = (
        jnp.einsum("in,hpn->ihp", queries_f, state, precision=HIGH) * jnp.exp(running).T[:, :, None]
    )
    tail = jnp.exp(running[:, -1:] - running) * step_sizes_local
    fresh = jnp.einsum("hj,jhp,jn->hpn", tail, signal_f, keys_f, precision=HIGH)
    new_state = jnp.exp(running[:, -1])[:, None, None] * state + fresh
    return (new_state, inside + carried)


def join_states(earlier, later):
    decay_early, state_early = earlier
    decay_late, state_late = later
    return (decay_early + decay_late, jnp.exp(decay_late)[:, None, None] * state_early + state_late)


def body(
    signal, gate_input, state_in, state_out, step_size, log_decay, skip_gain, norm_gain, out_weight
):
    tokens_here = signal.shape[0]
    head_count = log_decay.shape[0]
    head_size = signal.shape[1] // head_count
    state_size = state_in.shape[1]
    width = min(256, tokens_here)
    blocks = tokens_here // width
    inputs = (
        signal.reshape(blocks, width, head_count, head_size),
        state_in.reshape(blocks, width, state_size),
        state_out.reshape(blocks, width, state_size),
        log_decay.reshape(head_count, blocks, width).transpose(1, 0, 2),
        step_size.reshape(head_count, blocks, width).transpose(1, 0, 2),
    )
    start = jnp.zeros((head_count, head_size, state_size), jnp.float32)
    local_state, outputs = lax.scan(ssd_block, start, inputs)
    device_running = jnp.cumsum(log_decay, axis=1)
    device_decay = device_running[:, -1]
    empty = (jnp.zeros_like(device_decay), jnp.zeros_like(local_state))
    before_decay, incoming = entering_2((device_decay, local_state), "seq", join_states, empty)
    queries_f = state_out.astype(jnp.float32)
    entering = (
        jnp.einsum("in,hpn->ihp", queries_f, incoming, precision=HIGH)
        * jnp.exp(device_running).T[:, :, None]
    )
    channels = signal.reshape(tokens_here, head_count, head_size).astype(jnp.float32)
    result = (
        outputs.reshape(tokens_here, head_count, head_size)
        + entering
        + skip_gain[None, :, None] * channels
    )
    gated = result.reshape(tokens_here, head_count * head_size) * jax.nn.silu(
        gate_input.astype(jnp.float32)
    )
    squares = lax.psum(jnp.sum(gated * gated, axis=1), "head")
    inner_total = head_count * head_size * lax.axis_size("head")
    scale_rows = lax.rsqrt(squares / inner_total + 1e-05)
    hidden = (gated * scale_rows[:, None] * norm_gain[None, :]).astype(jnp.bfloat16)
    partials = jnp.dot(
        hidden,
        lax.all_gather(out_weight, "seq", axis=1, tiled=True),
        preferred_element_type=jnp.float32,
    )
    summed = lax.psum_scatter(
        partials.astype(jnp.bfloat16), "head", scatter_dimension=1, tiled=True
    )
    return summed


def solution(mesh):
    in_specs = (
        P("seq", "head"),
        P("seq", "head"),
        P("seq", None),
        P("seq", None),
        P("head", "seq"),
        P("head", "seq"),
        P("head"),
        P("head"),
        P("head", "seq"),
    )
    out_specs = P("seq", "head")
    return jax.shard_map(body, mesh=mesh, in_specs=in_specs, out_specs=out_specs, check_vma=False)
```

profile of v0, /device:TPU:0, one launch (start us, length us, event | category | flops | bytes accessed | tf_op | source)
XLA Modules:
  0.0 190.1 jit_solution(2014814446369979985)
XLA Ops:
  6.5 1.0 reduce_window_sum.13
  7.6 0.2 slice_reduce_fusion
  7.7 0.8 multiply_bitcast_fusion
  8.6 1.3 copy.14
  9.9 0.0 copy-start.6
  9.9 0.0 copy-start.2
  9.9 0.0 copy-start.3
  9.9 2.3 %fusion.15 = bf16[32,64,128]{2,1,0:T(8,128)(2,1)} fusion(bf16[128,32,64]{0,2,1:T(8,128)(2,1)S(1)} %bitcast.46, f32[128,32]{0,1:T(8,128)S(1)} %get-tuple-element.84, f32[32]{0:T(128)S(1)} %exponential_multiply_fusion, bf16[128,128]{1,0:T(8,128)(2,1)} %param.13), kind=kOutput, calls=%fused_computation.23 | convolution fusion | flops 403701760 | bytes 1097856 | tf_op jit(solution)/shard_map/while/body/eval_jaxpr/hj,jhp,jn->hpn/dot_general | solution.py:46
  12.2 0.0 all-gather.7.cloned.1.call-update
  12.2 0.0 all-gather.5.cloned.1.call-start
  12.2 0.7 all-gather.5.cloned.1.call-update
  12.9 0.0 reduce-scatter.2.cloned.1.call-start
  13.0 0.6 dynamic-slice.4
  14.2 0.2 fusion.33
  14.4 0.2 dynamic-update-slice
  14.7 15.3 %all-reduce = bf16[256]{0:T(256)(128)(2,1)S(1)} all-reduce(bf16[256]{0:T(256)(128)(2,1)S(1)} %dynamic-update-slice), channel_id=2, replica_groups=mesh['seq'=8,'head'=4] {'seq'}, use_global_device_ids=true, to_apply=%add | all-reduce | flops 256 | bytes 1024
  30.0 0.1 reshape.68
  30.1 0.1 fusion.37
  30.3 2.6 %fusion.7 = f32[128,32,64]{0,2,1:T(8,128)S(1)} fusion(bf16[128,32,64]{0,2,1:T(8,128)(2,1)S(1)} %bitcast.47, f32[32,128]{1,0:T(8,128)S(1)} %copy-done.3, f32[128,128]{1,0:T(8,128)S(1)} %fusion.37, f32[32,128]{1,0:T(8,128)S(1)} %reduce_window_sum.13, pred[128,128]{1,0:T(8,128)(4,1)S(1)} %iota_compare_fusion), kind=kOutput, calls=%fused_computation.10 | convolution fusion | flops 405274624 | bytes 1687552 | tf_op jit(solution)/shard_map/while/body/eval_jaxpr/hij,jhp->ihp/dot_general | solution.py:41
  32.9 0.6 fusion.13
  33.5 18.3 %all-gather.7.cloned.1.call-done = bf16[256,64,128]{2,1,0:T(8,128)(2,1)} async-done(((bf16[32,64,128]{2,1,0:T(8,128)(2,1)}), bf16[256,64,128]{2,1,0:T(8,128)(2,1)}) %all-gather.7.cloned.1.call-update) | async-done | bytes 4194320 | tf_op jit(solution)/shard_map/all_gather | solution.py:12
  51.8 0.1 broadcast.25
  51.9 0.0 copy-start.4
  52.0 0.6 copy-done.4
  52.6 1.7 fusion.14
  54.3 1.6 copy.15
  55.8 0.4 multiply_reduce_fusion
  56.3 11.7 %psum.7 = f32[128]{0:T(128)S(1)} all-reduce(f32[128]{0:T(128)S(1)} %multiply_reduce_fusion), channel_id=1, replica_groups=mesh['seq'=8,'head'=4] {'head'}, use_global_device_ids=true, to_apply=%region_4.5 | all-reduce | flops 128 | bytes 1024 | tf_op jit(solution)/shard_map/psum | solution.py:93
  68.0 78.8 %all-gather.5.cloned.1.call-done = bf16[2048,4096]{1,0:T(8,128)(2,1)} async-done(((bf16[2048,512]{1,0:T(8,128)(2,1)}), bf16[2048,4096]{1,0:T(8,128)(2,1)}) %all-gather.5.cloned.1.call-update) | async-done | bytes 16777232 | tf_op jit(solution)/shard_map/all_gather | solution.py:99
  146.8 9.4 %convolution_convert_fusion = bf16[128,4096]{1,0:T(8,128)(2,1)} fusion(bf16[2048,4096]{1,0:T(8,128)(2,1)} %all-gather.5.cloned.1.call-done, f32[2048]{0:T(1024)S(1)} %copy-done.5, f32[128]{0:T(128)S(1)} %add_rsqrt_fusion, f32[128,2048]{1,0:T(8,128)S(1)} %copy.15, bf16[128,2048]{1,0:T(8,128)(2,1)S(1)} %copy-done.1), kind=kOutput, calls=%fused_computation.2 | convolution fusion | flops 2150367232 | bytes 19407360 | tf_op jit(solution)/shard_map/dot_general | solution.py:97
  156.3 0.0 reduce-scatter.2.cloned.1.call-update
  156.3 27.3 %reduce-scatter.2.cloned.1.call-done = bf16[128,1024]{1,0:T(8,128)(2,1)} async-done(((bf16[128,4096]{1,0:T(8,128)(2,1)}), bf16[128,1024]{1,0:T(8,128)(2,1)}) %reduce-scatter.2.cloned.1.call-update) | async-done | bytes 262160 | tf_op jit(solution)/shard_map/reduce_scatter | solution.py:102
  (15 shorter events, 0.1 us)
Async XLA Ops:
  6.5 23.6 %copy-start = (bf16[128,128]{1,0:T(8,128)(2,1)S(1)}, bf16[128,128]{1,0:T(8,128)(2,1)}, u32[]{:S(2)}) copy-start(bf16[128,128]{1,0:T(8,128)(2,1)} %param.14) | copy-start | bytes 98308
  6.5 45.3 %all-gather.7.cloned.1.call-start = ((), (), s32[]{:S(2)}) async-start(), calls=%async_computation.3 | async-start | bytes 4718592 | tf_op jit(solution)/shard_map/all_gather | solution.py:12
  9.9 3.1 %copy-start.6 = (u32[32]{0:T(128)S(1)}, u32[32]{0:T(128)}, u32[]{:S(2)}) copy-start(u32[32]{0:T(128)} %constant.58) | copy-start | bytes 388
  9.9 20.2 %copy-start.2 = (bf16[128,128]{1,0:T(8,128)(2,1)S(1)}, bf16[128,128]{1,0:T(8,128)(2,1)}, u32[]{:S(2)}) copy-start(bf16[128,128]{1,0:T(8,128)(2,1)} %param.13) | copy-start | bytes 98308
  9.9 20.4 %copy-start.3 = (f32[32,128]{1,0:T(8,128)S(1)}, f32[32,128]{1,0:T(8,128)}, u32[]{:S(2)}) copy-start(f32[32,128]{1,0:T(8,128)} %param.15) | copy-start | bytes 49156
  12.2 134.6 %all-gather.5.cloned.1.call-start = ((), (), s32[]{:S(2)}) async-start(), calls=%async_computation.1 | async-start | bytes 18874368 | tf_op jit(solution)/shard_map/all_gather | solution.py:99
  12.9 170.6 %reduce-scatter.2.cloned.1.call-start = ((), (), s32[]{:S(2)}) async-start(), calls=%async_computation.2 | async-start | bytes 1310720 | tf_op jit(solution)/shard_map/reduce_scatter | solution.py:102
  51.9 0.7 copy-start.4
  52.6 3.3 %copy-start.1 = (bf16[128,2048]{1,0:T(8,128)(2,1)S(1)}, bf16[128,2048]{1,0:T(8,128)(2,1)}, u32[]{:S(2)}) copy-start(bf16[128,2048]{1,0:T(8,128)(2,1)} %param.12) | copy-start | bytes 1572868
  54.3 92.6 %copy-start.5 = (f32[2048]{0:T(1024)S(1)}, f32[2048]{0:T(1024)}, u32[]{:S(2)}) copy-start(f32[2048]{0:T(1024)} %param.18) | copy-start | bytes 24580
Sparse Core Ops, SparseCore 0:
  12.3 39.4 all-gather.6
  53.7 93.1 all-gather.4
  156.4 27.1 reduce-scatter.1
where the time goes:
time: 191 us; the launch traced here: 190 us
  waiting for transfers between devices  125 us (65%)
  blocking collectives  27.1 us (14%)
  matrix products  16.7 us (9%)
  between operations  13.9 us (7%)
  local copies, waits for them, and re-layouts  4.93 us (3%)
  other arithmetic  2.29 us (1%)
    all_gather x1, waiting for transfers between devices, body(): lax.all_gather(out_weight, 'seq', axis=1, tiled=True)  78.8 us
    reduce_scatter x1, waiting for transfers between devices, body(): lax.psum_scatter(partials.astype(jnp.bfloat16), 'head', scatter_dimension...  27.3 us
    all_gather x1, waiting for transfers between devices, entering_2(): lax.all_gather(a.astype(kind), axis)  18.3 us
    unnamed x1, blocking collectives  15.3 us
    psum x1, blocking collectives, body(): squares = lax.psum(jnp.sum(gated * gated, axis=1), 'head')  11.7 us
    dot_general x1, matrix products, body(): jnp.dot(hidden, lax.all_gather(out_weight, 'seq', axis=1, tiled=True), pr...  9.42 us
  transfers between devices with their start and end apart: 3, of which 3 were waited for; matrix products, arithmetic and copies ran while one was open for 4% of the time, Pallas kernels for 0%

commit v1 on v0

v1 whole, which is shorter than its diff:
```python
import jax
import jax.numpy as jnp
from jax import lax
from jax.sharding import PartitionSpec as P

BOTH = ("seq", "head")


def split2(v):
    hi = v.astype(jnp.bfloat16)
    lo = (v - hi.astype(jnp.float32)).astype(jnp.bfloat16)
    return hi, lo


def body(n_chip, n_head, signal, gate_input, state_in, state_out, step_size, log_decay, skip_gain, norm_gain, out_weight):
    f32, bf16 = jnp.float32, jnp.bfloat16
    rows = signal.shape[0]
    heads = log_decay.shape[0]
    half = heads // 2
    wide = signal.shape[1] // 2
    size = signal.shape[1] // heads
    states = state_in.shape[1]
    k = lax.axis_index("seq") % 2
    sib = [(i, i ^ 1) for i in range(2 * n_chip)]

    def mine(a, axis):
        n = a.shape[axis] // 2
        return lax.dynamic_slice_in_dim(a, k * n, n, axis)

    def theirs(a, axis):
        n = a.shape[axis] // 2
        return lax.dynamic_slice_in_dim(a, (1 - k) * n, n, axis)

    def swap(a):
        return lax.ppermute(a, "seq", sib)

    def ordered(own, other):
        return jnp.where(k == 0, own, other), jnp.where(k == 0, other, own)

    rates = jnp.concatenate([step_size, log_decay], 0).reshape(2, heads, rows)
    first = jnp.concatenate([theirs(signal, 1), state_in], 1)
    got1 = swap(first)
    got_r = swap(theirs(rates, 1))
    second = jnp.concatenate([theirs(gate_input, 1), state_out], 1)
    got2 = swap(second)
    x2 = ordered(mine(signal, 1), got1[:, :wide])
    b2 = ordered(state_in, got1[:, wide:])
    z2 = ordered(mine(gate_input, 1), got2[:, :wide])
    c2 = ordered(state_out, got2[:, wide:])
    r2 = ordered(mine(rates, 1), got_r)

    def expand(v):
        return jnp.repeat(v.T, size, axis=1)

    part = []
    for x, b, r in zip(x2, b2, r2):
        dt, ld = r[0], r[1]
        run = jnp.cumsum(ld, axis=1)
        tail = jnp.exp(run[:, -1:] - run) * dt
        xs = (x.astype(f32) * expand(tail)).astype(bf16)
        st = lax.dot_general(b, xs, (((0,), (0,)), ((), ())), preferred_element_type=f32)
        part.append((run, st, jnp.exp(run[:, -1])))
    rep = lambda v: jnp.repeat(v, size)[None, :]
    chip_state = rep(part[1][2]) * part[0][1] + part[1][1]
    chip_decay = jnp.exp(part[0][0][:, -1] + part[1][0][:, -1])
    hi, lo = split2(rep(chip_decay))
    msg = jnp.concatenate([chip_state.astype(bf16), hi, lo, jnp.zeros((14, wide), bf16)], 0)
    got = [
        lax.ppermute(msg, "seq", [(s, s + 2 * j) for s in range(2 * n_chip - 2 * j)])
        for j in range(1, n_chip)
    ]
    y = []
    for (x, b, c, r, p) in zip(x2, b2, c2, r2, part):
        run, dt = p[0], r[0]
        scores = lax.dot_general(c, b, (((1,), (1,)), ((), ())), preferred_element_type=f32)
        lower = jnp.arange(rows)[:, None] >= jnp.arange(rows)[None, :]
        diff = jnp.where(lower, run[:, :, None] - run[:, None, :], -jnp.inf)
        w = (jnp.exp(diff) * scores[None] * dt[:, None, :]).astype(bf16)
        inside = jnp.einsum("hij,jhp->ihp", w, x.reshape(rows, half, size), preferred_element_type=f32)
        y.append(inside.reshape(rows, wide) + jnp.repeat(mine(skip_gain, 0), size)[None, :] * x.astype(f32))
    enter = jnp.zeros((states, wide), f32)
    for m in got[::-1]:
        f = m[states].astype(f32) + m[states + 1].astype(f32)
        enter = m[:states].astype(f32) + f[None, :] * enter
    enters = [enter, rep(part[0][2]) * enter + part[0][1]]
    gs, sq = [], []
    for yy, e, c, p, z in zip(y, enters, c2, part, z2):
        add = jnp.dot(c, e.astype(bf16), preferred_element_type=f32)
        yy = yy + add * expand(jnp.exp(p[0]))
        zf = z.astype(f32)
        gated = yy * zf / (1 + jnp.exp(-zf))
        sq.append(jnp.sum(gated * gated, axis=1))
        gs.append((gated * mine(norm_gain, 0)[None, :]).astype(bf16))
    tokens = 2 * rows
    sq = jnp.concatenate(sq)
    hi, lo = split2(sq)
    extra = jnp.pad(jnp.stack([hi, lo]), ((0, 14), (0, wide - tokens)))
    gmsg = jnp.concatenate(gs + [extra], 0)

    def pairs(f):
        out = []
        for s in range(2 * n_chip):
            for h in range(n_head):
                s2, h2 = f(s // 2, s % 2, h)
                out.append((s * n_head + h, s2 * n_head + h2))
        return out

    cols = out_weight.shape[1]
    z = []
    for m in range(n_head):
        across = pairs(lambda c, k, h: (2 * (c ^ h ^ m) + k, h))
        g1 = lax.ppermute(gmsg, BOTH, across)
        g2 = swap(g1)
        part_sum = jnp.dot(g1[:tokens], mine(out_weight, 0), preferred_element_type=f32)
        part_sum += jnp.dot(g2[:tokens], theirs(out_weight, 0), preferred_element_type=f32)
        sqs = g1[tokens:tokens + 2, :tokens].astype(f32) + g2[tokens:tokens + 2, :tokens].astype(f32)
        hi, lo = split2(sqs[0] + sqs[1])
        ext = jnp.zeros((16, cols), bf16)
        nrow = 2 * tokens // cols if 2 * tokens > cols else 1
        ext = jnp.concatenate([hi, lo]).reshape(nrow, -1)
        ext = jnp.pad(ext, ((0, 16 - nrow), (0, cols - ext.shape[1])))
        pmsg = jnp.concatenate([part_sum.astype(bf16), ext], 0)
        back = lax.ppermute(pmsg, BOTH, across)
        z.append(lax.ppermute(back, BOTH, pairs(lambda c, k, h: (2 * c + k, c ^ h ^ m))))
    total = sum(a[:tokens].astype(f32) for a in z)
    ss = sum(a[tokens:tokens + nrow].astype(f32).reshape(-1)[:2 * tokens] for a in z)
    ss = ss[:tokens] + ss[tokens:]
    scale = lax.rsqrt(ss / (2 * wide * n_head) + 1e-5)
    out = (total * scale[:, None]).astype(bf16)
    own, other = mine(out, 0), swap(theirs(out, 0))
    return jnp.concatenate(ordered(own, other), axis=1)


def solution(mesh):
    n_chip, n_head = mesh.shape["seq"] // 2, mesh.shape["head"]
    assert n_chip == n_head and n_head & (n_head - 1) == 0
    in_specs = (
        P("seq", "head"),
        P("seq", "head"),
        P("seq", None),
        P("seq", None),
        P("head", "seq"),
        P("head", "seq"),
        P("head"),
        P("head"),
        P("head", "seq"),
    )

    def run(*args):
        return body(n_chip, n_head, *args)

    return jax.shard_map(run, mesh=mesh, in_specs=in_specs, out_specs=P("seq", "head"), check_vma=False)
```

time: 191 us -> 132 us (0.69)
  the two profiles are of different devices: /device:TPU:0 before, /device:TPU:5 now
where the time goes in v1:
time: 132 us; the launch traced here: 131 us
  starting transfers between devices  51.2 us (39%)
  waiting for transfers between devices  39.1 us (30%)
  matrix products  16 us (12%)
  local copies, waits for them, and re-layouts  14.3 us (11%)
  other arithmetic  9.35 us (7%)
    ppermute x4, starting transfers between devices, body(): lax.ppermute(back, BOTH, pairs(lambda c, k, h: (2 * c + k, c ^ h ^ m)))  19.7 us
    ppermute x4, waiting for transfers between devices, body(): lax.ppermute(back, BOTH, pairs(lambda c, k, h: (2 * c + k, c ^ h ^ m)))  17.9 us
    ppermute x4, waiting for transfers between devices, body(): g1 = lax.ppermute(gmsg, BOTH, across)  17.2 us
    ppermute x4, starting transfers between devices, body(): back = lax.ppermute(pmsg, BOTH, across)  9.77 us
    ppermute x4, starting transfers between devices, body(): g1 = lax.ppermute(gmsg, BOTH, across)  9.07 us
    ppermute x8, starting transfers between devices, swap(): return lax.ppermute(a, 'seq', sib)  6.92 us
    ppermute x3, starting transfers between devices, body(): lax.ppermute(msg, 'seq', [(s, s + 2 * j) for s in range(2 * n_chip - 2 *...  5.7 us
    dot_general x2, matrix products, body(): jnp.einsum('hij,jhp->ihp', w, x.reshape(rows, half, size), preferred_elem...  4.4 us
  transfers between devices with their start and end apart: 23, of which 6 were waited for; matrix products, arithmetic and copies ran while one was open for 24% of the time, Pallas kernels for 0%

profile of v1, /device:TPU:5, one launch (start us, length us, event | category | flops | bytes accessed | tf_op | source)
XLA Modules:
  0.0 130.7 jit_solution(11988962779255344074)
XLA Ops:
  0.0 1.1 constant_dynamic-slice_fusion.3
  4.4 1.5 %pad_maximum_fusion.2 = bf16[128,1152]{1,0:T(8,128)(2,1)} fusion(bf16[128,128]{1,0:T(8,128)(2,1)} %param.12, bf16[128,1024]{1,0:T(8,128)(2,1)S(1)} %constant_dynamic-slice_fusion.1), kind=kLoop, calls=%fused_computation.81 | loop fusion | flops 589824 | bytes 589824 | tf_op jit(solution)/shard_map/concatenate | solution.py:44
  14.2 1.1 broadcast_select_fusion.1
  15.4 1.3 fusion.62
  16.7 1.0 add_convert_fusion.1
  19.4 1.4 %collective-permute-start.5 = (bf16[144,1024]{1,0:T(8,128)(2,1)}, bf16[144,1024]{1,0:T(8,128)(2,1)}, u32[]{:S(2)}, u32[]{:S(2)}) collective-permute-start(bf16[144,1024]{1,0:T(8,128)(2,1)} %maximum_maximum_fusion), channel_id=1, source_target_pairs={{0,24},{4,28},{1,25},{5,29},{2,26},{6,30},{3,27},{7,31}} | collective-permute-start | bytes 884744 | tf_op jit(solution)/shard_map/ppermute | solution.py:69
  20.8 1.3 collective-permute-start.4
  22.1 3.1 %collective-permute-start.3 = (bf16[144,1024]{1,0:T(8,128)(2,1)}, bf16[144,1024]{1,0:T(8,128)(2,1)}, u32[]{:S(2)}, u32[]{:S(2)}) collective-permute-start(bf16[144,1024]{1,0:T(8,128)(2,1)} %maximum_maximum_fusion), channel_id=1, source_target_pairs={{0,8},{4,12},{8,16},{12,20},{16,24},{20,28},{1,9},{5,13},{9,17},{1... | collective-permute-start | bytes 884744 | tf_op jit(solution)/shard_map/ppermute | solution.py:69
  26.1 2.3 %fusion.21 = f32[16,64,128]{2,1,0:T(8,128)} fusion(bf16[128,16,64]{0,2,1:T(8,128)(2,1)} %bitcast.51, f32[16,128]{1,0:T(8,128)S(1)} %get-tuple-element.26, f32[128,128]{1,0:T(8,128)S(1)} %fusion.75, f32[16,128]{1,0:T(8,128)S(1)} %reduce_window_sum.18, pred[128,128]{1,0:T(8,128)(4,1)S(1)} %iota_compare_fusion.3), kind=kOutput, calls=%fused_computation.39 | convolution fusion | flops 34865152 | bytes 884736 | tf_op jit(solution)/shard_map/hij,jhp->ihp/dot_general | solution.py:79
  29.5 2.1 %fusion.20 = f32[16,64,128]{2,1,0:T(8,128)} fusion(bf16[128,16,64]{0,2,1:T(8,128)(2,1)S(1)} %bitcast.52, f32[16,128]{1,0:T(8,128)S(1)} %get-tuple-element.39, f32[128,128]{1,0:T(8,128)S(1)} %fusion.74, f32[16,128]{1,0:T(8,128)S(1)} %reduce_window_sum.17, pred[128,128]{1,0:T(8,128)(4,1)} %copy-done.8), kind=kOutput, calls=%fused_computation.38 | convolution fusion | flops 34865152 | bytes 884736 | tf_op jit(solution)/shard_map/hij,jhp->ihp/dot_general | solution.py:79
  31.6 2.0 %copy.24 = f32[128,1024]{1,0:T(8,128)} copy(f32[128,1024]{0,1:T(8,128)} %bitcast.49) | data formatting | bytes 1048576 | tf_op jit(solution)/shard_map/reshape | solution.py:80
  33.6 2.0 %copy.19 = f32[128,1024]{1,0:T(8,128)} copy(f32[128,1024]{0,1:T(8,128)} %bitcast.50) | data formatting | bytes 1048576 | tf_op jit(solution)/shard_map/reshape | solution.py:80
  36.5 3.0 %collective-permute-done.4 = bf16[144,1024]{1,0:T(8,128)(2,1)} collective-permute-done((bf16[144,1024]{1,0:T(8,128)(2,1)}, bf16[144,1024]{1,0:T(8,128)(2,1)}, u32[]{:S(2)}, u32[]{:S(2)}) %collective-permute-start.4) | collective-permute-done | bytes 294944 | tf_op jit(solution)/shard_map/ppermute | solution.py:69
  41.1 2.2 %fusion.31 = f32[128,1024]{1,0:T(8,128)S(1)} fusion(f32[128,1024]{1,0:T(8,128)} %copy.24, bf16[128,1024]{1,0:T(8,128)(2,1)S(1)} %get-tuple-element.14, f32[128,1024]{1,0:T(8,128)} %copy.25, f32[128,1024]{1,0:T(8,128)S(1)} %fusion.62, f32[1024]{0:T(1024)S(1)} %copy-done.10, f32[1024]{0:T(1024)S(1)} %copy-done.9, pred[]{:T(512)S(6)} %eq.4, ...), kind=kOutput, calls=%fused_computation.49 | convolution fusion | flops 36454400 | bytes 3757568 | tf_op jit(solution)/shard_map/dot_general | solution.py:88
  43.4 1.8 %multiply_convert_fusion.6 = (bf16[128,1024]{1,0:T(8,128)(2,1)S(1)}, f32[128]{0:T(128)S(1)}, f32[128]{0:T(128)S(1)}, bf16[128,1024]{1,0:T(8,128)(2,1)S(1)}) fusion(f32[1024]{0:T(1024)S(1)} %dynamic-slice-done, f32[128,1024]{1,0:T(8,128)S(1)} %fusion.31, bf16[128,1152]{1,0:T(8,128)(2,1)} %collective-permute-done.2, bf16[128,2048]{1,0:T(8,128)(2,1)S(1)} %copy-done.7, ...), kind=kOutput, calls=%fused_computation.69 | convolution fusion | flops 37240576 | bytes 3758592 | tf_op jit(solution)/shard_map/dot_general | solution.py:88
  45.3 1.9 %collective-permute-start.18 = (bf16[272,1024]{1,0:T(8,128)(2,1)S(1)}, bf16[272,1024]{1,0:T(8,128)(2,1)S(1)}, u32[]{:S(2)}, u32[]{:S(2)}) collective-permute-start(bf16[272,1024]{1,0:T(8,128)(2,1)S(1)} %pad_maximum_fusion), channel_id=1, source_target_pairs={{0,24},{1,17},{2,10},{3,3},{4,28},{5,21},{6,14},{7,7},{8,16},{9,25... | collective-permute-start | bytes 1671176 | tf_op jit(solution)/shard_map/ppermute | solution.py:112
  47.2 2.6 %collective-permute-start.14 = (bf16[272,1024]{1,0:T(8,128)(2,1)S(1)}, bf16[272,1024]{1,0:T(8,128)(2,1)S(1)}, u32[]{:S(2)}, u32[]{:S(2)}) collective-permute-start(bf16[272,1024]{1,0:T(8,128)(2,1)S(1)} %pad_maximum_fusion), channel_id=1, source_target_pairs={{0,16},{1,25},{2,2},{3,11},{4,20},{5,29},{6,6},{7,15},{8,24},{9,17... | collective-permute-start | bytes 1671176 | tf_op jit(solution)/shard_map/ppermute | solution.py:112
  49.8 3.8 %collective-permute-start.10 = (bf16[272,1024]{1,0:T(8,128)(2,1)S(1)}, bf16[272,1024]{1,0:T(8,128)(2,1)S(1)}, u32[]{:S(2)}, u32[]{:S(2)}) collective-permute-start(bf16[272,1024]{1,0:T(8,128)(2,1)S(1)} %pad_maximum_fusion), channel_id=1, source_target_pairs={{0,8},{1,1},{2,26},{3,19},{4,12},{5,5},{6,30},{7,23},{8,0},{9,9},{... | collective-permute-start | bytes 1671176 | tf_op jit(solution)/shard_map/ppermute | solution.py:112
  54.4 7.1 %collective-permute-done.18 = bf16[272,1024]{1,0:T(8,128)(2,1)S(1)} collective-permute-done((bf16[272,1024]{1,0:T(8,128)(2,1)S(1)}, bf16[272,1024]{1,0:T(8,128)(2,1)S(1)}, u32[]{:S(2)}, u32[]{:S(2)}) %collective-permute-start.18) | collective-permute-done | bytes 557088 | tf_op jit(solution)/shard_map/ppermute | solution.py:112
  61.5 3.0 %collective-permute-start.19 = (bf16[272,1024]{1,0:T(8,128)(2,1)S(1)}, bf16[272,1024]{1,0:T(8,128)(2,1)S(1)}, u32[]{:S(2)}, u32[]{:S(2)}) collective-permute-start(bf16[272,1024]{1,0:T(8,128)(2,1)S(1)} %collective-permute-done.18), channel_id=1, source_target_pairs={{0,4},{4,0},{8,12},{12,8},{16,20},{20,16},{24,28},{28,24},{1,5},{5... | collective-permute-start | bytes 1671176 | tf_op jit(solution)/shard_map/ppermute | solution.py:35
  64.4 10.1 %collective-permute-done.14 = bf16[272,1024]{1,0:T(8,128)(2,1)S(1)} collective-permute-done((bf16[272,1024]{1,0:T(8,128)(2,1)S(1)}, bf16[272,1024]{1,0:T(8,128)(2,1)S(1)}, u32[]{:S(2)}, u32[]{:S(2)}) %collective-permute-start.14) | collective-permute-done | bytes 557088 | tf_op jit(solution)/shard_map/ppermute | solution.py:112
  77.9 1.9 %collective-permute-start.20 = (bf16[272,512]{1,0:T(8,128)(2,1)S(1)}, bf16[272,512]{1,0:T(8,128)(2,1)}, u32[]{:S(2)}, u32[]{:S(2)}) collective-permute-start(bf16[272,512]{1,0:T(8,128)(2,1)S(1)} %fusion.57), channel_id=1, source_target_pairs={{0,24},{1,17},{2,10},{3,3},{4,28},{5,21},{6,14},{7,7},{8,16},{9,25... | collective-permute-start | bytes 835592 | tf_op jit(solution)/shard_map/ppermute | solution.py:123
  80.4 2.6 %collective-permute-start.16 = (bf16[272,512]{1,0:T(8,128)(2,1)S(1)}, bf16[272,512]{1,0:T(8,128)(2,1)}, u32[]{:S(2)}, u32[]{:S(2)}) collective-permute-start(bf16[272,512]{1,0:T(8,128)(2,1)S(1)} %fusion.56), channel_id=1, source_target_pairs={{0,16},{1,25},{2,2},{3,11},{4,20},{5,29},{6,6},{7,15},{8,24},{9,17... | collective-permute-start | bytes 835592 | tf_op jit(solution)/shard_map/ppermute | solution.py:123
  83.6 3.8 %collective-permute-start.12 = (bf16[272,512]{1,0:T(8,128)(2,1)S(1)}, bf16[272,512]{1,0:T(8,128)(2,1)}, u32[]{:S(2)}, u32[]{:S(2)}) collective-permute-start(bf16[272,512]{1,0:T(8,128)(2,1)S(1)} %fusion.55), channel_id=1, source_target_pairs={{0,8},{1,1},{2,26},{3,19},{4,12},{5,5},{6,30},{7,23},{8,0},{9,9},{... | collective-permute-start | bytes 835592 | tf_op jit(solution)/shard_map/ppermute | solution.py:123
  88.0 1.4 %collective-permute-start.8 = (bf16[272,512]{1,0:T(8,128)(2,1)S(1)}, bf16[272,512]{1,0:T(8,128)(2,1)}, u32[]{:S(2)}, u32[]{:S(2)}) collective-permute-start(bf16[272,512]{1,0:T(8,128)(2,1)S(1)} %fusion.54), channel_id=1, source_target_pairs={{0,0},{1,9},{2,18},{3,27},{4,4},{5,13},{6,22},{7,31},{8,8},{9,1},{... | collective-permute-start | bytes 835592 | tf_op jit(solution)/shard_map/ppermute | solution.py:123
  89.4 8.8 %collective-permute-start.21 = (bf16[272,512]{1,0:T(8,128)(2,1)}, bf16[272,512]{1,0:T(8,128)(2,1)S(1)}, u32[]{:S(2)}, u32[]{:S(2)}) collective-permute-start(bf16[272,512]{1,0:T(8,128)(2,1)} %collective-permute-done.20), channel_id=1, source_target_pairs={{0,3},{1,2},{2,1},{3,0},{4,7},{5,6},{6,5},{7,4},{8,10},{9,11},{10,... | collective-permute-start | bytes 835592 | tf_op jit(solution)/shard_map/ppermute | solution.py:124
  98.2 1.6 %collective-permute-start.17 = (bf16[272,512]{1,0:T(8,128)(2,1)}, bf16[272,512]{1,0:T(8,128)(2,1)S(1)}, u32[]{:S(2)}, u32[]{:S(2)}) collective-permute-start(bf16[272,512]{1,0:T(8,128)(2,1)} %collective-permute-done.16), channel_id=1, source_target_pairs={{0,2},{1,3},{2,0},{3,1},{4,6},{5,7},{6,4},{7,5},{8,11},{9,10},{10,... | collective-permute-start | bytes 835592 | tf_op jit(solution)/shard_map/ppermute | solution.py:124
  99.8 4.8 %collective-permute-start.13 = (bf16[272,512]{1,0:T(8,128)(2,1)}, bf16[272,512]{1,0:T(8,128)(2,1)S(1)}, u32[]{:S(2)}, u32[]{:S(2)}) collective-permute-start(bf16[272,512]{1,0:T(8,128)(2,1)} %collective-permute-done.12), channel_id=1, source_target_pairs={{0,1},{1,0},{2,3},{3,2},{4,5},{5,4},{6,7},{7,6},{8,8},{9,9},{10,10... | collective-permute-start | bytes 835592 | tf_op jit(solution)/shard_map/ppermute | solution.py:124
  104.6 4.6 %collective-permute-start.9 = (bf16[272,512]{1,0:T(8,128)(2,1)}, bf16[272,512]{1,0:T(8,128)(2,1)S(1)}, u32[]{:S(2)}, u32[]{:S(2)}) collective-permute-start(bf16[272,512]{1,0:T(8,128)(2,1)} %collective-permute-done.8), channel_id=1, source_target_pairs={{0,0},{1,1},{2,2},{3,3},{4,4},{5,5},{6,6},{7,7},{8,9},{9,8},{10,11... | collective-permute-start | bytes 835592 | tf_op jit(solution)/shard_map/ppermute | solution.py:124
  109.2 1.6 %collective-permute-done.13 = bf16[272,512]{1,0:T(8,128)(2,1)S(1)} collective-permute-done((bf16[272,512]{1,0:T(8,128)(2,1)}, bf16[272,512]{1,0:T(8,128)(2,1)S(1)}, u32[]{:S(2)}, u32[]{:S(2)}) %collective-permute-start.13) | collective-permute-done | bytes 278560 | tf_op jit(solution)/shard_map/ppermute | solution.py:124
  110.9 16.3 %collective-permute-done.9 = bf16[272,512]{1,0:T(8,128)(2,1)S(1)} collective-permute-done((bf16[272,512]{1,0:T(8,128)(2,1)}, bf16[272,512]{1,0:T(8,128)(2,1)S(1)}, u32[]{:S(2)}, u32[]{:S(2)}) %collective-permute-start.9) | collective-permute-done | bytes 278560 | tf_op jit(solution)/shard_map/ppermute | solution.py:124
  127.3 1.6 %collective-permute-start.22 = (bf16[128,512]{1,0:T(8,128)(2,1)S(1)}, bf16[128,512]{1,0:T(8,128)(2,1)S(1)}, u32[]{:S(2)}, u32[]{:S(2)}) collective-permute-start(bf16[128,512]{1,0:T(8,128)(2,1)S(1)} %constant_dynamic-slice_fusion), channel_id=1, source_target_pairs={{0,4},{4,0},{8,12},{12,8},{16,20},{20,16},{24,28},{28,24},{1,5},{5... | collective-permute-start | bytes 393224 | tf_op jit(solution)/shard_map/ppermute | solution.py:35
  (137 shorter events, 25.1 us)
Async XLA Ops:
  0.0 75.0 %copy-start = (bf16[2048,512]{1,0:T(8,128)(2,1)S(1)}, bf16[2048,512]{1,0:T(8,128)(2,1)}, u32[]{:S(2)}) copy-start(bf16[2048,512]{1,0:T(8,128)(2,1)} %param.17) | copy-start | bytes 6291460
  0.0 6.4 %copy-start.12 = (f32[32]{0:T(128)S(1)}, f32[32]{0:T(128)}, u32[]{:S(2)}) copy-start(f32[32]{0:T(128)} %param.15) | copy-start | bytes 388
  1.9 12.3 %collective-permute-start = (bf16[128,1152]{1,0:T(8,128)(2,1)S(1)}, bf16[128,1152]{1,0:T(8,128)(2,1)}, u32[]{:S(2)}, u32[]{:S(2)}) collective-permute-start(bf16[128,1152]{1,0:T(8,128)(2,1)S(1)} %pad_maximum_fusion.1), channel_id=1, source_target_pairs={{0,4},{4,0},{8,12},{12,8},{16,20},{20,16},{24,28},{28,24},{1,5},{5... | collective-permute-start | bytes 884744 | tf_op jit(solution)/shard_map/ppermute | solution.py:35
  3.4 4.4 %collective-permute-start.1 = (f32[2,16,128]{2,1,0:T(8,128)S(1)}, f32[2,16,128]{2,1,0:T(8,128)S(1)}, u32[]{:S(2)}, u32[]{:S(2)}) collective-permute-start(f32[2,16,128]{2,1,0:T(8,128)S(1)} %constant_dynamic-slice_fusion.2), channel_id=1, source_target_pairs={{0,4},{4,0},{8,12},{12,8},{16,20},{20,16},{24,28},{28,24},{1,5},{5... | collective-permute-start | bytes 49160 | tf_op jit(solution)/shard_map/ppermute | solution.py:35
  5.9 19.2 %collective-permute-start.2 = (bf16[128,1152]{1,0:T(8,128)(2,1)}, bf16[128,1152]{1,0:T(8,128)(2,1)}, u32[]{:S(2)}, u32[]{:S(2)}) collective-permute-start(bf16[128,1152]{1,0:T(8,128)(2,1)} %pad_maximum_fusion.2), channel_id=1, source_target_pairs={{0,4},{4,0},{8,12},{12,8},{16,20},{20,16},{24,28},{28,24},{1,5},{5... | collective-permute-start | bytes 884744 | tf_op jit(solution)/shard_map/ppermute | solution.py:35
  6.4 19.6 %copy-start.8 = (pred[128,128]{1,0:T(8,128)(4,1)}, pred[128,128]{1,0:T(8,128)(4,1)S(1)}, u32[]{:S(2)}) copy-start(pred[128,128]{1,0:T(8,128)(4,1)S(1)} %iota_compare_fusion.3) | copy-start | bytes 49156
  10.1 4.2 %copy-start.3 = (bf16[128,2048]{1,0:T(8,128)(2,1)S(1)}, bf16[128,2048]{1,0:T(8,128)(2,1)}, u32[]{:S(2)}) copy-start(bf16[128,2048]{1,0:T(8,128)(2,1)} %param.9) | copy-start | bytes 1572868
  12.0 3.4 %copy-start.2 = (bf16[128,128]{1,0:T(8,128)(2,1)S(1)}, bf16[128,128]{1,0:T(8,128)(2,1)}, u32[]{:S(2)}) copy-start(bf16[128,128]{1,0:T(8,128)(2,1)} %param.11) | copy-start | bytes 98308
  14.2 4.4 %copy-start.11 = (bf16[144]{0:T(256)(128)(2,1)S(1)}, bf16[144]{0:T(256)(128)(2,1)}, u32[]{:S(2)}) copy-start(bf16[144]{0:T(256)(128)(2,1)} %pad.50.clone) | copy-start | bytes 868
  15.4 9.8 %copy-start.6 = (bf16[128,128]{1,0:T(8,128)(2,1)S(1)}, bf16[128,128]{1,0:T(8,128)(2,1)}, u32[]{:S(2)}) copy-start(bf16[128,128]{1,0:T(8,128)(2,1)} %param.12) | copy-start | bytes 98308
  19.4 16.3 %collective-permute-start.5 = (bf16[144,1024]{1,0:T(8,128)(2,1)}, bf16[144,1024]{1,0:T(8,128)(2,1)}, u32[]{:S(2)}, u32[]{:S(2)}) collective-permute-start(bf16[144,1024]{1,0:T(8,128)(2,1)} %maximum_maximum_fusion), channel_id=1, source_target_pairs={{0,24},{4,28},{1,25},{5,29},{2,26},{6,30},{3,27},{7,31}} | collective-permute-start | bytes 884744 | tf_op jit(solution)/shard_map/ppermute | solution.py:69
  20.8 18.7 %collective-permute-start.4 = (bf16[144,1024]{1,0:T(8,128)(2,1)}, bf16[144,1024]{1,0:T(8,128)(2,1)}, u32[]{:S(2)}, u32[]{:S(2)}) collective-permute-start(bf16[144,1024]{1,0:T(8,128)(2,1)} %maximum_maximum_fusion), channel_id=1, source_target_pairs={{0,16},{4,20},{8,24},{12,28},{1,17},{5,21},{9,25},{13,29},{2,18},{... | collective-permute-start | bytes 884744 | tf_op jit(solution)/shard_map/ppermute | solution.py:69
  22.1 18.2 %collective-permute-start.3 = (bf16[144,1024]{1,0:T(8,128)(2,1)}, bf16[144,1024]{1,0:T(8,128)(2,1)}, u32[]{:S(2)}, u32[]{:S(2)}) collective-permute-start(bf16[144,1024]{1,0:T(8,128)(2,1)} %maximum_maximum_fusion), channel_id=1, source_target_pairs={{0,8},{4,12},{8,16},{12,20},{16,24},{20,28},{1,9},{5,13},{9,17},{1... | collective-permute-start | bytes 884744 | tf_op jit(solution)/shard_map/ppermute | solution.py:69
  29.5 11.6 %copy-start.9 = (f32[1024]{0:T(1024)S(1)}, f32[1024]{0:T(1024)}, u32[]{:S(2)}) copy-start(f32[1024]{0:T(1024)} %mul.195) | copy-start | bytes 12292
  29.5 11.6 %copy-start.10 = (f32[1024]{0:T(1024)S(1)}, f32[1024]{0:T(1024)}, u32[]{:S(2)}) copy-start(f32[1024]{0:T(1024)} %mul.223) | copy-start | bytes 12292
  45.3 16.2 %collective-permute-start.18 = (bf16[272,1024]{1,0:T(8,128)(2,1)S(1)}, bf16[272,1024]{1,0:T(8,128)(2,1)S(1)}, u32[]{:S(2)}, u32[]{:S(2)}) collective-permute-start(bf16[272,1024]{1,0:T(8,128)(2,1)S(1)} %pad_maximum_fusion), channel_id=1, source_target_pairs={{0,24},{1,17},{2,10},{3,3},{4,28},{5,21},{6,14},{7,7},{8,16},{9,25... | collective-permute-start | bytes 1671176 | tf_op jit(solution)/shard_map/ppermute | solution.py:112
  47.2 27.3 %collective-permute-start.14 = (bf16[272,1024]{1,0:T(8,128)(2,1)S(1)}, bf16[272,1024]{1,0:T(8,128)(2,1)S(1)}, u32[]{:S(2)}, u32[]{:S(2)}) collective-permute-start(bf16[272,1024]{1,0:T(8,128)(2,1)S(1)} %pad_maximum_fusion), channel_id=1, source_target_pairs={{0,16},{1,25},{2,2},{3,11},{4,20},{5,29},{6,6},{7,15},{8,24},{9,17... | collective-permute-start | bytes 1671176 | tf_op jit(solution)/shard_map/ppermute | solution.py:112
  49.8 26.1 %collective-permute-start.10 = (bf16[272,1024]{1,0:T(8,128)(2,1)S(1)}, bf16[272,1024]{1,0:T(8,128)(2,1)S(1)}, u32[]{:S(2)}, u32[]{:S(2)}) collective-permute-start(bf16[272,1024]{1,0:T(8,128)(2,1)S(1)} %pad_maximum_fusion), channel_id=1, source_target_pairs={{0,8},{1,1},{2,26},{3,19},{4,12},{5,5},{6,30},{7,23},{8,0},{9,9},{... | collective-permute-start | bytes 1671176 | tf_op jit(solution)/shard_map/ppermute | solution.py:112
  53.7 22.4 %collective-permute-start.6 = (bf16[272,1024]{1,0:T(8,128)(2,1)S(1)}, bf16[272,1024]{1,0:T(8,128)(2,1)S(1)}, u32[]{:S(2)}, u32[]{:S(2)}) collective-permute-start(bf16[272,1024]{1,0:T(8,128)(2,1)S(1)} %pad_maximum_fusion), channel_id=1, source_target_pairs={{0,0},{1,9},{2,18},{3,27},{4,4},{5,13},{6,22},{7,31},{8,8},{9,1},{... | collective-permute-start | bytes 1671176 | tf_op jit(solution)/shard_map/ppermute | solution.py:112
  61.5 15.9 %collective-permute-start.19 = (bf16[272,1024]{1,0:T(8,128)(2,1)S(1)}, bf16[272,1024]{1,0:T(8,128)(2,1)S(1)}, u32[]{:S(2)}, u32[]{:S(2)}) collective-permute-start(bf16[272,1024]{1,0:T(8,128)(2,1)S(1)} %collective-permute-done.18), channel_id=1, source_target_pairs={{0,4},{4,0},{8,12},{12,8},{16,20},{20,16},{24,28},{28,24},{1,5},{5... | collective-permute-start | bytes 1671176 | tf_op jit(solution)/shard_map/ppermute | solution.py:35
  74.5 5.3 %collective-permute-start.15 = (bf16[272,1024]{1,0:T(8,128)(2,1)S(1)}, bf16[272,1024]{1,0:T(8,128)(2,1)S(1)}, u32[]{:S(2)}, u32[]{:S(2)}) collective-permute-start(bf16[272,1024]{1,0:T(8,128)(2,1)S(1)} %collective-permute-done.14), channel_id=1, source_target_pairs={{0,4},{4,0},{8,12},{12,8},{16,20},{20,16},{24,28},{28,24},{1,5},{5... | collective-permute-start | bytes 1671176 | tf_op jit(solution)/shard_map/ppermute | solution.py:35
  75.9 7.1 %collective-permute-start.11 = (bf16[272,1024]{1,0:T(8,128)(2,1)S(1)}, bf16[272,1024]{1,0:T(8,128)(2,1)S(1)}, u32[]{:S(2)}, u32[]{:S(2)}) collective-permute-start(bf16[272,1024]{1,0:T(8,128)(2,1)S(1)} %collective-permute-done.10), channel_id=1, source_target_pairs={{0,4},{4,0},{8,12},{12,8},{16,20},{20,16},{24,28},{28,24},{1,5},{5... | collective-permute-start | bytes 1671176 | tf_op jit(solution)/shard_map/ppermute | solution.py:35
  76.0 11.4 %collective-permute-start.7 = (bf16[272,1024]{1,0:T(8,128)(2,1)S(1)}, bf16[272,1024]{1,0:T(8,128)(2,1)S(1)}, u32[]{:S(2)}, u32[]{:S(2)}) collective-permute-start(bf16[272,1024]{1,0:T(8,128)(2,1)S(1)} %collective-permute-done.6), channel_id=1, source_target_pairs={{0,4},{4,0},{8,12},{12,8},{16,20},{20,16},{24,28},{28,24},{1,5},{5... | collective-permute-start | bytes 1671176 | tf_op jit(solution)/shard_map/ppermute | solution.py:35
  77.9 11.4 %collective-permute-start.20 = (bf16[272,512]{1,0:T(8,128)(2,1)S(1)}, bf16[272,512]{1,0:T(8,128)(2,1)}, u32[]{:S(2)}, u32[]{:S(2)}) collective-permute-start(bf16[272,512]{1,0:T(8,128)(2,1)S(1)} %fusion.57), channel_id=1, source_target_pairs={{0,24},{1,17},{2,10},{3,3},{4,28},{5,21},{6,14},{7,7},{8,16},{9,25... | collective-permute-start | bytes 835592 | tf_op jit(solution)/shard_map/ppermute | solution.py:123
  80.4 17.7 %collective-permute-start.16 = (bf16[272,512]{1,0:T(8,128)(2,1)S(1)}, bf16[272,512]{1,0:T(8,128)(2,1)}, u32[]{:S(2)}, u32[]{:S(2)}) collective-permute-start(bf16[272,512]{1,0:T(8,128)(2,1)S(1)} %fusion.56), channel_id=1, source_target_pairs={{0,16},{1,25},{2,2},{3,11},{4,20},{5,29},{6,6},{7,15},{8,24},{9,17... | collective-permute-start | bytes 835592 | tf_op jit(solution)/shard_map/ppermute | solution.py:123
  83.6 16.2 %collective-permute-start.12 = (bf16[272,512]{1,0:T(8,128)(2,1)S(1)}, bf16[272,512]{1,0:T(8,128)(2,1)}, u32[]{:S(2)}, u32[]{:S(2)}) collective-permute-start(bf16[272,512]{1,0:T(8,128)(2,1)S(1)} %fusion.55), channel_id=1, source_target_pairs={{0,8},{1,1},{2,26},{3,19},{4,12},{5,5},{6,30},{7,23},{8,0},{9,9},{... | collective-permute-start | bytes 835592 | tf_op jit(solution)/shard_map/ppermute | solution.py:123
  88.0 16.6 %collective-permute-start.8 = (bf16[272,512]{1,0:T(8,128)(2,1)S(1)}, bf16[272,512]{1,0:T(8,128)(2,1)}, u32[]{:S(2)}, u32[]{:S(2)}) collective-permute-start(bf16[272,512]{1,0:T(8,128)(2,1)S(1)} %fusion.54), channel_id=1, source_target_pairs={{0,0},{1,9},{2,18},{3,27},{4,4},{5,13},{6,22},{7,31},{8,8},{9,1},{... | collective-permute-start | bytes 835592 | tf_op jit(solution)/shard_map/ppermute | solution.py:123
  89.4 19.8 %collective-permute-start.21 = (bf16[272,512]{1,0:T(8,128)(2,1)}, bf16[272,512]{1,0:T(8,128)(2,1)S(1)}, u32[]{:S(2)}, u32[]{:S(2)}) collective-permute-start(bf16[272,512]{1,0:T(8,128)(2,1)} %collective-permute-done.20), channel_id=1, source_target_pairs={{0,3},{1,2},{2,1},{3,0},{4,7},{5,6},{6,5},{7,4},{8,10},{9,11},{10,... | collective-permute-start | bytes 835592 | tf_op jit(solution)/shard_map/ppermute | solution.py:124
  98.2 11.0 %collective-permute-start.17 = (bf16[272,512]{1,0:T(8,128)(2,1)}, bf16[272,512]{1,0:T(8,128)(2,1)S(1)}, u32[]{:S(2)}, u32[]{:S(2)}) collective-permute-start(bf16[272,512]{1,0:T(8,128)(2,1)} %collective-permute-done.16), channel_id=1, source_target_pairs={{0,2},{1,3},{2,0},{3,1},{4,6},{5,7},{6,4},{7,5},{8,11},{9,10},{10,... | collective-permute-start | bytes 835592 | tf_op jit(solution)/shard_map/ppermute | solution.py:124
  99.8 11.1 %collective-permute-start.13 = (bf16[272,512]{1,0:T(8,128)(2,1)}, bf16[272,512]{1,0:T(8,128)(2,1)S(1)}, u32[]{:S(2)}, u32[]{:S(2)}) collective-permute-start(bf16[272,512]{1,0:T(8,128)(2,1)} %collective-permute-done.12), channel_id=1, source_target_pairs={{0,1},{1,0},{2,3},{3,2},{4,5},{5,4},{6,7},{7,6},{8,8},{9,9},{10,10... | collective-permute-start | bytes 835592 | tf_op jit(solution)/shard_map/ppermute | solution.py:124
  104.6 22.5 %collective-permute-start.9 = (bf16[272,512]{1,0:T(8,128)(2,1)}, bf16[272,512]{1,0:T(8,128)(2,1)S(1)}, u32[]{:S(2)}, u32[]{:S(2)}) collective-permute-start(bf16[272,512]{1,0:T(8,128)(2,1)} %collective-permute-done.8), channel_id=1, source_target_pairs={{0,0},{1,1},{2,2},{3,3},{4,4},{5,5},{6,6},{7,7},{8,9},{9,8},{10,11... | collective-permute-start | bytes 835592 | tf_op jit(solution)/shard_map/ppermute | solution.py:124
  127.3 2.6 %collective-permute-start.22 = (bf16[128,512]{1,0:T(8,128)(2,1)S(1)}, bf16[128,512]{1,0:T(8,128)(2,1)S(1)}, u32[]{:S(2)}, u32[]{:S(2)}) collective-permute-start(bf16[128,512]{1,0:T(8,128)(2,1)S(1)} %constant_dynamic-slice_fusion), channel_id=1, source_target_pairs={{0,4},{4,0},{8,12},{12,8},{16,20},{20,16},{24,28},{28,24},{1,5},{5... | collective-permute-start | bytes 393224 | tf_op jit(solution)/shard_map/ppermute | solution.py:35
  (5 other events, 11.4 us)

commit v2 on v0

v2 whole, which is shorter than its diff:
```python
import jax
import jax.numpy as jnp
from jax import lax
from jax.experimental import pallas as pl
from jax.experimental.pallas import tpu as pltpu
from jax.sharding import PartitionSpec as P

BOTH = ("seq", "head")
HIGH = lax.Precision.HIGHEST
f32, bf16 = jnp.float32, jnp.bfloat16
EXT = 16
VMEM_LIMIT = 48 * 1024 * 1024


def call(kernel, scalars, ins, in_specs, outs, out_specs, scratch=(), flops=0):
    moved = sum(a.size * a.dtype.itemsize for a in ins) + sum(
        o.size * o.dtype.itemsize for o in outs
    )
    return pl.pallas_call(
        kernel,
        out_shape=outs,
        grid_spec=pltpu.PrefetchScalarGridSpec(
            num_scalar_prefetch=1,
            grid=(1,),
            in_specs=in_specs,
            out_specs=out_specs,
            scratch_shapes=scratch,
        ),
        cost_estimate=pl.CostEstimate(flops=flops, bytes_accessed=moved, transcendentals=0),
        compiler_params=pltpu.CompilerParams(vmem_limit_bytes=VMEM_LIMIT),
    )(scalars, *ins)


def full(a):
    return pl.BlockSpec(a.shape, lambda i, s: (0,) * len(a.shape))


def lane_half(a):
    return pl.BlockSpec((a.shape[0], a.shape[1] // 2), lambda i, s: (0, s[0]))


def shape(dims, kind):
    return jax.ShapeDtypeStruct(dims, kind)


def nn(a, b, precision=None):
    return jnp.dot(a, b, preferred_element_type=f32, precision=precision)


def nt(a, b, precision=None):
    return lax.dot_general(a, b, (((1,), (1,)), ((), ())), preferred_element_type=f32, precision=precision)


def tn(a, b, precision=None):
    return lax.dot_general(a, b, (((0,), (0,)), ((), ())), preferred_element_type=f32, precision=precision)


def split2(v):
    hi = v.astype(bf16).astype(f32)
    return hi, v - hi


def half_rows(ref, k):
    v = ref[...]
    n = v.shape[0] // 2
    return jnp.where(k == 0, v[:n], v[n:])


def channel_map(heads, wide):
    head = lax.broadcasted_iota(jnp.int32, (heads, wide), 0)
    lane = lax.broadcasted_iota(jnp.int32, (heads, wide), 1)
    size = wide // heads
    return ((lane >= head * size) & (lane < (head + 1) * size)).astype(bf16)


def spread(v, spots):
    hi, lo = split2(v)
    return tn(hi.astype(bf16), spots) + tn(lo.astype(bf16), spots)


def ones_upto(rows):
    i = lax.broadcasted_iota(jnp.int32, (rows, rows), 0)
    j = lax.broadcasted_iota(jnp.int32, (rows, rows), 1)
    return (j <= i), (i <= j)


def state_kernel(s, xo, xr, bo, br, dto, dtr, ldo, ldr, msg, first):
    k = s[0]
    rows, wide = xo.shape
    _, upper = ones_upto(rows)
    got = []
    for x, b, dt, ld in ((xo, bo, dto, ldo), (xr, br, dtr, ldr)):
        dt, ld = half_rows(dt, k), half_rows(ld, k)
        spots = channel_map(ld.shape[0], wide)
        run = nn(ld, upper.astype(f32), HIGH)
        last = run[:, rows - 1 :]
        tail = jnp.exp(last - run) * dt
        scaled = (x[...].astype(f32) * spread(tail, spots)).astype(bf16)
        state = tn(b[...], scaled)
        decay = spread(jnp.exp(jnp.broadcast_to(last, (last.shape[0], 8))), spots)
        got.append((state, decay))
    (so, do), (sr, dr) = got
    even = k == 0
    s1, s2 = jnp.where(even, so, sr), jnp.where(even, sr, so)
    d2 = jnp.where(even, dr, do)
    n = s1.shape[0]
    msg[:n] = (d2[:1] * s1 + s2).astype(bf16)
    hi, lo = split2(do * dr)
    msg[n:] = jnp.concatenate([hi, lo], 0).astype(bf16)
    first[...] = s1


def unpack(ref):
    n = ref.shape[0] - EXT
    ext = ref[n:].astype(f32)
    return ref[:n].astype(f32), ext[:8] + ext[8:]


def join_kernel(s, own, other, out, *, bit):
    later = (s[1] >> bit) & 1 == 1
    so, do = unpack(own)
    st, dt = unpack(other)
    n = so.shape[0]
    s1, s2 = jnp.where(later, st, so), jnp.where(later, so, st)
    d2 = jnp.where(later, do, dt)
    out[:n] = (d2[:1] * s1 + s2).astype(bf16)
    hi, lo = split2(do * dt)
    out[n:] = jnp.concatenate([hi, lo], 0).astype(bf16)


def inside_kernel(s, xo, xr, bo, br, co, cr, dto, dtr, ldo, ldr, skip, out):
    k = s[0]
    rows, wide = xo.shape
    low, upper = ones_upto(rows)
    for turn, (x, b, c, dt, ld) in enumerate(((xo, bo, co, dto, ldo), (xr, br, cr, dtr, ldr))):
        start = pl.multiple_of(jnp.where(k == turn, 0, rows), rows)
        dt, ld = half_rows(dt, k), half_rows(ld, k)
        heads = ld.shape[0]
        size = wide // heads
        run = nn(ld, upper.astype(f32), HIGH)
        down = nt(low.astype(f32), ld, HIGH)
        scores = jnp.where(low, nt(c[...], b[...]), 0.0)
        lane = lax.broadcasted_iota(jnp.int32, (rows, 2 * size), 1)
        for pair in range(heads // 2):
            w = []
            for h in (2 * pair, 2 * pair + 1):
                gap = jnp.minimum(down[:, h : h + 1] - run[h : h + 1, :], 0.0)
                w.append((jnp.exp(gap) * scores * dt[h : h + 1, :]).astype(bf16))
            xp = x[:, 2 * pair * size : 2 * (pair + 1) * size]
            zero = jnp.zeros_like(xp)
            both = jnp.concatenate([jnp.where(lane < size, xp, zero), jnp.where(lane < size, zero, xp)], 0)
            y = nn(jnp.concatenate(w, 1), both)
            at = slice(2 * pair * size, 2 * (pair + 1) * size)
            out[pl.ds(start, rows), at] = y + skip[:, at] * xp.astype(f32)


def gate_kernel(s, inside, first, co, cr, ldo, ldr, zo, zr, gain, *rest):
    *states, out = rest
    k = s[0]
    rows, wide = zo.shape
    _, upper = ones_upto(rows)
    even = k == 0
    enter, through = jnp.zeros_like(first[...]), None
    for bit, ref in enumerate(states):
        st, dec = unpack(ref)
        dec = dec[:1]
        later = (s[1] >> bit) & 1 == 1
        add = st if through is None else st * through
        enter = enter + jnp.where(later, add, 0.0)
        dec = jnp.where(later, dec, 1.0)
        through = dec if through is None else through * dec
    ld1 = jnp.where(even, half_rows(ldo, k), half_rows(ldr, k))
    ld2 = jnp.where(even, half_rows(ldr, k), half_rows(ldo, k))
    c1, c2 = jnp.where(even, co[...], cr[...]), jnp.where(even, cr[...], co[...])
    spots = channel_map(ld1.shape[0], wide)
    ones = jnp.ones((8, wide), bf16)
    for turn, (c, ld) in enumerate(((c1, ld1), (c2, ld2))):
        run = nn(ld, upper.astype(f32), HIGH)
        decays = spread(jnp.exp(run), spots)
        carried = nn(c, enter.astype(bf16)) * decays
        y = inside[turn * rows : (turn + 1) * rows] + carried
        zf = (jnp.where(even, zo[...], zr[...]) if turn == 0 else jnp.where(even, zr[...], zo[...])).astype(f32)
        gated = y * zf / (1.0 + jnp.exp(-zf))
        sq_hi, sq_lo = split2(gated * gated)
        sq = nt(ones, sq_hi.astype(bf16)) + nt(ones, sq_lo.astype(bf16))
        base = turn * (rows + EXT)
        out[base : base + rows] = (gated * gain[...]).astype(bf16)
        hi, lo = split2(sq)
        ext = jnp.concatenate([hi, lo], 0)
        if wide > rows:
            ext = jnp.concatenate([ext, jnp.zeros((EXT, wide - rows), f32)], 1)
        out[base + rows : base + rows + EXT] = ext.astype(bf16)
        if turn == 0:
            enter = decays[rows - 1 : rows] * enter + first[...]


def project_kernel(s, *refs):
    *g, w, out = refs
    k = s[0]
    parts = len(g) // 2
    step = g[0].shape[0] * parts // 2
    rows = step - EXT
    depth = g[0].shape[1]
    here = pl.ds(pl.multiple_of(k * depth, depth), depth)
    there = pl.ds(pl.multiple_of((1 - k) * depth, depth), depth)
    ext = []
    for turn in range(2):
        if parts == 1:
            a, b, base = g[0], g[1], turn * step
        else:
            a, b, base = g[turn], g[2 + turn], 0
        got = nn(a[base : base + rows], w[here]) + nn(b[base : base + rows], w[there])
        out[turn * rows : (turn + 1) * rows] = got.astype(bf16)
        at = slice(base + rows, base + rows + EXT)
        e = a[at, :rows].astype(f32) + b[at, :rows].astype(f32)
        hi, lo = split2(e[:4] + e[8:12])
        ext += [hi, lo]
    ext = jnp.concatenate(ext, 0)
    cols = out.shape[1]
    if cols > rows:
        ext = jnp.concatenate([ext, jnp.zeros((EXT, cols - rows), f32)], 1)
    out[2 * rows :] = ext.astype(bf16)


def choose_kernel(s, *refs):
    n = (len(refs) - 1) // 2
    ins, outs, sem = refs[:n], refs[n : 2 * n], refs[2 * n]
    for m in range(n):
        for j in range(n):

            @pl.when((s[2] ^ m) == j)
            def _():
                pltpu.make_async_copy(ins[j], outs[m], sem.at[m]).start()

    for m in range(n):
        pltpu.make_async_copy(ins[0], outs[m], sem.at[m]).wait()


def sum_kernel(s, *refs, inner):
    *z, mine, theirs = refs
    k = s[0]
    rows = mine.shape[0]
    ext = sum(a[2 * rows :, :rows].astype(f32) for a in z)
    i = lax.broadcasted_iota(jnp.int32, (rows, rows), 0)
    j = lax.broadcasted_iota(jnp.int32, (rows, rows), 1)
    done = []
    for turn in range(2):
        e = ext[turn * 8 : turn * 8 + 8]
        sq = e[:1] + e[4:5]
        row = lax.rsqrt(sq / inner + 1e-5)
        col = jnp.sum(jnp.where(i == j, jnp.broadcast_to(row, (rows, rows)), 0.0), axis=1, keepdims=True)
        total = sum(a[turn * rows : (turn + 1) * rows].astype(f32) for a in z)
        done.append((total * col).astype(bf16))
    even = k == 0
    mine[...] = jnp.where(even, done[0], done[1])
    theirs[...] = jnp.where(even, done[1], done[0])


def body(n, n_head, signal, gate_input, state_in, state_out, step_size, log_decay, skip_gain, norm_gain, out_weight):
    rows = signal.shape[0]
    heads = log_decay.shape[0]
    wide = signal.shape[1] // 2
    size = signal.shape[1] // heads
    states = state_in.shape[1]
    cols = out_weight.shape[1]
    place, z = lax.axis_index("seq"), lax.axis_index("head")
    k, chip = place % 2, place // 2
    s = jnp.stack([k, chip, chip ^ z]).astype(jnp.int32)

    def swap(a):
        return lax.ppermute(a, "seq", [(i, i ^ 1) for i in range(2 * n)])

    def across(a, j):
        return lax.ppermute(a, "seq", [(i, i ^ (2 * j)) for i in range(2 * n)])

    x2, b2 = swap(signal), swap(state_in)
    dt2, ld2 = swap(step_size), swap(log_decay)
    z2, c2 = swap(gate_input), swap(state_out)
    skip = jnp.repeat(skip_gain, size).reshape(1, 2 * wide)
    gain = norm_gain.reshape(1, 2 * wide)

    ins = (signal, x2, state_in, b2, step_size, dt2, log_decay, ld2)
    specs = [lane_half(signal)] * 2 + [full(state_in)] * 2 + [full(step_size)] * 4
    msg_shape = shape((states + EXT, wide), bf16)
    first_shape = shape((states, wide), f32)
    msg, first = call(state_kernel, s, ins, specs, [msg_shape, first_shape], [full(msg_shape), full(first_shape)])
    got = []
    bits = n.bit_length() - 1
    for bit in range(bits):
        step = 1 << bit
        pairs = [(i, i ^ (2 * step)) for i in range(2 * n)]
        if bit == bits - 1:
            pairs = [p for p in pairs if p[1] > p[0]]
        new = lax.ppermute(msg, "seq", pairs)
        got.append(new)
        if bit == 0:
            ins = (signal, x2, state_in, b2, state_out, c2, step_size, dt2, log_decay, ld2, skip)
            specs = [lane_half(signal)] * 2 + [full(state_in)] * 4 + [full(step_size)] * 4 + [lane_half(skip)]
            inside_shape = shape((2 * rows, wide), f32)
            (inside,) = call(inside_kernel, s, ins, specs, [inside_shape], [full(inside_shape)])
        if bit < bits - 1:

            def join(*refs, bit=bit):
                join_kernel(*refs, bit=bit)

            (msg,) = call(join, s, (msg, new), [full(msg)] * 2, [msg_shape], [full(msg_shape)])

    ins = (inside, first, state_out, c2, log_decay, ld2, gate_input, z2, gain, *got)
    specs = [full(inside), full(first), full(state_out), full(c2), full(log_decay), full(ld2)]
    specs += [lane_half(gate_input)] * 2 + [lane_half(gain)] + [full(m) for m in got]
    g_shape = shape((2 * (rows + EXT), wide), bf16)
    (g,) = call(gate_kernel, s, ins, specs, [g_shape], [full(g_shape)])

    p_shape = shape((2 * rows + EXT, cols), bf16)

    def project(*g):
        ins = (*g, *[swap(a) for a in g], out_weight)
        return call(project_kernel, s, ins, [full(a) for a in ins], [p_shape], [full(p_shape)])[0]

    hidden = [(g,)] + [None] * (n - 1)
    if n == 4:
        gx, gy = across(g, 1), across(g, 2)
        hidden[1], hidden[2] = (gx,), (gy,)
        hidden[3] = (across(gx[: rows + EXT], 2), across(gy[rows + EXT :], 1))
    else:
        for j in range(1, n):
            hidden[j] = (across(g, j),)
    blocks = [project(*hidden[j]) for j in range(n)]
    blocks = [blocks[0]] + [across(blocks[j], j) for j in range(1, n)]

    any_spec = pl.BlockSpec(memory_space=pl.ANY)
    blocks = call(
        choose_kernel, s, blocks, [any_spec] * n, [p_shape] * n, [any_spec] * n,
        scratch=[pltpu.SemaphoreType.DMA((n,))],
    )
    blocks = [blocks[0]] + [
        lax.ppermute(blocks[m], "head", [(i, i ^ m) for i in range(n)]) for m in range(1, n)
    ]
    half = shape((rows, cols), bf16)

    def add(*refs):
        sum_kernel(*refs, inner=2 * wide * n_head)

    mine, theirs = call(add, s, blocks, [full(p_shape)] * n, [half] * 2, [full(half)] * 2)
    other = swap(theirs)
    return jnp.where(k == 0, jnp.concatenate([mine, other], 1), jnp.concatenate([other, mine], 1))


def solution(mesh):
    n, n_head = mesh.shape["seq"] // 2, mesh.shape["head"]
    assert n == n_head and n & (n - 1) == 0
    in_specs = (
        P("seq", "head"),
        P("seq", "head"),
        P("seq", None),
        P("seq", None),
        P("head", "seq"),
        P("head", "seq"),
        P("head"),
        P("head"),
        P("head", "seq"),
    )

    def run(*args):
        return body(n, n_head, *args)

    return jax.shard_map(run, mesh=mesh, in_specs=in_specs, out_specs=P("seq", "head"), check_vma=False)
```

time: 191 us -> 111 us (0.58)
  the two profiles are of different devices: /device:TPU:0 before, /device:TPU:9 now
where the time goes in v2:
time: 111 us; the launch traced here: 110 us
  waiting for transfers between devices  61.1 us (55%)
  starting transfers between devices  22.4 us (20%)
  Pallas kernels  15.3 us (14%)
  local copies, waits for them, and re-layouts  10.3 us (9%)
    ppermute x7, waiting for transfers between devices, across(): return lax.ppermute(a, 'seq', [(i, i ^ 2 * j) for i in range(2 * n)])  27.1 us
    ppermute x3, waiting for transfers between devices, body(): lax.ppermute(blocks[m], 'head', [(i, i ^ m) for i in range(n)])  23.9 us
    pallas_call x10, Pallas kernels, call(): pl.pallas_call(kernel, out_shape=outs, grid_spec=pltpu.PrefetchScalarGrid...  15.3 us
    ppermute x12, starting transfers between devices, swap(): return lax.ppermute(a, 'seq', [(i, i ^ 1) for i in range(2 * n)])  9.61 us
    unnamed x42, local copies, waits for them, and re-layouts  7.57 us
    ppermute x2, waiting for transfers between devices, body(): new = lax.ppermute(msg, 'seq', pairs)  6.54 us
    ppermute x7, starting transfers between devices, across(): return lax.ppermute(a, 'seq', [(i, i ^ 2 * j) for i in range(2 * n)])  5.66 us
    ppermute x2, starting transfers between devices, body(): new = lax.ppermute(msg, 'seq', pairs)  4.46 us
  transfers between devices with their start and end apart: 24, of which 12 were waited for; matrix products, arithmetic and copies ran while one was open for 3% of the time, Pallas kernels for 8%

profile of v2, /device:TPU:9, one launch (start us, length us, event | category | flops | bytes accessed | tf_op | source)
XLA Modules:
  0.0 110.2 jit_solution(13921529274733164219)
XLA Ops:
  1.3 1.1 %collective-permute-done.3.dtr = f32[32,128]{1,0:T(8,128)S(1)} collective-permute-done((f32[32,128]{1,0:T(8,128)}, f32[32,128]{1,0:T(8,128)S(1)}, u32[]{:S(2)}, u32[]{:S(2)}) %collective-permute-start.3) | collective-permute-done | bytes 16416 | tf_op jit(solution)/shard_map/ppermute | solution.py:271
  2.6 1.1 copy-done.1
  5.9 2.2 %shard_map.92 = (bf16[144,1024]{1,0:T(8,128)(2,1)S(1)}, f32[128,1024]{1,0:T(8,128)S(1)}) custom-call(s32[3]{0:T(128)S(1)} %pad_add_fusion.s.refs_0_, bf16[128,2048]{1,0:T(8,128)(2,1)S(1)} %copy-done.1, bf16[128,2048]{1,0:T(8,128)(2,1)S(1)} %collective-permute-done.xr, bf16[128,128]{1,0:T(8,128)(2,1)S(1)} %copy-done.8, ...), custom_call_target="tpu_custom_call" | custom-call | bytes 1998848 | tf_op jit(solution)/shard_map/pallas_call | solution.py:19
  8.1 1.3 %collective-permute-start.6 = (bf16[144,1024]{1,0:T(8,128)(2,1)S(1)}, bf16[144,1024]{1,0:T(8,128)(2,1)S(1)}, u32[]{:S(2)}, u32[]{:S(2)}) collective-permute-start(bf16[144,1024]{1,0:T(8,128)(2,1)S(1)} %get-tuple-element.14.refs_1_), channel_id=1, source_target_pairs={{0,8},{4,12},{8,0},{12,4},{16,24},{20,28},{24,16},{28,20},{1,9},{5... | collective-permute-start | bytes 884744 | tf_op jit(solution)/shard_map/ppermute | solution.py:294
  10.0 6.5 %collective-permute-done.6.refs_2_.rest_0_ = bf16[144,1024]{1,0:T(8,128)(2,1)S(1)} collective-permute-done((bf16[144,1024]{1,0:T(8,128)(2,1)S(1)}, bf16[144,1024]{1,0:T(8,128)(2,1)S(1)}, u32[]{:S(2)}, u32[]{:S(2)}) %collective-permute-start.6) | collective-permute-done | bytes 294944 | tf_op jit(solution)/shard_map/ppermute | solution.py:294
  17.2 3.2 %collective-permute-start.7 = (bf16[144,1024]{1,0:T(8,128)(2,1)S(1)}, bf16[144,1024]{1,0:T(8,128)(2,1)S(1)}, u32[]{:S(2)}, u32[]{:S(2)}) collective-permute-start(bf16[144,1024]{1,0:T(8,128)(2,1)S(1)} %shard_map.93), channel_id=1, source_target_pairs={{0,16},{4,20},{8,24},{12,28},{1,17},{5,21},{9,25},{13,29},{2,18},{... | collective-permute-start | bytes 884744 | tf_op jit(solution)/shard_map/ppermute | solution.py:294
  20.4 1.4 %collective-permute-start.2 = (bf16[128,128]{1,0:T(8,128)(2,1)}, bf16[128,128]{1,0:T(8,128)(2,1)}, u32[]{:S(2)}, u32[]{:S(2)}) collective-permute-start(bf16[128,128]{1,0:T(8,128)(2,1)} %co.3), channel_id=1, source_target_pairs={{0,4},{4,0},{8,12},{12,8},{16,20},{20,16},{24,28},{28,24},{1,5},{5... | collective-permute-start | bytes 98312 | tf_op jit(solution)/shard_map/ppermute | solution.py:271
  21.8 1.3 %broadcast_in_dim.3 = f32[32,64]{1,0:T(8,128)} broadcast(f32[32]{0:T(128)} %param.15), dimensions={0} | broadcast | bytes 8320 | tf_op jit(solution)/shard_map/broadcast_in_dim | solution.py:279
  23.1 1.4 %reshape_reshape.3.skip = f32[1,2048]{1,0:T(1,128)} reshape(f32[32,64]{1,0:T(8,128)} %broadcast_in_dim.3) | data formatting | bytes 16384 | tf_op jit(solution)/shard_map/reshape;reshape | solution.py:279
  28.8 2.8 %shard_map.91.inside = f32[256,1024]{1,0:T(8,128)S(1)} custom-call(s32[3]{0:T(128)S(1)} %copy-done.17, bf16[128,2048]{1,0:T(8,128)(2,1)S(1)} %copy-done.2, bf16[128,2048]{1,0:T(8,128)(2,1)S(1)} %collective-permute-done.xr, bf16[128,128]{1,0:T(8,128)(2,1)S(1)} %copy-done.9, bf16[128,128]{1,0:T(8,128)(2,1)S(1)} %copy-done.11, bf16[128,128]{1,0:T(8,128)(2,1)S(1)} %copy-done.6, ...), custom_call_target="tpu_custom_call" | custom-call | bytes 2301952 | tf_op jit(solution)/shard_map/pallas_call | solution.py:19
  31.7 3.0 %shard_map.94.refs_0_ = bf16[288,1024]{1,0:T(8,128)(2,1)S(1)} custom-call(s32[3]{0:T(128)S(1)} %copy-done.18, f32[256,1024]{1,0:T(8,128)S(1)} %shard_map.91.inside, f32[128,1024]{1,0:T(8,128)S(1)} %get-tuple-element.13.first, bf16[128,128]{1,0:T(8,128)(2,1)S(1)} %copy-done.7, bf16[128,128]{1,0:T(8,128)(2,1)} %collective-permute-done.2.cr, ...), custom_call_target="tpu_custom_call" | custom-call | bytes 3907584 | tf_op jit(solution)/shard_map/pallas_call | solution.py:19
  34.7 1.3 %collective-permute-start.9 = (bf16[288,1024]{1,0:T(8,128)(2,1)S(1)}, bf16[288,1024]{1,0:T(8,128)(2,1)S(1)}, u32[]{:S(2)}, u32[]{:S(2)}) collective-permute-start(bf16[288,1024]{1,0:T(8,128)(2,1)S(1)} %shard_map.94.refs_0_), channel_id=1, source_target_pairs={{0,8},{4,12},{8,0},{12,4},{16,24},{20,28},{24,16},{28,20},{1,9},{5... | collective-permute-start | bytes 1769480 | tf_op jit(solution)/shard_map/ppermute | solution.py:274
  35.9 13.7 %collective-permute-done.12.refs_0_ = bf16[288,1024]{1,0:T(8,128)(2,1)S(1)} collective-permute-done((bf16[288,1024]{1,0:T(8,128)(2,1)S(1)}, bf16[288,1024]{1,0:T(8,128)(2,1)S(1)}, u32[]{:S(2)}, u32[]{:S(2)}) %collective-permute-start.12) | collective-permute-done | bytes 589856 | tf_op jit(solution)/shard_map/ppermute | solution.py:274
  49.7 1.3 %collective-permute-start.16 = (bf16[144,1024]{1,0:T(8,128)(2,1)S(1)}, bf16[144,1024]{1,0:T(8,128)(2,1)S(1)}, u32[]{:S(2)}, u32[]{:S(2)}) collective-permute-start(bf16[144,1024]{1,0:T(8,128)(2,1)S(1)} %slice.9), channel_id=1, source_target_pairs={{0,8},{4,12},{8,0},{12,4},{16,24},{20,28},{24,16},{28,20},{1,9},{5... | collective-permute-start | bytes 884744 | tf_op jit(solution)/shard_map/ppermute | solution.py:274
  51.2 1.2 %collective-permute-start.13 = (bf16[288,1024]{1,0:T(8,128)(2,1)S(1)}, bf16[288,1024]{1,0:T(8,128)(2,1)S(1)}, u32[]{:S(2)}, u32[]{:S(2)}) collective-permute-start(bf16[288,1024]{1,0:T(8,128)(2,1)S(1)} %collective-permute-done.12.refs_0_), channel_id=1, source_target_pairs={{0,4},{4,0},{8,12},{12,8},{16,20},{20,16},{24,28},{28,24},{1,5},{5... | collective-permute-start | bytes 1769480 | tf_op jit(solution)/shard_map/ppermute | solution.py:271
  52.9 4.6 %collective-permute-done.16.refs_1_ = bf16[144,1024]{1,0:T(8,128)(2,1)S(1)} collective-permute-done((bf16[144,1024]{1,0:T(8,128)(2,1)S(1)}, bf16[144,1024]{1,0:T(8,128)(2,1)S(1)}, u32[]{:S(2)}, u32[]{:S(2)}) %collective-permute-start.16) | collective-permute-done | bytes 294944 | tf_op jit(solution)/shard_map/ppermute | solution.py:274
  57.5 1.7 %collective-permute-start.18 = (bf16[144,1024]{1,0:T(8,128)(2,1)S(1)}, bf16[144,1024]{1,0:T(8,128)(2,1)S(1)}, u32[]{:S(2)}, u32[]{:S(2)}) collective-permute-start(bf16[144,1024]{1,0:T(8,128)(2,1)S(1)} %collective-permute-done.16.refs_1_), channel_id=1, source_target_pairs={{0,4},{4,0},{8,12},{12,8},{16,20},{20,16},{24,28},{28,24},{1,5},{5... | collective-permute-start | bytes 884744 | tf_op jit(solution)/shard_map/ppermute | solution.py:271
  59.2 1.3 %collective-permute-start.17 = (bf16[144,1024]{1,0:T(8,128)(2,1)S(1)}, bf16[144,1024]{1,0:T(8,128)(2,1)S(1)}, u32[]{:S(2)}, u32[]{:S(2)}) collective-permute-start(bf16[144,1024]{1,0:T(8,128)(2,1)S(1)} %collective-permute-done.15.refs_0_), channel_id=1, source_target_pairs={{0,4},{4,0},{8,12},{12,8},{16,20},{20,16},{24,28},{28,24},{1,5},{5... | collective-permute-start | bytes 884744 | tf_op jit(solution)/shard_map/ppermute | solution.py:271
  60.5 1.2 %collective-permute-done.17.refs_2_ = bf16[144,1024]{1,0:T(8,128)(2,1)S(1)} collective-permute-done((bf16[144,1024]{1,0:T(8,128)(2,1)S(1)}, bf16[144,1024]{1,0:T(8,128)(2,1)S(1)}, u32[]{:S(2)}, u32[]{:S(2)}) %collective-permute-start.17) | collective-permute-done | bytes 294944 | tf_op jit(solution)/shard_map/ppermute | solution.py:271
  61.7 1.3 %shard_map.98 = bf16[272,512]{1,0:T(8,128)(2,1)S(1)} custom-call(s32[3]{0:T(128)S(1)} %copy-done.18, bf16[144,1024]{1,0:T(8,128)(2,1)S(1)} %collective-permute-done.15.refs_0_, bf16[144,1024]{1,0:T(8,128)(2,1)S(1)} %collective-permute-done.16.refs_1_, bf16[144,1024]{1,0:T(8,128)(2,1)S(1)} %collective-permute-done.17.refs_2_, ...), custom_call_target="tpu_custom_call" | custom-call | bytes 3555328 | tf_op jit(solution)/shard_map/pallas_call | solution.py:19
  63.8 1.3 %shard_map.97 = bf16[272,512]{1,0:T(8,128)(2,1)S(1)} custom-call(s32[3]{0:T(128)S(1)} %copy-done.18, bf16[288,1024]{1,0:T(8,128)(2,1)S(1)} %collective-permute-done.12.refs_0_, bf16[288,1024]{1,0:T(8,128)(2,1)S(1)} %collective-permute-done.13.refs_1_, bf16[2048,512]{1,0:T(8,128)(2,1)S(1)} %copy-done), custom_call_target="tpu_custom_call" | custom-call | bytes 3555328 | tf_op jit(solution)/shard_map/pallas_call | solution.py:19
  65.9 1.3 %shard_map.96 = bf16[272,512]{1,0:T(8,128)(2,1)S(1)} custom-call(s32[3]{0:T(128)S(1)} %copy-done.18, bf16[288,1024]{1,0:T(8,128)(2,1)S(1)} %collective-permute-done.9.refs_0_, bf16[288,1024]{1,0:T(8,128)(2,1)S(1)} %collective-permute-done.10.refs_1_, bf16[2048,512]{1,0:T(8,128)(2,1)S(1)} %copy-done), custom_call_target="tpu_custom_call" | custom-call | bytes 3555328 | tf_op jit(solution)/shard_map/pallas_call | solution.py:19
  67.1 1.2 %collective-permute-start.11 = (bf16[272,512]{1,0:T(8,128)(2,1)S(1)}, bf16[272,512]{1,0:T(8,128)(2,1)S(1)}, u32[]{:S(2)}, u32[]{:S(2)}) collective-permute-start(bf16[272,512]{1,0:T(8,128)(2,1)S(1)} %shard_map.96), channel_id=1, source_target_pairs={{0,8},{4,12},{8,0},{12,4},{16,24},{20,28},{24,16},{28,20},{1,9},{5... | collective-permute-start | bytes 835592 | tf_op jit(solution)/shard_map/ppermute | solution.py:274
  68.3 1.3 %shard_map.95.refs_0_ = bf16[272,512]{1,0:T(8,128)(2,1)S(1)} custom-call(s32[3]{0:T(128)S(1)} %copy-done.18, bf16[288,1024]{1,0:T(8,128)(2,1)S(1)} %shard_map.94.refs_0_, bf16[288,1024]{1,0:T(8,128)(2,1)S(1)} %collective-permute-done.8.refs_1_, bf16[2048,512]{1,0:T(8,128)(2,1)S(1)} %copy-done), custom_call_target="tpu_custom_call" | custom-call | bytes 3555328 | tf_op jit(solution)/shard_map/pallas_call | solution.py:19
  69.6 2.2 %collective-permute-done.19.refs_3_ = bf16[272,512]{1,0:T(8,128)(2,1)S(1)} collective-permute-done((bf16[272,512]{1,0:T(8,128)(2,1)S(1)}, bf16[272,512]{1,0:T(8,128)(2,1)S(1)}, u32[]{:S(2)}, u32[]{:S(2)}) %collective-permute-start.19) | collective-permute-done | bytes 278560 | tf_op jit(solution)/shard_map/ppermute | solution.py:274
  71.8 6.6 %collective-permute-done.14.refs_2_ = bf16[272,512]{1,0:T(8,128)(2,1)S(1)} collective-permute-done((bf16[272,512]{1,0:T(8,128)(2,1)S(1)}, bf16[272,512]{1,0:T(8,128)(2,1)S(1)}, u32[]{:S(2)}, u32[]{:S(2)}) %collective-permute-start.14) | collective-permute-done | bytes 278560 | tf_op jit(solution)/shard_map/ppermute | solution.py:274
  79.6 2.3 %collective-permute-start.21 = (bf16[272,512]{1,0:T(8,128)(2,1)S(1)}, bf16[272,512]{1,0:T(8,128)(2,1)S(1)}, u32[]{:S(2)}, u32[]{:S(2)}) collective-permute-start(bf16[272,512]{1,0:T(8,128)(2,1)S(1)} %get-tuple-element.17), channel_id=1, source_target_pairs={{0,2},{1,3},{2,0},{3,1},{4,6},{5,7},{6,4},{7,5},{8,10},{9,11},{10,... | collective-permute-start | bytes 835592 | tf_op jit(solution)/shard_map/ppermute | solution.py:337
  82.0 8.4 %collective-permute-done.20.refs_2_ = bf16[272,512]{1,0:T(8,128)(2,1)S(1)} collective-permute-done((bf16[272,512]{1,0:T(8,128)(2,1)S(1)}, bf16[272,512]{1,0:T(8,128)(2,1)S(1)}, u32[]{:S(2)}, u32[]{:S(2)}) %collective-permute-start.20) | collective-permute-done | bytes 278560 | tf_op jit(solution)/shard_map/ppermute | solution.py:337
  90.4 3.8 %collective-permute-done.21.refs_3_ = bf16[272,512]{1,0:T(8,128)(2,1)S(1)} collective-permute-done((bf16[272,512]{1,0:T(8,128)(2,1)S(1)}, bf16[272,512]{1,0:T(8,128)(2,1)S(1)}, u32[]{:S(2)}, u32[]{:S(2)}) %collective-permute-start.21) | collective-permute-done | bytes 278560 | tf_op jit(solution)/shard_map/ppermute | solution.py:337
  94.1 11.8 %collective-permute-done.22.refs_4_ = bf16[272,512]{1,0:T(8,128)(2,1)S(1)} collective-permute-done((bf16[272,512]{1,0:T(8,128)(2,1)S(1)}, bf16[272,512]{1,0:T(8,128)(2,1)S(1)}, u32[]{:S(2)}, u32[]{:S(2)}) %collective-permute-start.22) | collective-permute-done | bytes 278560 | tf_op jit(solution)/shard_map/ppermute | solution.py:337
  106.7 1.7 %collective-permute-start.23 = (bf16[128,512]{1,0:T(8,128)(2,1)S(1)}, bf16[128,512]{1,0:T(8,128)(2,1)S(1)}, u32[]{:S(2)}, u32[]{:S(2)}) collective-permute-start(bf16[128,512]{1,0:T(8,128)(2,1)S(1)} %get-tuple-element.20), channel_id=1, source_target_pairs={{0,4},{4,0},{8,12},{12,8},{16,20},{20,16},{24,28},{28,24},{1,5},{5... | collective-permute-start | bytes 393224 | tf_op jit(solution)/shard_map/ppermute | solution.py:271
  108.4 1.0 collective-permute-done.23
  (74 shorter events, 14.5 us)
Async XLA Ops:
  0.0 24.5 %copy-start.13 = (f32[32,128]{1,0:T(8,128)S(1)}, f32[32,128]{1,0:T(8,128)}, u32[]{:S(2)}) copy-start(f32[32,128]{1,0:T(8,128)} %dto.3) | copy-start | bytes 49156
  0.0 24.5 %copy-start.5 = (f32[32,128]{1,0:T(8,128)S(1)}, f32[32,128]{1,0:T(8,128)}, u32[]{:S(2)}) copy-start(f32[32,128]{1,0:T(8,128)} %ldo.5) | copy-start | bytes 49156
  0.0 2.6 %collective-permute-start = (bf16[128,2048]{1,0:T(8,128)(2,1)}, bf16[128,2048]{1,0:T(8,128)(2,1)S(1)}, u32[]{:S(2)}, u32[]{:S(2)}) collective-permute-start(bf16[128,2048]{1,0:T(8,128)(2,1)} %xo.3), channel_id=1, source_target_pairs={{0,4},{4,0},{8,12},{12,8},{16,20},{20,16},{24,28},{28,24},{1,5},{5... | collective-permute-start | bytes 1572872 | tf_op jit(solution)/shard_map/ppermute | solution.py:271
  0.7 1.8 %collective-permute-start.3 = (f32[32,128]{1,0:T(8,128)}, f32[32,128]{1,0:T(8,128)S(1)}, u32[]{:S(2)}, u32[]{:S(2)}) collective-permute-start(f32[32,128]{1,0:T(8,128)} %dto.3), channel_id=1, source_target_pairs={{0,4},{4,0},{8,12},{12,8},{16,20},{20,16},{24,28},{28,24},{1,5},{5... | collective-permute-start | bytes 49160 | tf_op jit(solution)/shard_map/ppermute | solution.py:271
  0.8 1.7 %collective-permute-start.4 = (f32[32,128]{1,0:T(8,128)}, f32[32,128]{1,0:T(8,128)S(1)}, u32[]{:S(2)}, u32[]{:S(2)}) collective-permute-start(f32[32,128]{1,0:T(8,128)} %ldo.5), channel_id=1, source_target_pairs={{0,4},{4,0},{8,12},{12,8},{16,20},{20,16},{24,28},{28,24},{1,5},{5... | collective-permute-start | bytes 49160 | tf_op jit(solution)/shard_map/ppermute | solution.py:271
  1.2 1.4 %collective-permute-start.1 = (bf16[128,128]{1,0:T(8,128)(2,1)}, bf16[128,128]{1,0:T(8,128)(2,1)S(1)}, u32[]{:S(2)}, u32[]{:S(2)}) collective-permute-start(bf16[128,128]{1,0:T(8,128)(2,1)} %bo.3), channel_id=1, source_target_pairs={{0,4},{4,0},{8,12},{12,8},{16,20},{20,16},{24,28},{28,24},{1,5},{5... | collective-permute-start | bytes 98312 | tf_op jit(solution)/shard_map/ppermute | solution.py:271
  1.3 19.0 %copy-start.16 = (s32[3]{0:T(128)}, s32[3]{0:T(128)S(1)}, u32[]{:S(2)}) copy-start(s32[3]{0:T(128)S(1)} %pad_add_fusion.s.refs_0_) | copy-start | bytes 40
  2.5 5.6 %copy-start.14 = (f32[32,128]{1,0:T(8,128)}, f32[32,128]{1,0:T(8,128)S(1)}, u32[]{:S(2)}) copy-start(f32[32,128]{1,0:T(8,128)S(1)} %collective-permute-done.3.dtr) | copy-start | bytes 49156
  2.6 5.5 %copy-start.10 = (bf16[128,128]{1,0:T(8,128)(2,1)}, bf16[128,128]{1,0:T(8,128)(2,1)S(1)}, u32[]{:S(2)}) copy-start(bf16[128,128]{1,0:T(8,128)(2,1)S(1)} %collective-permute-done.1.br) | copy-start | bytes 98308
  5.9 18.7 %copy-start.2 = (bf16[128,2048]{1,0:T(8,128)(2,1)S(1)}, bf16[128,2048]{1,0:T(8,128)(2,1)}, u32[]{:S(2)}) copy-start(bf16[128,2048]{1,0:T(8,128)(2,1)} %xo.3) | copy-start | bytes 1572868
  5.9 25.8 %copy-start.3 = (bf16[128,2048]{1,0:T(8,128)(2,1)S(1)}, bf16[128,2048]{1,0:T(8,128)(2,1)}, u32[]{:S(2)}) copy-start(bf16[128,2048]{1,0:T(8,128)(2,1)} %zo.1) | copy-start | bytes 1572868
  8.1 8.4 %collective-permute-start.6 = (bf16[144,1024]{1,0:T(8,128)(2,1)S(1)}, bf16[144,1024]{1,0:T(8,128)(2,1)S(1)}, u32[]{:S(2)}, u32[]{:S(2)}) collective-permute-start(bf16[144,1024]{1,0:T(8,128)(2,1)S(1)} %get-tuple-element.14.refs_1_), channel_id=1, source_target_pairs={{0,8},{4,12},{8,0},{12,4},{16,24},{20,28},{24,16},{28,20},{1,9},{5... | collective-permute-start | bytes 884744 | tf_op jit(solution)/shard_map/ppermute | solution.py:294
  9.4 22.2 %collective-permute-start.5 = (bf16[128,2048]{1,0:T(8,128)(2,1)}, bf16[128,2048]{1,0:T(8,128)(2,1)S(1)}, u32[]{:S(2)}, u32[]{:S(2)}) collective-permute-start(bf16[128,2048]{1,0:T(8,128)(2,1)} %zo.1), channel_id=1, source_target_pairs={{0,4},{4,0},{8,12},{12,8},{16,20},{20,16},{24,28},{28,24},{1,5},{5... | collective-permute-start | bytes 1572872 | tf_op jit(solution)/shard_map/ppermute | solution.py:271
  17.2 14.5 %collective-permute-start.7 = (bf16[144,1024]{1,0:T(8,128)(2,1)S(1)}, bf16[144,1024]{1,0:T(8,128)(2,1)S(1)}, u32[]{:S(2)}, u32[]{:S(2)}) collective-permute-start(bf16[144,1024]{1,0:T(8,128)(2,1)S(1)} %shard_map.93), channel_id=1, source_target_pairs={{0,16},{4,20},{8,24},{12,28},{1,17},{5,21},{9,25},{13,29},{2,18},{... | collective-permute-start | bytes 884744 | tf_op jit(solution)/shard_map/ppermute | solution.py:294
  20.4 4.2 %collective-permute-start.2 = (bf16[128,128]{1,0:T(8,128)(2,1)}, bf16[128,128]{1,0:T(8,128)(2,1)}, u32[]{:S(2)}, u32[]{:S(2)}) collective-permute-start(bf16[128,128]{1,0:T(8,128)(2,1)} %co.3), channel_id=1, source_target_pairs={{0,4},{4,0},{8,12},{12,8},{16,20},{20,16},{24,28},{28,24},{1,5},{5... | collective-permute-start | bytes 98312 | tf_op jit(solution)/shard_map/ppermute | solution.py:271
  31.7 30.0 %copy-start = (bf16[2048,512]{1,0:T(8,128)(2,1)S(1)}, bf16[2048,512]{1,0:T(8,128)(2,1)}, u32[]{:S(2)}) copy-start(bf16[2048,512]{1,0:T(8,128)(2,1)} %refs_4_.1) | copy-start | bytes 6291460
  34.7 15.0 %collective-permute-start.12 = (bf16[288,1024]{1,0:T(8,128)(2,1)S(1)}, bf16[288,1024]{1,0:T(8,128)(2,1)S(1)}, u32[]{:S(2)}, u32[]{:S(2)}) collective-permute-start(bf16[288,1024]{1,0:T(8,128)(2,1)S(1)} %shard_map.94.refs_0_), channel_id=1, source_target_pairs={{0,16},{4,20},{8,24},{12,28},{16,0},{20,4},{24,8},{28,12},{1,17},{... | collective-permute-start | bytes 1769480 | tf_op jit(solution)/shard_map/ppermute | solution.py:274
  34.7 16.3 %collective-permute-start.9 = (bf16[288,1024]{1,0:T(8,128)(2,1)S(1)}, bf16[288,1024]{1,0:T(8,128)(2,1)S(1)}, u32[]{:S(2)}, u32[]{:S(2)}) collective-permute-start(bf16[288,1024]{1,0:T(8,128)(2,1)S(1)} %shard_map.94.refs_0_), channel_id=1, source_target_pairs={{0,8},{4,12},{8,0},{12,4},{16,24},{20,28},{24,16},{28,20},{1,9},{5... | collective-permute-start | bytes 1769480 | tf_op jit(solution)/shard_map/ppermute | solution.py:274
  49.7 7.8 %collective-permute-start.16 = (bf16[144,1024]{1,0:T(8,128)(2,1)S(1)}, bf16[144,1024]{1,0:T(8,128)(2,1)S(1)}, u32[]{:S(2)}, u32[]{:S(2)}) collective-permute-start(bf16[144,1024]{1,0:T(8,128)(2,1)S(1)} %slice.9), channel_id=1, source_target_pairs={{0,8},{4,12},{8,0},{12,4},{16,24},{20,28},{24,16},{28,20},{1,9},{5... | collective-permute-start | bytes 884744 | tf_op jit(solution)/shard_map/ppermute | solution.py:274
  51.0 8.2 %collective-permute-start.15 = (bf16[144,1024]{1,0:T(8,128)(2,1)S(1)}, bf16[144,1024]{1,0:T(8,128)(2,1)S(1)}, u32[]{:S(2)}, u32[]{:S(2)}) collective-permute-start(bf16[144,1024]{1,0:T(8,128)(2,1)S(1)} %slice.8), channel_id=1, source_target_pairs={{0,16},{4,20},{8,24},{12,28},{16,0},{20,4},{24,8},{28,12},{1,17},{... | collective-permute-start | bytes 884744 | tf_op jit(solution)/shard_map/ppermute | solution.py:274
  51.2 12.5 %collective-permute-start.13 = (bf16[288,1024]{1,0:T(8,128)(2,1)S(1)}, bf16[288,1024]{1,0:T(8,128)(2,1)S(1)}, u32[]{:S(2)}, u32[]{:S(2)}) collective-permute-start(bf16[288,1024]{1,0:T(8,128)(2,1)S(1)} %collective-permute-done.12.refs_0_), channel_id=1, source_target_pairs={{0,4},{4,0},{8,12},{12,8},{16,20},{20,16},{24,28},{28,24},{1,5},{5... | collective-permute-start | bytes 1769480 | tf_op jit(solution)/shard_map/ppermute | solution.py:271
  52.4 13.5 %collective-permute-start.10 = (bf16[288,1024]{1,0:T(8,128)(2,1)S(1)}, bf16[288,1024]{1,0:T(8,128)(2,1)S(1)}, u32[]{:S(2)}, u32[]{:S(2)}) collective-permute-start(bf16[288,1024]{1,0:T(8,128)(2,1)S(1)} %collective-permute-done.9.refs_0_), channel_id=1, source_target_pairs={{0,4},{4,0},{8,12},{12,8},{16,20},{20,16},{24,28},{28,24},{1,5},{5... | collective-permute-start | bytes 1769480 | tf_op jit(solution)/shard_map/ppermute | solution.py:271
  52.4 15.9 %collective-permute-start.8 = (bf16[288,1024]{1,0:T(8,128)(2,1)S(1)}, bf16[288,1024]{1,0:T(8,128)(2,1)S(1)}, u32[]{:S(2)}, u32[]{:S(2)}) collective-permute-start(bf16[288,1024]{1,0:T(8,128)(2,1)S(1)} %shard_map.94.refs_0_), channel_id=1, source_target_pairs={{0,4},{4,0},{8,12},{12,8},{16,20},{20,16},{24,28},{28,24},{1,5},{5... | collective-permute-start | bytes 1769480 | tf_op jit(solution)/shard_map/ppermute | solution.py:271
  57.5 3.0 %collective-permute-start.18 = (bf16[144,1024]{1,0:T(8,128)(2,1)S(1)}, bf16[144,1024]{1,0:T(8,128)(2,1)S(1)}, u32[]{:S(2)}, u32[]{:S(2)}) collective-permute-start(bf16[144,1024]{1,0:T(8,128)(2,1)S(1)} %collective-permute-done.16.refs_1_), channel_id=1, source_target_pairs={{0,4},{4,0},{8,12},{12,8},{16,20},{20,16},{24,28},{28,24},{1,5},{5... | collective-permute-start | bytes 884744 | tf_op jit(solution)/shard_map/ppermute | solution.py:271
  59.2 2.5 %collective-permute-start.17 = (bf16[144,1024]{1,0:T(8,128)(2,1)S(1)}, bf16[144,1024]{1,0:T(8,128)(2,1)S(1)}, u32[]{:S(2)}, u32[]{:S(2)}) collective-permute-start(bf16[144,1024]{1,0:T(8,128)(2,1)S(1)} %collective-permute-done.15.refs_0_), channel_id=1, source_target_pairs={{0,4},{4,0},{8,12},{12,8},{16,20},{20,16},{24,28},{28,24},{1,5},{5... | collective-permute-start | bytes 884744 | tf_op jit(solution)/shard_map/ppermute | solution.py:271
  62.9 8.9 %collective-permute-start.19 = (bf16[272,512]{1,0:T(8,128)(2,1)S(1)}, bf16[272,512]{1,0:T(8,128)(2,1)S(1)}, u32[]{:S(2)}, u32[]{:S(2)}) collective-permute-start(bf16[272,512]{1,0:T(8,128)(2,1)S(1)} %shard_map.98), channel_id=1, source_target_pairs={{0,24},{4,28},{8,16},{12,20},{16,8},{20,12},{24,0},{28,4},{1,25},{... | collective-permute-start | bytes 835592 | tf_op jit(solution)/shard_map/ppermute | solution.py:274
  65.0 13.4 %collective-permute-start.14 = (bf16[272,512]{1,0:T(8,128)(2,1)S(1)}, bf16[272,512]{1,0:T(8,128)(2,1)S(1)}, u32[]{:S(2)}, u32[]{:S(2)}) collective-permute-start(bf16[272,512]{1,0:T(8,128)(2,1)S(1)} %shard_map.97), channel_id=1, source_target_pairs={{0,16},{4,20},{8,24},{12,28},{16,0},{20,4},{24,8},{28,12},{1,17},{... | collective-permute-start | bytes 835592 | tf_op jit(solution)/shard_map/ppermute | solution.py:274
  67.1 11.3 %collective-permute-start.11 = (bf16[272,512]{1,0:T(8,128)(2,1)S(1)}, bf16[272,512]{1,0:T(8,128)(2,1)S(1)}, u32[]{:S(2)}, u32[]{:S(2)}) collective-permute-start(bf16[272,512]{1,0:T(8,128)(2,1)S(1)} %shard_map.96), channel_id=1, source_target_pairs={{0,8},{4,12},{8,0},{12,4},{16,24},{20,28},{24,16},{28,20},{1,9},{5... | collective-permute-start | bytes 835592 | tf_op jit(solution)/shard_map/ppermute | solution.py:274
  79.3 11.1 %collective-permute-start.20 = (bf16[272,512]{1,0:T(8,128)(2,1)S(1)}, bf16[272,512]{1,0:T(8,128)(2,1)S(1)}, u32[]{:S(2)}, u32[]{:S(2)}) collective-permute-start(bf16[272,512]{1,0:T(8,128)(2,1)S(1)} %get-tuple-element.16), channel_id=1, source_target_pairs={{0,1},{1,0},{2,3},{3,2},{4,5},{5,4},{6,7},{7,6},{8,9},{9,8},{10,11... | collective-permute-start | bytes 835592 | tf_op jit(solution)/shard_map/ppermute | solution.py:337
  79.6 14.6 %collective-permute-start.21 = (bf16[272,512]{1,0:T(8,128)(2,1)S(1)}, bf16[272,512]{1,0:T(8,128)(2,1)S(1)}, u32[]{:S(2)}, u32[]{:S(2)}) collective-permute-start(bf16[272,512]{1,0:T(8,128)(2,1)S(1)} %get-tuple-element.17), channel_id=1, source_target_pairs={{0,2},{1,3},{2,0},{3,1},{4,6},{5,7},{6,4},{7,5},{8,10},{9,11},{10,... | collective-permute-start | bytes 835592 | tf_op jit(solution)/shard_map/ppermute | solution.py:337
  81.9 24.1 %collective-permute-start.22 = (bf16[272,512]{1,0:T(8,128)(2,1)S(1)}, bf16[272,512]{1,0:T(8,128)(2,1)S(1)}, u32[]{:S(2)}, u32[]{:S(2)}) collective-permute-start(bf16[272,512]{1,0:T(8,128)(2,1)S(1)} %get-tuple-element.18), channel_id=1, source_target_pairs={{0,3},{1,2},{2,1},{3,0},{4,7},{5,6},{6,5},{7,4},{8,11},{9,10},{10,... | collective-permute-start | bytes 835592 | tf_op jit(solution)/shard_map/ppermute | solution.py:337
  106.7 2.7 %collective-permute-start.23 = (bf16[128,512]{1,0:T(8,128)(2,1)S(1)}, bf16[128,512]{1,0:T(8,128)(2,1)S(1)}, u32[]{:S(2)}, u32[]{:S(2)}) collective-permute-start(bf16[128,512]{1,0:T(8,128)(2,1)S(1)} %get-tuple-element.20), channel_id=1, source_target_pairs={{0,4},{4,0},{8,12},{12,8},{16,20},{20,16},{24,28},{28,24},{1,5},{5... | collective-permute-start | bytes 393224 | tf_op jit(solution)/shard_map/ppermute | solution.py:271
  (13 other events, 16.1 us)

commit v3 on v2

v3 whole, which is shorter than its diff:
```python
import jax
import jax.numpy as jnp
from jax import lax
from jax.experimental import pallas as pl
from jax.experimental.pallas import tpu as pltpu
from jax.sharding import PartitionSpec as P

BOTH = ("seq", "head")
HIGH = lax.Precision.HIGHEST
f32, bf16 = jnp.float32, jnp.bfloat16
EXT = 16
MIB = 1024 * 1024


def call(kernel, scalars, ins, in_specs, outs, out_specs, scratch=(), flops=0, limit=24):
    moved = sum(a.size * a.dtype.itemsize for a in ins) + sum(
        o.size * o.dtype.itemsize for o in outs
    )
    return pl.pallas_call(
        kernel,
        out_shape=outs,
        grid_spec=pltpu.PrefetchScalarGridSpec(
            num_scalar_prefetch=1,
            grid=(1,),
            in_specs=in_specs,
            out_specs=out_specs,
            scratch_shapes=scratch,
        ),
        cost_estimate=pl.CostEstimate(flops=flops, bytes_accessed=moved, transcendentals=0),
        compiler_params=pltpu.CompilerParams(vmem_limit_bytes=limit * MIB),
    )(scalars, *ins)


def full(a):
    return pl.BlockSpec(memory_space=pltpu.VMEM)


def shape(dims, kind):
    return jax.ShapeDtypeStruct(dims, kind)


def nn(a, b, precision=None):
    return jnp.dot(a, b, preferred_element_type=f32, precision=precision)


def nt(a, b, precision=None):
    return lax.dot_general(a, b, (((1,), (1,)), ((), ())), preferred_element_type=f32, precision=precision)


def tn(a, b, precision=None):
    return lax.dot_general(a, b, (((0,), (0,)), ((), ())), preferred_element_type=f32, precision=precision)


def split2(v):
    hi = v.astype(bf16).astype(f32)
    return hi, v - hi


def half_lanes(ref, k):
    n = ref.shape[1] // 2
    return ref[:, pl.ds(pl.multiple_of(k * n, n), n)]


def half_rows(ref, k):
    v = ref[...]
    n = v.shape[0] // 2
    return jnp.where(k == 0, v[:n], v[n:])


def channel_map(heads, wide):
    head = lax.broadcasted_iota(jnp.int32, (heads, wide), 0)
    lane = lax.broadcasted_iota(jnp.int32, (heads, wide), 1)
    size = wide // heads
    return ((lane >= head * size) & (lane < (head + 1) * size)).astype(bf16)


def spread(v, spots):
    hi, lo = split2(v)
    return tn(hi.astype(bf16), spots) + tn(lo.astype(bf16), spots)


def ones_upto(rows):
    i = lax.broadcasted_iota(jnp.int32, (rows, rows), 0)
    j = lax.broadcasted_iota(jnp.int32, (rows, rows), 1)
    return (j <= i), (i <= j)


def state_kernel(s, xo, xr, bo, br, dto, dtr, ldo, ldr, _, msg, first):
    k = s[0]
    rows, wide = xo.shape[0], xo.shape[1] // 2
    _, upper = ones_upto(rows)
    got = []
    for x, b, dt, ld in ((xo, bo, dto, ldo), (xr, br, dtr, ldr)):
        dt, ld = half_rows(dt, k), half_rows(ld, k)
        spots = channel_map(ld.shape[0], wide)
        run = nn(ld, upper.astype(f32), HIGH)
        last = run[:, rows - 1 :]
        tail = jnp.exp(last - run) * dt
        scaled = (half_lanes(x, k).astype(f32) * spread(tail, spots)).astype(bf16)
        state = tn(b[...], scaled)
        decay = spread(jnp.exp(jnp.broadcast_to(last, (last.shape[0], 8))), spots)
        got.append((state, decay))
    (so, do), (sr, dr) = got
    even = k == 0
    s1, s2 = jnp.where(even, so, sr), jnp.where(even, sr, so)
    d2 = jnp.where(even, dr, do)
    n = s1.shape[0]
    msg[:n] = (d2[:1] * s1 + s2).astype(bf16)
    hi, lo = split2(do * dr)
    msg[n:] = jnp.concatenate([hi, lo], 0).astype(bf16)
    first[...] = s1


def unpack(ref):
    n = ref.shape[0] - EXT
    ext = ref[n:].astype(f32)
    return ref[:n].astype(f32), ext[:8] + ext[8:]


def inside_kernel(s, xo, xr, bo, br, co, cr, dto, dtr, ldo, ldr, skip, out):
    k = s[0]
    rows, wide = xo.shape[0], xo.shape[1] // 2
    low, upper = ones_upto(rows)
    count = skip.shape[1] // 2
    gains = jnp.where(k == 0, skip[:, :count], skip[:, count:])
    hi, lo = split2(jnp.broadcast_to(gains, (8, count)))
    spots = channel_map(count, wide)
    gains = nn(hi.astype(bf16), spots) + nn(lo.astype(bf16), spots)
    for turn, (x, b, c, dt, ld) in enumerate(((xo, bo, co, dto, ldo), (xr, br, cr, dtr, ldr))):
        start = pl.multiple_of(jnp.where(k == turn, 0, rows), rows)
        dt, ld = half_rows(dt, k), half_rows(ld, k)
        heads = ld.shape[0]
        size = wide // heads
        run = nn(ld, upper.astype(f32), HIGH)
        down = nt(low.astype(f32), ld, HIGH)
        scores = jnp.where(low, nt(c[...], b[...]), 0.0)
        lane = lax.broadcasted_iota(jnp.int32, (rows, 2 * size), 1)
        for pair in range(heads // 2):
            w = []
            for h in (2 * pair, 2 * pair + 1):
                gap = jnp.minimum(down[:, h : h + 1] - run[h : h + 1, :], 0.0)
                w.append((jnp.exp(gap) * scores * dt[h : h + 1, :]).astype(bf16))
            xp = x[:, pl.ds(pl.multiple_of(k * wide + 2 * pair * size, 2 * size), 2 * size)]
            zero = jnp.zeros_like(xp)
            both = jnp.concatenate([jnp.where(lane < size, xp, zero), jnp.where(lane < size, zero, xp)], 0)
            y = nn(jnp.concatenate(w, 1), both)
            at = slice(2 * pair * size, 2 * (pair + 1) * size)
            out[pl.ds(start, rows), at] = y + gains[:1, at] * xp.astype(f32)


def gate_kernel(s, inside, first, co, cr, ldo, ldr, zo, zr, gain, *rest):
    *states, out, squares = rest
    k = s[0]
    rows, wide = zo.shape[0], zo.shape[1] // 2
    _, upper = ones_upto(rows)
    even = k == 0
    enter, through = jnp.zeros_like(first[...]), None
    for ref in states:
        st, dec = unpack(ref)
        enter = enter + (st if through is None else st * through)
        through = dec[:1] if through is None else through * dec[:1]
    ld1 = jnp.where(even, half_rows(ldo, k), half_rows(ldr, k))
    ld2 = jnp.where(even, half_rows(ldr, k), half_rows(ldo, k))
    c1, c2 = jnp.where(even, co[...], cr[...]), jnp.where(even, cr[...], co[...])
    spots = channel_map(ld1.shape[0], wide)
    ones = jnp.ones((8, wide), bf16)
    for turn, (c, ld) in enumerate(((c1, ld1), (c2, ld2))):
        run = nn(ld, upper.astype(f32), HIGH)
        decays = spread(jnp.exp(run), spots)
        carried = nn(c, enter.astype(bf16)) * decays
        y = inside[turn * rows : (turn + 1) * rows] + carried
        za, zb = (zo, zr) if turn == 0 else (zr, zo)
        zf = jnp.where(even, half_lanes(za, k), half_lanes(zb, k)).astype(f32)
        gated = y * zf / (1.0 + jnp.exp(-zf))
        sq_hi, sq_lo = split2(gated * gated)
        sq = nt(ones, sq_hi.astype(bf16)) + nt(ones, sq_lo.astype(bf16))
        out[turn * rows : (turn + 1) * rows] = (gated * half_lanes(gain, k)).astype(bf16)
        squares[8 * turn : 8 * turn + 8] = sq
        if turn == 0:
            enter = decays[rows - 1 : rows] * enter + first[...]


def project_kernel(s, *refs):
    *g, w, out = refs
    k = s[0]
    parts = len(g) // 2
    rows, depth = g[0].shape
    here = pl.ds(pl.multiple_of(k * depth, depth), depth)
    there = pl.ds(pl.multiple_of((1 - k) * depth, depth), depth)
    for turn in range(parts):
        got = nn(g[turn][...], w[here]) + nn(g[parts + turn][...], w[there])
        out[turn * rows : (turn + 1) * rows] = got.astype(bf16)


def choose_kernel(s, *refs):
    n = (len(refs) - 1) // 2
    ins, outs, sem = refs[:n], refs[n : 2 * n], refs[2 * n]
    for m in range(n):
        for j in range(n):

            @pl.when((s[2] ^ m) == j)
            def _():
                pltpu.make_async_copy(ins[j], outs[m], sem.at[m]).start()

    for m in range(n):
        pltpu.make_async_copy(ins[0], outs[m], sem.at[m]).wait()


def sum_kernel(s, *refs, inner):
    *z, squares, mine, theirs = refs
    k = s[0]
    rows = mine.shape[0]
    i = lax.broadcasted_iota(jnp.int32, (rows, rows), 0)
    j = lax.broadcasted_iota(jnp.int32, (rows, rows), 1)
    done = []
    for turn in range(2):
        row = lax.rsqrt(squares[8 * turn : 8 * turn + 1] / inner + 1e-5)
        col = jnp.sum(jnp.where(i == j, jnp.broadcast_to(row, (rows, rows)), 0.0), axis=1, keepdims=True)
        total = sum(a[turn * rows : (turn + 1) * rows].astype(f32) for a in z)
        done.append((total * col).astype(bf16))
    even = k == 0
    mine[...] = jnp.where(even, done[0], done[1])
    theirs[...] = jnp.where(even, done[1], done[0])


def body(n, n_head, signal, gate_input, state_in, state_out, step_size, log_decay, skip_gain, norm_gain, out_weight):
    rows = signal.shape[0]
    heads = log_decay.shape[0]
    wide = signal.shape[1] // 2
    size = signal.shape[1] // heads
    states = state_in.shape[1]
    cols = out_weight.shape[1]
    place, z = lax.axis_index("seq"), lax.axis_index("head")
    k, chip = place % 2, place // 2
    s = jnp.stack([k, chip, chip ^ z]).astype(jnp.int32)

    def swap(a):
        return lax.ppermute(a, "seq", [(i, i ^ 1) for i in range(2 * n)])

    def across(a, j):
        return lax.ppermute(a, "seq", [(i, i ^ (2 * j)) for i in range(2 * n)])

    x2, b2 = swap(signal), swap(state_in)
    dt2, ld2 = swap(step_size), swap(log_decay)
    z2, c2 = swap(gate_input), swap(state_out)
    skip = skip_gain.reshape(1, heads)
    gain = norm_gain.reshape(1, 2 * wide)

    any_spec = pl.BlockSpec(memory_space=pl.ANY)
    ins = (signal, x2, state_in, b2, step_size, dt2, log_decay, ld2, c2)
    specs = [full(signal)] * 2 + [full(state_in)] * 2 + [full(step_size)] * 4 + [any_spec]
    msg_shape = shape((states + EXT, wide), bf16)
    first_shape = shape((states, wide), f32)
    msg, first = call(state_kernel, s, ins, specs, [msg_shape, first_shape], [full(msg_shape), full(first_shape)])
    got = [
        lax.ppermute(msg, "seq", [(i, i + 2 * j) for i in range(2 * (n - j))]) for j in range(1, n)
    ]
    ins = (signal, x2, state_in, b2, state_out, c2, step_size, dt2, log_decay, ld2, skip)
    specs = [full(signal)] * 2 + [full(state_in)] * 4 + [full(step_size)] * 4 + [full(skip)]
    inside_shape = shape((2 * rows, wide), f32)
    (inside,) = call(inside_kernel, s, ins, specs, [inside_shape], [full(inside_shape)])

    ins = (inside, first, state_out, c2, log_decay, ld2, gate_input, z2, gain, *got)
    specs = [full(inside), full(first), full(state_out), full(c2), full(log_decay), full(ld2)]
    specs += [full(gate_input)] * 2 + [full(gain)] + [full(m) for m in got]
    g_shape, sq_shape = shape((2 * rows, wide), bf16), shape((16, rows), f32)
    g, squares = call(gate_kernel, s, ins, specs, [g_shape, sq_shape], [full(g_shape), full(sq_shape)])

    p_shape = shape((2 * rows, cols), bf16)

    def project(*g):
        ins = (*g, *[swap(a) for a in g], out_weight)
        return call(project_kernel, s, ins, [full(a) for a in ins], [p_shape], [full(p_shape)])[0]

    if n == 4:
        gx, gy = across(g, 1), across(g, 2)
        squares = squares + swap(squares)
        for bit in range(2):
            squares = squares + lax.ppermute(squares, "head", [(i, i ^ (1 << bit)) for i in range(n)])
        own = project(g)
        gx, gy, own, squares = lax.optimization_barrier((gx, gy, own, squares))
        fx, fy = across(gx[:rows], 2), across(gy[rows:], 1)
        px, py = project(gx), project(gy)
        fx, fy, px, py = lax.optimization_barrier((fx, fy, px, py))
        blocks = [own, px, py, project(fx, fy)]
    else:
        squares = squares + swap(squares)
        for bit in range(n.bit_length() - 1):
            squares = squares + lax.ppermute(squares, "head", [(i, i ^ (1 << bit)) for i in range(n)])
        blocks = [project(g)] + [project(across(g, j)) for j in range(1, n)]
    blocks = [blocks[0]] + [across(blocks[j], j) for j in range(1, n)]

    blocks = call(
        choose_kernel, s, blocks, [any_spec] * n, [p_shape] * n, [any_spec] * n,
        scratch=[pltpu.SemaphoreType.DMA((n,))],
    )
    blocks = [blocks[0]] + [
        lax.ppermute(blocks[m], "head", [(i, i ^ m) for i in range(n)]) for m in range(1, n)
    ]
    half = shape((rows, cols), bf16)

    def add(*refs):
        sum_kernel(*refs, inner=2 * wide * n_head)

    ins = (*blocks, squares)
    mine, theirs = call(add, s, ins, [full(a) for a in ins], [half] * 2, [full(half)] * 2)
    other = swap(theirs)
    return jnp.where(k == 0, jnp.concatenate([mine, other], 1), jnp.concatenate([other, mine], 1))


def solution(mesh):
    n, n_head = mesh.shape["seq"] // 2, mesh.shape["head"]
    assert n == n_head and n & (n - 1) == 0
    in_specs = (
        P("seq", "head"),
        P("seq", "head"),
        P("seq", None),
        P("seq", None),
        P("head", "seq"),
        P("head", "seq"),
        P("head"),
        P("head"),
        P("head", "seq"),
    )

    def run(*args):
        return body(n, n_head, *args)

    return jax.shard_map(run, mesh=mesh, in_specs=in_specs, out_specs=P("seq", "head"), check_vma=False)
```

time: 111 us -> 101 us (0.910)
  the two profiles are of different devices: /device:TPU:9 before, /device:TPU:0 now
where the time goes in v3:
time: 101 us; the launch traced here: 98.9 us
  waiting for transfers between devices  46.7 us (46%)
  starting transfers between devices  31.9 us (32%)
  Pallas kernels  13.1 us (13%)
  local copies, waits for them, and re-layouts  6.12 us (6%)
    ppermute x3, waiting for transfers between devices, body(): lax.ppermute(blocks[m], 'head', [(i, i ^ m) for i in range(n)])  18.6 us
    ppermute x7, waiting for transfers between devices, across(): return lax.ppermute(a, 'seq', [(i, i ^ 2 * j) for i in range(2 * n)])  15.1 us
    pallas_call x9, Pallas kernels, call(): pl.pallas_call(kernel, out_shape=outs, grid_spec=pltpu.PrefetchScalarGrid...  13.1 us
    ppermute x7, starting transfers between devices, across(): return lax.ppermute(a, 'seq', [(i, i ^ 2 * j) for i in range(2 * n)])  10.8 us
    ppermute x3, starting transfers between devices, body(): lax.ppermute(msg, 'seq', [(i, i + 2 * j) for i in range(2 * (n - j))])  9.48 us
    unnamed x22, local copies, waits for them, and re-layouts  6.08 us
    ppermute x13, waiting for transfers between devices, swap(): return lax.ppermute(a, 'seq', [(i, i ^ 1) for i in range(2 * n)])  5 us
    ppermute x3, starting transfers between devices, body(): lax.ppermute(blocks[m], 'head', [(i, i ^ m) for i in range(n)])  4.45 us
  transfers between devices with their start and end apart: 28, of which 14 were waited for; matrix products, arithmetic and copies ran while one was open for 0% of the time, Pallas kernels for 9%

profile of v3, /device:TPU:0, one launch (start us, length us, event | category | flops | bytes accessed | tf_op | source)
XLA Modules:
  0.0 98.9 jit_solution(6250221866506142157)
XLA Ops:
  1.5 1.5 %collective-permute-done.4.ldr = f32[32,128]{1,0:T(8,128)S(1)} collective-permute-done((f32[32,128]{1,0:T(8,128)}, f32[32,128]{1,0:T(8,128)S(1)}, u32[]{:S(2)}, u32[]{:S(2)}) %collective-permute-start.4) | collective-permute-done | bytes 16416 | tf_op jit(solution)/shard_map/ppermute | solution.py:238
  4.4 1.0 %copy-done.1 = bf16[128,2048]{1,0:T(8,128)(2,1)S(1)} copy-done((bf16[128,2048]{1,0:T(8,128)(2,1)S(1)}, bf16[128,2048]{1,0:T(8,128)(2,1)}, u32[]{:S(2)}) %copy-start.1) | copy-done | bytes 524312
  7.7 2.2 %shard_map.92 = (bf16[144,1024]{1,0:T(8,128)(2,1)S(1)}, f32[128,1024]{1,0:T(8,128)S(1)}) custom-call(s32[3]{0:T(128)S(1)} %pad_add_fusion.s.refs_0_, bf16[128,2048]{1,0:T(8,128)(2,1)S(1)} %copy-done.1, bf16[128,2048]{1,0:T(8,128)(2,1)S(1)} %collective-permute-done.xr, bf16[128,128]{1,0:T(8,128)(2,1)S(1)} %copy-done.6, ...), custom_call_target="tpu_custom_call" | custom-call | bytes 2031616 | tf_op jit(solution)/shard_map/pallas_call | solution.py:19
  9.9 4.8 %collective-permute-start.6 = (bf16[144,1024]{1,0:T(8,128)(2,1)S(1)}, bf16[144,1024]{1,0:T(8,128)(2,1)S(1)}, u32[]{:S(2)}, u32[]{:S(2)}) collective-permute-start(bf16[144,1024]{1,0:T(8,128)(2,1)S(1)} %get-tuple-element.24), channel_id=1, source_target_pairs={{0,8},{4,12},{8,16},{12,20},{16,24},{20,28},{1,9},{5,13},{9,17},{1... | collective-permute-start | bytes 884744 | tf_op jit(solution)/shard_map/ppermute | solution.py:256
  14.6 3.4 %collective-permute-start.7 = (bf16[144,1024]{1,0:T(8,128)(2,1)S(1)}, bf16[144,1024]{1,0:T(8,128)(2,1)S(1)}, u32[]{:S(2)}, u32[]{:S(2)}) collective-permute-start(bf16[144,1024]{1,0:T(8,128)(2,1)S(1)} %get-tuple-element.24), channel_id=1, source_target_pairs={{0,16},{4,20},{8,24},{12,28},{1,17},{5,21},{9,25},{13,29},{2,18},{... | collective-permute-start | bytes 884744 | tf_op jit(solution)/shard_map/ppermute | solution.py:256
  18.1 1.3 %collective-permute-start.8 = (bf16[144,1024]{1,0:T(8,128)(2,1)S(1)}, bf16[144,1024]{1,0:T(8,128)(2,1)S(1)}, u32[]{:S(2)}, u32[]{:S(2)}) collective-permute-start(bf16[144,1024]{1,0:T(8,128)(2,1)S(1)} %get-tuple-element.24), channel_id=1, source_target_pairs={{0,24},{4,28},{1,25},{5,29},{2,26},{6,30},{3,27},{7,31}} | collective-permute-start | bytes 884744 | tf_op jit(solution)/shard_map/ppermute | solution.py:256
  22.2 2.1 %shard_map.91.inside = f32[256,1024]{1,0:T(8,128)S(1)} custom-call(s32[3]{0:T(128)S(1)} %pad_add_fusion.s.refs_0_, bf16[128,2048]{1,0:T(8,128)(2,1)S(1)} %copy-done.1, bf16[128,2048]{1,0:T(8,128)(2,1)S(1)} %collective-permute-done.xr, bf16[128,128]{1,0:T(8,128)(2,1)S(1)} %copy-done.6, bf16[128,128]{1,0:T(8,128)(2,1)S(1)} %collective-permute-done.1.br, ...), custom_call_target="tpu_custom_call" | custom-call | bytes 2293888 | tf_op jit(solution)/shard_map/pallas_call | solution.py:19
  24.4 4.0 %collective-permute-done.7.rest_1_ = bf16[144,1024]{1,0:T(8,128)(2,1)S(1)} collective-permute-done((bf16[144,1024]{1,0:T(8,128)(2,1)S(1)}, bf16[144,1024]{1,0:T(8,128)(2,1)S(1)}, u32[]{:S(2)}, u32[]{:S(2)}) %collective-permute-start.7) | collective-permute-done | bytes 294944 | tf_op jit(solution)/shard_map/ppermute | solution.py:256
  28.5 2.2 %shard_map.93 = (bf16[256,1024]{1,0:T(8,128)(2,1)S(1)}, f32[16,128]{1,0:T(8,128)S(1)}) custom-call(s32[3]{0:T(128)S(1)} %pad_add_fusion.s.refs_0_, f32[256,1024]{1,0:T(8,128)S(1)} %shard_map.91.inside, f32[128,1024]{1,0:T(8,128)S(1)} %get-tuple-element.23.first, bf16[128,128]{1,0:T(8,128)(2,1)S(1)} %copy-done.5, ...), custom_call_target="tpu_custom_call" | custom-call | bytes 4145152 | tf_op jit(solution)/shard_map/pallas_call | solution.py:19
  30.7 2.5 %collective-permute-start.10 = (bf16[256,1024]{1,0:T(8,128)(2,1)S(1)}, bf16[256,1024]{1,0:T(8,128)(2,1)S(1)}, u32[]{:S(2)}, u32[]{:S(2)}) collective-permute-start(bf16[256,1024]{1,0:T(8,128)(2,1)S(1)} %get-tuple-element.25.refs_0_), channel_id=1, source_target_pairs={{0,16},{4,20},{8,24},{12,28},{16,0},{20,4},{24,8},{28,12},{1,17},{... | collective-permute-start | bytes 1572872 | tf_op jit(solution)/shard_map/ppermute | solution.py:241
  33.2 1.9 %collective-permute-start.9 = (bf16[256,1024]{1,0:T(8,128)(2,1)S(1)}, bf16[256,1024]{1,0:T(8,128)(2,1)S(1)}, u32[]{:S(2)}, u32[]{:S(2)}) collective-permute-start(bf16[256,1024]{1,0:T(8,128)(2,1)S(1)} %get-tuple-element.25.refs_0_), channel_id=1, source_target_pairs={{0,8},{4,12},{8,0},{12,4},{16,24},{20,28},{24,16},{28,20},{1,9},{5... | collective-permute-start | bytes 1572872 | tf_op jit(solution)/shard_map/ppermute | solution.py:241
  35.1 1.2 %collective-permute-done.12 = f32[16,128]{1,0:T(8,128)S(1)} collective-permute-done((f32[16,128]{1,0:T(8,128)S(1)}, f32[16,128]{1,0:T(8,128)S(1)}, u32[]{:S(2)}, u32[]{:S(2)}) %collective-permute-start.12) | collective-permute-done | bytes 8224 | tf_op jit(solution)/shard_map/ppermute | solution.py:238
  36.2 1.6 %collective-permute-start.13 = (f32[16,128]{1,0:T(8,128)S(1)}, f32[16,128]{1,0:T(8,128)S(1)}, u32[]{:S(2)}, u32[]{:S(2)}) collective-permute-start(f32[16,128]{1,0:T(8,128)S(1)} %add.15), channel_id=1, source_target_pairs={{0,1},{1,0},{2,3},{3,2},{4,5},{5,4},{6,7},{7,6},{8,9},{9,8},{10,11... | collective-permute-start | bytes 24584 | tf_op jit(solution)/shard_map/ppermute | solution.py:279
  37.8 2.1 %collective-permute-done.13 = f32[16,128]{1,0:T(8,128)S(1)} collective-permute-done((f32[16,128]{1,0:T(8,128)S(1)}, f32[16,128]{1,0:T(8,128)S(1)}, u32[]{:S(2)}, u32[]{:S(2)}) %collective-permute-start.13) | collective-permute-done | bytes 8224 | tf_op jit(solution)/shard_map/ppermute | solution.py:279
  39.9 2.6 %collective-permute-start.14 = (f32[16,128]{1,0:T(8,128)S(1)}, f32[16,128]{1,0:T(8,128)S(1)}, u32[]{:S(2)}, u32[]{:S(2)}) collective-permute-start(f32[16,128]{1,0:T(8,128)S(1)} %add.16), channel_id=1, source_target_pairs={{0,2},{1,3},{2,0},{3,1},{4,6},{5,7},{6,4},{7,5},{8,10},{9,11},{10,... | collective-permute-start | bytes 24584 | tf_op jit(solution)/shard_map/ppermute | solution.py:279
  42.5 2.0 %collective-permute-done.14 = f32[16,128]{1,0:T(8,128)S(1)} collective-permute-done((f32[16,128]{1,0:T(8,128)S(1)}, f32[16,128]{1,0:T(8,128)S(1)}, u32[]{:S(2)}, u32[]{:S(2)}) %collective-permute-start.14) | collective-permute-done | bytes 8224 | tf_op jit(solution)/shard_map/ppermute | solution.py:279
  44.5 1.2 %shard_map.94.refs_0_ = bf16[256,512]{1,0:T(8,128)(2,1)S(1)} custom-call(s32[3]{0:T(128)S(1)} %pad_add_fusion.s.refs_0_, bf16[256,1024]{1,0:T(8,128)(2,1)S(1)} %get-tuple-element.25.refs_0_, bf16[256,1024]{1,0:T(8,128)(2,1)S(1)} %collective-permute-done.11.refs_1_, bf16[2048,512]{1,0:T(8,128)(2,1)S(1)} %copy-done), custom_call_target="tpu_custom_call" | custom-call | bytes 3407872 | tf_op jit(solution)/shard_map/pallas_call | solution.py:19
  45.8 1.6 %collective-permute-done.9.refs_0_ = bf16[256,1024]{1,0:T(8,128)(2,1)S(1)} collective-permute-done((bf16[256,1024]{1,0:T(8,128)(2,1)S(1)}, bf16[256,1024]{1,0:T(8,128)(2,1)S(1)}, u32[]{:S(2)}, u32[]{:S(2)}) %collective-permute-start.9) | collective-permute-done | bytes 524320 | tf_op jit(solution)/shard_map/ppermute | solution.py:241
  48.3 1.8 %collective-permute-start.16 = (bf16[128,1024]{1,0:T(8,128)(2,1)S(1)}, bf16[128,1024]{1,0:T(8,128)(2,1)S(1)}, u32[]{:S(2)}, u32[]{:S(2)}) collective-permute-start(bf16[128,1024]{1,0:T(8,128)(2,1)S(1)} %slice.7), channel_id=1, source_target_pairs={{0,8},{4,12},{8,0},{12,4},{16,24},{20,28},{24,16},{28,20},{1,9},{5... | collective-permute-start | bytes 786440 | tf_op jit(solution)/shard_map/ppermute | solution.py:241
  50.0 1.2 %shard_map.96 = bf16[256,512]{1,0:T(8,128)(2,1)S(1)} custom-call(s32[3]{0:T(128)S(1)} %pad_add_fusion.s.refs_0_, bf16[256,1024]{1,0:T(8,128)(2,1)S(1)} %collective-permute-done.10.refs_0_, bf16[256,1024]{1,0:T(8,128)(2,1)S(1)} %collective-permute-done.18.refs_1_, bf16[2048,512]{1,0:T(8,128)(2,1)S(1)} %copy-done), custom_call_target="tpu_custom_call" | custom-call | bytes 3407872 | tf_op jit(solution)/shard_map/pallas_call | solution.py:19
  51.3 1.2 %shard_map.95 = bf16[256,512]{1,0:T(8,128)(2,1)S(1)} custom-call(s32[3]{0:T(128)S(1)} %pad_add_fusion.s.refs_0_, bf16[256,1024]{1,0:T(8,128)(2,1)S(1)} %collective-permute-done.9.refs_0_, bf16[256,1024]{1,0:T(8,128)(2,1)S(1)} %collective-permute-done.17.refs_1_, bf16[2048,512]{1,0:T(8,128)(2,1)S(1)} %copy-done), custom_call_target="tpu_custom_call" | custom-call | bytes 3407872 | tf_op jit(solution)/shard_map/pallas_call | solution.py:19
  52.6 3.7 %collective-permute-done.15.refs_0_ = bf16[128,1024]{1,0:T(8,128)(2,1)S(1)} collective-permute-done((bf16[128,1024]{1,0:T(8,128)(2,1)S(1)}, bf16[128,1024]{1,0:T(8,128)(2,1)S(1)}, u32[]{:S(2)}, u32[]{:S(2)}) %collective-permute-start.15) | collective-permute-done | bytes 262176 | tf_op jit(solution)/shard_map/ppermute | solution.py:241
  56.8 1.7 %collective-permute-start.19 = (bf16[256,512]{1,0:T(8,128)(2,1)S(1)}, bf16[256,512]{1,0:T(8,128)(2,1)S(1)}, u32[]{:S(2)}, u32[]{:S(2)}) collective-permute-start(bf16[256,512]{1,0:T(8,128)(2,1)S(1)} %shard_map.95), channel_id=1, source_target_pairs={{0,8},{4,12},{8,0},{12,4},{16,24},{20,28},{24,16},{28,20},{1,9},{5... | collective-permute-start | bytes 786440 | tf_op jit(solution)/shard_map/ppermute | solution.py:241
  58.6 1.7 %collective-permute-start.20 = (bf16[256,512]{1,0:T(8,128)(2,1)S(1)}, bf16[256,512]{1,0:T(8,128)(2,1)S(1)}, u32[]{:S(2)}, u32[]{:S(2)}) collective-permute-start(bf16[256,512]{1,0:T(8,128)(2,1)S(1)} %shard_map.96), channel_id=1, source_target_pairs={{0,16},{4,20},{8,24},{12,28},{16,0},{20,4},{24,8},{28,12},{1,17},{... | collective-permute-start | bytes 786440 | tf_op jit(solution)/shard_map/ppermute | solution.py:241
  60.2 1.3 %shard_map.97 = bf16[256,512]{1,0:T(8,128)(2,1)S(1)} custom-call(s32[3]{0:T(128)S(1)} %pad_add_fusion.s.refs_0_, bf16[128,1024]{1,0:T(8,128)(2,1)S(1)} %collective-permute-done.15.refs_0_, bf16[128,1024]{1,0:T(8,128)(2,1)S(1)} %collective-permute-done.16.refs_1_, bf16[128,1024]{1,0:T(8,128)(2,1)S(1)} %collective-permute-done.21.refs_2_, ...), custom_call_target="tpu_custom_call" | custom-call | bytes 3407872 | tf_op jit(solution)/shard_map/pallas_call | solution.py:19
  62.4 3.6 %collective-permute-done.19.refs_1_ = bf16[256,512]{1,0:T(8,128)(2,1)S(1)} collective-permute-done((bf16[256,512]{1,0:T(8,128)(2,1)S(1)}, bf16[256,512]{1,0:T(8,128)(2,1)S(1)}, u32[]{:S(2)}, u32[]{:S(2)}) %collective-permute-start.19) | collective-permute-done | bytes 262176 | tf_op jit(solution)/shard_map/ppermute | solution.py:241
  66.0 6.1 %collective-permute-done.20.refs_2_ = bf16[256,512]{1,0:T(8,128)(2,1)S(1)} collective-permute-done((bf16[256,512]{1,0:T(8,128)(2,1)S(1)}, bf16[256,512]{1,0:T(8,128)(2,1)S(1)}, u32[]{:S(2)}, u32[]{:S(2)}) %collective-permute-start.20) | collective-permute-done | bytes 262176 | tf_op jit(solution)/shard_map/ppermute | solution.py:241
  72.9 1.6 %collective-permute-start.24 = (bf16[256,512]{1,0:T(8,128)(2,1)S(1)}, bf16[256,512]{1,0:T(8,128)(2,1)S(1)}, u32[]{:S(2)}, u32[]{:S(2)}) collective-permute-start(bf16[256,512]{1,0:T(8,128)(2,1)S(1)} %get-tuple-element.35), channel_id=1, source_target_pairs={{0,1},{1,0},{2,3},{3,2},{4,5},{5,4},{6,7},{7,6},{8,9},{9,8},{10,11... | collective-permute-start | bytes 786440 | tf_op jit(solution)/shard_map/ppermute | solution.py:298
  74.5 2.6 %collective-permute-start.25 = (bf16[256,512]{1,0:T(8,128)(2,1)S(1)}, bf16[256,512]{1,0:T(8,128)(2,1)S(1)}, u32[]{:S(2)}, u32[]{:S(2)}) collective-permute-start(bf16[256,512]{1,0:T(8,128)(2,1)S(1)} %get-tuple-element.36), channel_id=1, source_target_pairs={{0,2},{1,3},{2,0},{3,1},{4,6},{5,7},{6,4},{7,5},{8,10},{9,11},{10,... | collective-permute-start | bytes 786440 | tf_op jit(solution)/shard_map/ppermute | solution.py:298
  77.4 7.0 %collective-permute-done.24.refs_2_ = bf16[256,512]{1,0:T(8,128)(2,1)S(1)} collective-permute-done((bf16[256,512]{1,0:T(8,128)(2,1)S(1)}, bf16[256,512]{1,0:T(8,128)(2,1)S(1)}, u32[]{:S(2)}, u32[]{:S(2)}) %collective-permute-start.24) | collective-permute-done | bytes 262176 | tf_op jit(solution)/shard_map/ppermute | solution.py:298
  84.3 11.6 %collective-permute-done.25.refs_3_ = bf16[256,512]{1,0:T(8,128)(2,1)S(1)} collective-permute-done((bf16[256,512]{1,0:T(8,128)(2,1)S(1)}, bf16[256,512]{1,0:T(8,128)(2,1)S(1)}, u32[]{:S(2)}, u32[]{:S(2)}) %collective-permute-start.25) | collective-permute-done | bytes 262176 | tf_op jit(solution)/shard_map/ppermute | solution.py:298
  96.7 1.3 %collective-permute-done.27 = bf16[128,512]{1,0:T(8,128)(2,1)S(1)} collective-permute-done((bf16[128,512]{1,0:T(8,128)(2,1)S(1)}, bf16[128,512]{1,0:T(8,128)(2,1)S(1)}, u32[]{:S(2)}, u32[]{:S(2)}) %collective-permute-start.27) | collective-permute-done | bytes 131104 | tf_op jit(solution)/shard_map/ppermute | solution.py:238
  (62 shorter events, 13.0 us)
Async XLA Ops:
  0.0 28.5 %copy-start.9 = (f32[2048]{0:T(1024)S(1)}, f32[2048]{0:T(1024)}, u32[]{:S(2)}) copy-start(f32[2048]{0:T(1024)} %param.16) | copy-start | bytes 24580
  0.0 4.4 %collective-permute-start = (bf16[128,2048]{1,0:T(8,128)(2,1)}, bf16[128,2048]{1,0:T(8,128)(2,1)S(1)}, u32[]{:S(2)}, u32[]{:S(2)}) collective-permute-start(bf16[128,2048]{1,0:T(8,128)(2,1)} %xo.3), channel_id=1, source_target_pairs={{0,4},{4,0},{8,12},{12,8},{16,20},{20,16},{24,28},{28,24},{1,5},{5... | collective-permute-start | bytes 1572872 | tf_op jit(solution)/shard_map/ppermute | solution.py:238
  0.5 24.0 %collective-permute-start.5 = (bf16[128,2048]{1,0:T(8,128)(2,1)}, bf16[128,2048]{1,0:T(8,128)(2,1)S(1)}, u32[]{:S(2)}, u32[]{:S(2)}) collective-permute-start(bf16[128,2048]{1,0:T(8,128)(2,1)} %zo.1), channel_id=1, source_target_pairs={{0,4},{4,0},{8,12},{12,8},{16,20},{20,16},{24,28},{28,24},{1,5},{5... | collective-permute-start | bytes 1572872 | tf_op jit(solution)/shard_map/ppermute | solution.py:238
  0.5 2.5 %collective-permute-start.4 = (f32[32,128]{1,0:T(8,128)}, f32[32,128]{1,0:T(8,128)S(1)}, u32[]{:S(2)}, u32[]{:S(2)}) collective-permute-start(f32[32,128]{1,0:T(8,128)} %ldo.5), channel_id=1, source_target_pairs={{0,4},{4,0},{8,12},{12,8},{16,20},{20,16},{24,28},{28,24},{1,5},{5... | collective-permute-start | bytes 49160 | tf_op jit(solution)/shard_map/ppermute | solution.py:238
  1.0 3.4 %collective-permute-start.2 = (bf16[128,128]{1,0:T(8,128)(2,1)}, bf16[128,128]{1,0:T(8,128)(2,1)S(1)}, u32[]{:S(2)}, u32[]{:S(2)}) collective-permute-start(bf16[128,128]{1,0:T(8,128)(2,1)} %co.3), channel_id=1, source_target_pairs={{0,4},{4,0},{8,12},{12,8},{16,20},{20,16},{24,28},{28,24},{1,5},{5... | collective-permute-start | bytes 98312 | tf_op jit(solution)/shard_map/ppermute | solution.py:238
  1.0 3.4 %collective-permute-start.1 = (bf16[128,128]{1,0:T(8,128)(2,1)}, bf16[128,128]{1,0:T(8,128)(2,1)S(1)}, u32[]{:S(2)}, u32[]{:S(2)}) collective-permute-start(bf16[128,128]{1,0:T(8,128)(2,1)} %bo.3), channel_id=1, source_target_pairs={{0,4},{4,0},{8,12},{12,8},{16,20},{20,16},{24,28},{28,24},{1,5},{5... | collective-permute-start | bytes 98312 | tf_op jit(solution)/shard_map/ppermute | solution.py:238
  3.0 1.4 %collective-permute-start.3 = (f32[32,128]{1,0:T(8,128)}, f32[32,128]{1,0:T(8,128)S(1)}, u32[]{:S(2)}, u32[]{:S(2)}) collective-permute-start(f32[32,128]{1,0:T(8,128)} %dto.3), channel_id=1, source_target_pairs={{0,4},{4,0},{8,12},{12,8},{16,20},{20,16},{24,28},{28,24},{1,5},{5... | collective-permute-start | bytes 49160 | tf_op jit(solution)/shard_map/ppermute | solution.py:238
  4.4 1.0 %copy-start.1 = (bf16[128,2048]{1,0:T(8,128)(2,1)S(1)}, bf16[128,2048]{1,0:T(8,128)(2,1)}, u32[]{:S(2)}) copy-start(bf16[128,2048]{1,0:T(8,128)(2,1)} %xo.3) | copy-start | bytes 1572868
  7.7 20.8 %copy-start.2 = (bf16[128,2048]{1,0:T(8,128)(2,1)S(1)}, bf16[128,2048]{1,0:T(8,128)(2,1)}, u32[]{:S(2)}) copy-start(bf16[128,2048]{1,0:T(8,128)(2,1)} %zo.1) | copy-start | bytes 1572868
  9.9 14.5 %collective-permute-start.6 = (bf16[144,1024]{1,0:T(8,128)(2,1)S(1)}, bf16[144,1024]{1,0:T(8,128)(2,1)S(1)}, u32[]{:S(2)}, u32[]{:S(2)}) collective-permute-start(bf16[144,1024]{1,0:T(8,128)(2,1)S(1)} %get-tuple-element.24), channel_id=1, source_target_pairs={{0,8},{4,12},{8,16},{12,20},{16,24},{20,28},{1,9},{5,13},{9,17},{1... | collective-permute-start | bytes 884744 | tf_op jit(solution)/shard_map/ppermute | solution.py:256
  14.6 13.8 %collective-permute-start.7 = (bf16[144,1024]{1,0:T(8,128)(2,1)S(1)}, bf16[144,1024]{1,0:T(8,128)(2,1)S(1)}, u32[]{:S(2)}, u32[]{:S(2)}) collective-permute-start(bf16[144,1024]{1,0:T(8,128)(2,1)S(1)} %get-tuple-element.24), channel_id=1, source_target_pairs={{0,16},{4,20},{8,24},{12,28},{1,17},{5,21},{9,25},{13,29},{2,18},{... | collective-permute-start | bytes 884744 | tf_op jit(solution)/shard_map/ppermute | solution.py:256
  18.1 10.4 %collective-permute-start.8 = (bf16[144,1024]{1,0:T(8,128)(2,1)S(1)}, bf16[144,1024]{1,0:T(8,128)(2,1)S(1)}, u32[]{:S(2)}, u32[]{:S(2)}) collective-permute-start(bf16[144,1024]{1,0:T(8,128)(2,1)S(1)} %get-tuple-element.24), channel_id=1, source_target_pairs={{0,24},{4,28},{1,25},{5,29},{2,26},{6,30},{3,27},{7,31}} | collective-permute-start | bytes 884744 | tf_op jit(solution)/shard_map/ppermute | solution.py:256
  24.4 20.1 %copy-start = (bf16[2048,512]{1,0:T(8,128)(2,1)S(1)}, bf16[2048,512]{1,0:T(8,128)(2,1)}, u32[]{:S(2)}) copy-start(bf16[2048,512]{1,0:T(8,128)(2,1)} %refs_4_.1) | copy-start | bytes 6291460
  30.7 13.8 %collective-permute-start.11 = (bf16[256,1024]{1,0:T(8,128)(2,1)S(1)}, bf16[256,1024]{1,0:T(8,128)(2,1)S(1)}, u32[]{:S(2)}, u32[]{:S(2)}) collective-permute-start(bf16[256,1024]{1,0:T(8,128)(2,1)S(1)} %get-tuple-element.25.refs_0_), channel_id=1, source_target_pairs={{0,4},{4,0},{8,12},{12,8},{16,20},{20,16},{24,28},{28,24},{1,5},{5... | collective-permute-start | bytes 1572872 | tf_op jit(solution)/shard_map/ppermute | solution.py:238
  30.7 15.1 %collective-permute-start.10 = (bf16[256,1024]{1,0:T(8,128)(2,1)S(1)}, bf16[256,1024]{1,0:T(8,128)(2,1)S(1)}, u32[]{:S(2)}, u32[]{:S(2)}) collective-permute-start(bf16[256,1024]{1,0:T(8,128)(2,1)S(1)} %get-tuple-element.25.refs_0_), channel_id=1, source_target_pairs={{0,16},{4,20},{8,24},{12,28},{16,0},{20,4},{24,8},{28,12},{1,17},{... | collective-permute-start | bytes 1572872 | tf_op jit(solution)/shard_map/ppermute | solution.py:241
  33.2 14.2 %collective-permute-start.9 = (bf16[256,1024]{1,0:T(8,128)(2,1)S(1)}, bf16[256,1024]{1,0:T(8,128)(2,1)S(1)}, u32[]{:S(2)}, u32[]{:S(2)}) collective-permute-start(bf16[256,1024]{1,0:T(8,128)(2,1)S(1)} %get-tuple-element.25.refs_0_), channel_id=1, source_target_pairs={{0,8},{4,12},{8,0},{12,4},{16,24},{20,28},{24,16},{28,20},{1,9},{5... | collective-permute-start | bytes 1572872 | tf_op jit(solution)/shard_map/ppermute | solution.py:241
  35.1 1.2 %collective-permute-start.12 = (f32[16,128]{1,0:T(8,128)S(1)}, f32[16,128]{1,0:T(8,128)S(1)}, u32[]{:S(2)}, u32[]{:S(2)}) collective-permute-start(f32[16,128]{1,0:T(8,128)S(1)} %get-tuple-element.26), channel_id=1, source_target_pairs={{0,4},{4,0},{8,12},{12,8},{16,20},{20,16},{24,28},{28,24},{1,5},{5... | collective-permute-start | bytes 24584 | tf_op jit(solution)/shard_map/ppermute | solution.py:238
  36.2 3.7 %collective-permute-start.13 = (f32[16,128]{1,0:T(8,128)S(1)}, f32[16,128]{1,0:T(8,128)S(1)}, u32[]{:S(2)}, u32[]{:S(2)}) collective-permute-start(f32[16,128]{1,0:T(8,128)S(1)} %add.15), channel_id=1, source_target_pairs={{0,1},{1,0},{2,3},{3,2},{4,5},{5,4},{6,7},{7,6},{8,9},{9,8},{10,11... | collective-permute-start | bytes 24584 | tf_op jit(solution)/shard_map/ppermute | solution.py:279
  39.9 4.5 %collective-permute-start.14 = (f32[16,128]{1,0:T(8,128)S(1)}, f32[16,128]{1,0:T(8,128)S(1)}, u32[]{:S(2)}, u32[]{:S(2)}) collective-permute-start(f32[16,128]{1,0:T(8,128)S(1)} %add.16), channel_id=1, source_target_pairs={{0,2},{1,3},{2,0},{3,1},{4,6},{5,7},{6,4},{7,5},{8,10},{9,11},{10,... | collective-permute-start | bytes 24584 | tf_op jit(solution)/shard_map/ppermute | solution.py:279
  47.4 2.7 %collective-permute-start.18 = (bf16[256,1024]{1,0:T(8,128)(2,1)S(1)}, bf16[256,1024]{1,0:T(8,128)(2,1)S(1)}, u32[]{:S(2)}, u32[]{:S(2)}) collective-permute-start(bf16[256,1024]{1,0:T(8,128)(2,1)S(1)} %collective-permute-done.10.refs_0_), channel_id=1, source_target_pairs={{0,4},{4,0},{8,12},{12,8},{16,20},{20,16},{24,28},{28,24},{1,5},{5... | collective-permute-start | bytes 1572872 | tf_op jit(solution)/shard_map/ppermute | solution.py:238
  47.4 3.9 %collective-permute-start.17 = (bf16[256,1024]{1,0:T(8,128)(2,1)S(1)}, bf16[256,1024]{1,0:T(8,128)(2,1)S(1)}, u32[]{:S(2)}, u32[]{:S(2)}) collective-permute-start(bf16[256,1024]{1,0:T(8,128)(2,1)S(1)} %collective-permute-done.9.refs_0_), channel_id=1, source_target_pairs={{0,4},{4,0},{8,12},{12,8},{16,20},{20,16},{24,28},{28,24},{1,5},{5... | collective-permute-start | bytes 1572872 | tf_op jit(solution)/shard_map/ppermute | solution.py:238
  47.9 8.3 %collective-permute-start.15 = (bf16[128,1024]{1,0:T(8,128)(2,1)S(1)}, bf16[128,1024]{1,0:T(8,128)(2,1)S(1)}, u32[]{:S(2)}, u32[]{:S(2)}) collective-permute-start(bf16[128,1024]{1,0:T(8,128)(2,1)S(1)} %slice.6), channel_id=1, source_target_pairs={{0,16},{4,20},{8,24},{12,28},{16,0},{20,4},{24,8},{28,12},{1,17},{... | collective-permute-start | bytes 786440 | tf_op jit(solution)/shard_map/ppermute | solution.py:241
  48.3 8.0 %collective-permute-start.16 = (bf16[128,1024]{1,0:T(8,128)(2,1)S(1)}, bf16[128,1024]{1,0:T(8,128)(2,1)S(1)}, u32[]{:S(2)}, u32[]{:S(2)}) collective-permute-start(bf16[128,1024]{1,0:T(8,128)(2,1)S(1)} %slice.7), channel_id=1, source_target_pairs={{0,8},{4,12},{8,0},{12,4},{16,24},{20,28},{24,16},{28,20},{1,9},{5... | collective-permute-start | bytes 786440 | tf_op jit(solution)/shard_map/ppermute | solution.py:241
  56.3 3.9 %collective-permute-start.21 = (bf16[128,1024]{1,0:T(8,128)(2,1)S(1)}, bf16[128,1024]{1,0:T(8,128)(2,1)S(1)}, u32[]{:S(2)}, u32[]{:S(2)}) collective-permute-start(bf16[128,1024]{1,0:T(8,128)(2,1)S(1)} %collective-permute-done.15.refs_0_), channel_id=1, source_target_pairs={{0,4},{4,0},{8,12},{12,8},{16,20},{20,16},{24,28},{28,24},{1,5},{5... | collective-permute-start | bytes 786440 | tf_op jit(solution)/shard_map/ppermute | solution.py:238
  56.3 3.9 %collective-permute-start.22 = (bf16[128,1024]{1,0:T(8,128)(2,1)S(1)}, bf16[128,1024]{1,0:T(8,128)(2,1)S(1)}, u32[]{:S(2)}, u32[]{:S(2)}) collective-permute-start(bf16[128,1024]{1,0:T(8,128)(2,1)S(1)} %collective-permute-done.16.refs_1_), channel_id=1, source_target_pairs={{0,4},{4,0},{8,12},{12,8},{16,20},{20,16},{24,28},{28,24},{1,5},{5... | collective-permute-start | bytes 786440 | tf_op jit(solution)/shard_map/ppermute | solution.py:238
  56.8 9.2 %collective-permute-start.19 = (bf16[256,512]{1,0:T(8,128)(2,1)S(1)}, bf16[256,512]{1,0:T(8,128)(2,1)S(1)}, u32[]{:S(2)}, u32[]{:S(2)}) collective-permute-start(bf16[256,512]{1,0:T(8,128)(2,1)S(1)} %shard_map.95), channel_id=1, source_target_pairs={{0,8},{4,12},{8,0},{12,4},{16,24},{20,28},{24,16},{28,20},{1,9},{5... | collective-permute-start | bytes 786440 | tf_op jit(solution)/shard_map/ppermute | solution.py:241
  58.6 13.6 %collective-permute-start.20 = (bf16[256,512]{1,0:T(8,128)(2,1)S(1)}, bf16[256,512]{1,0:T(8,128)(2,1)S(1)}, u32[]{:S(2)}, u32[]{:S(2)}) collective-permute-start(bf16[256,512]{1,0:T(8,128)(2,1)S(1)} %shard_map.96), channel_id=1, source_target_pairs={{0,16},{4,20},{8,24},{12,28},{16,0},{20,4},{24,8},{28,12},{1,17},{... | collective-permute-start | bytes 786440 | tf_op jit(solution)/shard_map/ppermute | solution.py:241
  61.5 10.6 %collective-permute-start.23 = (bf16[256,512]{1,0:T(8,128)(2,1)S(1)}, bf16[256,512]{1,0:T(8,128)(2,1)S(1)}, u32[]{:S(2)}, u32[]{:S(2)}) collective-permute-start(bf16[256,512]{1,0:T(8,128)(2,1)S(1)} %shard_map.97), channel_id=1, source_target_pairs={{0,24},{4,28},{8,16},{12,20},{16,8},{20,12},{24,0},{28,4},{1,25},{... | collective-permute-start | bytes 786440 | tf_op jit(solution)/shard_map/ppermute | solution.py:241
  72.9 11.4 %collective-permute-start.24 = (bf16[256,512]{1,0:T(8,128)(2,1)S(1)}, bf16[256,512]{1,0:T(8,128)(2,1)S(1)}, u32[]{:S(2)}, u32[]{:S(2)}) collective-permute-start(bf16[256,512]{1,0:T(8,128)(2,1)S(1)} %get-tuple-element.35), channel_id=1, source_target_pairs={{0,1},{1,0},{2,3},{3,2},{4,5},{5,4},{6,7},{7,6},{8,9},{9,8},{10,11... | collective-permute-start | bytes 786440 | tf_op jit(solution)/shard_map/ppermute | solution.py:298
  74.5 21.4 %collective-permute-start.25 = (bf16[256,512]{1,0:T(8,128)(2,1)S(1)}, bf16[256,512]{1,0:T(8,128)(2,1)S(1)}, u32[]{:S(2)}, u32[]{:S(2)}) collective-permute-start(bf16[256,512]{1,0:T(8,128)(2,1)S(1)} %get-tuple-element.36), channel_id=1, source_target_pairs={{0,2},{1,3},{2,0},{3,1},{4,6},{5,7},{6,4},{7,5},{8,10},{9,11},{10,... | collective-permute-start | bytes 786440 | tf_op jit(solution)/shard_map/ppermute | solution.py:298
  77.1 18.8 %collective-permute-start.26 = (bf16[256,512]{1,0:T(8,128)(2,1)S(1)}, bf16[256,512]{1,0:T(8,128)(2,1)S(1)}, u32[]{:S(2)}, u32[]{:S(2)}) collective-permute-start(bf16[256,512]{1,0:T(8,128)(2,1)S(1)} %get-tuple-element.37), channel_id=1, source_target_pairs={{0,3},{1,2},{2,1},{3,0},{4,7},{5,6},{6,5},{7,4},{8,11},{9,10},{10,... | collective-permute-start | bytes 786440 | tf_op jit(solution)/shard_map/ppermute | solution.py:298
  96.7 1.4 %collective-permute-start.27 = (bf16[128,512]{1,0:T(8,128)(2,1)S(1)}, bf16[128,512]{1,0:T(8,128)(2,1)S(1)}, u32[]{:S(2)}, u32[]{:S(2)}) collective-permute-start(bf16[128,512]{1,0:T(8,128)(2,1)S(1)} %get-tuple-element.40), channel_id=1, source_target_pairs={{0,4},{4,0},{8,12},{12,8},{16,20},{20,16},{24,28},{28,24},{1,5},{5... | collective-permute-start | bytes 393224 | tf_op jit(solution)/shard_map/ppermute | solution.py:238
  (7 other events, 5.0 us)

commit v4 on v3

v4 whole, which is shorter than its diff:
```python
import jax
import jax.numpy as jnp
from jax import lax
from jax.experimental import pallas as pl
from jax.experimental.pallas import tpu as pltpu
from jax.sharding import PartitionSpec as P

BOTH = ("seq", "head")
HIGH = lax.Precision.HIGHEST
f32, bf16 = jnp.float32, jnp.bfloat16
EXT = 16
LANES = 128
MIB = 1024 * 1024


def call(kernel, scalars, ins, in_specs, outs, out_specs, scratch=(), flops=0, limit=24):
    moved = sum(a.size * a.dtype.itemsize for a in ins) + sum(
        o.size * o.dtype.itemsize for o in outs
    )
    return pl.pallas_call(
        kernel,
        out_shape=outs,
        grid_spec=pltpu.PrefetchScalarGridSpec(
            num_scalar_prefetch=1,
            grid=(1,),
            in_specs=in_specs,
            out_specs=out_specs,
            scratch_shapes=scratch,
        ),
        cost_estimate=pl.CostEstimate(flops=flops, bytes_accessed=moved, transcendentals=0),
        compiler_params=pltpu.CompilerParams(vmem_limit_bytes=limit * MIB),
    )(scalars, *ins)


def full(a):
    return pl.BlockSpec(memory_space=pltpu.VMEM)


def shape(dims, kind):
    return jax.ShapeDtypeStruct(dims, kind)


def nn(a, b, precision=None):
    return jnp.dot(a, b, preferred_element_type=f32, precision=precision)


def nt(a, b, precision=None):
    return lax.dot_general(a, b, (((1,), (1,)), ((), ())), preferred_element_type=f32, precision=precision)


def tn(a, b, precision=None):
    return lax.dot_general(a, b, (((0,), (0,)), ((), ())), preferred_element_type=f32, precision=precision)


def split2(v):
    hi = v.astype(bf16).astype(f32)
    return hi, v - hi


def half_lanes(ref, k):
    n = ref.shape[1] // 2
    return ref[:, pl.ds(pl.multiple_of(k * n, n), n)]


def half_rows(ref, k):
    v = ref[...]
    n = v.shape[0] // 4
    return tuple(jnp.where(k == 0, v[i : i + n], v[i + n : i + 2 * n]) for i in (0, 2 * n))


def channel_map(heads, wide):
    head = lax.broadcasted_iota(jnp.int32, (heads, wide), 0)
    lane = lax.broadcasted_iota(jnp.int32, (heads, wide), 1)
    size = wide // heads
    return ((lane >= head * size) & (lane < (head + 1) * size)).astype(bf16)


def spread(v, spots):
    hi, lo = split2(v)
    return tn(hi.astype(bf16), spots) + tn(lo.astype(bf16), spots)


def ones_upto(rows):
    i = lax.broadcasted_iota(jnp.int32, (rows, rows), 0)
    j = lax.broadcasted_iota(jnp.int32, (rows, rows), 1)
    return (j <= i), (i <= j)


def state_kernel(s, xo, xr, bo, br, ro, rr, msg, first):
    k = s[0]
    rows, wide = xo.shape
    half = pl.ds(pl.multiple_of(k * wide, wide), wide)
    _, upper = ones_upto(rows)
    got = []
    for x, bc, rates in ((xo[...], bo, ro), (xr[:, half], br, rr)):
        dt, ld = half_rows(rates, k)
        spots = channel_map(ld.shape[0], wide)
        run = nn(ld, upper.astype(f32), HIGH)
        last = run[:, rows - 1 :]
        tail = jnp.exp(last - run) * dt
        scaled = (x.astype(f32) * spread(tail, spots)).astype(bf16)
        state = tn(bc[:, : bc.shape[1] // 2], scaled)
        decay = spread(jnp.exp(jnp.broadcast_to(last, (last.shape[0], 8))), spots)
        got.append((state, decay))
    (so, do), (sr, dr) = got
    even = k == 0
    s1, s2 = jnp.where(even, so, sr), jnp.where(even, sr, so)
    d2 = jnp.where(even, dr, do)
    n = s1.shape[0]
    flat(msg, (d2[:1] * s1 + s2).astype(bf16))
    msg[wide * n // LANES :] = pair(jnp.concatenate([(do * dr)[:1, i : i + LANES] for i in range(0, wide, LANES)], 0))
    first[...] = s1


def flat(ref, value):
    rows = value.shape[0]
    for i in range(value.shape[1] // LANES):
        ref[i * rows : (i + 1) * rows] = value[:, i * LANES : (i + 1) * LANES]


def pair(v):
    if v.shape[0] < 8:
        v = jnp.concatenate([v, jnp.zeros((8 - v.shape[0], v.shape[1]), f32)], 0)
    hi, lo = split2(v)
    return jnp.concatenate([hi, lo], 0).astype(bf16)


def unpair(v):
    v = v.astype(f32)
    return v[:8] + v[8:]


def unpack(ref, n, wide):
    count = wide // LANES
    state = jnp.concatenate([ref[i * n : (i + 1) * n].astype(f32) for i in range(count)], 1)
    ext = unpair(ref[count * n :])
    return state, jnp.concatenate([ext[i : i + 1] for i in range(count)], 1)


def inside_kernel(s, xo, xr, bo, br, ro, rr, zo, zr, skip, out, decays, gates):
    k = s[0]
    rows, wide = xo.shape
    half = pl.ds(pl.multiple_of(k * wide, wide), wide)
    low, upper = ones_upto(rows)
    count = skip.shape[1] // 2
    gains = jnp.where(k == 0, skip[:, :count], skip[:, count:])
    hi, lo = split2(jnp.broadcast_to(gains, (8, count)))
    spots = channel_map(count, wide)
    gains = nn(hi.astype(bf16), spots) + nn(lo.astype(bf16), spots)
    for turn, (bc, rates, z) in enumerate(((bo, ro, zo), (br, rr, zr))):
        start = turn * rows
        dt, ld = half_rows(rates, k)
        heads = ld.shape[0]
        size = wide // heads
        run = nn(ld, upper.astype(f32), HIGH)
        down = nt(low.astype(f32), ld, HIGH)
        decays[start : start + rows] = spread(jnp.exp(run), spots)
        zf = z[:, half].astype(f32)
        gates[start : start + rows] = zf / (1.0 + jnp.exp(-zf))
        states = bc.shape[1] // 2
        scores = jnp.where(low, nt(bc[:, states:], bc[:, :states]), 0.0)
        lane = lax.broadcasted_iota(jnp.int32, (rows, 2 * size), 1)
        for pair in range(heads // 2):
            w = []
            for h in (2 * pair, 2 * pair + 1):
                gap = jnp.minimum(down[:, h : h + 1] - run[h : h + 1, :], 0.0)
                w.append((jnp.exp(gap) * scores * dt[h : h + 1, :]).astype(bf16))
            at = slice(2 * pair * size, 2 * (pair + 1) * size)
            if turn == 0:
                xp = xo[:, at]
            else:
                xp = xr[:, pl.ds(pl.multiple_of(k * wide + 2 * pair * size, 2 * size), 2 * size)]
            zero = jnp.zeros_like(xp)
            both = jnp.concatenate([jnp.where(lane < size, xp, zero), jnp.where(lane < size, zero, xp)], 0)
            y = nn(jnp.concatenate(w, 1), both)
            out[start : start + rows, at] = y + gains[:1, at] * xp.astype(f32)


def gate_kernel(s, inside, decays, gates, first, bo, br, gain, _, *rest):
    *states, mine, theirs, sq_mine, sq_theirs = rest
    k = s[0]
    rows, wide = mine.shape
    even = k == 0
    enter, through = None, None
    for ref in states:
        st, dec = unpack(ref, first.shape[0], wide)
        enter = st if enter is None else enter + st * through
        through = dec if through is None else through * dec
    whole = jnp.where(even, decays[rows - 1 : rows], decays[2 * rows - 1 : 2 * rows])
    second = whole * enter + first[...]
    ones = jnp.ones((8, wide), bf16)
    for turn, (bc, out, sq) in enumerate(((bo, mine, sq_mine), (br, theirs, sq_theirs))):
        at = slice(turn * rows, (turn + 1) * rows)
        e = jnp.where(even, enter, second) if turn == 0 else jnp.where(even, second, enter)
        y = inside[at] + nn(bc[:, bc.shape[1] // 2 :], e.astype(bf16)) * decays[at]
        gated = y * gates[at]
        hi, lo = split2(gated * gated)
        sq[...] = nt(ones, hi.astype(bf16)) + nt(ones, lo.astype(bf16))
        out[...] = (gated * half_lanes(gain, k)).astype(bf16)


def project_kernel(s, *refs, count, extra):
    u, v = refs[:count], refs[count : 2 * count]
    w_own, w_other = refs[2 * count : 2 * count + 2]
    outs = refs[2 * count + 2 + extra :]
    k = s[0]
    rows, depth = u[0].shape
    cols = w_own.shape[1]
    here = pl.ds(pl.multiple_of(k * depth, depth), depth)
    there = pl.ds(pl.multiple_of((1 - k) * depth, depth), depth)
    uu = jnp.concatenate([a[...] for a in u], 0)
    vv = jnp.concatenate([a[...] for a in v], 0)
    for w, place in ((w_own, k), (w_other, 1 - k)):
        got = (nn(uu, w[here]) + nn(vv, w[there])).astype(bf16)
        groups = cols // LANES
        for i, out in enumerate(outs):
            for j in range(groups):
                at = pl.ds(pl.multiple_of((place * groups + j) * rows, rows), rows)
                out[at] = got[i * rows : (i + 1) * rows, j * LANES : (j + 1) * LANES]


def pick(s, m, blocks, do):
    for j, block in enumerate(blocks):

        @pl.when((s[1] ^ m) == j)
        def _():
            do(block)


def choose_kernel(s, *refs, steps):
    count = len(refs) - 1 - len(steps)
    blocks, squares, outs = refs[:count], refs[count], refs[count + 1 :]
    n = blocks[0].shape[0]
    for m, out in zip(steps, outs):

        def copy(block, out=out):
            out[:n] = block[...]

        pick(s, m, blocks, copy)
        out[n:] = pair(squares[...])


def halves_kernel(s, *refs):
    *blocks, squares, top, low, other = refs
    n = low.shape[0]

    def cut(block):
        top[:n] = block[:n]
        low[...] = block[n:]

    def copy(block):
        other[: 2 * n] = block[...]

    pick(s, 3, blocks, cut)
    pick(s, 1, blocks, copy)
    ext = pair(squares[...])
    top[n:] = ext
    other[2 * n :] = ext


def join_kernel(s, *refs, base):
    *blocks, squares, got, out = refs
    n = blocks[0].shape[0] // 2

    def add(block):
        out[:n] = (block[base * n : (base + 1) * n].astype(f32) + got[:n].astype(f32)).astype(bf16)

    pick(s, 2, blocks, add)
    if base == 0:
        out[n:] = pair(squares[...] + unpair(got[n:]))


def sum_kernel(s, *refs, inner, count):
    blocks, (squares, *got, out) = refs[:count], refs[count:]
    rows = out.shape[0]
    groups = out.shape[1] // LANES
    size = groups * rows
    i = lax.broadcasted_iota(jnp.int32, (rows, rows), 0)
    j = lax.broadcasted_iota(jnp.int32, (rows, rows), 1)
    total = squares[...] + sum(unpair(a[a.shape[0] - EXT :]) for a in got if a.shape[0] % size % (size // 2) == EXT)
    row = lax.rsqrt(total[:1] / inner + 1e-5)
    col = jnp.sum(jnp.where(i == j, jnp.broadcast_to(row, (rows, rows)), 0.0), axis=1, keepdims=True)

    def finish(block):
        for g in range(groups):
            v = block[g * rows : (g + 1) * rows].astype(f32)
            at = 0
            for a in got:
                span = a.shape[0] // rows
                if span == groups:
                    v += a[g * rows : (g + 1) * rows].astype(f32)
                else:
                    if at <= g < at + span:
                        v += a[(g - at) * rows : (g - at + 1) * rows].astype(f32)
                    at += span
            out[:, g * LANES : (g + 1) * LANES] = (v * col).astype(bf16)

    pick(s, 0, blocks, finish)


def body(n, n_head, signal, gate_input, state_in, state_out, step_size, log_decay, skip_gain, norm_gain, out_weight):
    rows = signal.shape[0]
    heads = log_decay.shape[0]
    wide = signal.shape[1] // 2
    states = state_in.shape[1]
    cols = out_weight.shape[1]
    place, z = lax.axis_index("seq"), lax.axis_index("head")
    k, chip = place % 2, place // 2
    s = jnp.stack([k, chip ^ z]).astype(jnp.int32)
    any_spec = pl.BlockSpec(memory_space=pl.ANY)

    def swap(a):
        return lax.ppermute(a, "seq", [(i, i ^ 1) for i in range(2 * n)])

    def across(a, j):
        return lax.ppermute(a, "seq", [(i, i ^ (2 * j)) for i in range(2 * n)])

    def along(a, m):
        return lax.ppermute(a, "head", [(i, i ^ m) for i in range(n)])

    x2 = swap(signal)
    rates1 = jnp.concatenate([step_size, log_decay], 0)
    bc1 = jnp.concatenate([state_in, state_out], 1)
    rates2, bc2 = swap(rates1), swap(bc1)
    z2 = swap(gate_input)
    x1 = lax.dynamic_slice_in_dim(signal, k * wide, wide, 1)
    skip = skip_gain.reshape(1, heads)
    gain = norm_gain.reshape(1, 2 * wide)

    ins = (x1, x2, bc1, bc2, rates1, rates2)
    outs = [shape((states * wide // LANES + EXT, LANES), bf16), shape((states, wide), f32)]
    msg, first = call(state_kernel, s, ins, [full(a) for a in ins], outs, [full(a) for a in outs])
    w2 = swap(lax.optimization_barrier((out_weight, msg))[0])
    got = [
        lax.ppermute(msg, "seq", [(i, i + 2 * j) for i in range(2 * (n - j))]) for j in range(1, n)
    ]
    ins = (x1, x2, bc1, bc2, rates1, rates2, gate_input, z2, skip)
    big = shape((2 * rows, wide), f32)
    inside, decays, gates = call(
        inside_kernel, s, ins, [full(a) for a in ins], [big] * 3, [full(big)] * 3
    )
    ins = (inside, decays, gates, first, bc1, bc2, gain, w2, *got)
    specs = [full(a) for a in ins[:7]] + [any_spec] + [full(a) for a in got]
    outs = [shape((rows, wide), bf16)] * 2 + [shape((8, rows), f32)] * 2
    u, v, sq_mine, sq_theirs = call(gate_kernel, s, ins, specs, outs, [full(a) for a in outs])
    squares = sq_mine + swap(sq_theirs)

    size = 2 * cols // LANES * rows
    p_shape = shape((size, LANES), bf16)

    def project(u, v, after=()):
        ins = (*u, *v, out_weight, w2, *after)
        specs = [full(a) for a in ins[: len(ins) - len(after)]] + [any_spec] * len(after)

        def kernel(*refs):
            project_kernel(*refs, count=len(u), extra=len(after))

        return call(kernel, s, ins, specs, [p_shape] * len(u), [full(p_shape)] * len(u))

    if n == 4:
        ux, vy = across(u, 1), across(v, 2)
        vx, uy = across(v, 1), across(u, 2)
        (own,) = project([u], [swap(v)])
        ux, vy, own = lax.optimization_barrier((ux, vy, own))
        ud, vd = lax.optimization_barrier((across(ux, 2), across(vy, 1)))
        near = project([ux, uy], [swap(vx), swap(vy)], after=[own])
        blocks = [own] + [across(near[0], 1), across(near[1], 2)]
        (far,) = project([ud], [swap(vd)], after=blocks[1:])
        blocks.append(across(far, 3))
    else:
        blocks = list(project([u], [swap(v)]))
        for j in range(1, n):
            (p,) = project([across(u, j)], [swap(across(v, j))])
            blocks.append(across(p, j))
    message = shape((size + EXT, LANES), bf16)

    def send(kernel, ins, outs, **kw):
        def run(*refs):
            kernel(*refs, **kw)

        return call(run, s, ins, [full(a) for a in ins], outs, [full(a) for a in outs])

    if n == 4:
        tall, short = shape((size // 2 + EXT, LANES), bf16), shape((size // 2, LANES), bf16)
        top, low, other = send(halves_kernel, (*blocks, squares), [tall, short, message])
        top, low, other = along(top, 1), along(low, 1), along(other, 1)
        (top,) = send(join_kernel, (*blocks, squares, top), [tall], base=0)
        (low,) = send(join_kernel, (*blocks, squares, low), [short], base=1)
        got = (other, along(top, 2), along(low, 2))
    else:
        steps = range(1, n)
        got = send(choose_kernel, (*blocks, squares), [message] * (n - 1), steps=steps)
        got = [along(a, m) for a, m in zip(got, steps)]
    return send(
        sum_kernel, (*blocks, squares, *got), [shape((rows, 2 * cols), bf16)],
        inner=2 * wide * n_head, count=n,
    )[0]


def solution(mesh):
    n, n_head = mesh.shape["seq"] // 2, mesh.shape["head"]
    assert n == n_head and n & (n - 1) == 0
    in_specs = (
        P("seq", "head"),
        P("seq", "head"),
        P("seq", None),
        P("seq", None),
        P("head", "seq"),
        P("head", "seq"),
        P("head"),
        P("head"),
        P("head", "seq"),
    )

    def run(*args):
        return body(n, n_head, *args)

    return jax.shard_map(run, mesh=mesh, in_specs=in_specs, out_specs=P("seq", "head"), check_vma=False)
```

time: 101 us -> 93.7 us (0.928); the launches traced: 98.9 us -> 93.2 us
  waiting for transfers between devices: 46.7 us -> 42.6 us
  local copies, waits for them, and re-layouts: 6.12 us -> 4.6 us
    ppermute x5, waiting for transfers between devices: 22.6 us -> 11.8 us  [along(): return lax.ppermute(a, 'head', [(i, i ^ m) for i in range(n)])]
    ppermute x7 -> x9, waiting for transfers between devices: 15.1 us -> 23.4 us  [across(): return lax.ppermute(a, 'seq', [(i, i ^ 2 * j) for i in range(2 * n)])]
    unnamed x22 -> x10, local copies, waits for them, and re-layouts: 6.08 us -> 2.15 us
    ppermute x13 -> x10, waiting for transfers between devices: 5 us -> 1.19 us  [swap(): return lax.ppermute(a, 'seq', [(i, i ^ 1) for i in range(2 * n)])]
    ppermute x3, waiting for transfers between devices: 4.04 us -> 6.17 us  [body(): lax.ppermute(msg, 'seq', [(i, i + 2 * j) for i in range(2 * (n - j))])]
    ppermute x7 -> x9, starting transfers between devices: 10.8 us -> 12.5 us  [across(): return lax.ppermute(a, 'seq', [(i, i ^ 2 * j) for i in range(2 * n)])]
    concatenate x0 -> x2, local copies, waits for them, and re-layouts: none -> 1.49 us  [the longest x1 0.77 us: body(): bc1 = jnp.concatenate([state_in, state_out], 1)]
    ppermute x13 -> x10, starting transfers between devices: 2.99 us -> 2.11 us  [swap(): return lax.ppermute(a, 'seq', [(i, i ^ 1) for i in range(2 * n)])]
  transfers between devices with their start and end apart: 28 -> 27, of which waited for: 14 -> 14; matrix products, arithmetic and copies ran while one was open for 0% -> 4% of each run, Pallas kernels for 9% -> 7%
where the time goes in v4:
time: 93.7 us; the launch traced here: 93.2 us
  waiting for transfers between devices  42.6 us (45%)
  starting transfers between devices  32.1 us (34%)
  Pallas kernels  13.7 us (15%)
  local copies, waits for them, and re-layouts  4.6 us (5%)
    ppermute x9, waiting for transfers between devices, across(): return lax.ppermute(a, 'seq', [(i, i ^ 2 * j) for i in range(2 * n)])  23.4 us
    pallas_call x10, Pallas kernels, call(): pl.pallas_call(kernel, out_shape=outs, grid_spec=pltpu.PrefetchScalarGrid...  13.7 us
    ppermute x9, starting transfers between devices, across(): return lax.ppermute(a, 'seq', [(i, i ^ 2 * j) for i in range(2 * n)])  12.5 us
    ppermute x5, waiting for transfers between devices, along(): return lax.ppermute(a, 'head', [(i, i ^ m) for i in range(n)])  11.8 us
    ppermute x3, starting transfers between devices, body(): lax.ppermute(msg, 'seq', [(i, i + 2 * j) for i in range(2 * (n - j))])  9.33 us
    ppermute x5, starting transfers between devices, along(): return lax.ppermute(a, 'head', [(i, i ^ m) for i in range(n)])  8.12 us
    ppermute x3, waiting for transfers between devices, body(): lax.ppermute(msg, 'seq', [(i, i + 2 * j) for i in range(2 * (n - j))])  6.17 us
    unnamed x10, local copies, waits for them, and re-layouts  2.15 us
  transfers between devices with their start and end apart: 27, of which 14 were waited for; matrix products, arithmetic and copies ran while one was open for 4% of the time, Pallas kernels for 7%

profile of v4, /device:TPU:0, one launch (start us, length us, event | category | flops | bytes accessed | tf_op | source)
XLA Modules:
  0.0 93.2 jit_solution(1598053457595479840)
XLA Ops:
  5.1 2.2 %shard_map.92 = (bf16[1040,128]{1,0:T(8,128)(2,1)S(1)}, f32[128,1024]{1,0:T(8,128)S(1)}) custom-call(s32[2]{0:T(128)S(1)} %pad_add_fusion.s.refs_0_, bf16[128,1024]{1,0:T(8,128)(2,1)S(1)} %constant_dynamic-slice_fusion.xo, bf16[128,2048]{1,0:T(8,128)(2,1)S(1)} %collective-permute-done.xr, bf16[128,256]{1,0:T(8,128)(2,1)S(1)} %constant_dynamic-update-slice_fusion.bo, ...), custom_call_target="tpu_custom_call" | custom-call | bytes 1773568 | tf_op jit(solution)/shard_map/pallas_call | solution.py:20
  7.9 5.5 %collective-permute-start.7 = (bf16[1040,128]{1,0:T(8,128)(2,1)S(1)}, bf16[1040,128]{1,0:T(8,128)(2,1)S(1)}, u32[]{:S(2)}, u32[]{:S(2)}) collective-permute-start(bf16[1040,128]{1,0:T(8,128)(2,1)S(1)} %get-tuple-element.29), channel_id=1, source_target_pairs={{0,24},{4,28},{1,25},{5,29},{2,26},{6,30},{3,27},{7,31}} | collective-permute-start | bytes 798728 | tf_op jit(solution)/shard_map/ppermute | solution.py:335
  13.4 1.3 %collective-permute-start.6 = (bf16[1040,128]{1,0:T(8,128)(2,1)S(1)}, bf16[1040,128]{1,0:T(8,128)(2,1)S(1)}, u32[]{:S(2)}, u32[]{:S(2)}) collective-permute-start(bf16[1040,128]{1,0:T(8,128)(2,1)S(1)} %get-tuple-element.29), channel_id=1, source_target_pairs={{0,16},{4,20},{8,24},{12,28},{1,17},{5,21},{9,25},{13,29},{2,18},{... | collective-permute-start | bytes 798728 | tf_op jit(solution)/shard_map/ppermute | solution.py:335
  14.7 2.5 %collective-permute-start.5 = (bf16[1040,128]{1,0:T(8,128)(2,1)S(1)}, bf16[1040,128]{1,0:T(8,128)(2,1)S(1)}, u32[]{:S(2)}, u32[]{:S(2)}) collective-permute-start(bf16[1040,128]{1,0:T(8,128)(2,1)S(1)} %get-tuple-element.29), channel_id=1, source_target_pairs={{0,8},{4,12},{8,16},{12,20},{16,24},{20,28},{1,9},{5,13},{9,17},{1... | collective-permute-start | bytes 798728 | tf_op jit(solution)/shard_map/ppermute | solution.py:335
  17.9 2.5 %shard_map.91 = (f32[256,1024]{1,0:T(8,128)S(1)}, f32[256,1024]{1,0:T(8,128)S(1)}, f32[256,1024]{1,0:T(8,128)S(1)}) custom-call(s32[2]{0:T(128)S(1)} %pad_add_fusion.s.refs_0_, bf16[128,1024]{1,0:T(8,128)(2,1)S(1)} %constant_dynamic-slice_fusion.xo, bf16[128,2048]{1,0:T(8,128)(2,1)S(1)} %collective-permute-done.xr, ...), custom_call_target="tpu_custom_call" | custom-call | bytes 5177472 | tf_op jit(solution)/shard_map/pallas_call | solution.py:20
  20.4 6.2 %collective-permute-done.6.rest_1_ = bf16[1040,128]{1,0:T(8,128)(2,1)S(1)} collective-permute-done((bf16[1040,128]{1,0:T(8,128)(2,1)S(1)}, bf16[1040,128]{1,0:T(8,128)(2,1)S(1)}, u32[]{:S(2)}, u32[]{:S(2)}) %collective-permute-start.6) | collective-permute-done | bytes 266272 | tf_op jit(solution)/shard_map/ppermute | solution.py:335
  26.6 1.4 %shard_map.93 = (bf16[128,1024]{1,0:T(8,128)(2,1)S(1)}, bf16[128,1024]{1,0:T(8,128)(2,1)S(1)}, f32[8,128]{1,0:T(8,128)S(1)}, f32[8,128]{1,0:T(8,128)S(1)}) custom-call(s32[2]{0:T(128)S(1)} %pad_add_fusion.s.refs_0_, f32[256,1024]{1,0:T(8,128)S(1)} %get-tuple-element.25.inside, f32[256,1024]{1,0:T(8,128)S(1)} %get-tuple-element.26.decays, ...), custom_call_target="tpu_custom_call" | custom-call | bytes 7237632 | tf_op jit(solution)/shard_map/pallas_call | solution.py:20
  28.0 1.2 %collective-permute-start.8 = (bf16[128,1024]{1,0:T(8,128)(2,1)S(1)}, bf16[128,1024]{1,0:T(8,128)(2,1)S(1)}, u32[]{:S(2)}, u32[]{:S(2)}) collective-permute-start(bf16[128,1024]{1,0:T(8,128)(2,1)S(1)} %get-tuple-element.31.refs_1_), channel_id=1, source_target_pairs={{0,8},{4,12},{8,0},{12,4},{16,24},{20,28},{24,16},{28,20},{1,9},{5... | collective-permute-start | bytes 786440 | tf_op jit(solution)/shard_map/ppermute | solution.py:316
  29.2 1.5 %collective-permute-start.9 = (bf16[128,1024]{1,0:T(8,128)(2,1)S(1)}, bf16[128,1024]{1,0:T(8,128)(2,1)S(1)}, u32[]{:S(2)}, u32[]{:S(2)}) collective-permute-start(bf16[128,1024]{1,0:T(8,128)(2,1)S(1)} %get-tuple-element.32), channel_id=1, source_target_pairs={{0,16},{4,20},{8,24},{12,28},{16,0},{20,4},{24,8},{28,12},{1,17},{... | collective-permute-start | bytes 786440 | tf_op jit(solution)/shard_map/ppermute | solution.py:316
  30.7 1.8 %collective-permute-start.12 = (bf16[128,1024]{1,0:T(8,128)(2,1)S(1)}, bf16[128,1024]{1,0:T(8,128)(2,1)S(1)}, u32[]{:S(2)}, u32[]{:S(2)}) collective-permute-start(bf16[128,1024]{1,0:T(8,128)(2,1)S(1)} %get-tuple-element.32), channel_id=1, source_target_pairs={{0,8},{4,12},{8,0},{12,4},{16,24},{20,28},{24,16},{28,20},{1,9},{5... | collective-permute-start | bytes 786440 | tf_op jit(solution)/shard_map/ppermute | solution.py:316
  32.5 1.3 %shard_map.94.refs_7_.refs_1_ = bf16[1024,128]{1,0:T(8,128)(2,1)S(1)} custom-call(s32[2]{0:T(128)S(1)} %pad_add_fusion.s.refs_0_, bf16[128,1024]{1,0:T(8,128)(2,1)S(1)} %get-tuple-element.31.refs_1_, bf16[128,1024]{1,0:T(8,128)(2,1)S(1)} %collective-permute-done.10.refs_2_, bf16[2048,512]{1,0:T(8,128)(2,1)S(1)} %copy-done, ...), custom_call_target="tpu_custom_call" | custom-call | bytes 4980736 | tf_op jit(solution)/shard_map/pallas_call | solution.py:20
  33.8 3.3 %collective-permute-done.8.refs_1_ = bf16[128,1024]{1,0:T(8,128)(2,1)S(1)} collective-permute-done((bf16[128,1024]{1,0:T(8,128)(2,1)S(1)}, bf16[128,1024]{1,0:T(8,128)(2,1)S(1)}, u32[]{:S(2)}, u32[]{:S(2)}) %collective-permute-start.8) | collective-permute-done | bytes 262176 | tf_op jit(solution)/shard_map/ppermute | solution.py:316
  37.6 2.0 %collective-permute-start.17 = (bf16[128,1024]{1,0:T(8,128)(2,1)S(1)}, bf16[128,1024]{1,0:T(8,128)(2,1)S(1)}, u32[]{:S(2)}, u32[]{:S(2)}) collective-permute-start(bf16[128,1024]{1,0:T(8,128)(2,1)S(1)} %collective-permute-done.8.refs_1_), channel_id=1, source_target_pairs={{0,16},{4,20},{8,24},{12,28},{16,0},{20,4},{24,8},{28,12},{1,17},{... | collective-permute-start | bytes 786440 | tf_op jit(solution)/shard_map/ppermute | solution.py:316
  39.6 1.3 %collective-permute-start.18 = (bf16[128,1024]{1,0:T(8,128)(2,1)S(1)}, bf16[128,1024]{1,0:T(8,128)(2,1)S(1)}, u32[]{:S(2)}, u32[]{:S(2)}) collective-permute-start(bf16[128,1024]{1,0:T(8,128)(2,1)S(1)} %collective-permute-done.9), channel_id=1, source_target_pairs={{0,8},{4,12},{8,0},{12,4},{16,24},{20,28},{24,16},{28,20},{1,9},{5... | collective-permute-start | bytes 786440 | tf_op jit(solution)/shard_map/ppermute | solution.py:316
  41.2 1.5 %collective-permute-done.12 = bf16[128,1024]{1,0:T(8,128)(2,1)S(1)} collective-permute-done((bf16[128,1024]{1,0:T(8,128)(2,1)S(1)}, bf16[128,1024]{1,0:T(8,128)(2,1)S(1)}, u32[]{:S(2)}, u32[]{:S(2)}) %collective-permute-start.12) | collective-permute-done | bytes 262176 | tf_op jit(solution)/shard_map/ppermute | solution.py:316
  43.2 3.6 %collective-permute-done.17.refs_1_ = bf16[128,1024]{1,0:T(8,128)(2,1)S(1)} collective-permute-done((bf16[128,1024]{1,0:T(8,128)(2,1)S(1)}, bf16[128,1024]{1,0:T(8,128)(2,1)S(1)}, u32[]{:S(2)}, u32[]{:S(2)}) %collective-permute-start.17) | collective-permute-done | bytes 262176 | tf_op jit(solution)/shard_map/ppermute | solution.py:316
  47.9 3.0 %collective-permute-done.11.refs_2_ = bf16[128,1024]{1,0:T(8,128)(2,1)S(1)} collective-permute-done((bf16[128,1024]{1,0:T(8,128)(2,1)S(1)}, bf16[128,1024]{1,0:T(8,128)(2,1)S(1)}, u32[]{:S(2)}, u32[]{:S(2)}) %collective-permute-start.11) | collective-permute-done | bytes 262176 | tf_op jit(solution)/shard_map/ppermute | solution.py:316
  51.0 1.8 %shard_map.95 = (bf16[1024,128]{1,0:T(8,128)(2,1)S(1)}, bf16[1024,128]{1,0:T(8,128)(2,1)S(1)}) custom-call(s32[2]{0:T(128)S(1)} %pad_add_fusion.s.refs_0_, bf16[128,1024]{1,0:T(8,128)(2,1)S(1)} %collective-permute-done.8.refs_1_, bf16[128,1024]{1,0:T(8,128)(2,1)S(1)} %collective-permute-done.11.refs_2_, ...), custom_call_target="tpu_custom_call" | custom-call | bytes 6029312 | tf_op jit(solution)/shard_map/pallas_call | solution.py:20
  52.8 1.8 %collective-permute-start.15 = (bf16[1024,128]{1,0:T(8,128)(2,1)S(1)}, bf16[1024,128]{1,0:T(8,128)(2,1)S(1)}, u32[]{:S(2)}, u32[]{:S(2)}) collective-permute-start(bf16[1024,128]{1,0:T(8,128)(2,1)S(1)} %get-tuple-element.36), channel_id=1, source_target_pairs={{0,8},{4,12},{8,0},{12,4},{16,24},{20,28},{24,16},{28,20},{1,9},{5... | collective-permute-start | bytes 786440 | tf_op jit(solution)/shard_map/ppermute | solution.py:316
  54.6 1.4 %collective-permute-start.16 = (bf16[1024,128]{1,0:T(8,128)(2,1)S(1)}, bf16[1024,128]{1,0:T(8,128)(2,1)S(1)}, u32[]{:S(2)}, u32[]{:S(2)}) collective-permute-start(bf16[1024,128]{1,0:T(8,128)(2,1)S(1)} %get-tuple-element.37), channel_id=1, source_target_pairs={{0,16},{4,20},{8,24},{12,28},{16,0},{20,4},{24,8},{28,12},{1,17},{... | collective-permute-start | bytes 786440 | tf_op jit(solution)/shard_map/ppermute | solution.py:316
  56.0 3.9 %collective-permute-done.15.refs_5_.refs_2_ = bf16[1024,128]{1,0:T(8,128)(2,1)S(1)} collective-permute-done((bf16[1024,128]{1,0:T(8,128)(2,1)S(1)}, bf16[1024,128]{1,0:T(8,128)(2,1)S(1)}, u32[]{:S(2)}, u32[]{:S(2)}) %collective-permute-start.15) | collective-permute-done | bytes 262176 | tf_op jit(solution)/shard_map/ppermute | solution.py:316
  59.9 1.5 %collective-permute-done.16.refs_6_.refs_3_ = bf16[1024,128]{1,0:T(8,128)(2,1)S(1)} collective-permute-done((bf16[1024,128]{1,0:T(8,128)(2,1)S(1)}, bf16[1024,128]{1,0:T(8,128)(2,1)S(1)}, u32[]{:S(2)}, u32[]{:S(2)}) %collective-permute-start.16) | collective-permute-done | bytes 262176 | tf_op jit(solution)/shard_map/ppermute | solution.py:316
  61.4 1.3 %shard_map.96 = bf16[1024,128]{1,0:T(8,128)(2,1)S(1)} custom-call(s32[2]{0:T(128)S(1)} %pad_add_fusion.s.refs_0_, bf16[128,1024]{1,0:T(8,128)(2,1)S(1)} %collective-permute-done.17.refs_1_, bf16[128,1024]{1,0:T(8,128)(2,1)S(1)} %collective-permute-done.19.refs_2_, bf16[2048,512]{1,0:T(8,128)(2,1)S(1)} %copy-done, ...), custom_call_target="tpu_custom_call" | custom-call | bytes 5505024 | tf_op jit(solution)/shard_map/pallas_call | solution.py:20
  65.0 5.0 %collective-permute-done.20.refs_4_ = bf16[1024,128]{1,0:T(8,128)(2,1)S(1)} collective-permute-done((bf16[1024,128]{1,0:T(8,128)(2,1)S(1)}, bf16[1024,128]{1,0:T(8,128)(2,1)S(1)}, u32[]{:S(2)}, u32[]{:S(2)}) %collective-permute-start.20) | collective-permute-done | bytes 262176 | tf_op jit(solution)/shard_map/ppermute | solution.py:316
  70.6 1.6 %collective-permute-start.23 = (bf16[528,128]{1,0:T(8,128)(2,1)S(1)}, bf16[528,128]{1,0:T(8,128)(2,1)S(1)}, u32[]{:S(2)}, u32[]{:S(2)}) collective-permute-start(bf16[528,128]{1,0:T(8,128)(2,1)S(1)} %get-tuple-element.43), channel_id=1, source_target_pairs={{0,1},{1,0},{2,3},{3,2},{4,5},{5,4},{6,7},{7,6},{8,9},{9,8},{10,11... | collective-permute-start | bytes 405512 | tf_op jit(solution)/shard_map/ppermute | solution.py:319
  72.7 1.6 %collective-permute-start.25 = (bf16[512,128]{1,0:T(8,128)(2,1)S(1)}, bf16[512,128]{1,0:T(8,128)(2,1)S(1)}, u32[]{:S(2)}, u32[]{:S(2)}) collective-permute-start(bf16[512,128]{1,0:T(8,128)(2,1)S(1)} %get-tuple-element.44), channel_id=1, source_target_pairs={{0,1},{1,0},{2,3},{3,2},{4,5},{5,4},{6,7},{7,6},{8,9},{9,8},{10,11... | collective-permute-start | bytes 393224 | tf_op jit(solution)/shard_map/ppermute | solution.py:319
  74.3 4.1 %collective-permute-done.23.refs_6_ = bf16[528,128]{1,0:T(8,128)(2,1)S(1)} collective-permute-done((bf16[528,128]{1,0:T(8,128)(2,1)S(1)}, bf16[528,128]{1,0:T(8,128)(2,1)S(1)}, u32[]{:S(2)}, u32[]{:S(2)}) %collective-permute-start.23) | collective-permute-done | bytes 135200 | tf_op jit(solution)/shard_map/ppermute | solution.py:319
  79.0 1.7 %collective-permute-start.24 = (bf16[528,128]{1,0:T(8,128)(2,1)S(1)}, bf16[528,128]{1,0:T(8,128)(2,1)S(1)}, u32[]{:S(2)}, u32[]{:S(2)}) collective-permute-start(bf16[528,128]{1,0:T(8,128)(2,1)S(1)} %shard_map.98), channel_id=1, source_target_pairs={{0,2},{1,3},{2,0},{3,1},{4,6},{5,7},{6,4},{7,5},{8,10},{9,11},{10,... | collective-permute-start | bytes 405512 | tf_op jit(solution)/shard_map/ppermute | solution.py:319
  80.7 3.1 %collective-permute-done.25.refs_6_ = bf16[512,128]{1,0:T(8,128)(2,1)S(1)} collective-permute-done((bf16[512,128]{1,0:T(8,128)(2,1)S(1)}, bf16[512,128]{1,0:T(8,128)(2,1)S(1)}, u32[]{:S(2)}, u32[]{:S(2)}) %collective-permute-start.25) | collective-permute-done | bytes 131104 | tf_op jit(solution)/shard_map/ppermute | solution.py:319
  84.4 2.7 %collective-permute-start.26 = (bf16[512,128]{1,0:T(8,128)(2,1)S(1)}, bf16[512,128]{1,0:T(8,128)(2,1)S(1)}, u32[]{:S(2)}, u32[]{:S(2)}) collective-permute-start(bf16[512,128]{1,0:T(8,128)(2,1)S(1)} %shard_map.99), channel_id=1, source_target_pairs={{0,2},{1,3},{2,0},{3,1},{4,6},{5,7},{6,4},{7,5},{8,10},{9,11},{10,... | collective-permute-start | bytes 393224 | tf_op jit(solution)/shard_map/ppermute | solution.py:319
  87.1 4.6 %collective-permute-done.26.refs_8_ = bf16[512,128]{1,0:T(8,128)(2,1)S(1)} collective-permute-done((bf16[512,128]{1,0:T(8,128)(2,1)S(1)}, bf16[512,128]{1,0:T(8,128)(2,1)S(1)}, u32[]{:S(2)}, u32[]{:S(2)}) %collective-permute-start.26) | collective-permute-done | bytes 131104 | tf_op jit(solution)/shard_map/ppermute | solution.py:319
  91.8 1.5 %shard_map.100 = bf16[128,1024]{1,0:T(8,128)(2,1)} custom-call(s32[2]{0:T(128)S(1)} %pad_add_fusion.s.refs_0_, bf16[1024,128]{1,0:T(8,128)(2,1)S(1)} %shard_map.94.refs_7_.refs_1_, bf16[1024,128]{1,0:T(8,128)(2,1)S(1)} %collective-permute-done.15.refs_5_.refs_2_, bf16[1024,128]{1,0:T(8,128)(2,1)S(1)} %collective-permute-done.16.refs_6_.refs_3_, ...), custom_call_target="tpu_custom_call" | custom-call | bytes 1847296 | tf_op jit(solution)/shard_map/pallas_call | solution.py:20
  (47 shorter events, 13.3 us)
Async XLA Ops:
  0.0 17.2 %copy-start.1 = (bf16[128,2048]{1,0:T(8,128)(2,1)S(1)}, bf16[128,2048]{1,0:T(8,128)(2,1)}, u32[]{:S(2)}) copy-start(bf16[128,2048]{1,0:T(8,128)(2,1)} %zo.1) | copy-start | bytes 1572868
  0.0 26.5 %copy-start.2 = (f32[2048]{0:T(1024)S(1)}, f32[2048]{0:T(1024)}, u32[]{:S(2)}) copy-start(f32[2048]{0:T(1024)} %param.16) | copy-start | bytes 24580
  0.0 5.1 %collective-permute-start = (bf16[128,2048]{1,0:T(8,128)(2,1)}, bf16[128,2048]{1,0:T(8,128)(2,1)S(1)}, u32[]{:S(2)}, u32[]{:S(2)}) collective-permute-start(bf16[128,2048]{1,0:T(8,128)(2,1)} %param.9), channel_id=1, source_target_pairs={{0,4},{4,0},{8,12},{12,8},{16,20},{20,16},{24,28},{28,24},{1,5},{5... | collective-permute-start | bytes 1572872 | tf_op jit(solution)/shard_map/ppermute | solution.py:313
  1.9 3.2 %collective-permute-start.2 = (f32[64,128]{1,0:T(8,128)S(1)}, f32[64,128]{1,0:T(8,128)S(1)}, u32[]{:S(2)}, u32[]{:S(2)}) collective-permute-start(f32[64,128]{1,0:T(8,128)S(1)} %constant_dynamic-update-slice_fusion.2.ro), channel_id=1, source_target_pairs={{0,4},{4,0},{8,12},{12,8},{16,20},{20,16},{24,28},{28,24},{1,5},{5... | collective-permute-start | bytes 98312 | tf_op jit(solution)/shard_map/ppermute | solution.py:313
  3.5 1.5 %collective-permute-start.1 = (bf16[128,256]{1,0:T(8,128)(2,1)S(1)}, bf16[128,256]{1,0:T(8,128)(2,1)S(1)}, u32[]{:S(2)}, u32[]{:S(2)}) collective-permute-start(bf16[128,256]{1,0:T(8,128)(2,1)S(1)} %constant_dynamic-update-slice_fusion.bo), channel_id=1, source_target_pairs={{0,4},{4,0},{8,12},{12,8},{16,20},{20,16},{24,28},{28,24},{1,5},{5... | collective-permute-start | bytes 196616 | tf_op jit(solution)/shard_map/ppermute | solution.py:313
  7.3 19.3 %collective-permute-start.4 = (bf16[2048,512]{1,0:T(8,128)(2,1)}, bf16[2048,512]{1,0:T(8,128)(2,1)S(1)}, u32[]{:S(2)}, u32[]{:S(2)}) collective-permute-start(bf16[2048,512]{1,0:T(8,128)(2,1)} %refs_3_.3), channel_id=1, source_target_pairs={{0,4},{4,0},{8,12},{12,8},{16,20},{20,16},{24,28},{28,24},{1,5},{5... | collective-permute-start | bytes 6291464 | tf_op jit(solution)/shard_map/ppermute | solution.py:313
  7.5 9.7 %collective-permute-start.3 = (bf16[128,2048]{1,0:T(8,128)(2,1)}, bf16[128,2048]{1,0:T(8,128)(2,1)S(1)}, u32[]{:S(2)}, u32[]{:S(2)}) collective-permute-start(bf16[128,2048]{1,0:T(8,128)(2,1)} %zo.1), channel_id=1, source_target_pairs={{0,4},{4,0},{8,12},{12,8},{16,20},{20,16},{24,28},{28,24},{1,5},{5... | collective-permute-start | bytes 1572872 | tf_op jit(solution)/shard_map/ppermute | solution.py:313
  7.9 12.5 %collective-permute-start.7 = (bf16[1040,128]{1,0:T(8,128)(2,1)S(1)}, bf16[1040,128]{1,0:T(8,128)(2,1)S(1)}, u32[]{:S(2)}, u32[]{:S(2)}) collective-permute-start(bf16[1040,128]{1,0:T(8,128)(2,1)S(1)} %get-tuple-element.29), channel_id=1, source_target_pairs={{0,24},{4,28},{1,25},{5,29},{2,26},{6,30},{3,27},{7,31}} | collective-permute-start | bytes 798728 | tf_op jit(solution)/shard_map/ppermute | solution.py:335
  13.4 13.1 %collective-permute-start.6 = (bf16[1040,128]{1,0:T(8,128)(2,1)S(1)}, bf16[1040,128]{1,0:T(8,128)(2,1)S(1)}, u32[]{:S(2)}, u32[]{:S(2)}) collective-permute-start(bf16[1040,128]{1,0:T(8,128)(2,1)S(1)} %get-tuple-element.29), channel_id=1, source_target_pairs={{0,16},{4,20},{8,24},{12,28},{1,17},{5,21},{9,25},{13,29},{2,18},{... | collective-permute-start | bytes 798728 | tf_op jit(solution)/shard_map/ppermute | solution.py:335
  14.7 11.8 %collective-permute-start.5 = (bf16[1040,128]{1,0:T(8,128)(2,1)S(1)}, bf16[1040,128]{1,0:T(8,128)(2,1)S(1)}, u32[]{:S(2)}, u32[]{:S(2)}) collective-permute-start(bf16[1040,128]{1,0:T(8,128)(2,1)S(1)} %get-tuple-element.29), channel_id=1, source_target_pairs={{0,8},{4,12},{8,16},{12,20},{16,24},{20,28},{1,9},{5,13},{9,17},{1... | collective-permute-start | bytes 798728 | tf_op jit(solution)/shard_map/ppermute | solution.py:335
  17.2 0.7 copy-start.3
  26.5 6.0 %copy-start = (bf16[2048,512]{1,0:T(8,128)(2,1)S(1)}, bf16[2048,512]{1,0:T(8,128)(2,1)}, u32[]{:S(2)}) copy-start(bf16[2048,512]{1,0:T(8,128)(2,1)} %refs_3_.3) | copy-start | bytes 6291460
  28.0 4.6 %collective-permute-start.10 = (bf16[128,1024]{1,0:T(8,128)(2,1)S(1)}, bf16[128,1024]{1,0:T(8,128)(2,1)S(1)}, u32[]{:S(2)}, u32[]{:S(2)}) collective-permute-start(bf16[128,1024]{1,0:T(8,128)(2,1)S(1)} %get-tuple-element.32), channel_id=1, source_target_pairs={{0,4},{4,0},{8,12},{12,8},{16,20},{20,16},{24,28},{28,24},{1,5},{5... | collective-permute-start | bytes 786440 | tf_op jit(solution)/shard_map/ppermute | solution.py:313
  28.0 9.1 %collective-permute-start.8 = (bf16[128,1024]{1,0:T(8,128)(2,1)S(1)}, bf16[128,1024]{1,0:T(8,128)(2,1)S(1)}, u32[]{:S(2)}, u32[]{:S(2)}) collective-permute-start(bf16[128,1024]{1,0:T(8,128)(2,1)S(1)} %get-tuple-element.31.refs_1_), channel_id=1, source_target_pairs={{0,8},{4,12},{8,0},{12,4},{16,24},{20,28},{24,16},{28,20},{1,9},{5... | collective-permute-start | bytes 786440 | tf_op jit(solution)/shard_map/ppermute | solution.py:316
  29.2 8.4 %collective-permute-start.9 = (bf16[128,1024]{1,0:T(8,128)(2,1)S(1)}, bf16[128,1024]{1,0:T(8,128)(2,1)S(1)}, u32[]{:S(2)}, u32[]{:S(2)}) collective-permute-start(bf16[128,1024]{1,0:T(8,128)(2,1)S(1)} %get-tuple-element.32), channel_id=1, source_target_pairs={{0,16},{4,20},{8,24},{12,28},{16,0},{20,4},{24,8},{28,12},{1,17},{... | collective-permute-start | bytes 786440 | tf_op jit(solution)/shard_map/ppermute | solution.py:316
  30.7 12.1 %collective-permute-start.12 = (bf16[128,1024]{1,0:T(8,128)(2,1)S(1)}, bf16[128,1024]{1,0:T(8,128)(2,1)S(1)}, u32[]{:S(2)}, u32[]{:S(2)}) collective-permute-start(bf16[128,1024]{1,0:T(8,128)(2,1)S(1)} %get-tuple-element.32), channel_id=1, source_target_pairs={{0,8},{4,12},{8,0},{12,4},{16,24},{20,28},{24,16},{28,20},{1,9},{5... | collective-permute-start | bytes 786440 | tf_op jit(solution)/shard_map/ppermute | solution.py:316
  37.6 9.2 %collective-permute-start.17 = (bf16[128,1024]{1,0:T(8,128)(2,1)S(1)}, bf16[128,1024]{1,0:T(8,128)(2,1)S(1)}, u32[]{:S(2)}, u32[]{:S(2)}) collective-permute-start(bf16[128,1024]{1,0:T(8,128)(2,1)S(1)} %collective-permute-done.8.refs_1_), channel_id=1, source_target_pairs={{0,16},{4,20},{8,24},{12,28},{16,0},{20,4},{24,8},{28,12},{1,17},{... | collective-permute-start | bytes 786440 | tf_op jit(solution)/shard_map/ppermute | solution.py:316
  39.6 8.3 %collective-permute-start.18 = (bf16[128,1024]{1,0:T(8,128)(2,1)S(1)}, bf16[128,1024]{1,0:T(8,128)(2,1)S(1)}, u32[]{:S(2)}, u32[]{:S(2)}) collective-permute-start(bf16[128,1024]{1,0:T(8,128)(2,1)S(1)} %collective-permute-done.9), channel_id=1, source_target_pairs={{0,8},{4,12},{8,0},{12,4},{16,24},{20,28},{24,16},{28,20},{1,9},{5... | collective-permute-start | bytes 786440 | tf_op jit(solution)/shard_map/ppermute | solution.py:316
  40.9 10.1 %collective-permute-start.11 = (bf16[128,1024]{1,0:T(8,128)(2,1)S(1)}, bf16[128,1024]{1,0:T(8,128)(2,1)S(1)}, u32[]{:S(2)}, u32[]{:S(2)}) collective-permute-start(bf16[128,1024]{1,0:T(8,128)(2,1)S(1)} %get-tuple-element.31.refs_1_), channel_id=1, source_target_pairs={{0,16},{4,20},{8,24},{12,28},{16,0},{20,4},{24,8},{28,12},{1,17},{... | collective-permute-start | bytes 786440 | tf_op jit(solution)/shard_map/ppermute | solution.py:316
  42.7 8.3 %collective-permute-start.13 = (bf16[128,1024]{1,0:T(8,128)(2,1)S(1)}, bf16[128,1024]{1,0:T(8,128)(2,1)S(1)}, u32[]{:S(2)}, u32[]{:S(2)}) collective-permute-start(bf16[128,1024]{1,0:T(8,128)(2,1)S(1)} %collective-permute-done.12), channel_id=1, source_target_pairs={{0,4},{4,0},{8,12},{12,8},{16,20},{20,16},{24,28},{28,24},{1,5},{5... | collective-permute-start | bytes 786440 | tf_op jit(solution)/shard_map/ppermute | solution.py:313
  42.7 8.3 %collective-permute-start.14 = (bf16[128,1024]{1,0:T(8,128)(2,1)S(1)}, bf16[128,1024]{1,0:T(8,128)(2,1)S(1)}, u32[]{:S(2)}, u32[]{:S(2)}) collective-permute-start(bf16[128,1024]{1,0:T(8,128)(2,1)S(1)} %collective-permute-done.9), channel_id=1, source_target_pairs={{0,4},{4,0},{8,12},{12,8},{16,20},{20,16},{24,28},{28,24},{1,5},{5... | collective-permute-start | bytes 786440 | tf_op jit(solution)/shard_map/ppermute | solution.py:313
  47.9 8.1 %collective-permute-start.19 = (bf16[128,1024]{1,0:T(8,128)(2,1)S(1)}, bf16[128,1024]{1,0:T(8,128)(2,1)S(1)}, u32[]{:S(2)}, u32[]{:S(2)}) collective-permute-start(bf16[128,1024]{1,0:T(8,128)(2,1)S(1)} %collective-permute-done.18), channel_id=1, source_target_pairs={{0,4},{4,0},{8,12},{12,8},{16,20},{20,16},{24,28},{28,24},{1,5},{5... | collective-permute-start | bytes 786440 | tf_op jit(solution)/shard_map/ppermute | solution.py:313
  52.8 7.1 %collective-permute-start.15 = (bf16[1024,128]{1,0:T(8,128)(2,1)S(1)}, bf16[1024,128]{1,0:T(8,128)(2,1)S(1)}, u32[]{:S(2)}, u32[]{:S(2)}) collective-permute-start(bf16[1024,128]{1,0:T(8,128)(2,1)S(1)} %get-tuple-element.36), channel_id=1, source_target_pairs={{0,8},{4,12},{8,0},{12,4},{16,24},{20,28},{24,16},{28,20},{1,9},{5... | collective-permute-start | bytes 786440 | tf_op jit(solution)/shard_map/ppermute | solution.py:316
  54.6 6.8 %collective-permute-start.16 = (bf16[1024,128]{1,0:T(8,128)(2,1)S(1)}, bf16[1024,128]{1,0:T(8,128)(2,1)S(1)}, u32[]{:S(2)}, u32[]{:S(2)}) collective-permute-start(bf16[1024,128]{1,0:T(8,128)(2,1)S(1)} %get-tuple-element.37), channel_id=1, source_target_pairs={{0,16},{4,20},{8,24},{12,28},{16,0},{20,4},{24,8},{28,12},{1,17},{... | collective-permute-start | bytes 786440 | tf_op jit(solution)/shard_map/ppermute | solution.py:316
  62.6 7.3 %collective-permute-start.20 = (bf16[1024,128]{1,0:T(8,128)(2,1)S(1)}, bf16[1024,128]{1,0:T(8,128)(2,1)S(1)}, u32[]{:S(2)}, u32[]{:S(2)}) collective-permute-start(bf16[1024,128]{1,0:T(8,128)(2,1)S(1)} %shard_map.96), channel_id=1, source_target_pairs={{0,24},{4,28},{8,16},{12,20},{16,8},{20,12},{24,0},{28,4},{1,25},{... | collective-permute-start | bytes 786440 | tf_op jit(solution)/shard_map/ppermute | solution.py:316
  63.8 1.2 %collective-permute-start.21 = (f32[8,128]{1,0:T(8,128)S(1)}, f32[8,128]{1,0:T(8,128)S(1)}, u32[]{:S(2)}, u32[]{:S(2)}) collective-permute-start(f32[8,128]{1,0:T(8,128)S(1)} %get-tuple-element.41), channel_id=1, source_target_pairs={{0,4},{4,0},{8,12},{12,8},{16,20},{20,16},{24,28},{28,24},{1,5},{5... | collective-permute-start | bytes 12296 | tf_op jit(solution)/shard_map/ppermute | solution.py:313
  70.6 7.7 %collective-permute-start.23 = (bf16[528,128]{1,0:T(8,128)(2,1)S(1)}, bf16[528,128]{1,0:T(8,128)(2,1)S(1)}, u32[]{:S(2)}, u32[]{:S(2)}) collective-permute-start(bf16[528,128]{1,0:T(8,128)(2,1)S(1)} %get-tuple-element.43), channel_id=1, source_target_pairs={{0,1},{1,0},{2,3},{3,2},{4,5},{5,4},{6,7},{7,6},{8,9},{9,8},{10,11... | collective-permute-start | bytes 405512 | tf_op jit(solution)/shard_map/ppermute | solution.py:319
  72.3 19.5 %collective-permute-start.22 = (bf16[1040,128]{1,0:T(8,128)(2,1)S(1)}, bf16[1040,128]{1,0:T(8,128)(2,1)S(1)}, u32[]{:S(2)}, u32[]{:S(2)}) collective-permute-start(bf16[1040,128]{1,0:T(8,128)(2,1)S(1)} %get-tuple-element.42), channel_id=1, source_target_pairs={{0,1},{1,0},{2,3},{3,2},{4,5},{5,4},{6,7},{7,6},{8,9},{9,8},{10,11... | collective-permute-start | bytes 798728 | tf_op jit(solution)/shard_map/ppermute | solution.py:319
  72.7 11.1 %collective-permute-start.25 = (bf16[512,128]{1,0:T(8,128)(2,1)S(1)}, bf16[512,128]{1,0:T(8,128)(2,1)S(1)}, u32[]{:S(2)}, u32[]{:S(2)}) collective-permute-start(bf16[512,128]{1,0:T(8,128)(2,1)S(1)} %get-tuple-element.44), channel_id=1, source_target_pairs={{0,1},{1,0},{2,3},{3,2},{4,5},{5,4},{6,7},{7,6},{8,9},{9,8},{10,11... | collective-permute-start | bytes 393224 | tf_op jit(solution)/shard_map/ppermute | solution.py:319
  79.0 12.8 %collective-permute-start.24 = (bf16[528,128]{1,0:T(8,128)(2,1)S(1)}, bf16[528,128]{1,0:T(8,128)(2,1)S(1)}, u32[]{:S(2)}, u32[]{:S(2)}) collective-permute-start(bf16[528,128]{1,0:T(8,128)(2,1)S(1)} %shard_map.98), channel_id=1, source_target_pairs={{0,2},{1,3},{2,0},{3,1},{4,6},{5,7},{6,4},{7,5},{8,10},{9,11},{10,... | collective-permute-start | bytes 405512 | tf_op jit(solution)/shard_map/ppermute | solution.py:319
  84.4 7.3 %collective-permute-start.26 = (bf16[512,128]{1,0:T(8,128)(2,1)S(1)}, bf16[512,128]{1,0:T(8,128)(2,1)S(1)}, u32[]{:S(2)}, u32[]{:S(2)}) collective-permute-start(bf16[512,128]{1,0:T(8,128)(2,1)S(1)} %shard_map.99), channel_id=1, source_target_pairs={{0,2},{1,3},{2,0},{3,1},{4,6},{5,7},{6,4},{7,5},{8,10},{9,11},{10,... | collective-permute-start | bytes 393224 | tf_op jit(solution)/shard_map/ppermute | solution.py:319

commit v5 on v4

--- a/solution.py
+++ b/solution.py
@@ -182,8 +182,9 @@
     rows, wide = mine.shape
     even = k == 0
     enter, through = None, None
-    for ref in states:
+    for j, ref in enumerate(states):
         st, dec = unpack(ref, first.shape[0], wide)
+        st = jnp.where(s[2] > j, st, 0.0)
         enter = st if enter is None else enter + st * through
         through = dec if through is None else through * dec
     whole = jnp.where(even, decays[rows - 1 : rows], decays[2 * rows - 1 : 2 * rows])
@@ -206,13 +207,13 @@
     k = s[0]
     rows, depth = u[0].shape
     cols = w_own.shape[1]
+    groups = cols // LANES
     here = pl.ds(pl.multiple_of(k * depth, depth), depth)
     there = pl.ds(pl.multiple_of((1 - k) * depth, depth), depth)
     uu = jnp.concatenate([a[...] for a in u], 0)
     vv = jnp.concatenate([a[...] for a in v], 0)
     for w, place in ((w_own, k), (w_other, 1 - k)):
         got = (nn(uu, w[here]) + nn(vv, w[there])).astype(bf16)
-        groups = cols // LANES
         for i, out in enumerate(outs):
             for j in range(groups):
                 at = pl.ds(pl.multiple_of((place * groups + j) * rows, rows), rows)
@@ -228,8 +229,7 @@
 
 
 def choose_kernel(s, *refs, steps):
-    count = len(refs) - 1 - len(steps)
-    blocks, squares, outs = refs[:count], refs[count], refs[count + 1 :]
+    blocks, squares, outs = refs[:-1 - len(steps)], refs[-1 - len(steps)], refs[-len(steps) :]
     n = blocks[0].shape[0]
     for m, out in zip(steps, outs):
 
@@ -240,62 +240,62 @@
         out[n:] = pair(squares[...])
 
 
-def halves_kernel(s, *refs):
-    *blocks, squares, top, low, other = refs
-    n = low.shape[0]
-
-    def cut(block):
-        top[:n] = block[:n]
-        low[...] = block[n:]
-
-    def copy(block):
-        other[: 2 * n] = block[...]
-
-    pick(s, 3, blocks, cut)
-    pick(s, 1, blocks, copy)
-    ext = pair(squares[...])
-    top[n:] = ext
-    other[2 * n :] = ext
-
-
-def join_kernel(s, *refs, base):
-    *blocks, squares, got, out = refs
-    n = blocks[0].shape[0] // 2
-
-    def add(block):
-        out[:n] = (block[base * n : (base + 1) * n].astype(f32) + got[:n].astype(f32)).astype(bf16)
-
-    pick(s, 2, blocks, add)
-    if base == 0:
-        out[n:] = pair(squares[...] + unpair(got[n:]))
-
-
-def sum_kernel(s, *refs, inner, count):
-    blocks, (squares, *got, out) = refs[:count], refs[count:]
-    rows = out.shape[0]
-    groups = out.shape[1] // LANES
-    size = groups * rows
+def give_kernel(s, even, odd, *refs):
+    out = refs[-1]
+    n = even.shape[0]
+    out[:n] = jnp.where((s[1] & 1) == 0, even[...], odd[...])
+    if out.shape[0] > n:
+        out[n:] = pair(refs[0][...])
+
+
+def join_kernel(s, even, odd, got, squares, ext, *rest):
+    out = rest[-1]
+    n = even.shape[0]
+    kept = jnp.where((s[1] & 1) == 0, even[...], odd[...])
+    out[:n] = (kept.astype(f32) + got[:n].astype(f32)).astype(bf16)
+    out[n:] = pair(squares[...] + unpair(ext[n:]))
+
+
+def row_scale(total, inner, rows):
     i = lax.broadcasted_iota(jnp.int32, (rows, rows), 0)
     j = lax.broadcasted_iota(jnp.int32, (rows, rows), 1)
-    total = squares[...] + sum(unpair(a[a.shape[0] - EXT :]) for a in got if a.shape[0] % size % (size // 2) == EXT)
     row = lax.rsqrt(total[:1] / inner + 1e-5)
-    col = jnp.sum(jnp.where(i == j, jnp.broadcast_to(row, (rows, rows)), 0.0), axis=1, keepdims=True)
+    return jnp.sum(jnp.where(i == j, jnp.broadcast_to(row, (rows, rows)), 0.0), axis=1, keepdims=True)
+
+
+def sum_kernel(s, *refs, inner):
+    count = len(refs) // 2 - 1
+    blocks, squares, got, out = refs[: count + 1], refs[count + 1], refs[count + 2 : -1], refs[-1]
+    rows = out.shape[0]
+    n = blocks[0].shape[0]
+    col = row_scale(squares[...] + sum(unpair(a[n:]) for a in got), inner, rows)
 
     def finish(block):
-        for g in range(groups):
-            v = block[g * rows : (g + 1) * rows].astype(f32)
-            at = 0
-            for a in got:
-                span = a.shape[0] // rows
-                if span == groups:
-                    v += a[g * rows : (g + 1) * rows].astype(f32)
-                else:
-                    if at <= g < at + span:
-                        v += a[(g - at) * rows : (g - at + 1) * rows].astype(f32)
-                    at += span
+        for g in range(n // rows):
+            at = slice(g * rows, (g + 1) * rows)
+            v = block[at].astype(f32) + sum(a[at].astype(f32) for a in got)
             out[:, g * LANES : (g + 1) * LANES] = (v * col).astype(bf16)
 
     pick(s, 0, blocks, finish)
+
+
+def last_kernel(s, own, x, y, far, got1, got2, sum1, sum2, squares, out, *, inner):
+    rows = out.shape[0]
+    n = own.shape[0]
+    base = squares[...] + unpair(got1[n:])
+
+    def finish(block, got, other):
+        col = row_scale(base + unpair(other[n:]), inner, rows)
+        for g in range(n // rows):
+            at = slice(g * rows, (g + 1) * rows)
+            v = block[at].astype(f32) + got[at].astype(f32) + other[at].astype(f32)
+            out[:, g * LANES : (g + 1) * LANES] = (v * col).astype(bf16)
+
+    for turn, args in enumerate(((own, got2, sum2), (x, got1, sum1), (y, got1, sum1), (far, got2, sum2))):
+
+        @pl.when(s[1] == turn)
+        def _():
+            finish(*args)
 
 
 def body(n, n_head, signal, gate_input, state_in, state_out, step_size, log_decay, skip_gain, norm_gain, out_weight):
@@ -306,7 +306,7 @@
     cols = out_weight.shape[1]
     place, z = lax.axis_index("seq"), lax.axis_index("head")
     k, chip = place % 2, place // 2
-    s = jnp.stack([k, chip ^ z]).astype(jnp.int32)
+    s = jnp.stack([k, chip ^ z, chip]).astype(jnp.int32)
     any_spec = pl.BlockSpec(memory_space=pl.ANY)
 
     def swap(a):
@@ -319,8 +319,9 @@
         return lax.ppermute(a, "head", [(i, i ^ m) for i in range(n)])
 
     x2 = swap(signal)
-    rates1 = jnp.concatenate([step_size, log_decay], 0)
-    bc1 = jnp.concatenate([state_in, state_out], 1)
+    rates1 = jnp.pad(step_size, ((0, heads), (0, 0))) + jnp.pad(log_decay, ((heads, 0), (0, 0)))
+    states = state_in.shape[1]
+    bc1 = jnp.pad(state_in, ((0, 0), (0, states))) + jnp.pad(state_out, ((0, 0), (states, 0)))
     rates2, bc2 = swap(rates1), swap(bc1)
     z2 = swap(gate_input)
     x1 = lax.dynamic_slice_in_dim(signal, k * wide, wide, 1)
@@ -332,7 +333,7 @@
     msg, first = call(state_kernel, s, ins, [full(a) for a in ins], outs, [full(a) for a in outs])
     w2 = swap(lax.optimization_barrier((out_weight, msg))[0])
     got = [
-        lax.ppermute(msg, "seq", [(i, i + 2 * j) for i in range(2 * (n - j))]) for j in range(1, n)
+        lax.ppermute(msg, "seq", [(i, (i + 2 * j) % (2 * n)) for i in range(2 * n)]) for j in range(1, n)
     ]
     ins = (x1, x2, bc1, bc2, rates1, rates2, gate_input, z2, skip)
     big = shape((2 * rows, wide), f32)
@@ -362,11 +363,13 @@
         vx, uy = across(v, 1), across(u, 2)
         (own,) = project([u], [swap(v)])
         ux, vy, own = lax.optimization_barrier((ux, vy, own))
+        vy = swap(vy)
         ud, vd = lax.optimization_barrier((across(ux, 2), across(vy, 1)))
-        near = project([ux, uy], [swap(vx), swap(vy)], after=[own])
-        blocks = [own] + [across(near[0], 1), across(near[1], 2)]
-        (far,) = project([ud], [swap(vd)], after=blocks[1:])
-        blocks.append(across(far, 3))
+        vx, uy = lax.optimization_barrier((vx, uy))
+        px, py = project([ux, uy], [swap(vx), vy], after=[own])
+        px, py = across(px, 1), across(py, 2)
+        (far_here,) = project([ud], [vd])
+        far = across(far_here, 3)
     else:
         blocks = list(project([u], [swap(v)]))
         for j in range(1, n):
@@ -380,21 +383,31 @@
 
         return call(run, s, ins, [full(a) for a in ins], outs, [full(a) for a in outs])
 
+    inner = 2 * wide * n_head
+    out = [shape((rows, 2 * cols), bf16)]
     if n == 4:
-        tall, short = shape((size // 2 + EXT, LANES), bf16), shape((size // 2, LANES), bf16)
-        top, low, other = send(halves_kernel, (*blocks, squares), [tall, short, message])
-        top, low, other = along(top, 1), along(low, 1), along(other, 1)
-        (top,) = send(join_kernel, (*blocks, squares, top), [tall], base=0)
-        (low,) = send(join_kernel, (*blocks, squares, low), [short], base=1)
-        got = (other, along(top, 2), along(low, 2))
-    else:
-        steps = range(1, n)
-        got = send(choose_kernel, (*blocks, squares), [message] * (n - 1), steps=steps)
-        got = [along(a, m) for a, m in zip(got, steps)]
-    return send(
-        sum_kernel, (*blocks, squares, *got), [shape((rows, 2 * cols), bf16)],
-        inner=2 * wide * n_head, count=n,
-    )[0]
+
+        def over(a, roles):
+            pairs = [
+                ((2 * c + core) * n + h, (2 * c + core) * n + (h ^ 2))
+                for c in range(n) for core in range(2) for h in range(n) if c ^ h in roles
+            ]
+            return lax.ppermute(a, BOTH, pairs)
+
+        (got1,) = send(give_kernel, (px, py, squares), [message])
+        got1 = along(got1, 1)
+        (got2,) = send(give_kernel, (far, own), [p_shape])
+        (sum1,) = send(join_kernel, (py, px, got1, squares, got1, got2), [message])
+        sum1 = over(sum1, (0, 3))
+        got2 = along(got2, 1)
+        (sum2,) = send(join_kernel, (own, far, got2, squares, got1), [message])
+        sum2 = over(sum2, (1, 2))
+        ins = (own, px, py, far, got1, got2, sum1, sum2, squares)
+        return send(last_kernel, ins, out, inner=inner)[0]
+    steps = range(1, n)
+    got = send(choose_kernel, (*blocks, squares), [message] * (n - 1), steps=steps)
+    got = [along(a, m) for a, m in zip(got, steps)]
+    return send(sum_kernel, (*blocks, squares, *got), out, inner=inner)[0]
 
 
 def solution(mesh):

time: 93.7 us -> 85.1 us (0.908)
  starting transfers between devices: 32.1 us -> 26.1 us
  local copies, waits for them, and re-layouts: 4.6 us -> 1.64 us
  waiting for transfers between devices: 42.6 us -> 40.6 us
  other arithmetic: 0.08 us -> 1.6 us
    ppermute x3 -> x5, waiting for transfers between devices: 6.17 us -> 21.3 us  [the longest x2 11.5 us: over(): return lax.ppermute(a, BOTH, pairs)]
    ppermute x5 -> x2, waiting for transfers between devices: 11.8 us -> 1.08 us  [along(): return lax.ppermute(a, 'head', [(i, i ^ m) for i in range(n)])]
    ppermute x9, waiting for transfers between devices: 23.4 us -> 17 us  [across(): return lax.ppermute(a, 'seq', [(i, i ^ 2 * j) for i in range(2 * n)])]
    ppermute x5 -> x2, starting transfers between devices: 8.12 us -> 3.29 us  [along(): return lax.ppermute(a, 'head', [(i, i ^ m) for i in range(n)])]
    ppermute x9, starting transfers between devices: 12.5 us -> 10.7 us  [across(): return lax.ppermute(a, 'seq', [(i, i ^ 2 * j) for i in range(2 * n)])]
    add x0 -> x2, other arithmetic: none -> 1.52 us  [the longest x1 0.78 us: body(): jnp.pad(state_in, ((0, 0), (0, states)))]
    concatenate x2 -> x0, local copies, waits for them, and re-layouts: 1.49 us -> none  [the longest x1 0.77 us: body(): bc1 = jnp.concatenate([state_in, state_out], 1)]
    unnamed x10 -> x8, local copies, waits for them, and re-layouts: 2.15 us -> 0.67 us
  transfers between devices with their start and end apart: 27 -> 25, of which waited for: 14 -> 14; matrix products, arithmetic and copies ran while one was open for 4% -> 3% of each run, Pallas kernels for 7% -> 11%
where the time goes in v5:
time: 85.1 us; the launch traced here: 84.4 us
  waiting for transfers between devices  40.6 us (48%)
  starting transfers between devices  26.1 us (31%)
  Pallas kernels  14.4 us (17%)
  local copies, waits for them, and re-layouts  1.64 us (2%)
  other arithmetic  1.6 us (2%)
    ppermute x9, waiting for transfers between devices, across(): return lax.ppermute(a, 'seq', [(i, i ^ 2 * j) for i in range(2 * n)])  17 us
    pallas_call x11, Pallas kernels, call(): pl.pallas_call(kernel, out_shape=outs, grid_spec=pltpu.PrefetchScalarGrid...  14.4 us
    ppermute x2, waiting for transfers between devices, over(): return lax.ppermute(a, BOTH, pairs)  11.5 us
    ppermute x9, starting transfers between devices, across(): return lax.ppermute(a, 'seq', [(i, i ^ 2 * j) for i in range(2 * n)])  10.7 us
    ppermute x3, waiting for transfers between devices, body(): lax.ppermute(msg, 'seq', [(i, (i + 2 * j) % (2 * n)) for i in range(2 * n)])  9.81 us
    ppermute x2, starting transfers between devices, over(): return lax.ppermute(a, BOTH, pairs)  5.8 us
    ppermute x3, starting transfers between devices, body(): lax.ppermute(msg, 'seq', [(i, (i + 2 * j) % (2 * n)) for i in range(2 * n)])  4.72 us
    ppermute x2, starting transfers between devices, along(): return lax.ppermute(a, 'head', [(i, i ^ m) for i in range(n)])  3.29 us
  transfers between devices with their start and end apart: 25, of which 14 were waited for; matrix products, arithmetic and copies ran while one was open for 3% of the time, Pallas kernels for 11%

profile of v5, /device:TPU:0, one launch (start us, length us, event | category | flops | bytes accessed | tf_op | source)
XLA Modules:
  0.0 84.4 jit_solution(13183542639603498960)
XLA Ops:
  1.3 0.8 pad_add_fusion.bo
  2.6 1.0 %constant_dynamic-slice_fusion.xo = bf16[128,1024]{1,0:T(8,128)(2,1)S(1)} fusion(bf16[128,2048]{1,0:T(8,128)(2,1)} %param.9, s32[]{:T(128)S(6)} %select_n.16), kind=kLoop, calls=%fused_computation.3 | loop fusion | bytes 524292 | tf_op jit(solution)/shard_map/dynamic_slice | solution.py:327
  3.6 2.2 %shard_map.92 = (bf16[1040,128]{1,0:T(8,128)(2,1)S(1)}, f32[128,1024]{1,0:T(8,128)S(1)}) custom-call(s32[3]{0:T(128)S(1)} %pad_add_fusion.2.s.refs_0_, bf16[128,1024]{1,0:T(8,128)(2,1)S(1)} %constant_dynamic-slice_fusion.xo, bf16[128,2048]{1,0:T(8,128)(2,1)S(1)} %collective-permute-done.xr, bf16[128,256]{1,0:T(8,128)(2,1)S(1)} %pad_add_fusion.bo, ...), custom_call_target="tpu_custom_call" | custom-call | bytes 1773568 | tf_op jit(solution)/shard_map/pallas_call | solution.py:20
  6.4 3.6 %collective-permute-start.7 = (bf16[1040,128]{1,0:T(8,128)(2,1)S(1)}, bf16[1040,128]{1,0:T(8,128)(2,1)S(1)}, u32[]{:S(2)}, u32[]{:S(2)}) collective-permute-start(bf16[1040,128]{1,0:T(8,128)(2,1)S(1)} %get-tuple-element.28), channel_id=1, source_target_pairs={{0,24},{4,28},{8,0},{12,4},{16,8},{20,12},{24,16},{28,20},{1,25},{... | collective-permute-start | bytes 798728 | tf_op jit(solution)/shard_map/ppermute | solution.py:336
  11.8 2.5 %shard_map.91 = (f32[256,1024]{1,0:T(8,128)S(1)}, f32[256,1024]{1,0:T(8,128)S(1)}, f32[256,1024]{1,0:T(8,128)S(1)}) custom-call(s32[3]{0:T(128)S(1)} %pad_add_fusion.2.s.refs_0_, bf16[128,1024]{1,0:T(8,128)(2,1)S(1)} %constant_dynamic-slice_fusion.xo, bf16[128,2048]{1,0:T(8,128)(2,1)S(1)} %collective-permute-done.xr, bf16[128,256]{1,0:T(8,128)(2,1)S(1)} %pad_add_fusion.bo, ...), custom_call_target="tpu_custom_call" | custom-call | bytes 5177472 | tf_op jit(solution)/shard_map/pallas_call | solution.py:20
  14.3 2.6 %collective-permute-done.7.rest_2_ = bf16[1040,128]{1,0:T(8,128)(2,1)S(1)} collective-permute-done((bf16[1040,128]{1,0:T(8,128)(2,1)S(1)}, bf16[1040,128]{1,0:T(8,128)(2,1)S(1)}, u32[]{:S(2)}, u32[]{:S(2)}) %collective-permute-start.7) | collective-permute-done | bytes 266272 | tf_op jit(solution)/shard_map/ppermute | solution.py:336
  16.8 7.3 %collective-permute-done.6.rest_1_ = bf16[1040,128]{1,0:T(8,128)(2,1)S(1)} collective-permute-done((bf16[1040,128]{1,0:T(8,128)(2,1)S(1)}, bf16[1040,128]{1,0:T(8,128)(2,1)S(1)}, u32[]{:S(2)}, u32[]{:S(2)}) %collective-permute-start.6) | collective-permute-done | bytes 266272 | tf_op jit(solution)/shard_map/ppermute | solution.py:336
  24.1 1.4 %shard_map.93 = (bf16[128,1024]{1,0:T(8,128)(2,1)S(1)}, bf16[128,1024]{1,0:T(8,128)(2,1)S(1)}, f32[8,128]{1,0:T(8,128)S(1)}, f32[8,128]{1,0:T(8,128)S(1)}) custom-call(s32[3]{0:T(128)S(1)} %pad_add_fusion.2.s.refs_0_, f32[256,1024]{1,0:T(8,128)S(1)} %get-tuple-element.24.inside, f32[256,1024]{1,0:T(8,128)S(1)} %get-tuple-element.25.decays, ...), custom_call_target="tpu_custom_call" | custom-call | bytes 7237632 | tf_op jit(solution)/shard_map/pallas_call | solution.py:20
  25.9 0.8 collective-permute-start.9
  26.7 1.2 %collective-permute-start.12 = (bf16[128,1024]{1,0:T(8,128)(2,1)S(1)}, bf16[128,1024]{1,0:T(8,128)(2,1)S(1)}, u32[]{:S(2)}, u32[]{:S(2)}) collective-permute-start(bf16[128,1024]{1,0:T(8,128)(2,1)S(1)} %get-tuple-element.30.refs_1_), channel_id=1, source_target_pairs={{0,16},{4,20},{8,24},{12,28},{16,0},{20,4},{24,8},{28,12},{1,17},{... | collective-permute-start | bytes 786440 | tf_op jit(solution)/shard_map/ppermute | solution.py:316
  27.9 1.7 %collective-permute-start.11 = (bf16[128,1024]{1,0:T(8,128)(2,1)S(1)}, bf16[128,1024]{1,0:T(8,128)(2,1)S(1)}, u32[]{:S(2)}, u32[]{:S(2)}) collective-permute-start(bf16[128,1024]{1,0:T(8,128)(2,1)S(1)} %get-tuple-element.31), channel_id=1, source_target_pairs={{0,8},{4,12},{8,0},{12,4},{16,24},{20,28},{24,16},{28,20},{1,9},{5... | collective-permute-start | bytes 786440 | tf_op jit(solution)/shard_map/ppermute | solution.py:316
  29.7 1.3 %shard_map.94.refs_7_.refs_2_.refs_1_ = bf16[1024,128]{1,0:T(8,128)(2,1)S(1)} custom-call(s32[3]{0:T(128)S(1)} %pad_add_fusion.2.s.refs_0_, bf16[128,1024]{1,0:T(8,128)(2,1)S(1)} %get-tuple-element.30.refs_1_, bf16[128,1024]{1,0:T(8,128)(2,1)S(1)} %collective-permute-done.10.refs_2_, bf16[2048,512]{1,0:T(8,128)(2,1)S(1)} %copy-done, ...), custom_call_target="tpu_custom_call" | custom-call | bytes 4980736 | tf_op jit(solution)/shard_map/pallas_call | solution.py:20
  31.0 3.7 %collective-permute-done.8.refs_1_ = bf16[128,1024]{1,0:T(8,128)(2,1)S(1)} collective-permute-done((bf16[128,1024]{1,0:T(8,128)(2,1)S(1)}, bf16[128,1024]{1,0:T(8,128)(2,1)S(1)}, u32[]{:S(2)}, u32[]{:S(2)}) %collective-permute-start.8) | collective-permute-done | bytes 262176 | tf_op jit(solution)/shard_map/ppermute | solution.py:316
  35.0 4.9 %collective-permute-done.12.refs_2_ = bf16[128,1024]{1,0:T(8,128)(2,1)S(1)} collective-permute-done((bf16[128,1024]{1,0:T(8,128)(2,1)S(1)}, bf16[128,1024]{1,0:T(8,128)(2,1)S(1)}, u32[]{:S(2)}, u32[]{:S(2)}) %collective-permute-start.12) | collective-permute-done | bytes 262176 | tf_op jit(solution)/shard_map/ppermute | solution.py:316
  40.0 0.8 collective-permute-start.17
  40.8 1.4 %collective-permute-start.18 = (bf16[128,1024]{1,0:T(8,128)(2,1)S(1)}, bf16[128,1024]{1,0:T(8,128)(2,1)S(1)}, u32[]{:S(2)}, u32[]{:S(2)}) collective-permute-start(bf16[128,1024]{1,0:T(8,128)(2,1)S(1)} %collective-permute-done.14.refs_4_), channel_id=1, source_target_pairs={{0,8},{4,12},{8,0},{12,4},{16,24},{20,28},{24,16},{28,20},{1,9},{5... | collective-permute-start | bytes 786440 | tf_op jit(solution)/shard_map/ppermute | solution.py:316
  42.2 1.8 %shard_map.95 = (bf16[1024,128]{1,0:T(8,128)(2,1)S(1)}, bf16[1024,128]{1,0:T(8,128)(2,1)S(1)}) custom-call(s32[3]{0:T(128)S(1)} %pad_add_fusion.2.s.refs_0_, bf16[128,1024]{1,0:T(8,128)(2,1)S(1)} %collective-permute-done.8.refs_1_, bf16[128,1024]{1,0:T(8,128)(2,1)S(1)} %collective-permute-done.12.refs_2_, ...), custom_call_target="tpu_custom_call" | custom-call | bytes 6029312 | tf_op jit(solution)/shard_map/pallas_call | solution.py:20
  44.0 1.1 %collective-permute-start.15 = (bf16[1024,128]{1,0:T(8,128)(2,1)S(1)}, bf16[1024,128]{1,0:T(8,128)(2,1)S(1)}, u32[]{:S(2)}, u32[]{:S(2)}) collective-permute-start(bf16[1024,128]{1,0:T(8,128)(2,1)S(1)} %get-tuple-element.37), channel_id=1, source_target_pairs={{0,8},{4,12},{8,0},{12,4},{16,24},{20,28},{24,16},{28,20},{1,9},{5... | collective-permute-start | bytes 786440 | tf_op jit(solution)/shard_map/ppermute | solution.py:316
  45.1 0.8 collective-permute-start.16
  45.9 3.2 %collective-permute-done.17.refs_1_ = bf16[128,1024]{1,0:T(8,128)(2,1)S(1)} collective-permute-done((bf16[128,1024]{1,0:T(8,128)(2,1)S(1)}, bf16[128,1024]{1,0:T(8,128)(2,1)S(1)}, u32[]{:S(2)}, u32[]{:S(2)}) %collective-permute-start.17) | collective-permute-done | bytes 262176 | tf_op jit(solution)/shard_map/ppermute | solution.py:316
  49.1 0.8 collective-permute-done.18.refs_2_
  49.9 1.3 %shard_map.96 = bf16[1024,128]{1,0:T(8,128)(2,1)S(1)} custom-call(s32[3]{0:T(128)S(1)} %pad_add_fusion.2.s.refs_0_, bf16[128,1024]{1,0:T(8,128)(2,1)S(1)} %collective-permute-done.17.refs_1_, bf16[128,1024]{1,0:T(8,128)(2,1)S(1)} %collective-permute-done.18.refs_2_, bf16[2048,512]{1,0:T(8,128)(2,1)S(1)} %copy-done, ...), custom_call_target="tpu_custom_call" | custom-call | bytes 4980736 | tf_op jit(solution)/shard_map/pallas_call | solution.py:20
  51.2 2.5 %collective-permute-start.19 = (bf16[1024,128]{1,0:T(8,128)(2,1)S(1)}, bf16[1024,128]{1,0:T(8,128)(2,1)S(1)}, u32[]{:S(2)}, u32[]{:S(2)}) collective-permute-start(bf16[1024,128]{1,0:T(8,128)(2,1)S(1)} %shard_map.96), channel_id=1, source_target_pairs={{0,24},{4,28},{8,16},{12,20},{16,8},{20,12},{24,0},{28,4},{1,25},{... | collective-permute-start | bytes 786440 | tf_op jit(solution)/shard_map/ppermute | solution.py:316
  53.6 1.2 %collective-permute-done.20 = f32[8,128]{1,0:T(8,128)S(1)} collective-permute-done((f32[8,128]{1,0:T(8,128)S(1)}, f32[8,128]{1,0:T(8,128)S(1)}, u32[]{:S(2)}, u32[]{:S(2)}) %collective-permute-start.20) | collective-permute-done | bytes 4128 | tf_op jit(solution)/shard_map/ppermute | solution.py:313
  56.1 1.6 %collective-permute-start.21 = (bf16[1040,128]{1,0:T(8,128)(2,1)S(1)}, bf16[1040,128]{1,0:T(8,128)(2,1)S(1)}, u32[]{:S(2)}, u32[]{:S(2)}) collective-permute-start(bf16[1040,128]{1,0:T(8,128)(2,1)S(1)} %shard_map.97), channel_id=1, source_target_pairs={{0,1},{1,0},{2,3},{3,2},{4,5},{5,4},{6,7},{7,6},{8,9},{9,8},{10,11... | collective-permute-start | bytes 798728 | tf_op jit(solution)/shard_map/ppermute | solution.py:319
  57.8 3.3 %collective-permute-done.19.refs_1_.refs_2_.refs_4_ = bf16[1024,128]{1,0:T(8,128)(2,1)S(1)} collective-permute-done((bf16[1024,128]{1,0:T(8,128)(2,1)S(1)}, bf16[1024,128]{1,0:T(8,128)(2,1)S(1)}, u32[]{:S(2)}, u32[]{:S(2)}) %collective-permute-start.19) | collective-permute-done | bytes 262176 | tf_op jit(solution)/shard_map/ppermute | solution.py:316
  61.7 1.6 %collective-permute-start.22 = (bf16[1024,128]{1,0:T(8,128)(2,1)S(1)}, bf16[1024,128]{1,0:T(8,128)(2,1)S(1)}, u32[]{:S(2)}, u32[]{:S(2)}) collective-permute-start(bf16[1024,128]{1,0:T(8,128)(2,1)S(1)} %shard_map.98.refs_6_), channel_id=1, source_target_pairs={{0,1},{1,0},{2,3},{3,2},{4,5},{5,4},{6,7},{7,6},{8,9},{9,8},{10,11... | collective-permute-start | bytes 786440 | tf_op jit(solution)/shard_map/ppermute | solution.py:319
  64.7 4.5 %collective-permute-start.23 = (bf16[1040,128]{1,0:T(8,128)(2,1)S(1)}, bf16[1040,128]{1,0:T(8,128)(2,1)S(1)}, u32[]{:S(2)}, u32[]{:S(2)}) collective-permute-start(bf16[1040,128]{1,0:T(8,128)(2,1)S(1)} %shard_map.99), channel_id=1, source_target_pairs={{0,2},{3,1},{4,6},{7,5},{9,11},{10,8},{13,15},{14,12},{17,19},{18,... | collective-permute-start | bytes 798728 | tf_op jit(solution)/shard_map/ppermute | solution.py:395
  70.2 1.3 %collective-permute-start.24 = (bf16[1040,128]{1,0:T(8,128)(2,1)S(1)}, bf16[1040,128]{1,0:T(8,128)(2,1)S(1)}, u32[]{:S(2)}, u32[]{:S(2)}) collective-permute-start(bf16[1040,128]{1,0:T(8,128)(2,1)S(1)} %shard_map.100), channel_id=1, source_target_pairs={{1,3},{2,0},{5,7},{6,4},{8,10},{11,9},{12,14},{15,13},{16,18},{19,... | collective-permute-start | bytes 798728 | tf_op jit(solution)/shard_map/ppermute | solution.py:395
  71.5 2.8 %collective-permute-done.23.refs_7_ = bf16[1040,128]{1,0:T(8,128)(2,1)S(1)} collective-permute-done((bf16[1040,128]{1,0:T(8,128)(2,1)S(1)}, bf16[1040,128]{1,0:T(8,128)(2,1)S(1)}, u32[]{:S(2)}, u32[]{:S(2)}) %collective-permute-start.23) | collective-permute-done | bytes 266272 | tf_op jit(solution)/shard_map/ppermute | solution.py:395
  74.4 8.6 %collective-permute-done.24.refs_8_ = bf16[1040,128]{1,0:T(8,128)(2,1)S(1)} collective-permute-done((bf16[1040,128]{1,0:T(8,128)(2,1)S(1)}, bf16[1040,128]{1,0:T(8,128)(2,1)S(1)}, u32[]{:S(2)}, u32[]{:S(2)}) %collective-permute-start.24) | collective-permute-done | bytes 266272 | tf_op jit(solution)/shard_map/ppermute | solution.py:395
  83.0 1.4 %shard_map.101 = bf16[128,1024]{1,0:T(8,128)(2,1)} custom-call(s32[3]{0:T(128)S(1)} %pad_add_fusion.2.s.refs_0_, bf16[1024,128]{1,0:T(8,128)(2,1)S(1)} %shard_map.94.refs_7_.refs_2_.refs_1_, bf16[1024,128]{1,0:T(8,128)(2,1)S(1)} %collective-permute-done.15.refs_1_.refs_2_, bf16[1024,128]{1,0:T(8,128)(2,1)S(1)} %collective-permute-done.16.refs_2_.refs_1_.refs_3_, ...), custom_call_target="tpu_custom_call" | custom-call | bytes 2375680 | tf_op jit(solution)/shard_map/pallas_call | solution.py:20
  (42 shorter events, 9.2 us)
Async XLA Ops:
  0.0 11.1 %copy-start.1 = (bf16[128,2048]{1,0:T(8,128)(2,1)S(1)}, bf16[128,2048]{1,0:T(8,128)(2,1)}, u32[]{:S(2)}) copy-start(bf16[128,2048]{1,0:T(8,128)(2,1)} %zo.1) | copy-start | bytes 1572868
  0.0 24.1 %copy-start.2 = (f32[2048]{0:T(1024)S(1)}, f32[2048]{0:T(1024)}, u32[]{:S(2)}) copy-start(f32[2048]{0:T(1024)} %param.16) | copy-start | bytes 24580
  0.0 3.6 %collective-permute-start = (bf16[128,2048]{1,0:T(8,128)(2,1)}, bf16[128,2048]{1,0:T(8,128)(2,1)S(1)}, u32[]{:S(2)}, u32[]{:S(2)}) collective-permute-start(bf16[128,2048]{1,0:T(8,128)(2,1)} %param.9), channel_id=1, source_target_pairs={{0,4},{4,0},{8,12},{12,8},{16,20},{20,16},{24,28},{28,24},{1,5},{5... | collective-permute-start | bytes 1572872 | tf_op jit(solution)/shard_map/ppermute | solution.py:313
  1.2 2.4 %collective-permute-start.2 = (f32[64,128]{1,0:T(8,128)S(1)}, f32[64,128]{1,0:T(8,128)S(1)}, u32[]{:S(2)}, u32[]{:S(2)}) collective-permute-start(f32[64,128]{1,0:T(8,128)S(1)} %pad_add_fusion.1.ro), channel_id=1, source_target_pairs={{0,4},{4,0},{8,12},{12,8},{16,20},{20,16},{24,28},{28,24},{1,5},{5... | collective-permute-start | bytes 98312 | tf_op jit(solution)/shard_map/ppermute | solution.py:313
  2.1 1.5 %collective-permute-start.1 = (bf16[128,256]{1,0:T(8,128)(2,1)S(1)}, bf16[128,256]{1,0:T(8,128)(2,1)S(1)}, u32[]{:S(2)}, u32[]{:S(2)}) collective-permute-start(bf16[128,256]{1,0:T(8,128)(2,1)S(1)} %pad_add_fusion.bo), channel_id=1, source_target_pairs={{0,4},{4,0},{8,12},{12,8},{16,20},{20,16},{24,28},{28,24},{1,5},{5... | collective-permute-start | bytes 196616 | tf_op jit(solution)/shard_map/ppermute | solution.py:313
  5.8 18.3 %collective-permute-start.4 = (bf16[2048,512]{1,0:T(8,128)(2,1)}, bf16[2048,512]{1,0:T(8,128)(2,1)S(1)}, u32[]{:S(2)}, u32[]{:S(2)}) collective-permute-start(bf16[2048,512]{1,0:T(8,128)(2,1)} %refs_3_.3), channel_id=1, source_target_pairs={{0,4},{4,0},{8,12},{12,8},{16,20},{20,16},{24,28},{28,24},{1,5},{5... | collective-permute-start | bytes 6291464 | tf_op jit(solution)/shard_map/ppermute | solution.py:313
  6.1 5.0 %collective-permute-start.3 = (bf16[128,2048]{1,0:T(8,128)(2,1)}, bf16[128,2048]{1,0:T(8,128)(2,1)S(1)}, u32[]{:S(2)}, u32[]{:S(2)}) collective-permute-start(bf16[128,2048]{1,0:T(8,128)(2,1)} %zo.1), channel_id=1, source_target_pairs={{0,4},{4,0},{8,12},{12,8},{16,20},{20,16},{24,28},{28,24},{1,5},{5... | collective-permute-start | bytes 1572872 | tf_op jit(solution)/shard_map/ppermute | solution.py:313
  6.4 10.4 %collective-permute-start.7 = (bf16[1040,128]{1,0:T(8,128)(2,1)S(1)}, bf16[1040,128]{1,0:T(8,128)(2,1)S(1)}, u32[]{:S(2)}, u32[]{:S(2)}) collective-permute-start(bf16[1040,128]{1,0:T(8,128)(2,1)S(1)} %get-tuple-element.28), channel_id=1, source_target_pairs={{0,24},{4,28},{8,0},{12,4},{16,8},{20,12},{24,16},{28,20},{1,25},{... | collective-permute-start | bytes 798728 | tf_op jit(solution)/shard_map/ppermute | solution.py:336
  10.0 14.0 %collective-permute-start.6 = (bf16[1040,128]{1,0:T(8,128)(2,1)S(1)}, bf16[1040,128]{1,0:T(8,128)(2,1)S(1)}, u32[]{:S(2)}, u32[]{:S(2)}) collective-permute-start(bf16[1040,128]{1,0:T(8,128)(2,1)S(1)} %get-tuple-element.28), channel_id=1, source_target_pairs={{0,16},{4,20},{8,24},{12,28},{16,0},{20,4},{24,8},{28,12},{1,17},{... | collective-permute-start | bytes 798728 | tf_op jit(solution)/shard_map/ppermute | solution.py:336
  10.6 13.5 %collective-permute-start.5 = (bf16[1040,128]{1,0:T(8,128)(2,1)S(1)}, bf16[1040,128]{1,0:T(8,128)(2,1)S(1)}, u32[]{:S(2)}, u32[]{:S(2)}) collective-permute-start(bf16[1040,128]{1,0:T(8,128)(2,1)S(1)} %get-tuple-element.28), channel_id=1, source_target_pairs={{0,8},{4,12},{8,16},{12,20},{16,24},{20,28},{24,0},{28,4},{1,9},{5... | collective-permute-start | bytes 798728 | tf_op jit(solution)/shard_map/ppermute | solution.py:336
  11.1 0.7 copy-start.3
  24.1 5.6 %copy-start = (bf16[2048,512]{1,0:T(8,128)(2,1)S(1)}, bf16[2048,512]{1,0:T(8,128)(2,1)}, u32[]{:S(2)}) copy-start(bf16[2048,512]{1,0:T(8,128)(2,1)} %refs_3_.3) | copy-start | bytes 6291460
  25.6 4.1 %collective-permute-start.10 = (bf16[128,1024]{1,0:T(8,128)(2,1)S(1)}, bf16[128,1024]{1,0:T(8,128)(2,1)S(1)}, u32[]{:S(2)}, u32[]{:S(2)}) collective-permute-start(bf16[128,1024]{1,0:T(8,128)(2,1)S(1)} %get-tuple-element.31), channel_id=1, source_target_pairs={{0,4},{4,0},{8,12},{12,8},{16,20},{20,16},{24,28},{28,24},{1,5},{5... | collective-permute-start | bytes 786440 | tf_op jit(solution)/shard_map/ppermute | solution.py:313
  25.6 9.1 %collective-permute-start.8 = (bf16[128,1024]{1,0:T(8,128)(2,1)S(1)}, bf16[128,1024]{1,0:T(8,128)(2,1)S(1)}, u32[]{:S(2)}, u32[]{:S(2)}) collective-permute-start(bf16[128,1024]{1,0:T(8,128)(2,1)S(1)} %get-tuple-element.30.refs_1_), channel_id=1, source_target_pairs={{0,8},{4,12},{8,0},{12,4},{16,24},{20,28},{24,16},{28,20},{1,9},{5... | collective-permute-start | bytes 786440 | tf_op jit(solution)/shard_map/ppermute | solution.py:316
  25.9 9.1 %collective-permute-start.9 = (bf16[128,1024]{1,0:T(8,128)(2,1)S(1)}, bf16[128,1024]{1,0:T(8,128)(2,1)S(1)}, u32[]{:S(2)}, u32[]{:S(2)}) collective-permute-start(bf16[128,1024]{1,0:T(8,128)(2,1)S(1)} %get-tuple-element.31), channel_id=1, source_target_pairs={{0,16},{4,20},{8,24},{12,28},{16,0},{20,4},{24,8},{28,12},{1,17},{... | collective-permute-start | bytes 786440 | tf_op jit(solution)/shard_map/ppermute | solution.py:316
  26.7 13.3 %collective-permute-start.12 = (bf16[128,1024]{1,0:T(8,128)(2,1)S(1)}, bf16[128,1024]{1,0:T(8,128)(2,1)S(1)}, u32[]{:S(2)}, u32[]{:S(2)}) collective-permute-start(bf16[128,1024]{1,0:T(8,128)(2,1)S(1)} %get-tuple-element.30.refs_1_), channel_id=1, source_target_pairs={{0,16},{4,20},{8,24},{12,28},{16,0},{20,4},{24,8},{28,12},{1,17},{... | collective-permute-start | bytes 786440 | tf_op jit(solution)/shard_map/ppermute | solution.py:316
  27.9 12.0 %collective-permute-start.11 = (bf16[128,1024]{1,0:T(8,128)(2,1)S(1)}, bf16[128,1024]{1,0:T(8,128)(2,1)S(1)}, u32[]{:S(2)}, u32[]{:S(2)}) collective-permute-start(bf16[128,1024]{1,0:T(8,128)(2,1)S(1)} %get-tuple-element.31), channel_id=1, source_target_pairs={{0,8},{4,12},{8,0},{12,4},{16,24},{20,28},{24,16},{28,20},{1,9},{5... | collective-permute-start | bytes 786440 | tf_op jit(solution)/shard_map/ppermute | solution.py:316
  35.0 5.7 %collective-permute-start.14 = (bf16[128,1024]{1,0:T(8,128)(2,1)S(1)}, bf16[128,1024]{1,0:T(8,128)(2,1)S(1)}, u32[]{:S(2)}, u32[]{:S(2)}) collective-permute-start(bf16[128,1024]{1,0:T(8,128)(2,1)S(1)} %collective-permute-done.9), channel_id=1, source_target_pairs={{0,4},{4,0},{8,12},{12,8},{16,20},{20,16},{24,28},{28,24},{1,5},{5... | collective-permute-start | bytes 786440 | tf_op jit(solution)/shard_map/ppermute | solution.py:313
  40.0 2.2 %collective-permute-start.13 = (bf16[128,1024]{1,0:T(8,128)(2,1)S(1)}, bf16[128,1024]{1,0:T(8,128)(2,1)S(1)}, u32[]{:S(2)}, u32[]{:S(2)}) collective-permute-start(bf16[128,1024]{1,0:T(8,128)(2,1)S(1)} %collective-permute-done.11), channel_id=1, source_target_pairs={{0,4},{4,0},{8,12},{12,8},{16,20},{20,16},{24,28},{28,24},{1,5},{5... | collective-permute-start | bytes 786440 | tf_op jit(solution)/shard_map/ppermute | solution.py:313
  40.0 9.1 %collective-permute-start.17 = (bf16[128,1024]{1,0:T(8,128)(2,1)S(1)}, bf16[128,1024]{1,0:T(8,128)(2,1)S(1)}, u32[]{:S(2)}, u32[]{:S(2)}) collective-permute-start(bf16[128,1024]{1,0:T(8,128)(2,1)S(1)} %collective-permute-done.8.refs_1_), channel_id=1, source_target_pairs={{0,16},{4,20},{8,24},{12,28},{16,0},{20,4},{24,8},{28,12},{1,17},{... | collective-permute-start | bytes 786440 | tf_op jit(solution)/shard_map/ppermute | solution.py:316
  40.8 9.1 %collective-permute-start.18 = (bf16[128,1024]{1,0:T(8,128)(2,1)S(1)}, bf16[128,1024]{1,0:T(8,128)(2,1)S(1)}, u32[]{:S(2)}, u32[]{:S(2)}) collective-permute-start(bf16[128,1024]{1,0:T(8,128)(2,1)S(1)} %collective-permute-done.14.refs_4_), channel_id=1, source_target_pairs={{0,8},{4,12},{8,0},{12,4},{16,24},{20,28},{24,16},{28,20},{1,9},{5... | collective-permute-start | bytes 786440 | tf_op jit(solution)/shard_map/ppermute | solution.py:316
  44.0 11.5 %collective-permute-start.15 = (bf16[1024,128]{1,0:T(8,128)(2,1)S(1)}, bf16[1024,128]{1,0:T(8,128)(2,1)S(1)}, u32[]{:S(2)}, u32[]{:S(2)}) collective-permute-start(bf16[1024,128]{1,0:T(8,128)(2,1)S(1)} %get-tuple-element.37), channel_id=1, source_target_pairs={{0,8},{4,12},{8,0},{12,4},{16,24},{20,28},{24,16},{28,20},{1,9},{5... | collective-permute-start | bytes 786440 | tf_op jit(solution)/shard_map/ppermute | solution.py:316
  45.1 10.4 %collective-permute-start.16 = (bf16[1024,128]{1,0:T(8,128)(2,1)S(1)}, bf16[1024,128]{1,0:T(8,128)(2,1)S(1)}, u32[]{:S(2)}, u32[]{:S(2)}) collective-permute-start(bf16[1024,128]{1,0:T(8,128)(2,1)S(1)} %get-tuple-element.38), channel_id=1, source_target_pairs={{0,16},{4,20},{8,24},{12,28},{16,0},{20,4},{24,8},{28,12},{1,17},{... | collective-permute-start | bytes 786440 | tf_op jit(solution)/shard_map/ppermute | solution.py:316
  51.2 9.9 %collective-permute-start.19 = (bf16[1024,128]{1,0:T(8,128)(2,1)S(1)}, bf16[1024,128]{1,0:T(8,128)(2,1)S(1)}, u32[]{:S(2)}, u32[]{:S(2)}) collective-permute-start(bf16[1024,128]{1,0:T(8,128)(2,1)S(1)} %shard_map.96), channel_id=1, source_target_pairs={{0,24},{4,28},{8,16},{12,20},{16,8},{20,12},{24,0},{28,4},{1,25},{... | collective-permute-start | bytes 786440 | tf_op jit(solution)/shard_map/ppermute | solution.py:316
  53.6 1.2 %collective-permute-start.20 = (f32[8,128]{1,0:T(8,128)S(1)}, f32[8,128]{1,0:T(8,128)S(1)}, u32[]{:S(2)}, u32[]{:S(2)}) collective-permute-start(f32[8,128]{1,0:T(8,128)S(1)} %get-tuple-element.42), channel_id=1, source_target_pairs={{0,4},{4,0},{8,12},{12,8},{16,20},{20,16},{24,28},{28,24},{1,5},{5... | collective-permute-start | bytes 12296 | tf_op jit(solution)/shard_map/ppermute | solution.py:313
  56.1 8.0 %collective-permute-start.21 = (bf16[1040,128]{1,0:T(8,128)(2,1)S(1)}, bf16[1040,128]{1,0:T(8,128)(2,1)S(1)}, u32[]{:S(2)}, u32[]{:S(2)}) collective-permute-start(bf16[1040,128]{1,0:T(8,128)(2,1)S(1)} %shard_map.97), channel_id=1, source_target_pairs={{0,1},{1,0},{2,3},{3,2},{4,5},{5,4},{6,7},{7,6},{8,9},{9,8},{10,11... | collective-permute-start | bytes 798728 | tf_op jit(solution)/shard_map/ppermute | solution.py:319
  61.7 7.9 %collective-permute-start.22 = (bf16[1024,128]{1,0:T(8,128)(2,1)S(1)}, bf16[1024,128]{1,0:T(8,128)(2,1)S(1)}, u32[]{:S(2)}, u32[]{:S(2)}) collective-permute-start(bf16[1024,128]{1,0:T(8,128)(2,1)S(1)} %shard_map.98.refs_6_), channel_id=1, source_target_pairs={{0,1},{1,0},{2,3},{3,2},{4,5},{5,4},{6,7},{7,6},{8,9},{9,8},{10,11... | collective-permute-start | bytes 786440 | tf_op jit(solution)/shard_map/ppermute | solution.py:319
  64.7 9.7 %collective-permute-start.23 = (bf16[1040,128]{1,0:T(8,128)(2,1)S(1)}, bf16[1040,128]{1,0:T(8,128)(2,1)S(1)}, u32[]{:S(2)}, u32[]{:S(2)}) collective-permute-start(bf16[1040,128]{1,0:T(8,128)(2,1)S(1)} %shard_map.99), channel_id=1, source_target_pairs={{0,2},{3,1},{4,6},{7,5},{9,11},{10,8},{13,15},{14,12},{17,19},{18,... | collective-permute-start | bytes 798728 | tf_op jit(solution)/shard_map/ppermute | solution.py:395
  70.2 12.8 %collective-permute-start.24 = (bf16[1040,128]{1,0:T(8,128)(2,1)S(1)}, bf16[1040,128]{1,0:T(8,128)(2,1)S(1)}, u32[]{:S(2)}, u32[]{:S(2)}) collective-permute-start(bf16[1040,128]{1,0:T(8,128)(2,1)S(1)} %shard_map.100), channel_id=1, source_target_pairs={{1,3},{2,0},{5,7},{6,4},{8,10},{11,9},{12,14},{15,13},{16,18},{19,... | collective-permute-start | bytes 798728 | tf_op jit(solution)/shard_map/ppermute | solution.py:395

commit v6 on v5

--- a/solution.py
+++ b/solution.py
@@ -62,10 +62,11 @@
     return ref[:, pl.ds(pl.multiple_of(k * n, n), n)]
 
 
-def half_rows(ref, k):
-    v = ref[...]
-    n = v.shape[0] // 4
-    return tuple(jnp.where(k == 0, v[i : i + n], v[i + n : i + 2 * n]) for i in (0, 2 * n))
+def parts_of(ref, k, rows):
+    n = (ref.shape[0] - 2 * rows) // 4
+    dt, ld = [jnp.where(k == 0, ref[i : i + n], ref[i + n : i + 2 * n]) for i in (0, 2 * n)]
+    b, c = [ref[4 * n + i : 4 * n + i + rows].astype(bf16) for i in (0, rows)]
+    return dt, ld, b, c
 
 
 def channel_map(heads, wide):
@@ -86,20 +87,20 @@
     return (j <= i), (i <= j)
 
 
-def state_kernel(s, xo, xr, bo, br, ro, rr, msg, first):
+def state_kernel(s, xo, xr, so, sr, msg, first):
     k = s[0]
     rows, wide = xo.shape
     half = pl.ds(pl.multiple_of(k * wide, wide), wide)
     _, upper = ones_upto(rows)
     got = []
-    for x, bc, rates in ((xo[...], bo, ro), (xr[:, half], br, rr)):
-        dt, ld = half_rows(rates, k)
+    for x, small in ((xo[...], so), (xr[:, half], sr)):
+        dt, ld, b, _ = parts_of(small, k, rows)
         spots = channel_map(ld.shape[0], wide)
         run = nn(ld, upper.astype(f32), HIGH)
         last = run[:, rows - 1 :]
         tail = jnp.exp(last - run) * dt
         scaled = (x.astype(f32) * spread(tail, spots)).astype(bf16)
-        state = tn(bc[:, : bc.shape[1] // 2], scaled)
+        state = tn(b, scaled)
         decay = spread(jnp.exp(jnp.broadcast_to(last, (last.shape[0], 8))), spots)
         got.append((state, decay))
     (so, do), (sr, dr) = got
@@ -137,7 +138,7 @@
     return state, jnp.concatenate([ext[i : i + 1] for i in range(count)], 1)
 
 
-def inside_kernel(s, xo, xr, bo, br, ro, rr, zo, zr, skip, out, decays, gates):
+def inside_kernel(s, xo, xr, so, sr, zo, zr, skip, out, decays, gates):
     k = s[0]
     rows, wide = xo.shape
     half = pl.ds(pl.multiple_of(k * wide, wide), wide)
@@ -147,9 +148,9 @@
     hi, lo = split2(jnp.broadcast_to(gains, (8, count)))
     spots = channel_map(count, wide)
     gains = nn(hi.astype(bf16), spots) + nn(lo.astype(bf16), spots)
-    for turn, (bc, rates, z) in enumerate(((bo, ro, zo), (br, rr, zr))):
+    for turn, (small, z) in enumerate(((so, zo), (sr, zr))):
         start = turn * rows
-        dt, ld = half_rows(rates, k)
+        dt, ld, b, c = parts_of(small, k, rows)
         heads = ld.shape[0]
         size = wide // heads
         run = nn(ld, upper.astype(f32), HIGH)
@@ -157,8 +158,7 @@
         decays[start : start + rows] = spread(jnp.exp(run), spots)
         zf = z[:, half].astype(f32)
         gates[start : start + rows] = zf / (1.0 + jnp.exp(-zf))
-        states = bc.shape[1] // 2
-        scores = jnp.where(low, nt(bc[:, states:], bc[:, :states]), 0.0)
+        scores = jnp.where(low, nt(c, b), 0.0)
         lane = lax.broadcasted_iota(jnp.int32, (rows, 2 * size), 1)
         for pair in range(heads // 2):
             w = []
@@ -176,7 +176,7 @@
             out[start : start + rows, at] = y + gains[:1, at] * xp.astype(f32)
 
 
-def gate_kernel(s, inside, decays, gates, first, bo, br, gain, _, *rest):
+def gate_kernel(s, inside, decays, gates, first, so, sr, gain, _, *rest):
     *states, mine, theirs, sq_mine, sq_theirs = rest
     k = s[0]
     rows, wide = mine.shape
@@ -190,10 +190,10 @@
     whole = jnp.where(even, decays[rows - 1 : rows], decays[2 * rows - 1 : 2 * rows])
     second = whole * enter + first[...]
     ones = jnp.ones((8, wide), bf16)
-    for turn, (bc, out, sq) in enumerate(((bo, mine, sq_mine), (br, theirs, sq_theirs))):
+    for turn, (small, out, sq) in enumerate(((so, mine, sq_mine), (sr, theirs, sq_theirs))):
         at = slice(turn * rows, (turn + 1) * rows)
         e = jnp.where(even, enter, second) if turn == 0 else jnp.where(even, second, enter)
-        y = inside[at] + nn(bc[:, bc.shape[1] // 2 :], e.astype(bf16)) * decays[at]
+        y = inside[at] + nn(parts_of(small, k, rows)[3], e.astype(bf16)) * decays[at]
         gated = y * gates[at]
         hi, lo = split2(gated * gated)
         sq[...] = nt(ones, hi.astype(bf16)) + nt(ones, lo.astype(bf16))
@@ -319,61 +319,63 @@
         return lax.ppermute(a, "head", [(i, i ^ m) for i in range(n)])
 
     x2 = swap(signal)
-    rates1 = jnp.pad(step_size, ((0, heads), (0, 0))) + jnp.pad(log_decay, ((heads, 0), (0, 0)))
-    states = state_in.shape[1]
-    bc1 = jnp.pad(state_in, ((0, 0), (0, states))) + jnp.pad(state_out, ((0, 0), (states, 0)))
-    rates2, bc2 = swap(rates1), swap(bc1)
+    parts = (step_size, log_decay, state_in.astype(f32), state_out.astype(f32))
+    tall = sum(a.shape[0] for a in parts)
+    at, small1 = 0, 0.0
+    for a in parts:
+        small1 = small1 + jnp.pad(a, ((at, tall - at - a.shape[0]), (0, 0)))
+        at += a.shape[0]
+    small2 = swap(small1)
     z2 = swap(gate_input)
     x1 = lax.dynamic_slice_in_dim(signal, k * wide, wide, 1)
     skip = skip_gain.reshape(1, heads)
     gain = norm_gain.reshape(1, 2 * wide)
 
-    ins = (x1, x2, bc1, bc2, rates1, rates2)
+    ins = (x1, x2, small1, small2)
     outs = [shape((states * wide // LANES + EXT, LANES), bf16), shape((states, wide), f32)]
     msg, first = call(state_kernel, s, ins, [full(a) for a in ins], outs, [full(a) for a in outs])
     w2 = swap(lax.optimization_barrier((out_weight, msg))[0])
     got = [
         lax.ppermute(msg, "seq", [(i, (i + 2 * j) % (2 * n)) for i in range(2 * n)]) for j in range(1, n)
     ]
-    ins = (x1, x2, bc1, bc2, rates1, rates2, gate_input, z2, skip)
+    ins = (x1, x2, small1, small2, gate_input, z2, skip)
     big = shape((2 * rows, wide), f32)
     inside, decays, gates = call(
         inside_kernel, s, ins, [full(a) for a in ins], [big] * 3, [full(big)] * 3
     )
-    ins = (inside, decays, gates, first, bc1, bc2, gain, w2, *got)
+    ins = (inside, decays, gates, first, small1, small2, gain, w2, *got)
     specs = [full(a) for a in ins[:7]] + [any_spec] + [full(a) for a in got]
     outs = [shape((rows, wide), bf16)] * 2 + [shape((8, rows), f32)] * 2
     u, v, sq_mine, sq_theirs = call(gate_kernel, s, ins, specs, outs, [full(a) for a in outs])
+    v = swap(v)
     squares = sq_mine + swap(sq_theirs)
 
     size = 2 * cols // LANES * rows
     p_shape = shape((size, LANES), bf16)
 
-    def project(u, v, after=()):
+    def project(u, v, after=(), flops=0):
         ins = (*u, *v, out_weight, w2, *after)
         specs = [full(a) for a in ins[: len(ins) - len(after)]] + [any_spec] * len(after)
 
         def kernel(*refs):
             project_kernel(*refs, count=len(u), extra=len(after))
 
-        return call(kernel, s, ins, specs, [p_shape] * len(u), [full(p_shape)] * len(u))
+        return call(kernel, s, ins, specs, [p_shape] * len(u), [full(p_shape)] * len(u), flops=flops)
 
     if n == 4:
         ux, vy = across(u, 1), across(v, 2)
-        vx, uy = across(v, 1), across(u, 2)
-        (own,) = project([u], [swap(v)])
+        uy, vx = across(u, 2), across(v, 1)
+        (own,) = project([u], [v])
         ux, vy, own = lax.optimization_barrier((ux, vy, own))
-        vy = swap(vy)
         ud, vd = lax.optimization_barrier((across(ux, 2), across(vy, 1)))
-        vx, uy = lax.optimization_barrier((vx, uy))
-        px, py = project([ux, uy], [swap(vx), vy], after=[own])
+        px, py = project([ux, uy], [vx, vy], after=[own])
         px, py = across(px, 1), across(py, 2)
         (far_here,) = project([ud], [vd])
         far = across(far_here, 3)
     else:
-        blocks = list(project([u], [swap(v)]))
+        blocks = list(project([u], [v]))
         for j in range(1, n):
-            (p,) = project([across(u, j)], [swap(across(v, j))])
+            (p,) = project([across(u, j)], [across(v, j)])
             blocks.append(across(p, j))
     message = shape((size + EXT, LANES), bf16)
 
@@ -387,21 +389,24 @@
     out = [shape((rows, 2 * cols), bf16)]
     if n == 4:
 
-        def over(a, roles):
-            pairs = [
-                ((2 * c + core) * n + h, (2 * c + core) * n + (h ^ 2))
-                for c in range(n) for core in range(2) for h in range(n) if c ^ h in roles
-            ]
+        def over(a, ring):
+            after = dict(zip(ring, ring[1:] + ring[:1]))
+            pairs = []
+            for c in range(n):
+                for core in range(2):
+                    for h in range(n):
+                        place = (2 * c + core) * n
+                        pairs.append((place + h, place + (c ^ after[c ^ h])))
             return lax.ppermute(a, BOTH, pairs)
 
         (got1,) = send(give_kernel, (px, py, squares), [message])
         got1 = along(got1, 1)
         (got2,) = send(give_kernel, (far, own), [p_shape])
         (sum1,) = send(join_kernel, (py, px, got1, squares, got1, got2), [message])
-        sum1 = over(sum1, (0, 3))
+        sum1 = over(sum1, (0, 2, 3, 1))
         got2 = along(got2, 1)
         (sum2,) = send(join_kernel, (own, far, got2, squares, got1), [message])
-        sum2 = over(sum2, (1, 2))
+        sum2 = over(sum2, (2, 0, 1, 3))
         ins = (own, px, py, far, got1, got2, sum1, sum2, squares)
         return send(last_kernel, ins, out, inner=inner)[0]
     steps = range(1, n)

time: 85.1 us -> 81.8 us (0.961)
  starting transfers between devices: 26.1 us -> 17.9 us
  waiting for transfers between devices: 40.6 us -> 46.7 us
    ppermute x2, waiting for transfers between devices: 1.08 us -> 8.69 us  [along(): return lax.ppermute(a, 'head', [(i, i ^ m) for i in range(n)])]
    ppermute x2, waiting for transfers between devices: 11.5 us -> 5.43 us  [over(): return lax.ppermute(a, BOTH, pairs)]
    ppermute x9, starting transfers between devices: 10.7 us -> 5.47 us  [across(): return lax.ppermute(a, 'seq', [(i, i ^ 2 * j) for i in range(2 * n)])]
    ppermute x9, waiting for transfers between devices: 17 us -> 20.1 us  [across(): return lax.ppermute(a, 'seq', [(i, i ^ 2 * j) for i in range(2 * n)])]
    ppermute x2, starting transfers between devices: 5.8 us -> 4.3 us  [over(): return lax.ppermute(a, BOTH, pairs)]
    ppermute x9 -> x6, waiting for transfers between devices: 1.18 us -> 2.62 us  [swap(): return lax.ppermute(a, 'seq', [(i, i ^ 1) for i in range(2 * n)])]
    ppermute x2, starting transfers between devices: 3.29 us -> 2.16 us  [along(): return lax.ppermute(a, 'head', [(i, i ^ m) for i in range(n)])]
  transfers between devices with their start and end apart: 25 -> 22, of which waited for: 14 -> 15; matrix products, arithmetic and copies ran while one was open for 3% -> 2% of each run, Pallas kernels for 11% -> 11%
where the time goes in v6:
time: 81.8 us; the launch traced here: 81.6 us
  waiting for transfers between devices  46.7 us (57%)
  starting transfers between devices  17.9 us (22%)
  Pallas kernels  14.4 us (18%)
  local copies, waits for them, and re-layouts  1.64 us (2%)
  other arithmetic  0.9 us (1%)
    ppermute x9, waiting for transfers between devices, across(): return lax.ppermute(a, 'seq', [(i, i ^ 2 * j) for i in range(2 * n)])  20.1 us
    pallas_call x11, Pallas kernels, call(): pl.pallas_call(kernel, out_shape=outs, grid_spec=pltpu.PrefetchScalarGrid...  14.4 us
    ppermute x3, waiting for transfers between devices, body(): lax.ppermute(msg, 'seq', [(i, (i + 2 * j) % (2 * n)) for i in range(2 * n)])  9.82 us
    ppermute x2, waiting for transfers between devices, along(): return lax.ppermute(a, 'head', [(i, i ^ m) for i in range(n)])  8.69 us
    ppermute x9, starting transfers between devices, across(): return lax.ppermute(a, 'seq', [(i, i ^ 2 * j) for i in range(2 * n)])  5.47 us
    ppermute x2, waiting for transfers between devices, over(): return lax.ppermute(a, BOTH, pairs)  5.43 us
    ppermute x3, starting transfers between devices, body(): lax.ppermute(msg, 'seq', [(i, (i + 2 * j) % (2 * n)) for i in range(2 * n)])  4.73 us
    ppermute x2, starting transfers between devices, over(): return lax.ppermute(a, BOTH, pairs)  4.3 us
  transfers between devices with their start and end apart: 22, of which 15 were waited for; matrix products, arithmetic and copies ran while one was open for 2% of the time, Pallas kernels for 11%

profile of v6, /device:TPU:0, one launch (start us, length us, event | category | flops | bytes accessed | tf_op | source)
XLA Modules:
  0.0 81.6 jit_solution(10983239503087025994)
XLA Ops:
  0.5 0.8 %convert_add_fusion.so = f32[320,128]{1,0:T(8,128)S(1)} fusion(f32[32,128]{1,0:T(8,128)} %param.14, f32[32,128]{1,0:T(8,128)} %param.13, bf16[128,128]{1,0:T(8,128)(2,1)} %param.12, bf16[128,128]{1,0:T(8,128)(2,1)} %param.11), kind=kLoop, calls=%fused_computation | loop fusion | flops 204800 | bytes 262144 | tf_op jit(solution)/shard_map/add | solution.py:326
  1.5 1.0 %constant_dynamic-slice_fusion.xo = bf16[128,1024]{1,0:T(8,128)(2,1)S(1)} fusion(bf16[128,2048]{1,0:T(8,128)(2,1)} %param.9, s32[]{:T(128)S(6)} %select_n.16), kind=kLoop, calls=%fused_computation.2 | loop fusion | bytes 524292 | tf_op jit(solution)/shard_map/dynamic_slice | solution.py:330
  2.7 2.2 %shard_map.92 = (bf16[1040,128]{1,0:T(8,128)(2,1)S(1)}, f32[128,1024]{1,0:T(8,128)S(1)}) custom-call(s32[3]{0:T(128)S(1)} %pad_add_fusion.s.refs_0_, bf16[128,1024]{1,0:T(8,128)(2,1)S(1)} %constant_dynamic-slice_fusion.xo, bf16[128,2048]{1,0:T(8,128)(2,1)S(1)} %collective-permute-done.xr, f32[320,128]{1,0:T(8,128)S(1)} %convert_add_fusion.so, ...), custom_call_target="tpu_custom_call" | custom-call | bytes 1904640 | tf_op jit(solution)/shard_map/pallas_call | solution.py:20
  5.5 3.6 %collective-permute-start.6 = (bf16[1040,128]{1,0:T(8,128)(2,1)S(1)}, bf16[1040,128]{1,0:T(8,128)(2,1)S(1)}, u32[]{:S(2)}, u32[]{:S(2)}) collective-permute-start(bf16[1040,128]{1,0:T(8,128)(2,1)S(1)} %get-tuple-element.26), channel_id=1, source_target_pairs={{0,24},{4,28},{8,0},{12,4},{16,8},{20,12},{24,16},{28,20},{1,25},{... | collective-permute-start | bytes 798728 | tf_op jit(solution)/shard_map/ppermute | solution.py:339
  10.3 0.7 copy-done.3
  10.9 2.5 %shard_map.91 = (f32[256,1024]{1,0:T(8,128)S(1)}, f32[256,1024]{1,0:T(8,128)S(1)}, f32[256,1024]{1,0:T(8,128)S(1)}) custom-call(s32[3]{0:T(128)S(1)} %pad_add_fusion.s.refs_0_, bf16[128,1024]{1,0:T(8,128)(2,1)S(1)} %constant_dynamic-slice_fusion.xo, bf16[128,2048]{1,0:T(8,128)(2,1)S(1)} %collective-permute-done.xr, f32[320,128]{1,0:T(8,128)S(1)} %convert_add_fusion.so, ...), custom_call_target="tpu_custom_call" | custom-call | bytes 5308544 | tf_op jit(solution)/shard_map/pallas_call | solution.py:20
  13.4 2.5 %collective-permute-done.6.rest_2_ = bf16[1040,128]{1,0:T(8,128)(2,1)S(1)} collective-permute-done((bf16[1040,128]{1,0:T(8,128)(2,1)S(1)}, bf16[1040,128]{1,0:T(8,128)(2,1)S(1)}, u32[]{:S(2)}, u32[]{:S(2)}) %collective-permute-start.6) | collective-permute-done | bytes 266272 | tf_op jit(solution)/shard_map/ppermute | solution.py:339
  15.9 7.3 %collective-permute-done.5.rest_1_ = bf16[1040,128]{1,0:T(8,128)(2,1)S(1)} collective-permute-done((bf16[1040,128]{1,0:T(8,128)(2,1)S(1)}, bf16[1040,128]{1,0:T(8,128)(2,1)S(1)}, u32[]{:S(2)}, u32[]{:S(2)}) %collective-permute-start.5) | collective-permute-done | bytes 266272 | tf_op jit(solution)/shard_map/ppermute | solution.py:339
  23.2 1.5 %shard_map.93 = (bf16[128,1024]{1,0:T(8,128)(2,1)S(1)}, bf16[128,1024]{1,0:T(8,128)(2,1)S(1)}, f32[8,128]{1,0:T(8,128)S(1)}, f32[8,128]{1,0:T(8,128)S(1)}) custom-call(s32[3]{0:T(128)S(1)} %pad_add_fusion.s.refs_0_, f32[256,1024]{1,0:T(8,128)S(1)} %get-tuple-element.22.inside, f32[256,1024]{1,0:T(8,128)S(1)} %get-tuple-element.23.decays, ...), custom_call_target="tpu_custom_call" | custom-call | bytes 7434240 | tf_op jit(solution)/shard_map/pallas_call | solution.py:20
  25.1 1.2 %collective-permute-done.8.refs_2_ = bf16[128,1024]{1,0:T(8,128)(2,1)S(1)} collective-permute-done((bf16[128,1024]{1,0:T(8,128)(2,1)S(1)}, bf16[128,1024]{1,0:T(8,128)(2,1)S(1)}, u32[]{:S(2)}, u32[]{:S(2)}) %collective-permute-start.8) | collective-permute-done | bytes 262176 | tf_op jit(solution)/shard_map/ppermute | solution.py:313
  26.8 1.5 %collective-permute-start.10 = (bf16[128,1024]{1,0:T(8,128)(2,1)S(1)}, bf16[128,1024]{1,0:T(8,128)(2,1)S(1)}, u32[]{:S(2)}, u32[]{:S(2)}) collective-permute-start(bf16[128,1024]{1,0:T(8,128)(2,1)S(1)} %get-tuple-element.28.refs_1_), channel_id=1, source_target_pairs={{0,16},{4,20},{8,24},{12,28},{16,0},{20,4},{24,8},{28,12},{1,17},{... | collective-permute-start | bytes 786440 | tf_op jit(solution)/shard_map/ppermute | solution.py:316
  28.8 1.3 %shard_map.94.refs_7_.refs_2_.refs_1_ = bf16[1024,128]{1,0:T(8,128)(2,1)S(1)} custom-call(s32[3]{0:T(128)S(1)} %pad_add_fusion.s.refs_0_, bf16[128,1024]{1,0:T(8,128)(2,1)S(1)} %get-tuple-element.28.refs_1_, bf16[128,1024]{1,0:T(8,128)(2,1)S(1)} %collective-permute-done.8.refs_2_, bf16[2048,512]{1,0:T(8,128)(2,1)S(1)} %copy-done, ...), custom_call_target="tpu_custom_call" | custom-call | bytes 4980736 | tf_op jit(solution)/shard_map/pallas_call | solution.py:20
  30.1 3.8 %collective-permute-done.7.refs_1_ = bf16[128,1024]{1,0:T(8,128)(2,1)S(1)} collective-permute-done((bf16[128,1024]{1,0:T(8,128)(2,1)S(1)}, bf16[128,1024]{1,0:T(8,128)(2,1)S(1)}, u32[]{:S(2)}, u32[]{:S(2)}) %collective-permute-start.7) | collective-permute-done | bytes 262176 | tf_op jit(solution)/shard_map/ppermute | solution.py:316
  33.9 1.6 %collective-permute-done.9.refs_4_ = bf16[128,1024]{1,0:T(8,128)(2,1)S(1)} collective-permute-done((bf16[128,1024]{1,0:T(8,128)(2,1)S(1)}, bf16[128,1024]{1,0:T(8,128)(2,1)S(1)}, u32[]{:S(2)}, u32[]{:S(2)}) %collective-permute-start.9) | collective-permute-done | bytes 262176 | tf_op jit(solution)/shard_map/ppermute | solution.py:316
  36.5 4.5 %collective-permute-done.10.refs_2_ = bf16[128,1024]{1,0:T(8,128)(2,1)S(1)} collective-permute-done((bf16[128,1024]{1,0:T(8,128)(2,1)S(1)}, bf16[128,1024]{1,0:T(8,128)(2,1)S(1)}, u32[]{:S(2)}, u32[]{:S(2)}) %collective-permute-start.10) | collective-permute-done | bytes 262176 | tf_op jit(solution)/shard_map/ppermute | solution.py:316
  41.1 1.8 %shard_map.95 = (bf16[1024,128]{1,0:T(8,128)(2,1)S(1)}, bf16[1024,128]{1,0:T(8,128)(2,1)S(1)}) custom-call(s32[3]{0:T(128)S(1)} %pad_add_fusion.s.refs_0_, bf16[128,1024]{1,0:T(8,128)(2,1)S(1)} %collective-permute-done.7.refs_1_, bf16[128,1024]{1,0:T(8,128)(2,1)S(1)} %collective-permute-done.10.refs_2_, ...), custom_call_target="tpu_custom_call" | custom-call | bytes 6029312 | tf_op jit(solution)/shard_map/pallas_call | solution.py:20
  44.0 2.7 %collective-permute-done.14.refs_1_ = bf16[128,1024]{1,0:T(8,128)(2,1)S(1)} collective-permute-done((bf16[128,1024]{1,0:T(8,128)(2,1)S(1)}, bf16[128,1024]{1,0:T(8,128)(2,1)S(1)}, u32[]{:S(2)}, u32[]{:S(2)}) %collective-permute-start.14) | collective-permute-done | bytes 262176 | tf_op jit(solution)/shard_map/ppermute | solution.py:316
  46.7 1.3 %shard_map.96 = bf16[1024,128]{1,0:T(8,128)(2,1)S(1)} custom-call(s32[3]{0:T(128)S(1)} %pad_add_fusion.s.refs_0_, bf16[128,1024]{1,0:T(8,128)(2,1)S(1)} %collective-permute-done.14.refs_1_, bf16[128,1024]{1,0:T(8,128)(2,1)S(1)} %collective-permute-done.15.refs_2_, bf16[2048,512]{1,0:T(8,128)(2,1)S(1)} %copy-done, ...), custom_call_target="tpu_custom_call" | custom-call | bytes 4980736 | tf_op jit(solution)/shard_map/pallas_call | solution.py:20
  48.4 1.2 %collective-permute-done.17 = f32[8,128]{1,0:T(8,128)S(1)} collective-permute-done((f32[8,128]{1,0:T(8,128)S(1)}, f32[8,128]{1,0:T(8,128)S(1)}, u32[]{:S(2)}, u32[]{:S(2)}) %collective-permute-start.17) | collective-permute-done | bytes 4128 | tf_op jit(solution)/shard_map/ppermute | solution.py:313
  49.5 2.0 %collective-permute-done.12.refs_1_.refs_2_ = bf16[1024,128]{1,0:T(8,128)(2,1)S(1)} collective-permute-done((bf16[1024,128]{1,0:T(8,128)(2,1)S(1)}, bf16[1024,128]{1,0:T(8,128)(2,1)S(1)}, u32[]{:S(2)}, u32[]{:S(2)}) %collective-permute-start.12) | collective-permute-done | bytes 262176 | tf_op jit(solution)/shard_map/ppermute | solution.py:316
  51.5 5.6 %collective-permute-done.13.refs_2_.refs_1_.refs_3_ = bf16[1024,128]{1,0:T(8,128)(2,1)S(1)} collective-permute-done((bf16[1024,128]{1,0:T(8,128)(2,1)S(1)}, bf16[1024,128]{1,0:T(8,128)(2,1)S(1)}, u32[]{:S(2)}, u32[]{:S(2)}) %collective-permute-start.13) | collective-permute-done | bytes 262176 | tf_op jit(solution)/shard_map/ppermute | solution.py:316
  57.1 0.6 shard_map.97
  57.7 1.6 %collective-permute-start.18 = (bf16[1040,128]{1,0:T(8,128)(2,1)S(1)}, bf16[1040,128]{1,0:T(8,128)(2,1)S(1)}, u32[]{:S(2)}, u32[]{:S(2)}) collective-permute-start(bf16[1040,128]{1,0:T(8,128)(2,1)S(1)} %shard_map.97), channel_id=1, source_target_pairs={{0,1},{1,0},{2,3},{3,2},{4,5},{5,4},{6,7},{7,6},{8,9},{9,8},{10,11... | collective-permute-start | bytes 798728 | tf_op jit(solution)/shard_map/ppermute | solution.py:319
  59.4 0.6 shard_map.98.refs_6_
  60.5 8.2 %collective-permute-done.18.refs_3_.refs_5_ = bf16[1040,128]{1,0:T(8,128)(2,1)S(1)} collective-permute-done((bf16[1040,128]{1,0:T(8,128)(2,1)S(1)}, bf16[1040,128]{1,0:T(8,128)(2,1)S(1)}, u32[]{:S(2)}, u32[]{:S(2)}) %collective-permute-start.18) | collective-permute-done | bytes 266272 | tf_op jit(solution)/shard_map/ppermute | solution.py:319
  68.7 0.6 shard_map.99
  69.3 1.8 %collective-permute-start.20 = (bf16[1040,128]{1,0:T(8,128)(2,1)S(1)}, bf16[1040,128]{1,0:T(8,128)(2,1)S(1)}, u32[]{:S(2)}, u32[]{:S(2)}) collective-permute-start(bf16[1040,128]{1,0:T(8,128)(2,1)S(1)} %shard_map.99), channel_id=1, source_target_pairs={{0,2},{1,0},{2,3},{3,1},{4,6},{5,4},{6,7},{7,5},{8,9},{9,11},{10,8... | collective-permute-start | bytes 798728 | tf_op jit(solution)/shard_map/ppermute | solution.py:400
  71.6 0.7 shard_map.100
  72.2 2.5 %collective-permute-start.21 = (bf16[1040,128]{1,0:T(8,128)(2,1)S(1)}, bf16[1040,128]{1,0:T(8,128)(2,1)S(1)}, u32[]{:S(2)}, u32[]{:S(2)}) collective-permute-start(bf16[1040,128]{1,0:T(8,128)(2,1)S(1)} %shard_map.100), channel_id=1, source_target_pairs={{0,1},{1,3},{2,0},{3,2},{4,5},{5,7},{6,4},{7,6},{8,10},{9,8},{10,1... | collective-permute-start | bytes 798728 | tf_op jit(solution)/shard_map/ppermute | solution.py:400
  74.8 1.0 %collective-permute-done.20.refs_7_ = bf16[1040,128]{1,0:T(8,128)(2,1)S(1)} collective-permute-done((bf16[1040,128]{1,0:T(8,128)(2,1)S(1)}, bf16[1040,128]{1,0:T(8,128)(2,1)S(1)}, u32[]{:S(2)}, u32[]{:S(2)}) %collective-permute-start.20) | collective-permute-done | bytes 266272 | tf_op jit(solution)/shard_map/ppermute | solution.py:400
  75.8 4.4 %collective-permute-done.21.refs_8_ = bf16[1040,128]{1,0:T(8,128)(2,1)S(1)} collective-permute-done((bf16[1040,128]{1,0:T(8,128)(2,1)S(1)}, bf16[1040,128]{1,0:T(8,128)(2,1)S(1)}, u32[]{:S(2)}, u32[]{:S(2)}) %collective-permute-start.21) | collective-permute-done | bytes 266272 | tf_op jit(solution)/shard_map/ppermute | solution.py:400
  80.2 1.4 %shard_map.101 = bf16[128,1024]{1,0:T(8,128)(2,1)} custom-call(s32[3]{0:T(128)S(1)} %pad_add_fusion.s.refs_0_, bf16[1024,128]{1,0:T(8,128)(2,1)S(1)} %shard_map.94.refs_7_.refs_2_.refs_1_, bf16[1024,128]{1,0:T(8,128)(2,1)S(1)} %collective-permute-done.12.refs_1_.refs_2_, bf16[1024,128]{1,0:T(8,128)(2,1)S(1)} %collective-permute-done.13.refs_2_.refs_1_.refs_3_, ...), custom_call_target="tpu_custom_call" | custom-call | bytes 2375680 | tf_op jit(solution)/shard_map/pallas_call | solution.py:20
  (35 shorter events, 7.6 us)
Async XLA Ops:
  0.0 10.3 %copy-start.1 = (bf16[128,2048]{1,0:T(8,128)(2,1)S(1)}, bf16[128,2048]{1,0:T(8,128)(2,1)}, u32[]{:S(2)}) copy-start(bf16[128,2048]{1,0:T(8,128)(2,1)} %zo.1) | copy-start | bytes 1572868
  0.0 23.2 %copy-start.2 = (f32[2048]{0:T(1024)S(1)}, f32[2048]{0:T(1024)}, u32[]{:S(2)}) copy-start(f32[2048]{0:T(1024)} %param.16) | copy-start | bytes 24580
  0.0 2.7 %collective-permute-start = (bf16[128,2048]{1,0:T(8,128)(2,1)}, bf16[128,2048]{1,0:T(8,128)(2,1)S(1)}, u32[]{:S(2)}, u32[]{:S(2)}) collective-permute-start(bf16[128,2048]{1,0:T(8,128)(2,1)} %param.9), channel_id=1, source_target_pairs={{0,4},{4,0},{8,12},{12,8},{16,20},{20,16},{24,28},{28,24},{1,5},{5... | collective-permute-start | bytes 1572872 | tf_op jit(solution)/shard_map/ppermute | solution.py:313
  1.3 1.5 %collective-permute-start.1 = (f32[320,128]{1,0:T(8,128)S(1)}, f32[320,128]{1,0:T(8,128)S(1)}, u32[]{:S(2)}, u32[]{:S(2)}) collective-permute-start(f32[320,128]{1,0:T(8,128)S(1)} %convert_add_fusion.so), channel_id=1, source_target_pairs={{0,4},{4,0},{8,12},{12,8},{16,20},{20,16},{24,28},{28,24},{1,5},{5... | collective-permute-start | bytes 491528 | tf_op jit(solution)/shard_map/ppermute | solution.py:313
  5.0 18.3 %collective-permute-start.3 = (bf16[2048,512]{1,0:T(8,128)(2,1)}, bf16[2048,512]{1,0:T(8,128)(2,1)S(1)}, u32[]{:S(2)}, u32[]{:S(2)}) collective-permute-start(bf16[2048,512]{1,0:T(8,128)(2,1)} %refs_3_.3), channel_id=1, source_target_pairs={{0,4},{4,0},{8,12},{12,8},{16,20},{20,16},{24,28},{28,24},{1,5},{5... | collective-permute-start | bytes 6291464 | tf_op jit(solution)/shard_map/ppermute | solution.py:313
  5.2 5.1 %collective-permute-start.2 = (bf16[128,2048]{1,0:T(8,128)(2,1)}, bf16[128,2048]{1,0:T(8,128)(2,1)S(1)}, u32[]{:S(2)}, u32[]{:S(2)}) collective-permute-start(bf16[128,2048]{1,0:T(8,128)(2,1)} %zo.1), channel_id=1, source_target_pairs={{0,4},{4,0},{8,12},{12,8},{16,20},{20,16},{24,28},{28,24},{1,5},{5... | collective-permute-start | bytes 1572872 | tf_op jit(solution)/shard_map/ppermute | solution.py:313
  5.5 10.4 %collective-permute-start.6 = (bf16[1040,128]{1,0:T(8,128)(2,1)S(1)}, bf16[1040,128]{1,0:T(8,128)(2,1)S(1)}, u32[]{:S(2)}, u32[]{:S(2)}) collective-permute-start(bf16[1040,128]{1,0:T(8,128)(2,1)S(1)} %get-tuple-element.26), channel_id=1, source_target_pairs={{0,24},{4,28},{8,0},{12,4},{16,8},{20,12},{24,16},{28,20},{1,25},{... | collective-permute-start | bytes 798728 | tf_op jit(solution)/shard_map/ppermute | solution.py:339
  9.2 14.1 %collective-permute-start.5 = (bf16[1040,128]{1,0:T(8,128)(2,1)S(1)}, bf16[1040,128]{1,0:T(8,128)(2,1)S(1)}, u32[]{:S(2)}, u32[]{:S(2)}) collective-permute-start(bf16[1040,128]{1,0:T(8,128)(2,1)S(1)} %get-tuple-element.26), channel_id=1, source_target_pairs={{0,16},{4,20},{8,24},{12,28},{16,0},{20,4},{24,8},{28,12},{1,17},{... | collective-permute-start | bytes 798728 | tf_op jit(solution)/shard_map/ppermute | solution.py:339
  9.7 13.6 %collective-permute-start.4 = (bf16[1040,128]{1,0:T(8,128)(2,1)S(1)}, bf16[1040,128]{1,0:T(8,128)(2,1)S(1)}, u32[]{:S(2)}, u32[]{:S(2)}) collective-permute-start(bf16[1040,128]{1,0:T(8,128)(2,1)S(1)} %get-tuple-element.26), channel_id=1, source_target_pairs={{0,8},{4,12},{8,16},{12,20},{16,24},{20,28},{24,0},{28,4},{1,9},{5... | collective-permute-start | bytes 798728 | tf_op jit(solution)/shard_map/ppermute | solution.py:339
  10.3 0.7 copy-start.3
  23.2 5.6 %copy-start = (bf16[2048,512]{1,0:T(8,128)(2,1)S(1)}, bf16[2048,512]{1,0:T(8,128)(2,1)}, u32[]{:S(2)}) copy-start(bf16[2048,512]{1,0:T(8,128)(2,1)} %refs_3_.3) | copy-start | bytes 6291460
  24.7 1.6 %collective-permute-start.8 = (bf16[128,1024]{1,0:T(8,128)(2,1)S(1)}, bf16[128,1024]{1,0:T(8,128)(2,1)S(1)}, u32[]{:S(2)}, u32[]{:S(2)}) collective-permute-start(bf16[128,1024]{1,0:T(8,128)(2,1)S(1)} %get-tuple-element.29), channel_id=1, source_target_pairs={{0,4},{4,0},{8,12},{12,8},{16,20},{20,16},{24,28},{28,24},{1,5},{5... | collective-permute-start | bytes 786440 | tf_op jit(solution)/shard_map/ppermute | solution.py:313
  24.7 9.1 %collective-permute-start.7 = (bf16[128,1024]{1,0:T(8,128)(2,1)S(1)}, bf16[128,1024]{1,0:T(8,128)(2,1)S(1)}, u32[]{:S(2)}, u32[]{:S(2)}) collective-permute-start(bf16[128,1024]{1,0:T(8,128)(2,1)S(1)} %get-tuple-element.28.refs_1_), channel_id=1, source_target_pairs={{0,8},{4,12},{8,0},{12,4},{16,24},{20,28},{24,16},{28,20},{1,9},{5... | collective-permute-start | bytes 786440 | tf_op jit(solution)/shard_map/ppermute | solution.py:316
  26.3 9.2 %collective-permute-start.9 = (bf16[128,1024]{1,0:T(8,128)(2,1)S(1)}, bf16[128,1024]{1,0:T(8,128)(2,1)S(1)}, u32[]{:S(2)}, u32[]{:S(2)}) collective-permute-start(bf16[128,1024]{1,0:T(8,128)(2,1)S(1)} %collective-permute-done.8.refs_2_), channel_id=1, source_target_pairs={{0,16},{4,20},{8,24},{12,28},{16,0},{20,4},{24,8},{28,12},{1,17},{... | collective-permute-start | bytes 786440 | tf_op jit(solution)/shard_map/ppermute | solution.py:316
  26.8 14.3 %collective-permute-start.10 = (bf16[128,1024]{1,0:T(8,128)(2,1)S(1)}, bf16[128,1024]{1,0:T(8,128)(2,1)S(1)}, u32[]{:S(2)}, u32[]{:S(2)}) collective-permute-start(bf16[128,1024]{1,0:T(8,128)(2,1)S(1)} %get-tuple-element.28.refs_1_), channel_id=1, source_target_pairs={{0,16},{4,20},{8,24},{12,28},{16,0},{20,4},{24,8},{28,12},{1,17},{... | collective-permute-start | bytes 786440 | tf_op jit(solution)/shard_map/ppermute | solution.py:316
  28.3 12.8 %collective-permute-start.11 = (bf16[128,1024]{1,0:T(8,128)(2,1)S(1)}, bf16[128,1024]{1,0:T(8,128)(2,1)S(1)}, u32[]{:S(2)}, u32[]{:S(2)}) collective-permute-start(bf16[128,1024]{1,0:T(8,128)(2,1)S(1)} %collective-permute-done.8.refs_2_), channel_id=1, source_target_pairs={{0,8},{4,12},{8,0},{12,4},{16,24},{20,28},{24,16},{28,20},{1,9},{5... | collective-permute-start | bytes 786440 | tf_op jit(solution)/shard_map/ppermute | solution.py:316
  35.5 11.2 %collective-permute-start.14 = (bf16[128,1024]{1,0:T(8,128)(2,1)S(1)}, bf16[128,1024]{1,0:T(8,128)(2,1)S(1)}, u32[]{:S(2)}, u32[]{:S(2)}) collective-permute-start(bf16[128,1024]{1,0:T(8,128)(2,1)S(1)} %collective-permute-done.7.refs_1_), channel_id=1, source_target_pairs={{0,16},{4,20},{8,24},{12,28},{16,0},{20,4},{24,8},{28,12},{1,17},{... | collective-permute-start | bytes 786440 | tf_op jit(solution)/shard_map/ppermute | solution.py:316
  35.9 10.8 %collective-permute-start.15 = (bf16[128,1024]{1,0:T(8,128)(2,1)S(1)}, bf16[128,1024]{1,0:T(8,128)(2,1)S(1)}, u32[]{:S(2)}, u32[]{:S(2)}) collective-permute-start(bf16[128,1024]{1,0:T(8,128)(2,1)S(1)} %collective-permute-done.9.refs_4_), channel_id=1, source_target_pairs={{0,8},{4,12},{8,0},{12,4},{16,24},{20,28},{24,16},{28,20},{1,9},{5... | collective-permute-start | bytes 786440 | tf_op jit(solution)/shard_map/ppermute | solution.py:316
  42.9 8.6 %collective-permute-start.12 = (bf16[1024,128]{1,0:T(8,128)(2,1)S(1)}, bf16[1024,128]{1,0:T(8,128)(2,1)S(1)}, u32[]{:S(2)}, u32[]{:S(2)}) collective-permute-start(bf16[1024,128]{1,0:T(8,128)(2,1)S(1)} %get-tuple-element.33), channel_id=1, source_target_pairs={{0,8},{4,12},{8,0},{12,4},{16,24},{20,28},{24,16},{28,20},{1,9},{5... | collective-permute-start | bytes 786440 | tf_op jit(solution)/shard_map/ppermute | solution.py:316
  43.4 13.7 %collective-permute-start.13 = (bf16[1024,128]{1,0:T(8,128)(2,1)S(1)}, bf16[1024,128]{1,0:T(8,128)(2,1)S(1)}, u32[]{:S(2)}, u32[]{:S(2)}) collective-permute-start(bf16[1024,128]{1,0:T(8,128)(2,1)S(1)} %get-tuple-element.34), channel_id=1, source_target_pairs={{0,16},{4,20},{8,24},{12,28},{16,0},{20,4},{24,8},{28,12},{1,17},{... | collective-permute-start | bytes 786440 | tf_op jit(solution)/shard_map/ppermute | solution.py:316
  48.0 11.4 %collective-permute-start.16 = (bf16[1024,128]{1,0:T(8,128)(2,1)S(1)}, bf16[1024,128]{1,0:T(8,128)(2,1)S(1)}, u32[]{:S(2)}, u32[]{:S(2)}) collective-permute-start(bf16[1024,128]{1,0:T(8,128)(2,1)S(1)} %shard_map.96), channel_id=1, source_target_pairs={{0,24},{4,28},{8,16},{12,20},{16,8},{20,12},{24,0},{28,4},{1,25},{... | collective-permute-start | bytes 786440 | tf_op jit(solution)/shard_map/ppermute | solution.py:316
  48.4 1.2 %collective-permute-start.17 = (f32[8,128]{1,0:T(8,128)S(1)}, f32[8,128]{1,0:T(8,128)S(1)}, u32[]{:S(2)}, u32[]{:S(2)}) collective-permute-start(f32[8,128]{1,0:T(8,128)S(1)} %get-tuple-element.38), channel_id=1, source_target_pairs={{0,4},{4,0},{8,12},{12,8},{16,20},{20,16},{24,28},{28,24},{1,5},{5... | collective-permute-start | bytes 12296 | tf_op jit(solution)/shard_map/ppermute | solution.py:313
  57.7 11.0 %collective-permute-start.18 = (bf16[1040,128]{1,0:T(8,128)(2,1)S(1)}, bf16[1040,128]{1,0:T(8,128)(2,1)S(1)}, u32[]{:S(2)}, u32[]{:S(2)}) collective-permute-start(bf16[1040,128]{1,0:T(8,128)(2,1)S(1)} %shard_map.97), channel_id=1, source_target_pairs={{0,1},{1,0},{2,3},{3,2},{4,5},{5,4},{6,7},{7,6},{8,9},{9,8},{10,11... | collective-permute-start | bytes 798728 | tf_op jit(solution)/shard_map/ppermute | solution.py:319
  60.0 11.6 %collective-permute-start.19 = (bf16[1024,128]{1,0:T(8,128)(2,1)S(1)}, bf16[1024,128]{1,0:T(8,128)(2,1)S(1)}, u32[]{:S(2)}, u32[]{:S(2)}) collective-permute-start(bf16[1024,128]{1,0:T(8,128)(2,1)S(1)} %shard_map.98.refs_6_), channel_id=1, source_target_pairs={{0,1},{1,0},{2,3},{3,2},{4,5},{5,4},{6,7},{7,6},{8,9},{9,8},{10,11... | collective-permute-start | bytes 786440 | tf_op jit(solution)/shard_map/ppermute | solution.py:319
  69.3 6.5 %collective-permute-start.20 = (bf16[1040,128]{1,0:T(8,128)(2,1)S(1)}, bf16[1040,128]{1,0:T(8,128)(2,1)S(1)}, u32[]{:S(2)}, u32[]{:S(2)}) collective-permute-start(bf16[1040,128]{1,0:T(8,128)(2,1)S(1)} %shard_map.99), channel_id=1, source_target_pairs={{0,2},{1,0},{2,3},{3,1},{4,6},{5,4},{6,7},{7,5},{8,9},{9,11},{10,8... | collective-permute-start | bytes 798728 | tf_op jit(solution)/shard_map/ppermute | solution.py:400
  72.2 8.0 %collective-permute-start.21 = (bf16[1040,128]{1,0:T(8,128)(2,1)S(1)}, bf16[1040,128]{1,0:T(8,128)(2,1)S(1)}, u32[]{:S(2)}, u32[]{:S(2)}) collective-permute-start(bf16[1040,128]{1,0:T(8,128)(2,1)S(1)} %shard_map.100), channel_id=1, source_target_pairs={{0,1},{1,3},{2,0},{3,2},{4,5},{5,7},{6,4},{7,6},{8,10},{9,8},{10,1... | collective-permute-start | bytes 798728 | tf_op jit(solution)/shard_map/ppermute | solution.py:400

commit v7 on v6

--- a/solution.py
+++ b/solution.py
@@ -10,6 +10,8 @@
 f32, bf16 = jnp.float32, jnp.bfloat16
 EXT = 16
 LANES = 128
+HEAD_ROWS = 16
+HEAD_DIM = 64
 MIB = 1024 * 1024
 
 
@@ -63,7 +65,7 @@
 
 
 def parts_of(ref, k, rows):
-    n = (ref.shape[0] - 2 * rows) // 4
+    n = HEAD_ROWS
     dt, ld = [jnp.where(k == 0, ref[i : i + n], ref[i + n : i + 2 * n]) for i in (0, 2 * n)]
     b, c = [ref[4 * n + i : 4 * n + i + rows].astype(bf16) for i in (0, rows)]
     return dt, ld, b, c
@@ -72,13 +74,21 @@
 def channel_map(heads, wide):
     head = lax.broadcasted_iota(jnp.int32, (heads, wide), 0)
     lane = lax.broadcasted_iota(jnp.int32, (heads, wide), 1)
-    size = wide // heads
+    size = HEAD_DIM
     return ((lane >= head * size) & (lane < (head + 1) * size)).astype(bf16)
 
 
 def spread(v, spots):
     hi, lo = split2(v)
-    return tn(hi.astype(bf16), spots) + tn(lo.astype(bf16), spots)
+    return tn(jnp.concatenate([hi, lo], 0).astype(bf16), jnp.concatenate([spots, spots], 0))
+
+
+def sums(v, upper):
+    hi, rest = split2(v)
+    mid, low = split2(rest)
+    n = v.shape[0]
+    got = nn(jnp.concatenate([hi, mid, low], 0).astype(bf16), upper.astype(bf16))
+    return got[:n] + got[n : 2 * n] + got[2 * n :]
 
 
 def ones_upto(rows):
@@ -92,20 +102,20 @@
     rows, wide = xo.shape
     half = pl.ds(pl.multiple_of(k * wide, wide), wide)
     _, upper = ones_upto(rows)
-    got = []
-    for x, small in ((xo[...], so), (xr[:, half], sr)):
-        dt, ld, b, _ = parts_of(small, k, rows)
-        spots = channel_map(ld.shape[0], wide)
-        run = nn(ld, upper.astype(f32), HIGH)
-        last = run[:, rows - 1 :]
-        tail = jnp.exp(last - run) * dt
-        scaled = (x.astype(f32) * spread(tail, spots)).astype(bf16)
-        state = tn(b, scaled)
-        decay = spread(jnp.exp(jnp.broadcast_to(last, (last.shape[0], 8))), spots)
-        got.append((state, decay))
-    (so, do), (sr, dr) = got
     even = k == 0
-    s1, s2 = jnp.where(even, so, sr), jnp.where(even, sr, so)
+    own, other = parts_of(so, k, rows), parts_of(sr, k, rows)
+    runs = sums(jnp.concatenate([own[1], other[1]], 0), upper)
+    lasts = runs[:, rows - 1 :]
+    tails = jnp.exp(lasts - runs) * jnp.concatenate([own[0], other[0]], 0)
+    n = HEAD_ROWS
+    tails = jnp.concatenate([tails[:n], tails[n:]], 1)
+    lasts = jnp.broadcast_to(jnp.exp(lasts), (2 * n, LANES))
+    spots = channel_map(n, wide)
+    wide_tails = spread(tails, spots)
+    do, dr = spread(lasts[:n, :8], spots), spread(lasts[n:, :8], spots)
+    st_own = tn(own[2], (xo[...].astype(f32) * wide_tails[:rows]).astype(bf16))
+    st_other = tn(other[2], (xr[:, half].astype(f32) * wide_tails[rows:]).astype(bf16))
+    s1, s2 = jnp.where(even, st_own, st_other), jnp.where(even, st_other, st_own)
     d2 = jnp.where(even, dr, do)
     n = s1.shape[0]
     flat(msg, (d2[:1] * s1 + s2).astype(bf16))
@@ -138,7 +148,7 @@
     return state, jnp.concatenate([ext[i : i + 1] for i in range(count)], 1)
 
 
-def inside_kernel(s, xo, xr, so, sr, zo, zr, skip, out, decays, gates):
+def inside_kernel(s, xo, xr, so, sr, zo, zr, skip, out, decays, whole):
     k = s[0]
     rows, wide = xo.shape
     half = pl.ds(pl.multiple_of(k * wide, wide), wide)
@@ -148,35 +158,37 @@
     hi, lo = split2(jnp.broadcast_to(gains, (8, count)))
     spots = channel_map(count, wide)
     gains = nn(hi.astype(bf16), spots) + nn(lo.astype(bf16), spots)
+    spots = channel_map(HEAD_ROWS, wide)
     for turn, (small, z) in enumerate(((so, zo), (sr, zr))):
         start = turn * rows
         dt, ld, b, c = parts_of(small, k, rows)
-        heads = ld.shape[0]
-        size = wide // heads
-        run = nn(ld, upper.astype(f32), HIGH)
+        size = HEAD_DIM
+        run = sums(ld, upper)
         down = nt(low.astype(f32), ld, HIGH)
-        decays[start : start + rows] = spread(jnp.exp(run), spots)
         zf = z[:, half].astype(f32)
-        gates[start : start + rows] = zf / (1.0 + jnp.exp(-zf))
+        gates = zf / (1.0 + jnp.exp(-zf))
+        decay = spread(jnp.exp(run), spots)
+        decays[start : start + rows] = decay * gates
+        whole[8 * turn : 8 * turn + 8] = decay[rows - 8 :]
         scores = jnp.where(low, nt(c, b), 0.0)
         lane = lax.broadcasted_iota(jnp.int32, (rows, 2 * size), 1)
-        for pair in range(heads // 2):
+        for duo in range(wide // size // 2):
             w = []
-            for h in (2 * pair, 2 * pair + 1):
+            for h in (2 * duo, 2 * duo + 1):
                 gap = jnp.minimum(down[:, h : h + 1] - run[h : h + 1, :], 0.0)
                 w.append((jnp.exp(gap) * scores * dt[h : h + 1, :]).astype(bf16))
-            at = slice(2 * pair * size, 2 * (pair + 1) * size)
+            at = slice(2 * duo * size, 2 * (duo + 1) * size)
             if turn == 0:
                 xp = xo[:, at]
             else:
-                xp = xr[:, pl.ds(pl.multiple_of(k * wide + 2 * pair * size, 2 * size), 2 * size)]
+                xp = xr[:, pl.ds(pl.multiple_of(k * wide + 2 * duo * size, 2 * size), 2 * size)]
             zero = jnp.zeros_like(xp)
             both = jnp.concatenate([jnp.where(lane < size, xp, zero), jnp.where(lane < size, zero, xp)], 0)
             y = nn(jnp.concatenate(w, 1), both)
-            out[start : start + rows, at] = y + gains[:1, at] * xp.astype(f32)
-
-
-def gate_kernel(s, inside, decays, gates, first, so, sr, gain, _, *rest):
+            out[start : start + rows, at] = (y + gains[:1, at] * xp.astype(f32)) * gates[:, at]
+
+
+def gate_kernel(s, inside, decays, whole, first, so, sr, gain, _, *rest):
     *states, mine, theirs, sq_mine, sq_theirs = rest
     k = s[0]
     rows, wide = mine.shape
@@ -187,15 +199,14 @@
         st = jnp.where(s[2] > j, st, 0.0)
         enter = st if enter is None else enter + st * through
         through = dec if through is None else through * dec
-    whole = jnp.where(even, decays[rows - 1 : rows], decays[2 * rows - 1 : 2 * rows])
-    second = whole * enter + first[...]
-    ones = jnp.ones((8, wide), bf16)
+    second = jnp.where(even, whole[7:8], whole[15:16]) * enter + first[...]
+    ones = jnp.ones((8, LANES), bf16)
     for turn, (small, out, sq) in enumerate(((so, mine, sq_mine), (sr, theirs, sq_theirs))):
         at = slice(turn * rows, (turn + 1) * rows)
         e = jnp.where(even, enter, second) if turn == 0 else jnp.where(even, second, enter)
-        y = inside[at] + nn(parts_of(small, k, rows)[3], e.astype(bf16)) * decays[at]
-        gated = y * gates[at]
-        hi, lo = split2(gated * gated)
+        gated = inside[at] + nn(parts_of(small, k, rows)[3], e.astype(bf16)) * decays[at]
+        squared = gated * gated
+        hi, lo = split2(sum(squared[:, i : i + LANES] for i in range(0, wide, LANES)))
         sq[...] = nt(ones, hi.astype(bf16)) + nt(ones, lo.astype(bf16))
         out[...] = (gated * half_lanes(gain, k)).astype(bf16)
 
@@ -319,12 +330,16 @@
         return lax.ppermute(a, "head", [(i, i ^ m) for i in range(n)])
 
     x2 = swap(signal)
-    parts = (step_size, log_decay, state_in.astype(f32), state_out.astype(f32))
-    tall = sum(a.shape[0] for a in parts)
-    at, small1 = 0, 0.0
-    for a in parts:
-        small1 = small1 + jnp.pad(a, ((at, tall - at - a.shape[0]), (0, 0)))
-        at += a.shape[0]
+    half = heads // 2
+    if half == HEAD_ROWS:
+        parts, places = [step_size, log_decay], [0, 2 * HEAD_ROWS]
+    else:
+        parts = [a[i : i + half] for a in (step_size, log_decay) for i in (0, half)]
+        places = [i * HEAD_ROWS for i in range(4)]
+    parts += [state_in.astype(f32), state_out.astype(f32)]
+    places += [4 * HEAD_ROWS, 4 * HEAD_ROWS + rows]
+    tall = 4 * HEAD_ROWS + 2 * rows
+    small1 = sum(jnp.pad(a, ((at, tall - at - a.shape[0]), (0, 0))) for a, at in zip(parts, places))
     small2 = swap(small1)
     z2 = swap(gate_input)
     x1 = lax.dynamic_slice_in_dim(signal, k * wide, wide, 1)
@@ -336,14 +351,14 @@
     msg, first = call(state_kernel, s, ins, [full(a) for a in ins], outs, [full(a) for a in outs])
     w2 = swap(lax.optimization_barrier((out_weight, msg))[0])
     got = [
-        lax.ppermute(msg, "seq", [(i, (i + 2 * j) % (2 * n)) for i in range(2 * n)]) for j in range(1, n)
-    ]
+        lax.ppermute(msg, "seq", [(i, (i + 2 * j) % (2 * n)) for i in range(2 * n)]) for j in range(n - 1, 0, -1)
+    ][::-1]
     ins = (x1, x2, small1, small2, gate_input, z2, skip)
-    big = shape((2 * rows, wide), f32)
-    inside, decays, gates = call(
-        inside_kernel, s, ins, [full(a) for a in ins], [big] * 3, [full(big)] * 3
+    big, ends = shape((2 * rows, wide), f32), shape((16, wide), f32)
+    inside, decays, whole = call(
+        inside_kernel, s, ins, [full(a) for a in ins], [big, big, ends], [full(big)] * 3
     )
-    ins = (inside, decays, gates, first, small1, small2, gain, w2, *got)
+    ins = (inside, decays, whole, first, small1, small2, gain, w2, *got)
     specs = [full(a) for a in ins[:7]] + [any_spec] + [full(a) for a in got]
     outs = [shape((rows, wide), bf16)] * 2 + [shape((8, rows), f32)] * 2
     u, v, sq_mine, sq_theirs = call(gate_kernel, s, ins, specs, outs, [full(a) for a in outs])

time: 81.8 us -> 80.7 us (0.987)
  Pallas kernels: 14.4 us -> 13.3 us
    pallas_call x11, Pallas kernels: 14.4 us -> 13.3 us  [call(): pl.pallas_call(kernel, out_shape=outs, grid_spec=pltpu.PrefetchScalarGrid...]
where the time goes in v7:
time: 80.7 us; the launch traced here: 80.5 us
  waiting for transfers between devices  46.7 us (58%)
  starting transfers between devices  17.9 us (22%)
  Pallas kernels  13.3 us (16%)
  local copies, waits for them, and re-layouts  1.64 us (2%)
  other arithmetic  0.9 us (1%)
    ppermute x9, waiting for transfers between devices, across(): return lax.ppermute(a, 'seq', [(i, i ^ 2 * j) for i in range(2 * n)])  20.1 us
    pallas_call x11, Pallas kernels, call(): pl.pallas_call(kernel, out_shape=outs, grid_spec=pltpu.PrefetchScalarGrid...  13.3 us
    ppermute x3, waiting for transfers between devices, body(): lax.ppermute(msg, 'seq', [(i, (i + 2 * j) % (2 * n)) for i in range(2 * n)])  9.96 us
    ppermute x2, waiting for transfers between devices, along(): return lax.ppermute(a, 'head', [(i, i ^ m) for i in range(n)])  8.65 us
    ppermute x9, starting transfers between devices, across(): return lax.ppermute(a, 'seq', [(i, i ^ 2 * j) for i in range(2 * n)])  5.52 us
    ppermute x2, waiting for transfers between devices, over(): return lax.ppermute(a, BOTH, pairs)  5.44 us
    ppermute x3, starting transfers between devices, body(): lax.ppermute(msg, 'seq', [(i, (i + 2 * j) % (2 * n)) for i in range(2 * n)])  4.72 us
    ppermute x2, starting transfers between devices, over(): return lax.ppermute(a, BOTH, pairs)  4.3 us
  transfers between devices with their start and end apart: 22, of which 15 were waited for; matrix products, arithmetic and copies ran while one was open for 2% of the time, Pallas kernels for 11%

profile of v7, /device:TPU:0, one launch (start us, length us, event | category | flops | bytes accessed | tf_op | source)
XLA Modules:
  0.0 80.5 jit_solution(2771051459435293940)
XLA Ops:
  0.5 0.8 %convert_add_fusion.so = f32[320,128]{1,0:T(8,128)S(1)} fusion(f32[32,128]{1,0:T(8,128)} %param.14, f32[32,128]{1,0:T(8,128)} %param.13, bf16[128,128]{1,0:T(8,128)(2,1)} %param.12, bf16[128,128]{1,0:T(8,128)(2,1)} %param.11), kind=kLoop, calls=%fused_computation | loop fusion | flops 204800 | bytes 262144 | tf_op jit(solution)/shard_map/add | solution.py:342
  1.5 1.0 %constant_dynamic-slice_fusion.xo = bf16[128,1024]{1,0:T(8,128)(2,1)S(1)} fusion(bf16[128,2048]{1,0:T(8,128)(2,1)} %param.9, s32[]{:T(128)S(6)} %select_n.16), kind=kLoop, calls=%fused_computation.2 | loop fusion | bytes 524292 | tf_op jit(solution)/shard_map/dynamic_slice | solution.py:345
  2.7 1.3 %shard_map.92 = (bf16[1040,128]{1,0:T(8,128)(2,1)S(1)}, f32[128,1024]{1,0:T(8,128)S(1)}) custom-call(s32[3]{0:T(128)S(1)} %pad_add_fusion.s.refs_0_, bf16[128,1024]{1,0:T(8,128)(2,1)S(1)} %constant_dynamic-slice_fusion.xo, bf16[128,2048]{1,0:T(8,128)(2,1)S(1)} %collective-permute-done.xr, f32[320,128]{1,0:T(8,128)S(1)} %convert_add_fusion.so, ...), custom_call_target="tpu_custom_call" | custom-call | bytes 1904640 | tf_op jit(solution)/shard_map/pallas_call | solution.py:22
  4.7 3.6 %collective-permute-start.6 = (bf16[1040,128]{1,0:T(8,128)(2,1)S(1)}, bf16[1040,128]{1,0:T(8,128)(2,1)S(1)}, u32[]{:S(2)}, u32[]{:S(2)}) collective-permute-start(bf16[1040,128]{1,0:T(8,128)(2,1)S(1)} %get-tuple-element.26), channel_id=1, source_target_pairs={{0,24},{4,28},{8,0},{12,4},{16,8},{20,12},{24,16},{28,20},{1,25},{... | collective-permute-start | bytes 798728 | tf_op jit(solution)/shard_map/ppermute | solution.py:354
  9.4 0.7 copy-done.3
  10.1 2.3 %shard_map.91 = (f32[256,1024]{1,0:T(8,128)S(1)}, f32[256,1024]{1,0:T(8,128)S(1)}, f32[16,1024]{1,0:T(8,128)S(1)}) custom-call(s32[3]{0:T(128)S(1)} %pad_add_fusion.s.refs_0_, bf16[128,1024]{1,0:T(8,128)(2,1)S(1)} %constant_dynamic-slice_fusion.xo, bf16[128,2048]{1,0:T(8,128)(2,1)S(1)} %collective-permute-done.xr, f32[320,128]{1,0:T(8,128)S(1)} %convert_add_fusion.so, ...), custom_call_target="tpu_custom_call" | custom-call | bytes 4325504 | tf_op jit(solution)/shard_map/pallas_call | solution.py:22
  12.4 2.7 %collective-permute-done.6.rest_2_ = bf16[1040,128]{1,0:T(8,128)(2,1)S(1)} collective-permute-done((bf16[1040,128]{1,0:T(8,128)(2,1)S(1)}, bf16[1040,128]{1,0:T(8,128)(2,1)S(1)}, u32[]{:S(2)}, u32[]{:S(2)}) %collective-permute-start.6) | collective-permute-done | bytes 266272 | tf_op jit(solution)/shard_map/ppermute | solution.py:354
  15.1 7.3 %collective-permute-done.5.rest_1_ = bf16[1040,128]{1,0:T(8,128)(2,1)S(1)} collective-permute-done((bf16[1040,128]{1,0:T(8,128)(2,1)S(1)}, bf16[1040,128]{1,0:T(8,128)(2,1)S(1)}, u32[]{:S(2)}, u32[]{:S(2)}) %collective-permute-start.5) | collective-permute-done | bytes 266272 | tf_op jit(solution)/shard_map/ppermute | solution.py:354
  22.4 1.3 %shard_map.93 = (bf16[128,1024]{1,0:T(8,128)(2,1)S(1)}, bf16[128,1024]{1,0:T(8,128)(2,1)S(1)}, f32[8,128]{1,0:T(8,128)S(1)}, f32[8,128]{1,0:T(8,128)S(1)}) custom-call(s32[3]{0:T(128)S(1)} %pad_add_fusion.s.refs_0_, f32[256,1024]{1,0:T(8,128)S(1)} %get-tuple-element.22.inside, f32[256,1024]{1,0:T(8,128)S(1)} %get-tuple-element.23.decays, ...), custom_call_target="tpu_custom_call" | custom-call | bytes 6451200 | tf_op jit(solution)/shard_map/pallas_call | solution.py:22
  24.1 1.2 %collective-permute-done.8.refs_2_ = bf16[128,1024]{1,0:T(8,128)(2,1)S(1)} collective-permute-done((bf16[128,1024]{1,0:T(8,128)(2,1)S(1)}, bf16[128,1024]{1,0:T(8,128)(2,1)S(1)}, u32[]{:S(2)}, u32[]{:S(2)}) %collective-permute-start.8) | collective-permute-done | bytes 262176 | tf_op jit(solution)/shard_map/ppermute | solution.py:324
  25.7 1.5 %collective-permute-start.10 = (bf16[128,1024]{1,0:T(8,128)(2,1)S(1)}, bf16[128,1024]{1,0:T(8,128)(2,1)S(1)}, u32[]{:S(2)}, u32[]{:S(2)}) collective-permute-start(bf16[128,1024]{1,0:T(8,128)(2,1)S(1)} %get-tuple-element.28.refs_1_), channel_id=1, source_target_pairs={{0,16},{4,20},{8,24},{12,28},{16,0},{20,4},{24,8},{28,12},{1,17},{... | collective-permute-start | bytes 786440 | tf_op jit(solution)/shard_map/ppermute | solution.py:327
  27.8 1.3 %shard_map.94.refs_7_.refs_2_.refs_1_ = bf16[1024,128]{1,0:T(8,128)(2,1)S(1)} custom-call(s32[3]{0:T(128)S(1)} %pad_add_fusion.s.refs_0_, bf16[128,1024]{1,0:T(8,128)(2,1)S(1)} %get-tuple-element.28.refs_1_, bf16[128,1024]{1,0:T(8,128)(2,1)S(1)} %collective-permute-done.8.refs_2_, bf16[2048,512]{1,0:T(8,128)(2,1)S(1)} %copy-done, ...), custom_call_target="tpu_custom_call" | custom-call | bytes 4980736 | tf_op jit(solution)/shard_map/pallas_call | solution.py:22
  29.1 3.8 %collective-permute-done.7.refs_1_ = bf16[128,1024]{1,0:T(8,128)(2,1)S(1)} collective-permute-done((bf16[128,1024]{1,0:T(8,128)(2,1)S(1)}, bf16[128,1024]{1,0:T(8,128)(2,1)S(1)}, u32[]{:S(2)}, u32[]{:S(2)}) %collective-permute-start.7) | collective-permute-done | bytes 262176 | tf_op jit(solution)/shard_map/ppermute | solution.py:327
  32.8 1.6 %collective-permute-done.9.refs_4_ = bf16[128,1024]{1,0:T(8,128)(2,1)S(1)} collective-permute-done((bf16[128,1024]{1,0:T(8,128)(2,1)S(1)}, bf16[128,1024]{1,0:T(8,128)(2,1)S(1)}, u32[]{:S(2)}, u32[]{:S(2)}) %collective-permute-start.9) | collective-permute-done | bytes 262176 | tf_op jit(solution)/shard_map/ppermute | solution.py:327
  35.5 4.5 %collective-permute-done.10.refs_2_ = bf16[128,1024]{1,0:T(8,128)(2,1)S(1)} collective-permute-done((bf16[128,1024]{1,0:T(8,128)(2,1)S(1)}, bf16[128,1024]{1,0:T(8,128)(2,1)S(1)}, u32[]{:S(2)}, u32[]{:S(2)}) %collective-permute-start.10) | collective-permute-done | bytes 262176 | tf_op jit(solution)/shard_map/ppermute | solution.py:327
  40.0 1.8 %shard_map.95 = (bf16[1024,128]{1,0:T(8,128)(2,1)S(1)}, bf16[1024,128]{1,0:T(8,128)(2,1)S(1)}) custom-call(s32[3]{0:T(128)S(1)} %pad_add_fusion.s.refs_0_, bf16[128,1024]{1,0:T(8,128)(2,1)S(1)} %collective-permute-done.7.refs_1_, bf16[128,1024]{1,0:T(8,128)(2,1)S(1)} %collective-permute-done.10.refs_2_, ...), custom_call_target="tpu_custom_call" | custom-call | bytes 6029312 | tf_op jit(solution)/shard_map/pallas_call | solution.py:22
  43.0 2.7 %collective-permute-done.14.refs_1_ = bf16[128,1024]{1,0:T(8,128)(2,1)S(1)} collective-permute-done((bf16[128,1024]{1,0:T(8,128)(2,1)S(1)}, bf16[128,1024]{1,0:T(8,128)(2,1)S(1)}, u32[]{:S(2)}, u32[]{:S(2)}) %collective-permute-start.14) | collective-permute-done | bytes 262176 | tf_op jit(solution)/shard_map/ppermute | solution.py:327
  45.7 1.3 %shard_map.96 = bf16[1024,128]{1,0:T(8,128)(2,1)S(1)} custom-call(s32[3]{0:T(128)S(1)} %pad_add_fusion.s.refs_0_, bf16[128,1024]{1,0:T(8,128)(2,1)S(1)} %collective-permute-done.14.refs_1_, bf16[128,1024]{1,0:T(8,128)(2,1)S(1)} %collective-permute-done.15.refs_2_, bf16[2048,512]{1,0:T(8,128)(2,1)S(1)} %copy-done, ...), custom_call_target="tpu_custom_call" | custom-call | bytes 4980736 | tf_op jit(solution)/shard_map/pallas_call | solution.py:22
  47.3 1.2 %collective-permute-done.17 = f32[8,128]{1,0:T(8,128)S(1)} collective-permute-done((f32[8,128]{1,0:T(8,128)S(1)}, f32[8,128]{1,0:T(8,128)S(1)}, u32[]{:S(2)}, u32[]{:S(2)}) %collective-permute-start.17) | collective-permute-done | bytes 4128 | tf_op jit(solution)/shard_map/ppermute | solution.py:324
  48.5 2.0 %collective-permute-done.12.refs_1_.refs_2_ = bf16[1024,128]{1,0:T(8,128)(2,1)S(1)} collective-permute-done((bf16[1024,128]{1,0:T(8,128)(2,1)S(1)}, bf16[1024,128]{1,0:T(8,128)(2,1)S(1)}, u32[]{:S(2)}, u32[]{:S(2)}) %collective-permute-start.12) | collective-permute-done | bytes 262176 | tf_op jit(solution)/shard_map/ppermute | solution.py:327
  50.5 5.6 %collective-permute-done.13.refs_2_.refs_1_.refs_3_ = bf16[1024,128]{1,0:T(8,128)(2,1)S(1)} collective-permute-done((bf16[1024,128]{1,0:T(8,128)(2,1)S(1)}, bf16[1024,128]{1,0:T(8,128)(2,1)S(1)}, u32[]{:S(2)}, u32[]{:S(2)}) %collective-permute-start.13) | collective-permute-done | bytes 262176 | tf_op jit(solution)/shard_map/ppermute | solution.py:327
  56.1 0.6 shard_map.97
  56.7 1.6 %collective-permute-start.18 = (bf16[1040,128]{1,0:T(8,128)(2,1)S(1)}, bf16[1040,128]{1,0:T(8,128)(2,1)S(1)}, u32[]{:S(2)}, u32[]{:S(2)}) collective-permute-start(bf16[1040,128]{1,0:T(8,128)(2,1)S(1)} %shard_map.97), channel_id=1, source_target_pairs={{0,1},{1,0},{2,3},{3,2},{4,5},{5,4},{6,7},{7,6},{8,9},{9,8},{10,11... | collective-permute-start | bytes 798728 | tf_op jit(solution)/shard_map/ppermute | solution.py:330
  58.3 0.6 shard_map.98.refs_6_
  59.5 8.1 %collective-permute-done.18.refs_3_.refs_5_ = bf16[1040,128]{1,0:T(8,128)(2,1)S(1)} collective-permute-done((bf16[1040,128]{1,0:T(8,128)(2,1)S(1)}, bf16[1040,128]{1,0:T(8,128)(2,1)S(1)}, u32[]{:S(2)}, u32[]{:S(2)}) %collective-permute-start.18) | collective-permute-done | bytes 266272 | tf_op jit(solution)/shard_map/ppermute | solution.py:330
  67.6 0.6 shard_map.99
  68.2 1.8 %collective-permute-start.20 = (bf16[1040,128]{1,0:T(8,128)(2,1)S(1)}, bf16[1040,128]{1,0:T(8,128)(2,1)S(1)}, u32[]{:S(2)}, u32[]{:S(2)}) collective-permute-start(bf16[1040,128]{1,0:T(8,128)(2,1)S(1)} %shard_map.99), channel_id=1, source_target_pairs={{0,2},{1,0},{2,3},{3,1},{4,6},{5,4},{6,7},{7,5},{8,9},{9,11},{10,8... | collective-permute-start | bytes 798728 | tf_op jit(solution)/shard_map/ppermute | solution.py:415
  70.5 0.7 shard_map.100
  71.2 2.5 %collective-permute-start.21 = (bf16[1040,128]{1,0:T(8,128)(2,1)S(1)}, bf16[1040,128]{1,0:T(8,128)(2,1)S(1)}, u32[]{:S(2)}, u32[]{:S(2)}) collective-permute-start(bf16[1040,128]{1,0:T(8,128)(2,1)S(1)} %shard_map.100), channel_id=1, source_target_pairs={{0,1},{1,3},{2,0},{3,2},{4,5},{5,7},{6,4},{7,6},{8,10},{9,8},{10,1... | collective-permute-start | bytes 798728 | tf_op jit(solution)/shard_map/ppermute | solution.py:415
  73.7 1.0 %collective-permute-done.20.refs_7_ = bf16[1040,128]{1,0:T(8,128)(2,1)S(1)} collective-permute-done((bf16[1040,128]{1,0:T(8,128)(2,1)S(1)}, bf16[1040,128]{1,0:T(8,128)(2,1)S(1)}, u32[]{:S(2)}, u32[]{:S(2)}) %collective-permute-start.20) | collective-permute-done | bytes 266272 | tf_op jit(solution)/shard_map/ppermute | solution.py:415
  74.7 4.4 %collective-permute-done.21.refs_8_ = bf16[1040,128]{1,0:T(8,128)(2,1)S(1)} collective-permute-done((bf16[1040,128]{1,0:T(8,128)(2,1)S(1)}, bf16[1040,128]{1,0:T(8,128)(2,1)S(1)}, u32[]{:S(2)}, u32[]{:S(2)}) %collective-permute-start.21) | collective-permute-done | bytes 266272 | tf_op jit(solution)/shard_map/ppermute | solution.py:415
  79.1 1.4 %shard_map.101 = bf16[128,1024]{1,0:T(8,128)(2,1)} custom-call(s32[3]{0:T(128)S(1)} %pad_add_fusion.s.refs_0_, bf16[1024,128]{1,0:T(8,128)(2,1)S(1)} %shard_map.94.refs_7_.refs_2_.refs_1_, bf16[1024,128]{1,0:T(8,128)(2,1)S(1)} %collective-permute-done.12.refs_1_.refs_2_, bf16[1024,128]{1,0:T(8,128)(2,1)S(1)} %collective-permute-done.13.refs_2_.refs_1_.refs_3_, ...), custom_call_target="tpu_custom_call" | custom-call | bytes 2375680 | tf_op jit(solution)/shard_map/pallas_call | solution.py:22
  (35 shorter events, 7.7 us)
Async XLA Ops:
  0.0 9.4 %copy-start.1 = (bf16[128,2048]{1,0:T(8,128)(2,1)S(1)}, bf16[128,2048]{1,0:T(8,128)(2,1)}, u32[]{:S(2)}) copy-start(bf16[128,2048]{1,0:T(8,128)(2,1)} %zo.1) | copy-start | bytes 1572868
  0.0 22.4 %copy-start.2 = (f32[2048]{0:T(1024)S(1)}, f32[2048]{0:T(1024)}, u32[]{:S(2)}) copy-start(f32[2048]{0:T(1024)} %param.16) | copy-start | bytes 24580
  0.0 2.7 %collective-permute-start = (bf16[128,2048]{1,0:T(8,128)(2,1)}, bf16[128,2048]{1,0:T(8,128)(2,1)S(1)}, u32[]{:S(2)}, u32[]{:S(2)}) collective-permute-start(bf16[128,2048]{1,0:T(8,128)(2,1)} %param.9), channel_id=1, source_target_pairs={{0,4},{4,0},{8,12},{12,8},{16,20},{20,16},{24,28},{28,24},{1,5},{5... | collective-permute-start | bytes 1572872 | tf_op jit(solution)/shard_map/ppermute | solution.py:324
  1.3 1.5 %collective-permute-start.1 = (f32[320,128]{1,0:T(8,128)S(1)}, f32[320,128]{1,0:T(8,128)S(1)}, u32[]{:S(2)}, u32[]{:S(2)}) collective-permute-start(f32[320,128]{1,0:T(8,128)S(1)} %convert_add_fusion.so), channel_id=1, source_target_pairs={{0,4},{4,0},{8,12},{12,8},{16,20},{20,16},{24,28},{28,24},{1,5},{5... | collective-permute-start | bytes 491528 | tf_op jit(solution)/shard_map/ppermute | solution.py:324
  4.1 18.3 %collective-permute-start.3 = (bf16[2048,512]{1,0:T(8,128)(2,1)}, bf16[2048,512]{1,0:T(8,128)(2,1)S(1)}, u32[]{:S(2)}, u32[]{:S(2)}) collective-permute-start(bf16[2048,512]{1,0:T(8,128)(2,1)} %refs_3_.3), channel_id=1, source_target_pairs={{0,4},{4,0},{8,12},{12,8},{16,20},{20,16},{24,28},{28,24},{1,5},{5... | collective-permute-start | bytes 6291464 | tf_op jit(solution)/shard_map/ppermute | solution.py:324
  4.3 5.1 %collective-permute-start.2 = (bf16[128,2048]{1,0:T(8,128)(2,1)}, bf16[128,2048]{1,0:T(8,128)(2,1)S(1)}, u32[]{:S(2)}, u32[]{:S(2)}) collective-permute-start(bf16[128,2048]{1,0:T(8,128)(2,1)} %zo.1), channel_id=1, source_target_pairs={{0,4},{4,0},{8,12},{12,8},{16,20},{20,16},{24,28},{28,24},{1,5},{5... | collective-permute-start | bytes 1572872 | tf_op jit(solution)/shard_map/ppermute | solution.py:324
  4.7 10.4 %collective-permute-start.6 = (bf16[1040,128]{1,0:T(8,128)(2,1)S(1)}, bf16[1040,128]{1,0:T(8,128)(2,1)S(1)}, u32[]{:S(2)}, u32[]{:S(2)}) collective-permute-start(bf16[1040,128]{1,0:T(8,128)(2,1)S(1)} %get-tuple-element.26), channel_id=1, source_target_pairs={{0,24},{4,28},{8,0},{12,4},{16,8},{20,12},{24,16},{28,20},{1,25},{... | collective-permute-start | bytes 798728 | tf_op jit(solution)/shard_map/ppermute | solution.py:354
  8.3 14.0 %collective-permute-start.5 = (bf16[1040,128]{1,0:T(8,128)(2,1)S(1)}, bf16[1040,128]{1,0:T(8,128)(2,1)S(1)}, u32[]{:S(2)}, u32[]{:S(2)}) collective-permute-start(bf16[1040,128]{1,0:T(8,128)(2,1)S(1)} %get-tuple-element.26), channel_id=1, source_target_pairs={{0,16},{4,20},{8,24},{12,28},{16,0},{20,4},{24,8},{28,12},{1,17},{... | collective-permute-start | bytes 798728 | tf_op jit(solution)/shard_map/ppermute | solution.py:354
  8.8 13.5 %collective-permute-start.4 = (bf16[1040,128]{1,0:T(8,128)(2,1)S(1)}, bf16[1040,128]{1,0:T(8,128)(2,1)S(1)}, u32[]{:S(2)}, u32[]{:S(2)}) collective-permute-start(bf16[1040,128]{1,0:T(8,128)(2,1)S(1)} %get-tuple-element.26), channel_id=1, source_target_pairs={{0,8},{4,12},{8,16},{12,20},{16,24},{20,28},{24,0},{28,4},{1,9},{5... | collective-permute-start | bytes 798728 | tf_op jit(solution)/shard_map/ppermute | solution.py:354
  9.4 0.7 copy-start.3
  22.4 5.4 %copy-start = (bf16[2048,512]{1,0:T(8,128)(2,1)S(1)}, bf16[2048,512]{1,0:T(8,128)(2,1)}, u32[]{:S(2)}) copy-start(bf16[2048,512]{1,0:T(8,128)(2,1)} %refs_3_.3) | copy-start | bytes 6291460
  23.7 1.6 %collective-permute-start.8 = (bf16[128,1024]{1,0:T(8,128)(2,1)S(1)}, bf16[128,1024]{1,0:T(8,128)(2,1)S(1)}, u32[]{:S(2)}, u32[]{:S(2)}) collective-permute-start(bf16[128,1024]{1,0:T(8,128)(2,1)S(1)} %get-tuple-element.29), channel_id=1, source_target_pairs={{0,4},{4,0},{8,12},{12,8},{16,20},{20,16},{24,28},{28,24},{1,5},{5... | collective-permute-start | bytes 786440 | tf_op jit(solution)/shard_map/ppermute | solution.py:324
  23.7 9.2 %collective-permute-start.7 = (bf16[128,1024]{1,0:T(8,128)(2,1)S(1)}, bf16[128,1024]{1,0:T(8,128)(2,1)S(1)}, u32[]{:S(2)}, u32[]{:S(2)}) collective-permute-start(bf16[128,1024]{1,0:T(8,128)(2,1)S(1)} %get-tuple-element.28.refs_1_), channel_id=1, source_target_pairs={{0,8},{4,12},{8,0},{12,4},{16,24},{20,28},{24,16},{28,20},{1,9},{5... | collective-permute-start | bytes 786440 | tf_op jit(solution)/shard_map/ppermute | solution.py:327
  25.2 9.2 %collective-permute-start.9 = (bf16[128,1024]{1,0:T(8,128)(2,1)S(1)}, bf16[128,1024]{1,0:T(8,128)(2,1)S(1)}, u32[]{:S(2)}, u32[]{:S(2)}) collective-permute-start(bf16[128,1024]{1,0:T(8,128)(2,1)S(1)} %collective-permute-done.8.refs_2_), channel_id=1, source_target_pairs={{0,16},{4,20},{8,24},{12,28},{16,0},{20,4},{24,8},{28,12},{1,17},{... | collective-permute-start | bytes 786440 | tf_op jit(solution)/shard_map/ppermute | solution.py:327
  25.7 14.3 %collective-permute-start.10 = (bf16[128,1024]{1,0:T(8,128)(2,1)S(1)}, bf16[128,1024]{1,0:T(8,128)(2,1)S(1)}, u32[]{:S(2)}, u32[]{:S(2)}) collective-permute-start(bf16[128,1024]{1,0:T(8,128)(2,1)S(1)} %get-tuple-element.28.refs_1_), channel_id=1, source_target_pairs={{0,16},{4,20},{8,24},{12,28},{16,0},{20,4},{24,8},{28,12},{1,17},{... | collective-permute-start | bytes 786440 | tf_op jit(solution)/shard_map/ppermute | solution.py:327
  27.3 12.8 %collective-permute-start.11 = (bf16[128,1024]{1,0:T(8,128)(2,1)S(1)}, bf16[128,1024]{1,0:T(8,128)(2,1)S(1)}, u32[]{:S(2)}, u32[]{:S(2)}) collective-permute-start(bf16[128,1024]{1,0:T(8,128)(2,1)S(1)} %collective-permute-done.8.refs_2_), channel_id=1, source_target_pairs={{0,8},{4,12},{8,0},{12,4},{16,24},{20,28},{24,16},{28,20},{1,9},{5... | collective-permute-start | bytes 786440 | tf_op jit(solution)/shard_map/ppermute | solution.py:327
  34.4 11.2 %collective-permute-start.14 = (bf16[128,1024]{1,0:T(8,128)(2,1)S(1)}, bf16[128,1024]{1,0:T(8,128)(2,1)S(1)}, u32[]{:S(2)}, u32[]{:S(2)}) collective-permute-start(bf16[128,1024]{1,0:T(8,128)(2,1)S(1)} %collective-permute-done.7.refs_1_), channel_id=1, source_target_pairs={{0,16},{4,20},{8,24},{12,28},{16,0},{20,4},{24,8},{28,12},{1,17},{... | collective-permute-start | bytes 786440 | tf_op jit(solution)/shard_map/ppermute | solution.py:327
  34.9 10.8 %collective-permute-start.15 = (bf16[128,1024]{1,0:T(8,128)(2,1)S(1)}, bf16[128,1024]{1,0:T(8,128)(2,1)S(1)}, u32[]{:S(2)}, u32[]{:S(2)}) collective-permute-start(bf16[128,1024]{1,0:T(8,128)(2,1)S(1)} %collective-permute-done.9.refs_4_), channel_id=1, source_target_pairs={{0,8},{4,12},{8,0},{12,4},{16,24},{20,28},{24,16},{28,20},{1,9},{5... | collective-permute-start | bytes 786440 | tf_op jit(solution)/shard_map/ppermute | solution.py:327
  41.9 8.6 %collective-permute-start.12 = (bf16[1024,128]{1,0:T(8,128)(2,1)S(1)}, bf16[1024,128]{1,0:T(8,128)(2,1)S(1)}, u32[]{:S(2)}, u32[]{:S(2)}) collective-permute-start(bf16[1024,128]{1,0:T(8,128)(2,1)S(1)} %get-tuple-element.33), channel_id=1, source_target_pairs={{0,8},{4,12},{8,0},{12,4},{16,24},{20,28},{24,16},{28,20},{1,9},{5... | collective-permute-start | bytes 786440 | tf_op jit(solution)/shard_map/ppermute | solution.py:327
  42.4 13.6 %collective-permute-start.13 = (bf16[1024,128]{1,0:T(8,128)(2,1)S(1)}, bf16[1024,128]{1,0:T(8,128)(2,1)S(1)}, u32[]{:S(2)}, u32[]{:S(2)}) collective-permute-start(bf16[1024,128]{1,0:T(8,128)(2,1)S(1)} %get-tuple-element.34), channel_id=1, source_target_pairs={{0,16},{4,20},{8,24},{12,28},{16,0},{20,4},{24,8},{28,12},{1,17},{... | collective-permute-start | bytes 786440 | tf_op jit(solution)/shard_map/ppermute | solution.py:327
  46.9 11.4 %collective-permute-start.16 = (bf16[1024,128]{1,0:T(8,128)(2,1)S(1)}, bf16[1024,128]{1,0:T(8,128)(2,1)S(1)}, u32[]{:S(2)}, u32[]{:S(2)}) collective-permute-start(bf16[1024,128]{1,0:T(8,128)(2,1)S(1)} %shard_map.96), channel_id=1, source_target_pairs={{0,24},{4,28},{8,16},{12,20},{16,8},{20,12},{24,0},{28,4},{1,25},{... | collective-permute-start | bytes 786440 | tf_op jit(solution)/shard_map/ppermute | solution.py:327
  47.3 1.2 %collective-permute-start.17 = (f32[8,128]{1,0:T(8,128)S(1)}, f32[8,128]{1,0:T(8,128)S(1)}, u32[]{:S(2)}, u32[]{:S(2)}) collective-permute-start(f32[8,128]{1,0:T(8,128)S(1)} %get-tuple-element.38), channel_id=1, source_target_pairs={{0,4},{4,0},{8,12},{12,8},{16,20},{20,16},{24,28},{28,24},{1,5},{5... | collective-permute-start | bytes 12296 | tf_op jit(solution)/shard_map/ppermute | solution.py:324
  56.7 10.9 %collective-permute-start.18 = (bf16[1040,128]{1,0:T(8,128)(2,1)S(1)}, bf16[1040,128]{1,0:T(8,128)(2,1)S(1)}, u32[]{:S(2)}, u32[]{:S(2)}) collective-permute-start(bf16[1040,128]{1,0:T(8,128)(2,1)S(1)} %shard_map.97), channel_id=1, source_target_pairs={{0,1},{1,0},{2,3},{3,2},{4,5},{5,4},{6,7},{7,6},{8,9},{9,8},{10,11... | collective-permute-start | bytes 798728 | tf_op jit(solution)/shard_map/ppermute | solution.py:330
  58.9 11.6 %collective-permute-start.19 = (bf16[1024,128]{1,0:T(8,128)(2,1)S(1)}, bf16[1024,128]{1,0:T(8,128)(2,1)S(1)}, u32[]{:S(2)}, u32[]{:S(2)}) collective-permute-start(bf16[1024,128]{1,0:T(8,128)(2,1)S(1)} %shard_map.98.refs_6_), channel_id=1, source_target_pairs={{0,1},{1,0},{2,3},{3,2},{4,5},{5,4},{6,7},{7,6},{8,9},{9,8},{10,11... | collective-permute-start | bytes 786440 | tf_op jit(solution)/shard_map/ppermute | solution.py:330
  68.2 6.5 %collective-permute-start.20 = (bf16[1040,128]{1,0:T(8,128)(2,1)S(1)}, bf16[1040,128]{1,0:T(8,128)(2,1)S(1)}, u32[]{:S(2)}, u32[]{:S(2)}) collective-permute-start(bf16[1040,128]{1,0:T(8,128)(2,1)S(1)} %shard_map.99), channel_id=1, source_target_pairs={{0,2},{1,0},{2,3},{3,1},{4,6},{5,4},{6,7},{7,5},{8,9},{9,11},{10,8... | collective-permute-start | bytes 798728 | tf_op jit(solution)/shard_map/ppermute | solution.py:415
  71.2 8.0 %collective-permute-start.21 = (bf16[1040,128]{1,0:T(8,128)(2,1)S(1)}, bf16[1040,128]{1,0:T(8,128)(2,1)S(1)}, u32[]{:S(2)}, u32[]{:S(2)}) collective-permute-start(bf16[1040,128]{1,0:T(8,128)(2,1)S(1)} %shard_map.100), channel_id=1, source_target_pairs={{0,1},{1,3},{2,0},{3,2},{4,5},{5,7},{6,4},{7,6},{8,10},{9,8},{10,1... | collective-permute-start | bytes 798728 | tf_op jit(solution)/shard_map/ppermute | solution.py:415

commit v8 on v7

--- a/solution.py
+++ b/solution.py
@@ -5,7 +5,6 @@
 from jax.experimental.pallas import tpu as pltpu
 from jax.sharding import PartitionSpec as P
 
-BOTH = ("seq", "head")
 HIGH = lax.Precision.HIGHEST
 f32, bf16 = jnp.float32, jnp.bfloat16
 EXT = 16
@@ -97,7 +96,7 @@
     return (j <= i), (i <= j)
 
 
-def state_kernel(s, xo, xr, so, sr, msg, first):
+def state_kernel(s, xo, xr, so, sr, first, *messages):
     k = s[0]
     rows, wide = xo.shape
     half = pl.ds(pl.multiple_of(k * wide, wide), wide)
@@ -117,16 +116,39 @@
     st_other = tn(other[2], (xr[:, half].astype(f32) * wide_tails[rows:]).astype(bf16))
     s1, s2 = jnp.where(even, st_own, st_other), jnp.where(even, st_other, st_own)
     d2 = jnp.where(even, dr, do)
-    n = s1.shape[0]
-    flat(msg, (d2[:1] * s1 + s2).astype(bf16))
-    msg[wide * n // LANES :] = pair(jnp.concatenate([(do * dr)[:1, i : i + LANES] for i in range(0, wide, LANES)], 0))
+    write_state(messages, d2[:1] * s1 + s2, (do * dr)[:1])
     first[...] = s1
+
+
+def write_state(messages, state, decay):
+    n, wide = state.shape
+    part = wide // len(messages)
+    for i, msg in enumerate(messages):
+        at = slice(i * part, (i + 1) * part)
+        flat(msg, state[:, at].astype(bf16))
+        msg[part * n // LANES :] = pair(rows_of(decay[:, at]))
+
+
+def rows_of(v):
+    return jnp.concatenate([v[:, i : i + LANES] for i in range(0, v.shape[1], LANES)], 0)
+
+
+def group_kernel(s, own, other, out, *, bit, n, wide):
+    later = (s[2] >> bit) & 1 == 1
+    so, do = unpack(own, n, wide)
+    st, dt = unpack(other, n, wide)
+    s1, s2 = jnp.where(later, st, so), jnp.where(later, so, st)
+    write_state([out], jnp.where(later, do, dt) * s1 + s2, do * dt)
 
 
 def flat(ref, value):
     rows = value.shape[0]
     for i in range(value.shape[1] // LANES):
         ref[i * rows : (i + 1) * rows] = value[:, i * LANES : (i + 1) * LANES]
+
+
+def rows_of(v):
+    return jnp.concatenate([v[:, i : i + LANES] for i in range(0, v.shape[1], LANES)], 0)
 
 
 def pair(v):
@@ -193,12 +215,18 @@
     k = s[0]
     rows, wide = mine.shape
     even = k == 0
-    enter, through = None, None
-    for j, ref in enumerate(states):
-        st, dec = unpack(ref, first.shape[0], wide)
-        st = jnp.where(s[2] > j, st, 0.0)
-        enter = st if enter is None else enter + st * through
-        through = dec if through is None else through * dec
+    count = len(states) // 2
+    enters = []
+    for half in (states[:count], states[count:]):
+        enter, through = None, None
+        for bit, ref in enumerate(half):
+            st, dec = unpack(ref, first.shape[0], wide // 2)
+            earlier = (s[2] >> bit) & 1 == 1
+            st, dec = jnp.where(earlier, st, 0.0), jnp.where(earlier, dec, 1.0)
+            enter = st if enter is None else enter + st * through
+            through = dec if through is None else through * dec
+        enters.append(enter)
+    enter = jnp.concatenate(enters, 1)
     second = jnp.where(even, whole[7:8], whole[15:16]) * enter + first[...]
     ones = jnp.ones((8, LANES), bf16)
     for turn, (small, out, sq) in enumerate(((so, mine, sq_mine), (sr, theirs, sq_theirs))):
@@ -239,32 +267,20 @@
             do(block)
 
 
-def choose_kernel(s, *refs, steps):
-    blocks, squares, outs = refs[:-1 - len(steps)], refs[-1 - len(steps)], refs[-len(steps) :]
-    n = blocks[0].shape[0]
-    for m, out in zip(steps, outs):
+def choose_kernel(s, *refs):
+    n = len(refs) // 2
+    for m, out in enumerate(refs[n:]):
 
         def copy(block, out=out):
-            out[:n] = block[...]
-
-        pick(s, m, blocks, copy)
-        out[n:] = pair(squares[...])
-
-
-def give_kernel(s, even, odd, *refs):
-    out = refs[-1]
+            out[...] = block[...]
+
+        pick(s, m, refs[:n], copy)
+
+
+def give_kernel(s, even, odd, squares, out):
     n = even.shape[0]
     out[:n] = jnp.where((s[1] & 1) == 0, even[...], odd[...])
-    if out.shape[0] > n:
-        out[n:] = pair(refs[0][...])
-
-
-def join_kernel(s, even, odd, got, squares, ext, *rest):
-    out = rest[-1]
-    n = even.shape[0]
-    kept = jnp.where((s[1] & 1) == 0, even[...], odd[...])
-    out[:n] = (kept.astype(f32) + got[:n].astype(f32)).astype(bf16)
-    out[n:] = pair(squares[...] + unpair(ext[n:]))
+    out[n:] = pair(squares[...])
 
 
 def row_scale(total, inner, rows):
@@ -275,38 +291,13 @@
 
 
 def sum_kernel(s, *refs, inner):
-    count = len(refs) // 2 - 1
-    blocks, squares, got, out = refs[: count + 1], refs[count + 1], refs[count + 2 : -1], refs[-1]
+    *blocks, squares, out = refs
     rows = out.shape[0]
-    n = blocks[0].shape[0]
-    col = row_scale(squares[...] + sum(unpair(a[n:]) for a in got), inner, rows)
-
-    def finish(block):
-        for g in range(n // rows):
-            at = slice(g * rows, (g + 1) * rows)
-            v = block[at].astype(f32) + sum(a[at].astype(f32) for a in got)
-            out[:, g * LANES : (g + 1) * LANES] = (v * col).astype(bf16)
-
-    pick(s, 0, blocks, finish)
-
-
-def last_kernel(s, own, x, y, far, got1, got2, sum1, sum2, squares, out, *, inner):
-    rows = out.shape[0]
-    n = own.shape[0]
-    base = squares[...] + unpair(got1[n:])
-
-    def finish(block, got, other):
-        col = row_scale(base + unpair(other[n:]), inner, rows)
-        for g in range(n // rows):
-            at = slice(g * rows, (g + 1) * rows)
-            v = block[at].astype(f32) + got[at].astype(f32) + other[at].astype(f32)
-            out[:, g * LANES : (g + 1) * LANES] = (v * col).astype(bf16)
-
-    for turn, args in enumerate(((own, got2, sum2), (x, got1, sum1), (y, got1, sum1), (far, got2, sum2))):
-
-        @pl.when(s[1] == turn)
-        def _():
-            finish(*args)
+    col = row_scale(squares[...], inner, rows)
+    for g in range(out.shape[1] // LANES):
+        at = slice(g * rows, (g + 1) * rows)
+        total = sum(a[at].astype(f32) for a in blocks)
+        out[:, g * LANES : (g + 1) * LANES] = (total * col).astype(bf16)
 
 
 def body(n, n_head, signal, gate_input, state_in, state_out, step_size, log_decay, skip_gain, norm_gain, out_weight):
@@ -347,17 +338,26 @@
     gain = norm_gain.reshape(1, 2 * wide)
 
     ins = (x1, x2, small1, small2)
-    outs = [shape((states * wide // LANES + EXT, LANES), bf16), shape((states, wide), f32)]
-    msg, first = call(state_kernel, s, ins, [full(a) for a in ins], outs, [full(a) for a in outs])
-    w2 = swap(lax.optimization_barrier((out_weight, msg))[0])
-    got = [
-        lax.ppermute(msg, "seq", [(i, (i + 2 * j) % (2 * n)) for i in range(2 * n)]) for j in range(n - 1, 0, -1)
-    ][::-1]
+    msg_shape = shape((states * wide // 2 // LANES + EXT, LANES), bf16)
+    outs = [shape((states, wide), f32), msg_shape, msg_shape]
+    first, *msgs = call(state_kernel, s, ins, [full(a) for a in ins], outs, [full(a) for a in outs])
+    w2 = swap(lax.optimization_barrier((out_weight, msgs[0]))[0])
+    got = [[across(msg, 1)] for msg in msgs]
     ins = (x1, x2, small1, small2, gate_input, z2, skip)
     big, ends = shape((2 * rows, wide), f32), shape((16, wide), f32)
     inside, decays, whole = call(
         inside_kernel, s, ins, [full(a) for a in ins], [big, big, ends], [full(big)] * 3
     )
+    for bit in range(1, n.bit_length() - 1):
+
+        def group(*refs, bit=bit - 1):
+            group_kernel(*refs[:3], refs[-1], bit=bit, n=states, wide=wide // 2)
+
+        for i, msg in enumerate(msgs):
+            ins = (msg, got[i][-1])
+            (msgs[i],) = call(group, s, ins, [full(a) for a in ins[:2]] + [any_spec] * len(ins[2:]), [msg_shape], [full(msg_shape)])
+            got[i].append(across(msgs[i], 1 << bit))
+    got = got[0] + got[1]
     ins = (inside, decays, whole, first, small1, small2, gain, w2, *got)
     specs = [full(a) for a in ins[:7]] + [any_spec] + [full(a) for a in got]
     outs = [shape((rows, wide), bf16)] * 2 + [shape((8, rows), f32)] * 2
@@ -392,42 +392,44 @@
         for j in range(1, n):
             (p,) = project([across(u, j)], [across(v, j)])
             blocks.append(across(p, j))
-    message = shape((size + EXT, LANES), bf16)
-
-    def send(kernel, ins, outs, **kw):
-        def run(*refs):
-            kernel(*refs, **kw)
-
-        return call(run, s, ins, [full(a) for a in ins], outs, [full(a) for a in outs])
-
-    inner = 2 * wide * n_head
-    out = [shape((rows, 2 * cols), bf16)]
+    def attach(block, squares):
+        hi = lax.reduce_precision(squares, 8, 7)
+        return jnp.concatenate([block, hi.astype(bf16), (squares - hi).astype(bf16)], 0)
+
+    def cut(message):
+        more = message[size:].astype(f32)
+        return message[:size], more[:8] + more[8:]
+
     if n == 4:
-
-        def over(a, ring):
-            after = dict(zip(ring, ring[1:] + ring[:1]))
-            pairs = []
-            for c in range(n):
-                for core in range(2):
-                    for h in range(n):
-                        place = (2 * c + core) * n
-                        pairs.append((place + h, place + (c ^ after[c ^ h])))
-            return lax.ppermute(a, BOTH, pairs)
-
-        (got1,) = send(give_kernel, (px, py, squares), [message])
-        got1 = along(got1, 1)
-        (got2,) = send(give_kernel, (far, own), [p_shape])
-        (sum1,) = send(join_kernel, (py, px, got1, squares, got1, got2), [message])
-        sum1 = over(sum1, (0, 2, 3, 1))
-        got2 = along(got2, 1)
-        (sum2,) = send(join_kernel, (own, far, got2, squares, got1), [message])
-        sum2 = over(sum2, (2, 0, 1, 3))
-        ins = (own, px, py, far, got1, got2, sum1, sum2, squares)
-        return send(last_kernel, ins, out, inner=inner)[0]
-    steps = range(1, n)
-    got = send(choose_kernel, (*blocks, squares), [message] * (n - 1), steps=steps)
-    got = [along(a, m) for a, m in zip(got, steps)]
-    return send(sum_kernel, (*blocks, squares, *got), out, inner=inner)[0]
+        r = chip ^ z
+        even = r % 2 == 0
+        message = shape((size + EXT, LANES), bf16)
+        ins = (px, py, squares)
+        (give,) = call(give_kernel, s, ins, [full(a) for a in ins], [message], [full(message)])
+        got1, more = cut(along(give, 1))
+        got2 = along(jnp.where(even, far, own), 1)
+        squares = squares + more
+        kept1, kept2 = jnp.where(even, py, px), jnp.where(even, own, far)
+        first = kept1.astype(f32) + got1.astype(f32)
+        second = kept2.astype(f32) + got2.astype(f32)
+        outer = (r == 0) | (r == 3)
+        other, more = cut(along(attach(jnp.where(outer, first, second).astype(bf16), squares), 2))
+        squares = squares + more
+        blocks = (other, jnp.where(outer, kept2, kept1), jnp.where(outer, got2, got1))
+    else:
+        blocks = call(
+            choose_kernel, s, blocks, [full(p_shape)] * n, [p_shape] * n, [full(p_shape)] * n
+        )
+        blocks = [blocks[0]] + [along(blocks[m], m) for m in range(1, n)]
+        for bit in range(n.bit_length() - 1):
+            squares = squares + along(squares, 1 << bit)
+
+    def add(*refs):
+        sum_kernel(*refs, inner=2 * wide * n_head)
+
+    ins = (*blocks, squares)
+    out = shape((rows, 2 * cols), bf16)
+    return call(add, s, ins, [full(a) for a in ins], [out], [full(out)])[0]
 
 
 def solution(mesh):

time: 80.7 us -> 79.1 us (0.980)
  waiting for transfers between devices: 46.7 us -> 37.1 us
  starting transfers between devices: 17.9 us -> 27 us
    ppermute x9 -> x13, starting transfers between devices: 5.52 us -> 20.9 us  [across(): return lax.ppermute(a, 'seq', [(i, i ^ 2 * j) for i in range(2 * n)])]
    ppermute x5 -> x0, waiting for transfers between devices: 15.4 us -> none  [the longest x3 9.96 us: body(): lax.ppermute(msg, 'seq', [(i, (i + 2 * j) % (2 * n)) for i in range(2 * n)])]
    ppermute x5 -> x0, starting transfers between devices: 9.02 us -> none  [the longest x3 4.72 us: body(): lax.ppermute(msg, 'seq', [(i, (i + 2 * j) % (2 * n)) for i in range(2 * n)])]
    ppermute x2 -> x3, waiting for transfers between devices: 8.65 us -> 17.2 us  [along(): return lax.ppermute(a, 'head', [(i, i ^ m) for i in range(n)])]
    ppermute x2 -> x3, starting transfers between devices: 2.16 us -> 4.82 us  [along(): return lax.ppermute(a, 'head', [(i, i ^ m) for i in range(n)])]
    ppermute x9 -> x13, waiting for transfers between devices: 20.1 us -> 18.5 us  [across(): return lax.ppermute(a, 'seq', [(i, i ^ 2 * j) for i in range(2 * n)])]
    ppermute x6, waiting for transfers between devices: 2.61 us -> 1.41 us  [swap(): return lax.ppermute(a, 'seq', [(i, i ^ 1) for i in range(2 * n)])]
    pallas_call x11 -> x10, Pallas kernels: 13.3 us -> 12.5 us  [call(): pl.pallas_call(kernel, out_shape=outs, grid_spec=pltpu.PrefetchScalarGrid...]
  transfers between devices with their start and end apart: 22 -> 22, of which waited for: 15 -> 12; matrix products, arithmetic and copies ran while one was open for 2% -> 3% of each run, Pallas kernels for 11% -> 11%
where the time goes in v8:
time: 79.1 us; the launch traced here: 79 us
  waiting for transfers between devices  37.1 us (47%)
  starting transfers between devices  27 us (34%)
  Pallas kernels  12.5 us (16%)
  other arithmetic  1.25 us (2%)
  local copies, waits for them, and re-layouts  1 us (1%)
    ppermute x13, starting transfers between devices, across(): return lax.ppermute(a, 'seq', [(i, i ^ 2 * j) for i in range(2 * n)])  20.9 us
    ppermute x13, waiting for transfers between devices, across(): return lax.ppermute(a, 'seq', [(i, i ^ 2 * j) for i in range(2 * n)])  18.5 us
    ppermute x3, waiting for transfers between devices, along(): return lax.ppermute(a, 'head', [(i, i ^ m) for i in range(n)])  17.2 us
    pallas_call x10, Pallas kernels, call(): pl.pallas_call(kernel, out_shape=outs, grid_spec=pltpu.PrefetchScalarGrid...  12.5 us
    ppermute x3, starting transfers between devices, along(): return lax.ppermute(a, 'head', [(i, i ^ m) for i in range(n)])  4.82 us
  transfers between devices with their start and end apart: 22, of which 12 were waited for; matrix products, arithmetic and copies ran while one was open for 3% of the time, Pallas kernels for 11%

profile of v8, /device:TPU:0, one launch (start us, length us, event | category | flops | bytes accessed | tf_op | source)
XLA Modules:
  0.0 79.0 jit_solution(15531283738141444225)
XLA Ops:
  0.5 0.8 %convert_add_fusion.so = f32[320,128]{1,0:T(8,128)S(1)} fusion(f32[32,128]{1,0:T(8,128)} %param.14, f32[32,128]{1,0:T(8,128)} %param.13, bf16[128,128]{1,0:T(8,128)(2,1)} %param.12, bf16[128,128]{1,0:T(8,128)(2,1)} %param.11), kind=kLoop, calls=%fused_computation.7 | loop fusion | flops 204800 | bytes 262144 | tf_op jit(solution)/shard_map/add | solution.py:333
  1.5 1.0 %constant_dynamic-slice_fusion.xo = bf16[128,1024]{1,0:T(8,128)(2,1)S(1)} fusion(bf16[128,2048]{1,0:T(8,128)(2,1)} %param.9, s32[]{:T(128)S(6)} %select_n.55), kind=kLoop, calls=%fused_computation.18 | loop fusion | bytes 524292 | tf_op jit(solution)/shard_map/dynamic_slice | solution.py:336
  2.7 1.3 %shard_map.92 = (f32[128,1024]{1,0:T(8,128)S(1)}, bf16[528,128]{1,0:T(8,128)(2,1)S(1)}, bf16[528,128]{1,0:T(8,128)(2,1)S(1)}) custom-call(s32[3]{0:T(128)S(1)} %pad_add_fusion.s.refs_0_, bf16[128,1024]{1,0:T(8,128)(2,1)S(1)} %constant_dynamic-slice_fusion.xo, bf16[128,2048]{1,0:T(8,128)(2,1)S(1)} %collective-permute-done.xr, ...), custom_call_target="tpu_custom_call" | custom-call | bytes 1908736 | tf_op jit(solution)/shard_map/pallas_call | solution.py:21
  4.7 2.7 %collective-permute-start.4 = (bf16[528,128]{1,0:T(8,128)(2,1)S(1)}, bf16[528,128]{1,0:T(8,128)(2,1)S(1)}, u32[]{:S(2)}, u32[]{:S(2)}) collective-permute-start(bf16[528,128]{1,0:T(8,128)(2,1)S(1)} %get-tuple-element.27.refs_1_), channel_id=1, source_target_pairs={{0,8},{4,12},{8,0},{12,4},{16,24},{20,28},{24,16},{28,20},{1,9},{5... | collective-permute-start | bytes 405512 | tf_op jit(solution)/shard_map/ppermute | solution.py:318
  7.4 4.3 %collective-permute-done.4.refs_2_.rest_0_ = bf16[528,128]{1,0:T(8,128)(2,1)S(1)} collective-permute-done((bf16[528,128]{1,0:T(8,128)(2,1)S(1)}, bf16[528,128]{1,0:T(8,128)(2,1)S(1)}, u32[]{:S(2)}, u32[]{:S(2)}) %collective-permute-start.4) | collective-permute-done | bytes 135200 | tf_op jit(solution)/shard_map/ppermute | solution.py:318
  12.3 2.2 %collective-permute-start.5 = (bf16[528,128]{1,0:T(8,128)(2,1)S(1)}, bf16[528,128]{1,0:T(8,128)(2,1)S(1)}, u32[]{:S(2)}, u32[]{:S(2)}) collective-permute-start(bf16[528,128]{1,0:T(8,128)(2,1)S(1)} %shard_map.93), channel_id=1, source_target_pairs={{0,16},{4,20},{8,24},{12,28},{16,0},{20,4},{24,8},{28,12},{1,17},{... | collective-permute-start | bytes 405512 | tf_op jit(solution)/shard_map/ppermute | solution.py:318
  15.1 1.7 %collective-permute-start.7 = (bf16[528,128]{1,0:T(8,128)(2,1)S(1)}, bf16[528,128]{1,0:T(8,128)(2,1)S(1)}, u32[]{:S(2)}, u32[]{:S(2)}) collective-permute-start(bf16[528,128]{1,0:T(8,128)(2,1)S(1)} %shard_map.94), channel_id=1, source_target_pairs={{0,16},{4,20},{8,24},{12,28},{16,0},{20,4},{24,8},{28,12},{1,17},{... | collective-permute-start | bytes 405512 | tf_op jit(solution)/shard_map/ppermute | solution.py:318
  16.8 2.3 %shard_map.91 = (f32[256,1024]{1,0:T(8,128)S(1)}, f32[256,1024]{1,0:T(8,128)S(1)}, f32[16,1024]{1,0:T(8,128)S(1)}) custom-call(s32[3]{0:T(128)S(1)} %pad_add_fusion.s.refs_0_, bf16[128,1024]{1,0:T(8,128)(2,1)S(1)} %constant_dynamic-slice_fusion.xo, bf16[128,2048]{1,0:T(8,128)(2,1)S(1)} %collective-permute-done.xr, f32[320,128]{1,0:T(8,128)S(1)} %convert_add_fusion.so, ...), custom_call_target="tpu_custom_call" | custom-call | bytes 4325504 | tf_op jit(solution)/shard_map/pallas_call | solution.py:21
  19.1 1.2 %collective-permute-done.7.rest_3_ = bf16[528,128]{1,0:T(8,128)(2,1)S(1)} collective-permute-done((bf16[528,128]{1,0:T(8,128)(2,1)S(1)}, bf16[528,128]{1,0:T(8,128)(2,1)S(1)}, u32[]{:S(2)}, u32[]{:S(2)}) %collective-permute-start.7) | collective-permute-done | bytes 135200 | tf_op jit(solution)/shard_map/ppermute | solution.py:318
  20.4 1.2 %shard_map.95 = (bf16[128,1024]{1,0:T(8,128)(2,1)S(1)}, bf16[128,1024]{1,0:T(8,128)(2,1)S(1)}, f32[8,128]{1,0:T(8,128)S(1)}, f32[8,128]{1,0:T(8,128)S(1)}) custom-call(s32[3]{0:T(128)S(1)} %pad_add_fusion.s.refs_0_, f32[256,1024]{1,0:T(8,128)S(1)} %get-tuple-element.23.inside, f32[256,1024]{1,0:T(8,128)S(1)} %get-tuple-element.24.decays, ...), custom_call_target="tpu_custom_call" | custom-call | bytes 6193152 | tf_op jit(solution)/shard_map/pallas_call | solution.py:21
  21.6 2.0 %collective-permute-start.8 = (bf16[128,1024]{1,0:T(8,128)(2,1)S(1)}, bf16[128,1024]{1,0:T(8,128)(2,1)S(1)}, u32[]{:S(2)}, u32[]{:S(2)}) collective-permute-start(bf16[128,1024]{1,0:T(8,128)(2,1)S(1)} %get-tuple-element.30.refs_1_), channel_id=1, source_target_pairs={{0,8},{4,12},{8,0},{12,4},{16,24},{20,28},{24,16},{28,20},{1,9},{5... | collective-permute-start | bytes 786440 | tf_op jit(solution)/shard_map/ppermute | solution.py:318
  23.7 1.5 %collective-permute-start.10 = (bf16[128,1024]{1,0:T(8,128)(2,1)S(1)}, bf16[128,1024]{1,0:T(8,128)(2,1)S(1)}, u32[]{:S(2)}, u32[]{:S(2)}) collective-permute-start(bf16[128,1024]{1,0:T(8,128)(2,1)S(1)} %collective-permute-done.9.refs_2_), channel_id=1, source_target_pairs={{0,16},{4,20},{8,24},{12,28},{16,0},{20,4},{24,8},{28,12},{1,17},{... | collective-permute-start | bytes 786440 | tf_op jit(solution)/shard_map/ppermute | solution.py:318
  25.7 1.5 %collective-permute-start.12 = (bf16[128,1024]{1,0:T(8,128)(2,1)S(1)}, bf16[128,1024]{1,0:T(8,128)(2,1)S(1)}, u32[]{:S(2)}, u32[]{:S(2)}) collective-permute-start(bf16[128,1024]{1,0:T(8,128)(2,1)S(1)} %collective-permute-done.9.refs_2_), channel_id=1, source_target_pairs={{0,8},{4,12},{8,0},{12,4},{16,24},{20,28},{24,16},{28,20},{1,9},{5... | collective-permute-start | bytes 786440 | tf_op jit(solution)/shard_map/ppermute | solution.py:318
  27.2 1.3 %shard_map.96.refs_7_ = bf16[1024,128]{1,0:T(8,128)(2,1)S(1)} custom-call(s32[3]{0:T(128)S(1)} %pad_add_fusion.s.refs_0_, bf16[128,1024]{1,0:T(8,128)(2,1)S(1)} %get-tuple-element.30.refs_1_, bf16[128,1024]{1,0:T(8,128)(2,1)S(1)} %collective-permute-done.9.refs_2_, bf16[2048,512]{1,0:T(8,128)(2,1)S(1)} %copy-done, ...), custom_call_target="tpu_custom_call" | custom-call | bytes 4980736 | tf_op jit(solution)/shard_map/pallas_call | solution.py:21
  28.5 2.4 %collective-permute-done.8.refs_1_ = bf16[128,1024]{1,0:T(8,128)(2,1)S(1)} collective-permute-done((bf16[128,1024]{1,0:T(8,128)(2,1)S(1)}, bf16[128,1024]{1,0:T(8,128)(2,1)S(1)}, u32[]{:S(2)}, u32[]{:S(2)}) %collective-permute-start.8) | collective-permute-done | bytes 262176 | tf_op jit(solution)/shard_map/ppermute | solution.py:318
  30.8 2.0 %collective-permute-done.10.refs_4_ = bf16[128,1024]{1,0:T(8,128)(2,1)S(1)} collective-permute-done((bf16[128,1024]{1,0:T(8,128)(2,1)S(1)}, bf16[128,1024]{1,0:T(8,128)(2,1)S(1)}, u32[]{:S(2)}, u32[]{:S(2)}) %collective-permute-start.10) | collective-permute-done | bytes 262176 | tf_op jit(solution)/shard_map/ppermute | solution.py:318
  32.8 1.5 %collective-permute-start.17 = (bf16[128,1024]{1,0:T(8,128)(2,1)S(1)}, bf16[128,1024]{1,0:T(8,128)(2,1)S(1)}, u32[]{:S(2)}, u32[]{:S(2)}) collective-permute-start(bf16[128,1024]{1,0:T(8,128)(2,1)S(1)} %collective-permute-done.8.refs_1_), channel_id=1, source_target_pairs={{0,16},{4,20},{8,24},{12,28},{16,0},{20,4},{24,8},{28,12},{1,17},{... | collective-permute-start | bytes 786440 | tf_op jit(solution)/shard_map/ppermute | solution.py:318
  34.3 1.5 %collective-permute-start.18 = (bf16[128,1024]{1,0:T(8,128)(2,1)S(1)}, bf16[128,1024]{1,0:T(8,128)(2,1)S(1)}, u32[]{:S(2)}, u32[]{:S(2)}) collective-permute-start(bf16[128,1024]{1,0:T(8,128)(2,1)S(1)} %collective-permute-done.10.refs_4_), channel_id=1, source_target_pairs={{0,8},{4,12},{8,0},{12,4},{16,24},{20,28},{24,16},{28,20},{1,9},{5... | collective-permute-start | bytes 786440 | tf_op jit(solution)/shard_map/ppermute | solution.py:318
  35.8 2.6 %collective-permute-done.11.refs_2_ = bf16[128,1024]{1,0:T(8,128)(2,1)S(1)} collective-permute-done((bf16[128,1024]{1,0:T(8,128)(2,1)S(1)}, bf16[128,1024]{1,0:T(8,128)(2,1)S(1)}, u32[]{:S(2)}, u32[]{:S(2)}) %collective-permute-start.11) | collective-permute-done | bytes 262176 | tf_op jit(solution)/shard_map/ppermute | solution.py:318
  38.4 1.8 %shard_map.97 = (bf16[1024,128]{1,0:T(8,128)(2,1)S(1)}, bf16[1024,128]{1,0:T(8,128)(2,1)S(1)}) custom-call(s32[3]{0:T(128)S(1)} %pad_add_fusion.s.refs_0_, bf16[128,1024]{1,0:T(8,128)(2,1)S(1)} %collective-permute-done.8.refs_1_, bf16[128,1024]{1,0:T(8,128)(2,1)S(1)} %collective-permute-done.11.refs_2_, ...), custom_call_target="tpu_custom_call" | custom-call | bytes 6029312 | tf_op jit(solution)/shard_map/pallas_call | solution.py:21
  40.2 1.6 %collective-permute-start.14 = (bf16[1024,128]{1,0:T(8,128)(2,1)S(1)}, bf16[1024,128]{1,0:T(8,128)(2,1)S(1)}, u32[]{:S(2)}, u32[]{:S(2)}) collective-permute-start(bf16[1024,128]{1,0:T(8,128)(2,1)S(1)} %get-tuple-element.36), channel_id=1, source_target_pairs={{0,8},{4,12},{8,0},{12,4},{16,24},{20,28},{24,16},{28,20},{1,9},{5... | collective-permute-start | bytes 786440 | tf_op jit(solution)/shard_map/ppermute | solution.py:318
  41.8 1.5 %collective-permute-start.13 = (bf16[1024,128]{1,0:T(8,128)(2,1)S(1)}, bf16[1024,128]{1,0:T(8,128)(2,1)S(1)}, u32[]{:S(2)}, u32[]{:S(2)}) collective-permute-start(bf16[1024,128]{1,0:T(8,128)(2,1)S(1)} %get-tuple-element.35), channel_id=1, source_target_pairs={{0,16},{4,20},{8,24},{12,28},{16,0},{20,4},{24,8},{28,12},{1,17},{... | collective-permute-start | bytes 786440 | tf_op jit(solution)/shard_map/ppermute | solution.py:318
  43.9 1.3 %shard_map.99 = bf16[1024,128]{1,0:T(8,128)(2,1)S(1)} custom-call(s32[3]{0:T(128)S(1)} %pad_add_fusion.s.refs_0_, bf16[128,1024]{1,0:T(8,128)(2,1)S(1)} %collective-permute-done.17.refs_1_, bf16[128,1024]{1,0:T(8,128)(2,1)S(1)} %collective-permute-done.18.refs_2_, bf16[2048,512]{1,0:T(8,128)(2,1)S(1)} %copy-done, ...), custom_call_target="tpu_custom_call" | custom-call | bytes 4980736 | tf_op jit(solution)/shard_map/pallas_call | solution.py:21
  45.2 2.7 %collective-permute-start.19 = (bf16[1024,128]{1,0:T(8,128)(2,1)S(1)}, bf16[1024,128]{1,0:T(8,128)(2,1)S(1)}, u32[]{:S(2)}, u32[]{:S(2)}) collective-permute-start(bf16[1024,128]{1,0:T(8,128)(2,1)S(1)} %shard_map.99), channel_id=1, source_target_pairs={{0,24},{4,28},{8,16},{12,20},{16,8},{20,12},{24,0},{28,4},{1,25},{... | collective-permute-start | bytes 786440 | tf_op jit(solution)/shard_map/ppermute | solution.py:318
  47.9 1.2 %collective-permute-done.15 = f32[8,128]{1,0:T(8,128)S(1)} collective-permute-done((f32[8,128]{1,0:T(8,128)S(1)}, f32[8,128]{1,0:T(8,128)S(1)}, u32[]{:S(2)}, u32[]{:S(2)}) %collective-permute-start.15) | collective-permute-done | bytes 4128 | tf_op jit(solution)/shard_map/ppermute | solution.py:315
  49.0 5.5 %collective-permute-done.13.odd = bf16[1024,128]{1,0:T(8,128)(2,1)S(1)} collective-permute-done((bf16[1024,128]{1,0:T(8,128)(2,1)S(1)}, bf16[1024,128]{1,0:T(8,128)(2,1)S(1)}, u32[]{:S(2)}, u32[]{:S(2)}) %collective-permute-start.13) | collective-permute-done | bytes 262176 | tf_op jit(solution)/shard_map/ppermute | solution.py:318
  55.1 1.6 %collective-permute-start.16 = (bf16[1040,128]{1,0:T(8,128)(2,1)S(1)}, bf16[1040,128]{1,0:T(8,128)(2,1)S(1)}, u32[]{:S(2)}, u32[]{:S(2)}) collective-permute-start(bf16[1040,128]{1,0:T(8,128)(2,1)S(1)} %shard_map.98), channel_id=1, source_target_pairs={{0,1},{1,0},{2,3},{3,2},{4,5},{5,4},{6,7},{7,6},{8,9},{9,8},{10,11... | collective-permute-start | bytes 798728 | tf_op jit(solution)/shard_map/ppermute | solution.py:321
  57.4 4.4 %collective-permute-done.16 = bf16[1040,128]{1,0:T(8,128)(2,1)S(1)} collective-permute-done((bf16[1040,128]{1,0:T(8,128)(2,1)S(1)}, bf16[1040,128]{1,0:T(8,128)(2,1)S(1)}, u32[]{:S(2)}, u32[]{:S(2)}) %collective-permute-start.16) | collective-permute-done | bytes 266272 | tf_op jit(solution)/shard_map/ppermute | solution.py:321
  61.8 5.4 %collective-permute-done.20 = bf16[1024,128]{1,0:T(8,128)(2,1)S(1)} collective-permute-done((bf16[1024,128]{1,0:T(8,128)(2,1)S(1)}, bf16[1024,128]{1,0:T(8,128)(2,1)S(1)}, u32[]{:S(2)}, u32[]{:S(2)}) %collective-permute-start.20) | collective-permute-done | bytes 262176 | tf_op jit(solution)/shard_map/ppermute | solution.py:321
  67.5 2.7 %collective-permute-start.21 = (bf16[1040,128]{1,0:T(8,128)(2,1)S(1)}, bf16[1040,128]{1,0:T(8,128)(2,1)S(1)}, u32[]{:S(2)}, u32[]{:S(2)}) collective-permute-start(bf16[1040,128]{1,0:T(8,128)(2,1)S(1)} %pad_maximum_fusion), channel_id=1, source_target_pairs={{0,2},{1,3},{2,0},{3,1},{4,6},{5,7},{6,4},{7,5},{8,10},{9,11},{10,... | collective-permute-start | bytes 798728 | tf_op jit(solution)/shard_map/ppermute | solution.py:321
  70.2 7.4 %collective-permute-done.21 = bf16[1040,128]{1,0:T(8,128)(2,1)S(1)} collective-permute-done((bf16[1040,128]{1,0:T(8,128)(2,1)S(1)}, bf16[1040,128]{1,0:T(8,128)(2,1)S(1)}, u32[]{:S(2)}, u32[]{:S(2)}) %collective-permute-start.21) | collective-permute-done | bytes 266272 | tf_op jit(solution)/shard_map/ppermute | solution.py:321
  77.6 1.4 %shard_map.100 = bf16[128,1024]{1,0:T(8,128)(2,1)} custom-call(s32[3]{0:T(128)S(1)} %pad_add_fusion.s.refs_0_, bf16[1024,128]{1,0:T(8,128)(2,1)S(1)} %slice.36.refs_1_, bf16[1024,128]{1,0:T(8,128)(2,1)S(1)} %get-tuple-element.43.refs_2_, bf16[1024,128]{1,0:T(8,128)(2,1)S(1)} %broadcast_select_fusion.3.refs_3_, f32[8,128]{1,0:T(8,128)S(1)} %fusion.1.refs_4_), custom_call_target="tpu_custom_call" | custom-call | bytes 1052672 | tf_op jit(solution)/shard_map/pallas_call | solution.py:21
  (44 shorter events, 5.3 us)
Async XLA Ops:
  0.0 16.8 %copy-start.1 = (bf16[128,2048]{1,0:T(8,128)(2,1)S(1)}, bf16[128,2048]{1,0:T(8,128)(2,1)}, u32[]{:S(2)}) copy-start(bf16[128,2048]{1,0:T(8,128)(2,1)} %zo.1) | copy-start | bytes 1572868
  0.0 16.8 %copy-start.3 = (f32[32]{0:T(128)S(1)}, f32[32]{0:T(128)}, u32[]{:S(2)}) copy-start(f32[32]{0:T(128)} %param.15) | copy-start | bytes 388
  0.0 2.7 %collective-permute-start = (bf16[128,2048]{1,0:T(8,128)(2,1)}, bf16[128,2048]{1,0:T(8,128)(2,1)S(1)}, u32[]{:S(2)}, u32[]{:S(2)}) collective-permute-start(bf16[128,2048]{1,0:T(8,128)(2,1)} %param.9), channel_id=1, source_target_pairs={{0,4},{4,0},{8,12},{12,8},{16,20},{20,16},{24,28},{28,24},{1,5},{5... | collective-permute-start | bytes 1572872 | tf_op jit(solution)/shard_map/ppermute | solution.py:315
  1.3 1.5 %collective-permute-start.1 = (f32[320,128]{1,0:T(8,128)S(1)}, f32[320,128]{1,0:T(8,128)S(1)}, u32[]{:S(2)}, u32[]{:S(2)}) collective-permute-start(f32[320,128]{1,0:T(8,128)S(1)} %convert_add_fusion.so), channel_id=1, source_target_pairs={{0,4},{4,0},{8,12},{12,8},{16,20},{20,16},{24,28},{28,24},{1,5},{5... | collective-permute-start | bytes 491528 | tf_op jit(solution)/shard_map/ppermute | solution.py:315
  2.5 17.9 %copy-start.2 = (f32[2048]{0:T(1024)S(1)}, f32[2048]{0:T(1024)}, u32[]{:S(2)}) copy-start(f32[2048]{0:T(1024)} %param.16) | copy-start | bytes 24580
  4.1 16.3 %collective-permute-start.3 = (bf16[2048,512]{1,0:T(8,128)(2,1)}, bf16[2048,512]{1,0:T(8,128)(2,1)S(1)}, u32[]{:S(2)}, u32[]{:S(2)}) collective-permute-start(bf16[2048,512]{1,0:T(8,128)(2,1)} %refs_3_.3), channel_id=1, source_target_pairs={{0,4},{4,0},{8,12},{12,8},{16,20},{20,16},{24,28},{28,24},{1,5},{5... | collective-permute-start | bytes 6291464 | tf_op jit(solution)/shard_map/ppermute | solution.py:315
  4.3 12.4 %collective-permute-start.2 = (bf16[128,2048]{1,0:T(8,128)(2,1)}, bf16[128,2048]{1,0:T(8,128)(2,1)S(1)}, u32[]{:S(2)}, u32[]{:S(2)}) collective-permute-start(bf16[128,2048]{1,0:T(8,128)(2,1)} %zo.1), channel_id=1, source_target_pairs={{0,4},{4,0},{8,12},{12,8},{16,20},{20,16},{24,28},{28,24},{1,5},{5... | collective-permute-start | bytes 1572872 | tf_op jit(solution)/shard_map/ppermute | solution.py:315
  4.7 7.0 %collective-permute-start.4 = (bf16[528,128]{1,0:T(8,128)(2,1)S(1)}, bf16[528,128]{1,0:T(8,128)(2,1)S(1)}, u32[]{:S(2)}, u32[]{:S(2)}) collective-permute-start(bf16[528,128]{1,0:T(8,128)(2,1)S(1)} %get-tuple-element.27.refs_1_), channel_id=1, source_target_pairs={{0,8},{4,12},{8,0},{12,4},{16,24},{20,28},{24,16},{28,20},{1,9},{5... | collective-permute-start | bytes 405512 | tf_op jit(solution)/shard_map/ppermute | solution.py:318
  7.3 7.1 %collective-permute-start.6 = (bf16[528,128]{1,0:T(8,128)(2,1)S(1)}, bf16[528,128]{1,0:T(8,128)(2,1)S(1)}, u32[]{:S(2)}, u32[]{:S(2)}) collective-permute-start(bf16[528,128]{1,0:T(8,128)(2,1)S(1)} %get-tuple-element.29.refs_1_), channel_id=1, source_target_pairs={{0,8},{4,12},{8,0},{12,4},{16,24},{20,28},{24,16},{28,20},{1,9},{5... | collective-permute-start | bytes 405512 | tf_op jit(solution)/shard_map/ppermute | solution.py:318
  12.3 6.8 %collective-permute-start.5 = (bf16[528,128]{1,0:T(8,128)(2,1)S(1)}, bf16[528,128]{1,0:T(8,128)(2,1)S(1)}, u32[]{:S(2)}, u32[]{:S(2)}) collective-permute-start(bf16[528,128]{1,0:T(8,128)(2,1)S(1)} %shard_map.93), channel_id=1, source_target_pairs={{0,16},{4,20},{8,24},{12,28},{16,0},{20,4},{24,8},{28,12},{1,17},{... | collective-permute-start | bytes 405512 | tf_op jit(solution)/shard_map/ppermute | solution.py:318
  15.1 5.3 %collective-permute-start.7 = (bf16[528,128]{1,0:T(8,128)(2,1)S(1)}, bf16[528,128]{1,0:T(8,128)(2,1)S(1)}, u32[]{:S(2)}, u32[]{:S(2)}) collective-permute-start(bf16[528,128]{1,0:T(8,128)(2,1)S(1)} %shard_map.94), channel_id=1, source_target_pairs={{0,16},{4,20},{8,24},{12,28},{16,0},{20,4},{24,8},{28,12},{1,17},{... | collective-permute-start | bytes 405512 | tf_op jit(solution)/shard_map/ppermute | solution.py:318
  20.4 6.8 %copy-start = (bf16[2048,512]{1,0:T(8,128)(2,1)S(1)}, bf16[2048,512]{1,0:T(8,128)(2,1)}, u32[]{:S(2)}) copy-start(bf16[2048,512]{1,0:T(8,128)(2,1)} %refs_3_.3) | copy-start | bytes 6291460
  21.6 2.0 %collective-permute-start.9 = (bf16[128,1024]{1,0:T(8,128)(2,1)S(1)}, bf16[128,1024]{1,0:T(8,128)(2,1)S(1)}, u32[]{:S(2)}, u32[]{:S(2)}) collective-permute-start(bf16[128,1024]{1,0:T(8,128)(2,1)S(1)} %get-tuple-element.31), channel_id=1, source_target_pairs={{0,4},{4,0},{8,12},{12,8},{16,20},{20,16},{24,28},{28,24},{1,5},{5... | collective-permute-start | bytes 786440 | tf_op jit(solution)/shard_map/ppermute | solution.py:315
  21.6 9.2 %collective-permute-start.8 = (bf16[128,1024]{1,0:T(8,128)(2,1)S(1)}, bf16[128,1024]{1,0:T(8,128)(2,1)S(1)}, u32[]{:S(2)}, u32[]{:S(2)}) collective-permute-start(bf16[128,1024]{1,0:T(8,128)(2,1)S(1)} %get-tuple-element.30.refs_1_), channel_id=1, source_target_pairs={{0,8},{4,12},{8,0},{12,4},{16,24},{20,28},{24,16},{28,20},{1,9},{5... | collective-permute-start | bytes 786440 | tf_op jit(solution)/shard_map/ppermute | solution.py:318
  23.7 9.1 %collective-permute-start.10 = (bf16[128,1024]{1,0:T(8,128)(2,1)S(1)}, bf16[128,1024]{1,0:T(8,128)(2,1)S(1)}, u32[]{:S(2)}, u32[]{:S(2)}) collective-permute-start(bf16[128,1024]{1,0:T(8,128)(2,1)S(1)} %collective-permute-done.9.refs_2_), channel_id=1, source_target_pairs={{0,16},{4,20},{8,24},{12,28},{16,0},{20,4},{24,8},{28,12},{1,17},{... | collective-permute-start | bytes 786440 | tf_op jit(solution)/shard_map/ppermute | solution.py:318
  25.2 13.2 %collective-permute-start.11 = (bf16[128,1024]{1,0:T(8,128)(2,1)S(1)}, bf16[128,1024]{1,0:T(8,128)(2,1)S(1)}, u32[]{:S(2)}, u32[]{:S(2)}) collective-permute-start(bf16[128,1024]{1,0:T(8,128)(2,1)S(1)} %get-tuple-element.30.refs_1_), channel_id=1, source_target_pairs={{0,16},{4,20},{8,24},{12,28},{16,0},{20,4},{24,8},{28,12},{1,17},{... | collective-permute-start | bytes 786440 | tf_op jit(solution)/shard_map/ppermute | solution.py:318
  25.7 12.7 %collective-permute-start.12 = (bf16[128,1024]{1,0:T(8,128)(2,1)S(1)}, bf16[128,1024]{1,0:T(8,128)(2,1)S(1)}, u32[]{:S(2)}, u32[]{:S(2)}) collective-permute-start(bf16[128,1024]{1,0:T(8,128)(2,1)S(1)} %collective-permute-done.9.refs_2_), channel_id=1, source_target_pairs={{0,8},{4,12},{8,0},{12,4},{16,24},{20,28},{24,16},{28,20},{1,9},{5... | collective-permute-start | bytes 786440 | tf_op jit(solution)/shard_map/ppermute | solution.py:318
  32.8 11.1 %collective-permute-start.17 = (bf16[128,1024]{1,0:T(8,128)(2,1)S(1)}, bf16[128,1024]{1,0:T(8,128)(2,1)S(1)}, u32[]{:S(2)}, u32[]{:S(2)}) collective-permute-start(bf16[128,1024]{1,0:T(8,128)(2,1)S(1)} %collective-permute-done.8.refs_1_), channel_id=1, source_target_pairs={{0,16},{4,20},{8,24},{12,28},{16,0},{20,4},{24,8},{28,12},{1,17},{... | collective-permute-start | bytes 786440 | tf_op jit(solution)/shard_map/ppermute | solution.py:318
  34.3 9.6 %collective-permute-start.18 = (bf16[128,1024]{1,0:T(8,128)(2,1)S(1)}, bf16[128,1024]{1,0:T(8,128)(2,1)S(1)}, u32[]{:S(2)}, u32[]{:S(2)}) collective-permute-start(bf16[128,1024]{1,0:T(8,128)(2,1)S(1)} %collective-permute-done.10.refs_4_), channel_id=1, source_target_pairs={{0,8},{4,12},{8,0},{12,4},{16,24},{20,28},{24,16},{28,20},{1,9},{5... | collective-permute-start | bytes 786440 | tf_op jit(solution)/shard_map/ppermute | solution.py:318
  40.2 8.8 %collective-permute-start.14 = (bf16[1024,128]{1,0:T(8,128)(2,1)S(1)}, bf16[1024,128]{1,0:T(8,128)(2,1)S(1)}, u32[]{:S(2)}, u32[]{:S(2)}) collective-permute-start(bf16[1024,128]{1,0:T(8,128)(2,1)S(1)} %get-tuple-element.36), channel_id=1, source_target_pairs={{0,8},{4,12},{8,0},{12,4},{16,24},{20,28},{24,16},{28,20},{1,9},{5... | collective-permute-start | bytes 786440 | tf_op jit(solution)/shard_map/ppermute | solution.py:318
  41.8 12.7 %collective-permute-start.13 = (bf16[1024,128]{1,0:T(8,128)(2,1)S(1)}, bf16[1024,128]{1,0:T(8,128)(2,1)S(1)}, u32[]{:S(2)}, u32[]{:S(2)}) collective-permute-start(bf16[1024,128]{1,0:T(8,128)(2,1)S(1)} %get-tuple-element.35), channel_id=1, source_target_pairs={{0,16},{4,20},{8,24},{12,28},{16,0},{20,4},{24,8},{28,12},{1,17},{... | collective-permute-start | bytes 786440 | tf_op jit(solution)/shard_map/ppermute | solution.py:318
  45.2 11.6 %collective-permute-start.19 = (bf16[1024,128]{1,0:T(8,128)(2,1)S(1)}, bf16[1024,128]{1,0:T(8,128)(2,1)S(1)}, u32[]{:S(2)}, u32[]{:S(2)}) collective-permute-start(bf16[1024,128]{1,0:T(8,128)(2,1)S(1)} %shard_map.99), channel_id=1, source_target_pairs={{0,24},{4,28},{8,16},{12,20},{16,8},{20,12},{24,0},{28,4},{1,25},{... | collective-permute-start | bytes 786440 | tf_op jit(solution)/shard_map/ppermute | solution.py:318
  47.9 1.2 %collective-permute-start.15 = (f32[8,128]{1,0:T(8,128)S(1)}, f32[8,128]{1,0:T(8,128)S(1)}, u32[]{:S(2)}, u32[]{:S(2)}) collective-permute-start(f32[8,128]{1,0:T(8,128)S(1)} %get-tuple-element.38), channel_id=1, source_target_pairs={{0,4},{4,0},{8,12},{12,8},{16,20},{20,16},{24,28},{28,24},{1,5},{5... | collective-permute-start | bytes 12296 | tf_op jit(solution)/shard_map/ppermute | solution.py:315
  55.1 6.6 %collective-permute-start.16 = (bf16[1040,128]{1,0:T(8,128)(2,1)S(1)}, bf16[1040,128]{1,0:T(8,128)(2,1)S(1)}, u32[]{:S(2)}, u32[]{:S(2)}) collective-permute-start(bf16[1040,128]{1,0:T(8,128)(2,1)S(1)} %shard_map.98), channel_id=1, source_target_pairs={{0,1},{1,0},{2,3},{3,2},{4,5},{5,4},{6,7},{7,6},{8,9},{9,8},{10,11... | collective-permute-start | bytes 798728 | tf_op jit(solution)/shard_map/ppermute | solution.py:321
  56.9 10.4 %collective-permute-start.20 = (bf16[1024,128]{1,0:T(8,128)(2,1)S(1)}, bf16[1024,128]{1,0:T(8,128)(2,1)S(1)}, u32[]{:S(2)}, u32[]{:S(2)}) collective-permute-start(bf16[1024,128]{1,0:T(8,128)(2,1)S(1)} %get-tuple-element.44), channel_id=1, source_target_pairs={{0,1},{1,0},{2,3},{3,2},{4,5},{5,4},{6,7},{7,6},{8,9},{9,8},{10,11... | collective-permute-start | bytes 786440 | tf_op jit(solution)/shard_map/ppermute | solution.py:321
  67.5 10.1 %collective-permute-start.21 = (bf16[1040,128]{1,0:T(8,128)(2,1)S(1)}, bf16[1040,128]{1,0:T(8,128)(2,1)S(1)}, u32[]{:S(2)}, u32[]{:S(2)}) collective-permute-start(bf16[1040,128]{1,0:T(8,128)(2,1)S(1)} %pad_maximum_fusion), channel_id=1, source_target_pairs={{0,2},{1,3},{2,0},{3,1},{4,6},{5,7},{6,4},{7,5},{8,10},{9,11},{10,... | collective-permute-start | bytes 798728 | tf_op jit(solution)/shard_map/ppermute | solution.py:321

commit v9 on v8

--- a/solution.py
+++ b/solution.py
@@ -380,7 +380,7 @@
     if n == 4:
         ux, vy = across(u, 1), across(v, 2)
         uy, vx = across(u, 2), across(v, 1)
-        (own,) = project([u], [v])
+        (own,) = project([u], [v], after=[squares])
         ux, vy, own = lax.optimization_barrier((ux, vy, own))
         ud, vd = lax.optimization_barrier((across(ux, 2), across(vy, 1)))
         px, py = project([ux, uy], [vx, vy], after=[own])
@@ -404,18 +404,18 @@
         r = chip ^ z
         even = r % 2 == 0
         message = shape((size + EXT, LANES), bf16)
-        ins = (px, py, squares)
+        ins = (px, own, squares)
         (give,) = call(give_kernel, s, ins, [full(a) for a in ins], [message], [full(message)])
         got1, more = cut(along(give, 1))
-        got2 = along(jnp.where(even, far, own), 1)
+        got2 = along(jnp.where(even, far, py), 1)
         squares = squares + more
-        kept1, kept2 = jnp.where(even, py, px), jnp.where(even, own, far)
+        kept1, kept2 = jnp.where(even, own, px), jnp.where(even, py, far)
         first = kept1.astype(f32) + got1.astype(f32)
         second = kept2.astype(f32) + got2.astype(f32)
-        outer = (r == 0) | (r == 3)
-        other, more = cut(along(attach(jnp.where(outer, first, second).astype(bf16), squares), 2))
+        low = r < 2
+        other, more = cut(along(attach(jnp.where(low, second, first).astype(bf16), squares), 2))
         squares = squares + more
-        blocks = (other, jnp.where(outer, kept2, kept1), jnp.where(outer, got2, got1))
+        blocks = (other, jnp.where(low, kept1, kept2), jnp.where(low, got1, got2))
     else:
         blocks = call(
             choose_kernel, s, blocks, [full(p_shape)] * n, [p_shape] * n, [full(p_shape)] * n

time: 79.1 us -> 76.4 us (0.966)
  waiting for transfers between devices: 37.1 us -> 33.4 us
  starting transfers between devices: 27 us -> 28 us
    ppermute x3, waiting for transfers between devices: 17.2 us -> 15.6 us  [along(): return lax.ppermute(a, 'head', [(i, i ^ m) for i in range(n)])]
    ppermute x6, waiting for transfers between devices: 1.41 us -> 0.25 us  [swap(): return lax.ppermute(a, 'seq', [(i, i ^ 1) for i in range(2 * n)])]
    ppermute x3, starting transfers between devices: 4.82 us -> 5.93 us  [along(): return lax.ppermute(a, 'head', [(i, i ^ m) for i in range(n)])]
    ppermute x13, waiting for transfers between devices: 18.5 us -> 17.5 us  [across(): return lax.ppermute(a, 'seq', [(i, i ^ 2 * j) for i in range(2 * n)])]
  transfers between devices with their start and end apart: 22 -> 22, of which waited for: 12 -> 10; matrix products, arithmetic and copies ran while one was open for 3% -> 3% of each run, Pallas kernels for 11% -> 11%
where the time goes in v9:
time: 76.4 us; the launch traced here: 76.3 us
  waiting for transfers between devices  33.4 us (44%)
  starting transfers between devices  28 us (37%)
  Pallas kernels  12.5 us (16%)
  other arithmetic  1.27 us (2%)
  local copies, waits for them, and re-layouts  1 us (1%)
    ppermute x13, starting transfers between devices, across(): return lax.ppermute(a, 'seq', [(i, i ^ 2 * j) for i in range(2 * n)])  20.9 us
    ppermute x13, waiting for transfers between devices, across(): return lax.ppermute(a, 'seq', [(i, i ^ 2 * j) for i in range(2 * n)])  17.5 us
    ppermute x3, waiting for transfers between devices, along(): return lax.ppermute(a, 'head', [(i, i ^ m) for i in range(n)])  15.6 us
    pallas_call x10, Pallas kernels, call(): pl.pallas_call(kernel, out_shape=outs, grid_spec=pltpu.PrefetchScalarGrid...  12.5 us
    ppermute x3, starting transfers between devices, along(): return lax.ppermute(a, 'head', [(i, i ^ m) for i in range(n)])  5.93 us
  transfers between devices with their start and end apart: 22, of which 10 were waited for; matrix products, arithmetic and copies ran while one was open for 3% of the time, Pallas kernels for 11%

profile of v9, /device:TPU:0, one launch (start us, length us, event | category | flops | bytes accessed | tf_op | source)
XLA Modules:
  0.0 76.3 jit_solution(4912810001848656172)
XLA Ops:
  0.5 0.8 %convert_add_fusion.so = f32[320,128]{1,0:T(8,128)S(1)} fusion(f32[32,128]{1,0:T(8,128)} %param.14, f32[32,128]{1,0:T(8,128)} %param.13, bf16[128,128]{1,0:T(8,128)(2,1)} %param.12, bf16[128,128]{1,0:T(8,128)(2,1)} %param.11), kind=kLoop, calls=%fused_computation.7 | loop fusion | flops 204800 | bytes 262144 | tf_op jit(solution)/shard_map/add | solution.py:333
  1.5 1.0 %constant_dynamic-slice_fusion.xo = bf16[128,1024]{1,0:T(8,128)(2,1)S(1)} fusion(bf16[128,2048]{1,0:T(8,128)(2,1)} %param.9, s32[]{:T(128)S(6)} %select_n.55), kind=kLoop, calls=%fused_computation.18 | loop fusion | bytes 524292 | tf_op jit(solution)/shard_map/dynamic_slice | solution.py:336
  2.7 1.3 %shard_map.92 = (f32[128,1024]{1,0:T(8,128)S(1)}, bf16[528,128]{1,0:T(8,128)(2,1)S(1)}, bf16[528,128]{1,0:T(8,128)(2,1)S(1)}) custom-call(s32[3]{0:T(128)S(1)} %pad_add_fusion.s.refs_0_, bf16[128,1024]{1,0:T(8,128)(2,1)S(1)} %constant_dynamic-slice_fusion.xo, bf16[128,2048]{1,0:T(8,128)(2,1)S(1)} %collective-permute-done.xr, ...), custom_call_target="tpu_custom_call" | custom-call | bytes 1908736 | tf_op jit(solution)/shard_map/pallas_call | solution.py:21
  4.7 2.7 %collective-permute-start.4 = (bf16[528,128]{1,0:T(8,128)(2,1)S(1)}, bf16[528,128]{1,0:T(8,128)(2,1)S(1)}, u32[]{:S(2)}, u32[]{:S(2)}) collective-permute-start(bf16[528,128]{1,0:T(8,128)(2,1)S(1)} %get-tuple-element.27.refs_1_), channel_id=1, source_target_pairs={{0,8},{4,12},{8,0},{12,4},{16,24},{20,28},{24,16},{28,20},{1,9},{5... | collective-permute-start | bytes 405512 | tf_op jit(solution)/shard_map/ppermute | solution.py:318
  7.4 4.3 %collective-permute-done.4.refs_2_.rest_0_ = bf16[528,128]{1,0:T(8,128)(2,1)S(1)} collective-permute-done((bf16[528,128]{1,0:T(8,128)(2,1)S(1)}, bf16[528,128]{1,0:T(8,128)(2,1)S(1)}, u32[]{:S(2)}, u32[]{:S(2)}) %collective-permute-start.4) | collective-permute-done | bytes 135200 | tf_op jit(solution)/shard_map/ppermute | solution.py:318
  12.3 2.2 %collective-permute-start.5 = (bf16[528,128]{1,0:T(8,128)(2,1)S(1)}, bf16[528,128]{1,0:T(8,128)(2,1)S(1)}, u32[]{:S(2)}, u32[]{:S(2)}) collective-permute-start(bf16[528,128]{1,0:T(8,128)(2,1)S(1)} %shard_map.93), channel_id=1, source_target_pairs={{0,16},{4,20},{8,24},{12,28},{16,0},{20,4},{24,8},{28,12},{1,17},{... | collective-permute-start | bytes 405512 | tf_op jit(solution)/shard_map/ppermute | solution.py:318
  15.1 1.7 %collective-permute-start.7 = (bf16[528,128]{1,0:T(8,128)(2,1)S(1)}, bf16[528,128]{1,0:T(8,128)(2,1)S(1)}, u32[]{:S(2)}, u32[]{:S(2)}) collective-permute-start(bf16[528,128]{1,0:T(8,128)(2,1)S(1)} %shard_map.94), channel_id=1, source_target_pairs={{0,16},{4,20},{8,24},{12,28},{16,0},{20,4},{24,8},{28,12},{1,17},{... | collective-permute-start | bytes 405512 | tf_op jit(solution)/shard_map/ppermute | solution.py:318
  16.8 2.3 %shard_map.91 = (f32[256,1024]{1,0:T(8,128)S(1)}, f32[256,1024]{1,0:T(8,128)S(1)}, f32[16,1024]{1,0:T(8,128)S(1)}) custom-call(s32[3]{0:T(128)S(1)} %pad_add_fusion.s.refs_0_, bf16[128,1024]{1,0:T(8,128)(2,1)S(1)} %constant_dynamic-slice_fusion.xo, bf16[128,2048]{1,0:T(8,128)(2,1)S(1)} %collective-permute-done.xr, f32[320,128]{1,0:T(8,128)S(1)} %convert_add_fusion.so, ...), custom_call_target="tpu_custom_call" | custom-call | bytes 4325504 | tf_op jit(solution)/shard_map/pallas_call | solution.py:21
  19.1 1.2 %collective-permute-done.7.rest_3_ = bf16[528,128]{1,0:T(8,128)(2,1)S(1)} collective-permute-done((bf16[528,128]{1,0:T(8,128)(2,1)S(1)}, bf16[528,128]{1,0:T(8,128)(2,1)S(1)}, u32[]{:S(2)}, u32[]{:S(2)}) %collective-permute-start.7) | collective-permute-done | bytes 135200 | tf_op jit(solution)/shard_map/ppermute | solution.py:318
  20.4 1.2 %shard_map.95 = (bf16[128,1024]{1,0:T(8,128)(2,1)S(1)}, bf16[128,1024]{1,0:T(8,128)(2,1)S(1)}, f32[8,128]{1,0:T(8,128)S(1)}, f32[8,128]{1,0:T(8,128)S(1)}) custom-call(s32[3]{0:T(128)S(1)} %pad_add_fusion.s.refs_0_, f32[256,1024]{1,0:T(8,128)S(1)} %get-tuple-element.23.inside, f32[256,1024]{1,0:T(8,128)S(1)} %get-tuple-element.24.decays, ...), custom_call_target="tpu_custom_call" | custom-call | bytes 6193152 | tf_op jit(solution)/shard_map/pallas_call | solution.py:21
  21.6 2.0 %collective-permute-start.8 = (bf16[128,1024]{1,0:T(8,128)(2,1)S(1)}, bf16[128,1024]{1,0:T(8,128)(2,1)S(1)}, u32[]{:S(2)}, u32[]{:S(2)}) collective-permute-start(bf16[128,1024]{1,0:T(8,128)(2,1)S(1)} %get-tuple-element.30.refs_1_), channel_id=1, source_target_pairs={{0,8},{4,12},{8,0},{12,4},{16,24},{20,28},{24,16},{28,20},{1,9},{5... | collective-permute-start | bytes 786440 | tf_op jit(solution)/shard_map/ppermute | solution.py:318
  23.7 1.5 %collective-permute-start.10 = (bf16[128,1024]{1,0:T(8,128)(2,1)S(1)}, bf16[128,1024]{1,0:T(8,128)(2,1)S(1)}, u32[]{:S(2)}, u32[]{:S(2)}) collective-permute-start(bf16[128,1024]{1,0:T(8,128)(2,1)S(1)} %collective-permute-done.9.refs_2_), channel_id=1, source_target_pairs={{0,16},{4,20},{8,24},{12,28},{16,0},{20,4},{24,8},{28,12},{1,17},{... | collective-permute-start | bytes 786440 | tf_op jit(solution)/shard_map/ppermute | solution.py:318
  25.7 1.5 %collective-permute-start.13 = (bf16[128,1024]{1,0:T(8,128)(2,1)S(1)}, bf16[128,1024]{1,0:T(8,128)(2,1)S(1)}, u32[]{:S(2)}, u32[]{:S(2)}) collective-permute-start(bf16[128,1024]{1,0:T(8,128)(2,1)S(1)} %collective-permute-done.9.refs_2_), channel_id=1, source_target_pairs={{0,8},{4,12},{8,0},{12,4},{16,24},{20,28},{24,16},{28,20},{1,9},{5... | collective-permute-start | bytes 786440 | tf_op jit(solution)/shard_map/ppermute | solution.py:318
  27.2 1.3 %shard_map.96.refs_7_.odd = bf16[1024,128]{1,0:T(8,128)(2,1)S(1)} custom-call(s32[3]{0:T(128)S(1)} %pad_add_fusion.s.refs_0_, bf16[128,1024]{1,0:T(8,128)(2,1)S(1)} %get-tuple-element.30.refs_1_, bf16[128,1024]{1,0:T(8,128)(2,1)S(1)} %collective-permute-done.9.refs_2_, bf16[2048,512]{1,0:T(8,128)(2,1)S(1)} %copy-done, ...), custom_call_target="tpu_custom_call" | custom-call | bytes 4984832 | tf_op jit(solution)/shard_map/pallas_call | solution.py:21
  28.5 2.4 %collective-permute-done.8.refs_1_ = bf16[128,1024]{1,0:T(8,128)(2,1)S(1)} collective-permute-done((bf16[128,1024]{1,0:T(8,128)(2,1)S(1)}, bf16[128,1024]{1,0:T(8,128)(2,1)S(1)}, u32[]{:S(2)}, u32[]{:S(2)}) %collective-permute-start.8) | collective-permute-done | bytes 262176 | tf_op jit(solution)/shard_map/ppermute | solution.py:318
  30.8 2.0 %collective-permute-done.10.refs_4_ = bf16[128,1024]{1,0:T(8,128)(2,1)S(1)} collective-permute-done((bf16[128,1024]{1,0:T(8,128)(2,1)S(1)}, bf16[128,1024]{1,0:T(8,128)(2,1)S(1)}, u32[]{:S(2)}, u32[]{:S(2)}) %collective-permute-start.10) | collective-permute-done | bytes 262176 | tf_op jit(solution)/shard_map/ppermute | solution.py:318
  32.8 1.5 %collective-permute-start.15 = (bf16[128,1024]{1,0:T(8,128)(2,1)S(1)}, bf16[128,1024]{1,0:T(8,128)(2,1)S(1)}, u32[]{:S(2)}, u32[]{:S(2)}) collective-permute-start(bf16[128,1024]{1,0:T(8,128)(2,1)S(1)} %collective-permute-done.8.refs_1_), channel_id=1, source_target_pairs={{0,16},{4,20},{8,24},{12,28},{16,0},{20,4},{24,8},{28,12},{1,17},{... | collective-permute-start | bytes 786440 | tf_op jit(solution)/shard_map/ppermute | solution.py:318
  34.3 1.5 %collective-permute-start.16 = (bf16[128,1024]{1,0:T(8,128)(2,1)S(1)}, bf16[128,1024]{1,0:T(8,128)(2,1)S(1)}, u32[]{:S(2)}, u32[]{:S(2)}) collective-permute-start(bf16[128,1024]{1,0:T(8,128)(2,1)S(1)} %collective-permute-done.10.refs_4_), channel_id=1, source_target_pairs={{0,8},{4,12},{8,0},{12,4},{16,24},{20,28},{24,16},{28,20},{1,9},{5... | collective-permute-start | bytes 786440 | tf_op jit(solution)/shard_map/ppermute | solution.py:318
  35.8 2.6 %collective-permute-done.12.refs_2_ = bf16[128,1024]{1,0:T(8,128)(2,1)S(1)} collective-permute-done((bf16[128,1024]{1,0:T(8,128)(2,1)S(1)}, bf16[128,1024]{1,0:T(8,128)(2,1)S(1)}, u32[]{:S(2)}, u32[]{:S(2)}) %collective-permute-start.12) | collective-permute-done | bytes 262176 | tf_op jit(solution)/shard_map/ppermute | solution.py:318
  38.4 1.8 %shard_map.97 = (bf16[1024,128]{1,0:T(8,128)(2,1)S(1)}, bf16[1024,128]{1,0:T(8,128)(2,1)S(1)}) custom-call(s32[3]{0:T(128)S(1)} %pad_add_fusion.s.refs_0_, bf16[128,1024]{1,0:T(8,128)(2,1)S(1)} %collective-permute-done.8.refs_1_, bf16[128,1024]{1,0:T(8,128)(2,1)S(1)} %collective-permute-done.12.refs_2_, ...), custom_call_target="tpu_custom_call" | custom-call | bytes 6029312 | tf_op jit(solution)/shard_map/pallas_call | solution.py:21
  40.2 1.6 %collective-permute-start.19 = (bf16[1024,128]{1,0:T(8,128)(2,1)S(1)}, bf16[1024,128]{1,0:T(8,128)(2,1)S(1)}, u32[]{:S(2)}, u32[]{:S(2)}) collective-permute-start(bf16[1024,128]{1,0:T(8,128)(2,1)S(1)} %get-tuple-element.40), channel_id=1, source_target_pairs={{0,8},{4,12},{8,0},{12,4},{16,24},{20,28},{24,16},{28,20},{1,9},{5... | collective-permute-start | bytes 786440 | tf_op jit(solution)/shard_map/ppermute | solution.py:318
  41.8 1.5 %collective-permute-start.14 = (bf16[1024,128]{1,0:T(8,128)(2,1)S(1)}, bf16[1024,128]{1,0:T(8,128)(2,1)S(1)}, u32[]{:S(2)}, u32[]{:S(2)}) collective-permute-start(bf16[1024,128]{1,0:T(8,128)(2,1)S(1)} %get-tuple-element.37), channel_id=1, source_target_pairs={{0,16},{4,20},{8,24},{12,28},{16,0},{20,4},{24,8},{28,12},{1,17},{... | collective-permute-start | bytes 786440 | tf_op jit(solution)/shard_map/ppermute | solution.py:318
  43.9 1.3 %shard_map.98 = bf16[1024,128]{1,0:T(8,128)(2,1)S(1)} custom-call(s32[3]{0:T(128)S(1)} %pad_add_fusion.s.refs_0_, bf16[128,1024]{1,0:T(8,128)(2,1)S(1)} %collective-permute-done.15.refs_1_, bf16[128,1024]{1,0:T(8,128)(2,1)S(1)} %collective-permute-done.16.refs_2_, bf16[2048,512]{1,0:T(8,128)(2,1)S(1)} %copy-done, ...), custom_call_target="tpu_custom_call" | custom-call | bytes 4980736 | tf_op jit(solution)/shard_map/pallas_call | solution.py:21
  45.2 2.7 %collective-permute-start.17 = (bf16[1024,128]{1,0:T(8,128)(2,1)S(1)}, bf16[1024,128]{1,0:T(8,128)(2,1)S(1)}, u32[]{:S(2)}, u32[]{:S(2)}) collective-permute-start(bf16[1024,128]{1,0:T(8,128)(2,1)S(1)} %shard_map.98), channel_id=1, source_target_pairs={{0,24},{4,28},{8,16},{12,20},{16,8},{20,12},{24,0},{28,4},{1,25},{... | collective-permute-start | bytes 786440 | tf_op jit(solution)/shard_map/ppermute | solution.py:318
  47.8 0.6 shard_map.99
  48.5 1.6 %collective-permute-start.20 = (bf16[1040,128]{1,0:T(8,128)(2,1)S(1)}, bf16[1040,128]{1,0:T(8,128)(2,1)S(1)}, u32[]{:S(2)}, u32[]{:S(2)}) collective-permute-start(bf16[1040,128]{1,0:T(8,128)(2,1)S(1)} %shard_map.99), channel_id=1, source_target_pairs={{0,1},{1,0},{2,3},{3,2},{4,5},{5,4},{6,7},{7,6},{8,9},{9,8},{10,11... | collective-permute-start | bytes 798728 | tf_op jit(solution)/shard_map/ppermute | solution.py:321
  50.1 4.4 %collective-permute-done.14 = bf16[1024,128]{1,0:T(8,128)(2,1)S(1)} collective-permute-done((bf16[1024,128]{1,0:T(8,128)(2,1)S(1)}, bf16[1024,128]{1,0:T(8,128)(2,1)S(1)}, u32[]{:S(2)}, u32[]{:S(2)}) %collective-permute-start.14) | collective-permute-done | bytes 262176 | tf_op jit(solution)/shard_map/ppermute | solution.py:318
  54.6 1.6 %collective-permute-start.18 = (bf16[1024,128]{1,0:T(8,128)(2,1)S(1)}, bf16[1024,128]{1,0:T(8,128)(2,1)S(1)}, u32[]{:S(2)}, u32[]{:S(2)}) collective-permute-start(bf16[1024,128]{1,0:T(8,128)(2,1)S(1)} %get-tuple-element.44), channel_id=1, source_target_pairs={{0,1},{1,0},{2,3},{3,2},{4,5},{5,4},{6,7},{7,6},{8,9},{9,8},{10,11... | collective-permute-start | bytes 786440 | tf_op jit(solution)/shard_map/ppermute | solution.py:321
  56.3 5.4 %collective-permute-done.18 = bf16[1024,128]{1,0:T(8,128)(2,1)S(1)} collective-permute-done((bf16[1024,128]{1,0:T(8,128)(2,1)S(1)}, bf16[1024,128]{1,0:T(8,128)(2,1)S(1)}, u32[]{:S(2)}, u32[]{:S(2)}) %collective-permute-start.18) | collective-permute-done | bytes 262176 | tf_op jit(solution)/shard_map/ppermute | solution.py:321
  62.0 2.6 %collective-permute-start.21 = (bf16[1040,128]{1,0:T(8,128)(2,1)S(1)}, bf16[1040,128]{1,0:T(8,128)(2,1)S(1)}, u32[]{:S(2)}, u32[]{:S(2)}) collective-permute-start(bf16[1040,128]{1,0:T(8,128)(2,1)S(1)} %pad_maximum_fusion), channel_id=1, source_target_pairs={{0,2},{1,3},{2,0},{3,1},{4,6},{5,7},{6,4},{7,5},{8,10},{9,11},{10,... | collective-permute-start | bytes 798728 | tf_op jit(solution)/shard_map/ppermute | solution.py:321
  64.6 10.2 %collective-permute-done.21 = bf16[1040,128]{1,0:T(8,128)(2,1)S(1)} collective-permute-done((bf16[1040,128]{1,0:T(8,128)(2,1)S(1)}, bf16[1040,128]{1,0:T(8,128)(2,1)S(1)}, u32[]{:S(2)}, u32[]{:S(2)}) %collective-permute-start.21) | collective-permute-done | bytes 266272 | tf_op jit(solution)/shard_map/ppermute | solution.py:321
  74.9 1.4 %shard_map.100 = bf16[128,1024]{1,0:T(8,128)(2,1)} custom-call(s32[3]{0:T(128)S(1)} %pad_add_fusion.s.refs_0_, bf16[1024,128]{1,0:T(8,128)(2,1)S(1)} %slice.36.refs_1_, bf16[1024,128]{1,0:T(8,128)(2,1)S(1)} %get-tuple-element.43.refs_2_, bf16[1024,128]{1,0:T(8,128)(2,1)S(1)} %broadcast_select_fusion.3.refs_3_, f32[8,128]{1,0:T(8,128)S(1)} %fusion.1.refs_4_), custom_call_target="tpu_custom_call" | custom-call | bytes 1052672 | tf_op jit(solution)/shard_map/pallas_call | solution.py:21
  (44 shorter events, 4.3 us)
Async XLA Ops:
  0.0 16.8 %copy-start.1 = (bf16[128,2048]{1,0:T(8,128)(2,1)S(1)}, bf16[128,2048]{1,0:T(8,128)(2,1)}, u32[]{:S(2)}) copy-start(bf16[128,2048]{1,0:T(8,128)(2,1)} %zo.1) | copy-start | bytes 1572868
  0.0 16.8 %copy-start.3 = (f32[32]{0:T(128)S(1)}, f32[32]{0:T(128)}, u32[]{:S(2)}) copy-start(f32[32]{0:T(128)} %param.15) | copy-start | bytes 388
  0.0 2.7 %collective-permute-start = (bf16[128,2048]{1,0:T(8,128)(2,1)}, bf16[128,2048]{1,0:T(8,128)(2,1)S(1)}, u32[]{:S(2)}, u32[]{:S(2)}) collective-permute-start(bf16[128,2048]{1,0:T(8,128)(2,1)} %param.9), channel_id=1, source_target_pairs={{0,4},{4,0},{8,12},{12,8},{16,20},{20,16},{24,28},{28,24},{1,5},{5... | collective-permute-start | bytes 1572872 | tf_op jit(solution)/shard_map/ppermute | solution.py:315
  1.3 1.5 %collective-permute-start.1 = (f32[320,128]{1,0:T(8,128)S(1)}, f32[320,128]{1,0:T(8,128)S(1)}, u32[]{:S(2)}, u32[]{:S(2)}) collective-permute-start(f32[320,128]{1,0:T(8,128)S(1)} %convert_add_fusion.so), channel_id=1, source_target_pairs={{0,4},{4,0},{8,12},{12,8},{16,20},{20,16},{24,28},{28,24},{1,5},{5... | collective-permute-start | bytes 491528 | tf_op jit(solution)/shard_map/ppermute | solution.py:315
  2.5 17.9 %copy-start.2 = (f32[2048]{0:T(1024)S(1)}, f32[2048]{0:T(1024)}, u32[]{:S(2)}) copy-start(f32[2048]{0:T(1024)} %param.16) | copy-start | bytes 24580
  4.1 16.3 %collective-permute-start.3 = (bf16[2048,512]{1,0:T(8,128)(2,1)}, bf16[2048,512]{1,0:T(8,128)(2,1)S(1)}, u32[]{:S(2)}, u32[]{:S(2)}) collective-permute-start(bf16[2048,512]{1,0:T(8,128)(2,1)} %refs_3_.3), channel_id=1, source_target_pairs={{0,4},{4,0},{8,12},{12,8},{16,20},{20,16},{24,28},{28,24},{1,5},{5... | collective-permute-start | bytes 6291464 | tf_op jit(solution)/shard_map/ppermute | solution.py:315
  4.3 12.4 %collective-permute-start.2 = (bf16[128,2048]{1,0:T(8,128)(2,1)}, bf16[128,2048]{1,0:T(8,128)(2,1)S(1)}, u32[]{:S(2)}, u32[]{:S(2)}) collective-permute-start(bf16[128,2048]{1,0:T(8,128)(2,1)} %zo.1), channel_id=1, source_target_pairs={{0,4},{4,0},{8,12},{12,8},{16,20},{20,16},{24,28},{28,24},{1,5},{5... | collective-permute-start | bytes 1572872 | tf_op jit(solution)/shard_map/ppermute | solution.py:315
  4.7 7.0 %collective-permute-start.4 = (bf16[528,128]{1,0:T(8,128)(2,1)S(1)}, bf16[528,128]{1,0:T(8,128)(2,1)S(1)}, u32[]{:S(2)}, u32[]{:S(2)}) collective-permute-start(bf16[528,128]{1,0:T(8,128)(2,1)S(1)} %get-tuple-element.27.refs_1_), channel_id=1, source_target_pairs={{0,8},{4,12},{8,0},{12,4},{16,24},{20,28},{24,16},{28,20},{1,9},{5... | collective-permute-start | bytes 405512 | tf_op jit(solution)/shard_map/ppermute | solution.py:318
  7.3 7.1 %collective-permute-start.6 = (bf16[528,128]{1,0:T(8,128)(2,1)S(1)}, bf16[528,128]{1,0:T(8,128)(2,1)S(1)}, u32[]{:S(2)}, u32[]{:S(2)}) collective-permute-start(bf16[528,128]{1,0:T(8,128)(2,1)S(1)} %get-tuple-element.29.refs_1_), channel_id=1, source_target_pairs={{0,8},{4,12},{8,0},{12,4},{16,24},{20,28},{24,16},{28,20},{1,9},{5... | collective-permute-start | bytes 405512 | tf_op jit(solution)/shard_map/ppermute | solution.py:318
  12.3 6.8 %collective-permute-start.5 = (bf16[528,128]{1,0:T(8,128)(2,1)S(1)}, bf16[528,128]{1,0:T(8,128)(2,1)S(1)}, u32[]{:S(2)}, u32[]{:S(2)}) collective-permute-start(bf16[528,128]{1,0:T(8,128)(2,1)S(1)} %shard_map.93), channel_id=1, source_target_pairs={{0,16},{4,20},{8,24},{12,28},{16,0},{20,4},{24,8},{28,12},{1,17},{... | collective-permute-start | bytes 405512 | tf_op jit(solution)/shard_map/ppermute | solution.py:318
  15.1 5.3 %collective-permute-start.7 = (bf16[528,128]{1,0:T(8,128)(2,1)S(1)}, bf16[528,128]{1,0:T(8,128)(2,1)S(1)}, u32[]{:S(2)}, u32[]{:S(2)}) collective-permute-start(bf16[528,128]{1,0:T(8,128)(2,1)S(1)} %shard_map.94), channel_id=1, source_target_pairs={{0,16},{4,20},{8,24},{12,28},{16,0},{20,4},{24,8},{28,12},{1,17},{... | collective-permute-start | bytes 405512 | tf_op jit(solution)/shard_map/ppermute | solution.py:318
  20.4 6.8 %copy-start = (bf16[2048,512]{1,0:T(8,128)(2,1)S(1)}, bf16[2048,512]{1,0:T(8,128)(2,1)}, u32[]{:S(2)}) copy-start(bf16[2048,512]{1,0:T(8,128)(2,1)} %refs_3_.3) | copy-start | bytes 6291460
  21.6 2.0 %collective-permute-start.9 = (bf16[128,1024]{1,0:T(8,128)(2,1)S(1)}, bf16[128,1024]{1,0:T(8,128)(2,1)S(1)}, u32[]{:S(2)}, u32[]{:S(2)}) collective-permute-start(bf16[128,1024]{1,0:T(8,128)(2,1)S(1)} %get-tuple-element.31), channel_id=1, source_target_pairs={{0,4},{4,0},{8,12},{12,8},{16,20},{20,16},{24,28},{28,24},{1,5},{5... | collective-permute-start | bytes 786440 | tf_op jit(solution)/shard_map/ppermute | solution.py:315
  21.6 9.2 %collective-permute-start.8 = (bf16[128,1024]{1,0:T(8,128)(2,1)S(1)}, bf16[128,1024]{1,0:T(8,128)(2,1)S(1)}, u32[]{:S(2)}, u32[]{:S(2)}) collective-permute-start(bf16[128,1024]{1,0:T(8,128)(2,1)S(1)} %get-tuple-element.30.refs_1_), channel_id=1, source_target_pairs={{0,8},{4,12},{8,0},{12,4},{16,24},{20,28},{24,16},{28,20},{1,9},{5... | collective-permute-start | bytes 786440 | tf_op jit(solution)/shard_map/ppermute | solution.py:318
  23.7 9.1 %collective-permute-start.10 = (bf16[128,1024]{1,0:T(8,128)(2,1)S(1)}, bf16[128,1024]{1,0:T(8,128)(2,1)S(1)}, u32[]{:S(2)}, u32[]{:S(2)}) collective-permute-start(bf16[128,1024]{1,0:T(8,128)(2,1)S(1)} %collective-permute-done.9.refs_2_), channel_id=1, source_target_pairs={{0,16},{4,20},{8,24},{12,28},{16,0},{20,4},{24,8},{28,12},{1,17},{... | collective-permute-start | bytes 786440 | tf_op jit(solution)/shard_map/ppermute | solution.py:318
  25.2 2.0 %collective-permute-start.11 = (f32[8,128]{1,0:T(8,128)S(1)}, f32[8,128]{1,0:T(8,128)S(1)}, u32[]{:S(2)}, u32[]{:S(2)}) collective-permute-start(f32[8,128]{1,0:T(8,128)S(1)} %get-tuple-element.33), channel_id=1, source_target_pairs={{0,4},{4,0},{8,12},{12,8},{16,20},{20,16},{24,28},{28,24},{1,5},{5... | collective-permute-start | bytes 12296 | tf_op jit(solution)/shard_map/ppermute | solution.py:315
  25.2 13.2 %collective-permute-start.12 = (bf16[128,1024]{1,0:T(8,128)(2,1)S(1)}, bf16[128,1024]{1,0:T(8,128)(2,1)S(1)}, u32[]{:S(2)}, u32[]{:S(2)}) collective-permute-start(bf16[128,1024]{1,0:T(8,128)(2,1)S(1)} %get-tuple-element.30.refs_1_), channel_id=1, source_target_pairs={{0,16},{4,20},{8,24},{12,28},{16,0},{20,4},{24,8},{28,12},{1,17},{... | collective-permute-start | bytes 786440 | tf_op jit(solution)/shard_map/ppermute | solution.py:318
  25.7 12.7 %collective-permute-start.13 = (bf16[128,1024]{1,0:T(8,128)(2,1)S(1)}, bf16[128,1024]{1,0:T(8,128)(2,1)S(1)}, u32[]{:S(2)}, u32[]{:S(2)}) collective-permute-start(bf16[128,1024]{1,0:T(8,128)(2,1)S(1)} %collective-permute-done.9.refs_2_), channel_id=1, source_target_pairs={{0,8},{4,12},{8,0},{12,4},{16,24},{20,28},{24,16},{28,20},{1,9},{5... | collective-permute-start | bytes 786440 | tf_op jit(solution)/shard_map/ppermute | solution.py:318
  32.8 11.1 %collective-permute-start.15 = (bf16[128,1024]{1,0:T(8,128)(2,1)S(1)}, bf16[128,1024]{1,0:T(8,128)(2,1)S(1)}, u32[]{:S(2)}, u32[]{:S(2)}) collective-permute-start(bf16[128,1024]{1,0:T(8,128)(2,1)S(1)} %collective-permute-done.8.refs_1_), channel_id=1, source_target_pairs={{0,16},{4,20},{8,24},{12,28},{16,0},{20,4},{24,8},{28,12},{1,17},{... | collective-permute-start | bytes 786440 | tf_op jit(solution)/shard_map/ppermute | solution.py:318
  34.3 9.6 %collective-permute-start.16 = (bf16[128,1024]{1,0:T(8,128)(2,1)S(1)}, bf16[128,1024]{1,0:T(8,128)(2,1)S(1)}, u32[]{:S(2)}, u32[]{:S(2)}) collective-permute-start(bf16[128,1024]{1,0:T(8,128)(2,1)S(1)} %collective-permute-done.10.refs_4_), channel_id=1, source_target_pairs={{0,8},{4,12},{8,0},{12,4},{16,24},{20,28},{24,16},{28,20},{1,9},{5... | collective-permute-start | bytes 786440 | tf_op jit(solution)/shard_map/ppermute | solution.py:318
  40.2 7.6 %collective-permute-start.19 = (bf16[1024,128]{1,0:T(8,128)(2,1)S(1)}, bf16[1024,128]{1,0:T(8,128)(2,1)S(1)}, u32[]{:S(2)}, u32[]{:S(2)}) collective-permute-start(bf16[1024,128]{1,0:T(8,128)(2,1)S(1)} %get-tuple-element.40), channel_id=1, source_target_pairs={{0,8},{4,12},{8,0},{12,4},{16,24},{20,28},{24,16},{28,20},{1,9},{5... | collective-permute-start | bytes 786440 | tf_op jit(solution)/shard_map/ppermute | solution.py:318
  41.8 12.7 %collective-permute-start.14 = (bf16[1024,128]{1,0:T(8,128)(2,1)S(1)}, bf16[1024,128]{1,0:T(8,128)(2,1)S(1)}, u32[]{:S(2)}, u32[]{:S(2)}) collective-permute-start(bf16[1024,128]{1,0:T(8,128)(2,1)S(1)} %get-tuple-element.37), channel_id=1, source_target_pairs={{0,16},{4,20},{8,24},{12,28},{16,0},{20,4},{24,8},{28,12},{1,17},{... | collective-permute-start | bytes 786440 | tf_op jit(solution)/shard_map/ppermute | solution.py:318
  45.2 9.3 %collective-permute-start.17 = (bf16[1024,128]{1,0:T(8,128)(2,1)S(1)}, bf16[1024,128]{1,0:T(8,128)(2,1)S(1)}, u32[]{:S(2)}, u32[]{:S(2)}) collective-permute-start(bf16[1024,128]{1,0:T(8,128)(2,1)S(1)} %shard_map.98), channel_id=1, source_target_pairs={{0,24},{4,28},{8,16},{12,20},{16,8},{20,12},{24,0},{28,4},{1,25},{... | collective-permute-start | bytes 786440 | tf_op jit(solution)/shard_map/ppermute | solution.py:318
  48.5 7.8 %collective-permute-start.20 = (bf16[1040,128]{1,0:T(8,128)(2,1)S(1)}, bf16[1040,128]{1,0:T(8,128)(2,1)S(1)}, u32[]{:S(2)}, u32[]{:S(2)}) collective-permute-start(bf16[1040,128]{1,0:T(8,128)(2,1)S(1)} %shard_map.99), channel_id=1, source_target_pairs={{0,1},{1,0},{2,3},{3,2},{4,5},{5,4},{6,7},{7,6},{8,9},{9,8},{10,11... | collective-permute-start | bytes 798728 | tf_op jit(solution)/shard_map/ppermute | solution.py:321
  54.6 7.1 %collective-permute-start.18 = (bf16[1024,128]{1,0:T(8,128)(2,1)S(1)}, bf16[1024,128]{1,0:T(8,128)(2,1)S(1)}, u32[]{:S(2)}, u32[]{:S(2)}) collective-permute-start(bf16[1024,128]{1,0:T(8,128)(2,1)S(1)} %get-tuple-element.44), channel_id=1, source_target_pairs={{0,1},{1,0},{2,3},{3,2},{4,5},{5,4},{6,7},{7,6},{8,9},{9,8},{10,11... | collective-permute-start | bytes 786440 | tf_op jit(solution)/shard_map/ppermute | solution.py:321
  62.0 12.9 %collective-permute-start.21 = (bf16[1040,128]{1,0:T(8,128)(2,1)S(1)}, bf16[1040,128]{1,0:T(8,128)(2,1)S(1)}, u32[]{:S(2)}, u32[]{:S(2)}) collective-permute-start(bf16[1040,128]{1,0:T(8,128)(2,1)S(1)} %pad_maximum_fusion), channel_id=1, source_target_pairs={{0,2},{1,3},{2,0},{3,1},{4,6},{5,7},{6,4},{7,5},{8,10},{9,11},{10,... | collective-permute-start | bytes 798728 | tf_op jit(solution)/shard_map/ppermute | solution.py:321

commit v10 on v9

--- a/solution.py
+++ b/solution.py
@@ -291,13 +291,19 @@
 
 
 def sum_kernel(s, *refs, inner):
-    *blocks, squares, out = refs
+    *blocks, squares, result, out, sems = refs
     rows = out.shape[0]
     col = row_scale(squares[...], inner, rows)
+    copies = []
     for g in range(out.shape[1] // LANES):
         at = slice(g * rows, (g + 1) * rows)
         total = sum(a[at].astype(f32) for a in blocks)
-        out[:, g * LANES : (g + 1) * LANES] = (total * col).astype(bf16)
+        lanes = pl.ds(g * LANES, LANES)
+        out[:, lanes] = (total * col).astype(bf16)
+        copies.append(pltpu.make_async_copy(out.at[:, lanes], result.at[:, lanes], sems.at[g]))
+        copies[-1].start()
+    for copy in copies:
+        copy.wait()
 
 
 def body(n, n_head, signal, gate_input, state_in, state_out, step_size, log_decay, skip_gain, norm_gain, out_weight):
@@ -429,7 +435,10 @@
 
     ins = (*blocks, squares)
     out = shape((rows, 2 * cols), bf16)
-    return call(add, s, ins, [full(a) for a in ins], [out], [full(out)])[0]
+    return call(
+        add, s, ins, [full(a) for a in ins], [out], [pl.BlockSpec(memory_space=pl.ANY)],
+        scratch=[pltpu.VMEM(out.shape, bf16), pltpu.SemaphoreType.DMA((out.shape[1] // LANES,))],
+    )[0]
 
 
 def solution(mesh):

time: 76.4 us -> 76.5 us (level)
  no operation moved by 1% of the time
where the time goes in v10:
time: 76.5 us; the launch traced here: 76.3 us
  waiting for transfers between devices  33.4 us (44%)
  starting transfers between devices  28 us (37%)
  Pallas kernels  12.5 us (16%)
  other arithmetic  1.27 us (2%)
  local copies, waits for them, and re-layouts  1 us (1%)
    ppermute x13, starting transfers between devices, across(): return lax.ppermute(a, 'seq', [(i, i ^ 2 * j) for i in range(2 * n)])  20.9 us
    ppermute x13, waiting for transfers between devices, across(): return lax.ppermute(a, 'seq', [(i, i ^ 2 * j) for i in range(2 * n)])  17.5 us
    ppermute x3, waiting for transfers between devices, along(): return lax.ppermute(a, 'head', [(i, i ^ m) for i in range(n)])  15.6 us
    pallas_call x10, Pallas kernels, call(): pl.pallas_call(kernel, out_shape=outs, grid_spec=pltpu.PrefetchScalarGrid...  12.5 us
    ppermute x3, starting transfers between devices, along(): return lax.ppermute(a, 'head', [(i, i ^ m) for i in range(n)])  5.93 us
  transfers between devices with their start and end apart: 22, of which 10 were waited for; matrix products, arithmetic and copies ran while one was open for 3% of the time, Pallas kernels for 11%

profile of v10, /device:TPU:0, one launch (start us, length us, event | category | flops | bytes accessed | tf_op | source)
XLA Modules:
  0.0 76.3 jit_solution(12648239798453326612)
XLA Ops:
  0.5 0.8 %convert_add_fusion.so = f32[320,128]{1,0:T(8,128)S(1)} fusion(f32[32,128]{1,0:T(8,128)} %param.14, f32[32,128]{1,0:T(8,128)} %param.13, bf16[128,128]{1,0:T(8,128)(2,1)} %param.12, bf16[128,128]{1,0:T(8,128)(2,1)} %param.11), kind=kLoop, calls=%fused_computation.7 | loop fusion | flops 204800 | bytes 262144 | tf_op jit(solution)/shard_map/add | solution.py:339
  1.5 1.0 %constant_dynamic-slice_fusion.xo = bf16[128,1024]{1,0:T(8,128)(2,1)S(1)} fusion(bf16[128,2048]{1,0:T(8,128)(2,1)} %param.9, s32[]{:T(128)S(6)} %select_n.55), kind=kLoop, calls=%fused_computation.18 | loop fusion | bytes 524292 | tf_op jit(solution)/shard_map/dynamic_slice | solution.py:342
  2.7 1.3 %shard_map.92 = (f32[128,1024]{1,0:T(8,128)S(1)}, bf16[528,128]{1,0:T(8,128)(2,1)S(1)}, bf16[528,128]{1,0:T(8,128)(2,1)S(1)}) custom-call(s32[3]{0:T(128)S(1)} %pad_add_fusion.s.refs_0_, bf16[128,1024]{1,0:T(8,128)(2,1)S(1)} %constant_dynamic-slice_fusion.xo, bf16[128,2048]{1,0:T(8,128)(2,1)S(1)} %collective-permute-done.xr, ...), custom_call_target="tpu_custom_call" | custom-call | bytes 1908736 | tf_op jit(solution)/shard_map/pallas_call | solution.py:21
  4.7 2.7 %collective-permute-start.4 = (bf16[528,128]{1,0:T(8,128)(2,1)S(1)}, bf16[528,128]{1,0:T(8,128)(2,1)S(1)}, u32[]{:S(2)}, u32[]{:S(2)}) collective-permute-start(bf16[528,128]{1,0:T(8,128)(2,1)S(1)} %get-tuple-element.27.refs_1_), channel_id=1, source_target_pairs={{0,8},{4,12},{8,0},{12,4},{16,24},{20,28},{24,16},{28,20},{1,9},{5... | collective-permute-start | bytes 405512 | tf_op jit(solution)/shard_map/ppermute | solution.py:324
  7.4 4.3 %collective-permute-done.4.refs_2_.rest_0_ = bf16[528,128]{1,0:T(8,128)(2,1)S(1)} collective-permute-done((bf16[528,128]{1,0:T(8,128)(2,1)S(1)}, bf16[528,128]{1,0:T(8,128)(2,1)S(1)}, u32[]{:S(2)}, u32[]{:S(2)}) %collective-permute-start.4) | collective-permute-done | bytes 135200 | tf_op jit(solution)/shard_map/ppermute | solution.py:324
  12.3 2.2 %collective-permute-start.5 = (bf16[528,128]{1,0:T(8,128)(2,1)S(1)}, bf16[528,128]{1,0:T(8,128)(2,1)S(1)}, u32[]{:S(2)}, u32[]{:S(2)}) collective-permute-start(bf16[528,128]{1,0:T(8,128)(2,1)S(1)} %shard_map.93), channel_id=1, source_target_pairs={{0,16},{4,20},{8,24},{12,28},{16,0},{20,4},{24,8},{28,12},{1,17},{... | collective-permute-start | bytes 405512 | tf_op jit(solution)/shard_map/ppermute | solution.py:324
  15.1 1.7 %collective-permute-start.7 = (bf16[528,128]{1,0:T(8,128)(2,1)S(1)}, bf16[528,128]{1,0:T(8,128)(2,1)S(1)}, u32[]{:S(2)}, u32[]{:S(2)}) collective-permute-start(bf16[528,128]{1,0:T(8,128)(2,1)S(1)} %shard_map.94), channel_id=1, source_target_pairs={{0,16},{4,20},{8,24},{12,28},{16,0},{20,4},{24,8},{28,12},{1,17},{... | collective-permute-start | bytes 405512 | tf_op jit(solution)/shard_map/ppermute | solution.py:324
  16.8 2.3 %shard_map.91 = (f32[256,1024]{1,0:T(8,128)S(1)}, f32[256,1024]{1,0:T(8,128)S(1)}, f32[16,1024]{1,0:T(8,128)S(1)}) custom-call(s32[3]{0:T(128)S(1)} %pad_add_fusion.s.refs_0_, bf16[128,1024]{1,0:T(8,128)(2,1)S(1)} %constant_dynamic-slice_fusion.xo, bf16[128,2048]{1,0:T(8,128)(2,1)S(1)} %collective-permute-done.xr, f32[320,128]{1,0:T(8,128)S(1)} %convert_add_fusion.so, ...), custom_call_target="tpu_custom_call" | custom-call | bytes 4325504 | tf_op jit(solution)/shard_map/pallas_call | solution.py:21
  19.1 1.2 %collective-permute-done.7.rest_3_ = bf16[528,128]{1,0:T(8,128)(2,1)S(1)} collective-permute-done((bf16[528,128]{1,0:T(8,128)(2,1)S(1)}, bf16[528,128]{1,0:T(8,128)(2,1)S(1)}, u32[]{:S(2)}, u32[]{:S(2)}) %collective-permute-start.7) | collective-permute-done | bytes 135200 | tf_op jit(solution)/shard_map/ppermute | solution.py:324
  20.4 1.2 %shard_map.95 = (bf16[128,1024]{1,0:T(8,128)(2,1)S(1)}, bf16[128,1024]{1,0:T(8,128)(2,1)S(1)}, f32[8,128]{1,0:T(8,128)S(1)}, f32[8,128]{1,0:T(8,128)S(1)}) custom-call(s32[3]{0:T(128)S(1)} %pad_add_fusion.s.refs_0_, f32[256,1024]{1,0:T(8,128)S(1)} %get-tuple-element.23.inside, f32[256,1024]{1,0:T(8,128)S(1)} %get-tuple-element.24.decays, ...), custom_call_target="tpu_custom_call" | custom-call | bytes 6193152 | tf_op jit(solution)/shard_map/pallas_call | solution.py:21
  21.6 2.0 %collective-permute-start.8 = (bf16[128,1024]{1,0:T(8,128)(2,1)S(1)}, bf16[128,1024]{1,0:T(8,128)(2,1)S(1)}, u32[]{:S(2)}, u32[]{:S(2)}) collective-permute-start(bf16[128,1024]{1,0:T(8,128)(2,1)S(1)} %get-tuple-element.30.refs_1_), channel_id=1, source_target_pairs={{0,8},{4,12},{8,0},{12,4},{16,24},{20,28},{24,16},{28,20},{1,9},{5... | collective-permute-start | bytes 786440 | tf_op jit(solution)/shard_map/ppermute | solution.py:324
  23.7 1.5 %collective-permute-start.10 = (bf16[128,1024]{1,0:T(8,128)(2,1)S(1)}, bf16[128,1024]{1,0:T(8,128)(2,1)S(1)}, u32[]{:S(2)}, u32[]{:S(2)}) collective-permute-start(bf16[128,1024]{1,0:T(8,128)(2,1)S(1)} %collective-permute-done.9.refs_2_), channel_id=1, source_target_pairs={{0,16},{4,20},{8,24},{12,28},{16,0},{20,4},{24,8},{28,12},{1,17},{... | collective-permute-start | bytes 786440 | tf_op jit(solution)/shard_map/ppermute | solution.py:324
  25.7 1.5 %collective-permute-start.13 = (bf16[128,1024]{1,0:T(8,128)(2,1)S(1)}, bf16[128,1024]{1,0:T(8,128)(2,1)S(1)}, u32[]{:S(2)}, u32[]{:S(2)}) collective-permute-start(bf16[128,1024]{1,0:T(8,128)(2,1)S(1)} %collective-permute-done.9.refs_2_), channel_id=1, source_target_pairs={{0,8},{4,12},{8,0},{12,4},{16,24},{20,28},{24,16},{28,20},{1,9},{5... | collective-permute-start | bytes 786440 | tf_op jit(solution)/shard_map/ppermute | solution.py:324
  27.2 1.3 %shard_map.96.refs_7_.odd = bf16[1024,128]{1,0:T(8,128)(2,1)S(1)} custom-call(s32[3]{0:T(128)S(1)} %pad_add_fusion.s.refs_0_, bf16[128,1024]{1,0:T(8,128)(2,1)S(1)} %get-tuple-element.30.refs_1_, bf16[128,1024]{1,0:T(8,128)(2,1)S(1)} %collective-permute-done.9.refs_2_, bf16[2048,512]{1,0:T(8,128)(2,1)S(1)} %copy-done, ...), custom_call_target="tpu_custom_call" | custom-call | bytes 4984832 | tf_op jit(solution)/shard_map/pallas_call | solution.py:21
  28.5 2.4 %collective-permute-done.8.refs_1_ = bf16[128,1024]{1,0:T(8,128)(2,1)S(1)} collective-permute-done((bf16[128,1024]{1,0:T(8,128)(2,1)S(1)}, bf16[128,1024]{1,0:T(8,128)(2,1)S(1)}, u32[]{:S(2)}, u32[]{:S(2)}) %collective-permute-start.8) | collective-permute-done | bytes 262176 | tf_op jit(solution)/shard_map/ppermute | solution.py:324
  30.8 2.0 %collective-permute-done.10.refs_4_ = bf16[128,1024]{1,0:T(8,128)(2,1)S(1)} collective-permute-done((bf16[128,1024]{1,0:T(8,128)(2,1)S(1)}, bf16[128,1024]{1,0:T(8,128)(2,1)S(1)}, u32[]{:S(2)}, u32[]{:S(2)}) %collective-permute-start.10) | collective-permute-done | bytes 262176 | tf_op jit(solution)/shard_map/ppermute | solution.py:324
  32.8 1.5 %collective-permute-start.15 = (bf16[128,1024]{1,0:T(8,128)(2,1)S(1)}, bf16[128,1024]{1,0:T(8,128)(2,1)S(1)}, u32[]{:S(2)}, u32[]{:S(2)}) collective-permute-start(bf16[128,1024]{1,0:T(8,128)(2,1)S(1)} %collective-permute-done.8.refs_1_), channel_id=1, source_target_pairs={{0,16},{4,20},{8,24},{12,28},{16,0},{20,4},{24,8},{28,12},{1,17},{... | collective-permute-start | bytes 786440 | tf_op jit(solution)/shard_map/ppermute | solution.py:324
  34.3 1.5 %collective-permute-start.16 = (bf16[128,1024]{1,0:T(8,128)(2,1)S(1)}, bf16[128,1024]{1,0:T(8,128)(2,1)S(1)}, u32[]{:S(2)}, u32[]{:S(2)}) collective-permute-start(bf16[128,1024]{1,0:T(8,128)(2,1)S(1)} %collective-permute-done.10.refs_4_), channel_id=1, source_target_pairs={{0,8},{4,12},{8,0},{12,4},{16,24},{20,28},{24,16},{28,20},{1,9},{5... | collective-permute-start | bytes 786440 | tf_op jit(solution)/shard_map/ppermute | solution.py:324
  35.8 2.6 %collective-permute-done.12.refs_2_ = bf16[128,1024]{1,0:T(8,128)(2,1)S(1)} collective-permute-done((bf16[128,1024]{1,0:T(8,128)(2,1)S(1)}, bf16[128,1024]{1,0:T(8,128)(2,1)S(1)}, u32[]{:S(2)}, u32[]{:S(2)}) %collective-permute-start.12) | collective-permute-done | bytes 262176 | tf_op jit(solution)/shard_map/ppermute | solution.py:324
  38.4 1.8 %shard_map.97 = (bf16[1024,128]{1,0:T(8,128)(2,1)S(1)}, bf16[1024,128]{1,0:T(8,128)(2,1)S(1)}) custom-call(s32[3]{0:T(128)S(1)} %pad_add_fusion.s.refs_0_, bf16[128,1024]{1,0:T(8,128)(2,1)S(1)} %collective-permute-done.8.refs_1_, bf16[128,1024]{1,0:T(8,128)(2,1)S(1)} %collective-permute-done.12.refs_2_, ...), custom_call_target="tpu_custom_call" | custom-call | bytes 6029312 | tf_op jit(solution)/shard_map/pallas_call | solution.py:21
  40.2 1.6 %collective-permute-start.19 = (bf16[1024,128]{1,0:T(8,128)(2,1)S(1)}, bf16[1024,128]{1,0:T(8,128)(2,1)S(1)}, u32[]{:S(2)}, u32[]{:S(2)}) collective-permute-start(bf16[1024,128]{1,0:T(8,128)(2,1)S(1)} %get-tuple-element.40), channel_id=1, source_target_pairs={{0,8},{4,12},{8,0},{12,4},{16,24},{20,28},{24,16},{28,20},{1,9},{5... | collective-permute-start | bytes 786440 | tf_op jit(solution)/shard_map/ppermute | solution.py:324
  41.8 1.5 %collective-permute-start.14 = (bf16[1024,128]{1,0:T(8,128)(2,1)S(1)}, bf16[1024,128]{1,0:T(8,128)(2,1)S(1)}, u32[]{:S(2)}, u32[]{:S(2)}) collective-permute-start(bf16[1024,128]{1,0:T(8,128)(2,1)S(1)} %get-tuple-element.37), channel_id=1, source_target_pairs={{0,16},{4,20},{8,24},{12,28},{16,0},{20,4},{24,8},{28,12},{1,17},{... | collective-permute-start | bytes 786440 | tf_op jit(solution)/shard_map/ppermute | solution.py:324
  43.9 1.3 %shard_map.98 = bf16[1024,128]{1,0:T(8,128)(2,1)S(1)} custom-call(s32[3]{0:T(128)S(1)} %pad_add_fusion.s.refs_0_, bf16[128,1024]{1,0:T(8,128)(2,1)S(1)} %collective-permute-done.15.refs_1_, bf16[128,1024]{1,0:T(8,128)(2,1)S(1)} %collective-permute-done.16.refs_2_, bf16[2048,512]{1,0:T(8,128)(2,1)S(1)} %copy-done, ...), custom_call_target="tpu_custom_call" | custom-call | bytes 4980736 | tf_op jit(solution)/shard_map/pallas_call | solution.py:21
  45.2 2.7 %collective-permute-start.17 = (bf16[1024,128]{1,0:T(8,128)(2,1)S(1)}, bf16[1024,128]{1,0:T(8,128)(2,1)S(1)}, u32[]{:S(2)}, u32[]{:S(2)}) collective-permute-start(bf16[1024,128]{1,0:T(8,128)(2,1)S(1)} %shard_map.98), channel_id=1, source_target_pairs={{0,24},{4,28},{8,16},{12,20},{16,8},{20,12},{24,0},{28,4},{1,25},{... | collective-permute-start | bytes 786440 | tf_op jit(solution)/shard_map/ppermute | solution.py:324
  47.8 0.6 shard_map.99
  48.5 1.6 %collective-permute-start.20 = (bf16[1040,128]{1,0:T(8,128)(2,1)S(1)}, bf16[1040,128]{1,0:T(8,128)(2,1)S(1)}, u32[]{:S(2)}, u32[]{:S(2)}) collective-permute-start(bf16[1040,128]{1,0:T(8,128)(2,1)S(1)} %shard_map.99), channel_id=1, source_target_pairs={{0,1},{1,0},{2,3},{3,2},{4,5},{5,4},{6,7},{7,6},{8,9},{9,8},{10,11... | collective-permute-start | bytes 798728 | tf_op jit(solution)/shard_map/ppermute | solution.py:327
  50.1 4.4 %collective-permute-done.14 = bf16[1024,128]{1,0:T(8,128)(2,1)S(1)} collective-permute-done((bf16[1024,128]{1,0:T(8,128)(2,1)S(1)}, bf16[1024,128]{1,0:T(8,128)(2,1)S(1)}, u32[]{:S(2)}, u32[]{:S(2)}) %collective-permute-start.14) | collective-permute-done | bytes 262176 | tf_op jit(solution)/shard_map/ppermute | solution.py:324
  54.6 1.6 %collective-permute-start.18 = (bf16[1024,128]{1,0:T(8,128)(2,1)S(1)}, bf16[1024,128]{1,0:T(8,128)(2,1)S(1)}, u32[]{:S(2)}, u32[]{:S(2)}) collective-permute-start(bf16[1024,128]{1,0:T(8,128)(2,1)S(1)} %get-tuple-element.44), channel_id=1, source_target_pairs={{0,1},{1,0},{2,3},{3,2},{4,5},{5,4},{6,7},{7,6},{8,9},{9,8},{10,11... | collective-permute-start | bytes 786440 | tf_op jit(solution)/shard_map/ppermute | solution.py:327
  56.3 5.4 %collective-permute-done.18 = bf16[1024,128]{1,0:T(8,128)(2,1)S(1)} collective-permute-done((bf16[1024,128]{1,0:T(8,128)(2,1)S(1)}, bf16[1024,128]{1,0:T(8,128)(2,1)S(1)}, u32[]{:S(2)}, u32[]{:S(2)}) %collective-permute-start.18) | collective-permute-done | bytes 262176 | tf_op jit(solution)/shard_map/ppermute | solution.py:327
  62.0 2.6 %collective-permute-start.21 = (bf16[1040,128]{1,0:T(8,128)(2,1)S(1)}, bf16[1040,128]{1,0:T(8,128)(2,1)S(1)}, u32[]{:S(2)}, u32[]{:S(2)}) collective-permute-start(bf16[1040,128]{1,0:T(8,128)(2,1)S(1)} %pad_maximum_fusion), channel_id=1, source_target_pairs={{0,2},{1,3},{2,0},{3,1},{4,6},{5,7},{6,4},{7,5},{8,10},{9,11},{10,... | collective-permute-start | bytes 798728 | tf_op jit(solution)/shard_map/ppermute | solution.py:327
  64.6 10.2 %collective-permute-done.21 = bf16[1040,128]{1,0:T(8,128)(2,1)S(1)} collective-permute-done((bf16[1040,128]{1,0:T(8,128)(2,1)S(1)}, bf16[1040,128]{1,0:T(8,128)(2,1)S(1)}, u32[]{:S(2)}, u32[]{:S(2)}) %collective-permute-start.21) | collective-permute-done | bytes 266272 | tf_op jit(solution)/shard_map/ppermute | solution.py:327
  74.9 1.4 %shard_map.100 = bf16[128,1024]{1,0:T(8,128)(2,1)} custom-call(s32[3]{0:T(128)S(1)} %pad_add_fusion.s.refs_0_, bf16[1024,128]{1,0:T(8,128)(2,1)S(1)} %slice.36.refs_1_, bf16[1024,128]{1,0:T(8,128)(2,1)S(1)} %get-tuple-element.43.refs_2_, bf16[1024,128]{1,0:T(8,128)(2,1)S(1)} %broadcast_select_fusion.3.refs_3_, f32[8,128]{1,0:T(8,128)S(1)} %fusion.1.refs_4_), custom_call_target="tpu_custom_call" | custom-call | bytes 1052672 | tf_op jit(solution)/shard_map/pallas_call | solution.py:21
  (44 shorter events, 4.3 us)
Async XLA Ops:
  0.0 16.8 %copy-start.1 = (bf16[128,2048]{1,0:T(8,128)(2,1)S(1)}, bf16[128,2048]{1,0:T(8,128)(2,1)}, u32[]{:S(2)}) copy-start(bf16[128,2048]{1,0:T(8,128)(2,1)} %zo.1) | copy-start | bytes 1572868
  0.0 16.8 %copy-start.3 = (f32[32]{0:T(128)S(1)}, f32[32]{0:T(128)}, u32[]{:S(2)}) copy-start(f32[32]{0:T(128)} %param.15) | copy-start | bytes 388
  0.0 2.7 %collective-permute-start = (bf16[128,2048]{1,0:T(8,128)(2,1)}, bf16[128,2048]{1,0:T(8,128)(2,1)S(1)}, u32[]{:S(2)}, u32[]{:S(2)}) collective-permute-start(bf16[128,2048]{1,0:T(8,128)(2,1)} %param.9), channel_id=1, source_target_pairs={{0,4},{4,0},{8,12},{12,8},{16,20},{20,16},{24,28},{28,24},{1,5},{5... | collective-permute-start | bytes 1572872 | tf_op jit(solution)/shard_map/ppermute | solution.py:321
  1.3 1.5 %collective-permute-start.1 = (f32[320,128]{1,0:T(8,128)S(1)}, f32[320,128]{1,0:T(8,128)S(1)}, u32[]{:S(2)}, u32[]{:S(2)}) collective-permute-start(f32[320,128]{1,0:T(8,128)S(1)} %convert_add_fusion.so), channel_id=1, source_target_pairs={{0,4},{4,0},{8,12},{12,8},{16,20},{20,16},{24,28},{28,24},{1,5},{5... | collective-permute-start | bytes 491528 | tf_op jit(solution)/shard_map/ppermute | solution.py:321
  2.5 17.9 %copy-start.2 = (f32[2048]{0:T(1024)S(1)}, f32[2048]{0:T(1024)}, u32[]{:S(2)}) copy-start(f32[2048]{0:T(1024)} %param.16) | copy-start | bytes 24580
  4.1 16.3 %collective-permute-start.3 = (bf16[2048,512]{1,0:T(8,128)(2,1)}, bf16[2048,512]{1,0:T(8,128)(2,1)S(1)}, u32[]{:S(2)}, u32[]{:S(2)}) collective-permute-start(bf16[2048,512]{1,0:T(8,128)(2,1)} %refs_3_.3), channel_id=1, source_target_pairs={{0,4},{4,0},{8,12},{12,8},{16,20},{20,16},{24,28},{28,24},{1,5},{5... | collective-permute-start | bytes 6291464 | tf_op jit(solution)/shard_map/ppermute | solution.py:321
  4.3 12.4 %collective-permute-start.2 = (bf16[128,2048]{1,0:T(8,128)(2,1)}, bf16[128,2048]{1,0:T(8,128)(2,1)S(1)}, u32[]{:S(2)}, u32[]{:S(2)}) collective-permute-start(bf16[128,2048]{1,0:T(8,128)(2,1)} %zo.1), channel_id=1, source_target_pairs={{0,4},{4,0},{8,12},{12,8},{16,20},{20,16},{24,28},{28,24},{1,5},{5... | collective-permute-start | bytes 1572872 | tf_op jit(solution)/shard_map/ppermute | solution.py:321
  4.7 7.0 %collective-permute-start.4 = (bf16[528,128]{1,0:T(8,128)(2,1)S(1)}, bf16[528,128]{1,0:T(8,128)(2,1)S(1)}, u32[]{:S(2)}, u32[]{:S(2)}) collective-permute-start(bf16[528,128]{1,0:T(8,128)(2,1)S(1)} %get-tuple-element.27.refs_1_), channel_id=1, source_target_pairs={{0,8},{4,12},{8,0},{12,4},{16,24},{20,28},{24,16},{28,20},{1,9},{5... | collective-permute-start | bytes 405512 | tf_op jit(solution)/shard_map/ppermute | solution.py:324
  7.3 7.1 %collective-permute-start.6 = (bf16[528,128]{1,0:T(8,128)(2,1)S(1)}, bf16[528,128]{1,0:T(8,128)(2,1)S(1)}, u32[]{:S(2)}, u32[]{:S(2)}) collective-permute-start(bf16[528,128]{1,0:T(8,128)(2,1)S(1)} %get-tuple-element.29.refs_1_), channel_id=1, source_target_pairs={{0,8},{4,12},{8,0},{12,4},{16,24},{20,28},{24,16},{28,20},{1,9},{5... | collective-permute-start | bytes 405512 | tf_op jit(solution)/shard_map/ppermute | solution.py:324
  12.3 6.8 %collective-permute-start.5 = (bf16[528,128]{1,0:T(8,128)(2,1)S(1)}, bf16[528,128]{1,0:T(8,128)(2,1)S(1)}, u32[]{:S(2)}, u32[]{:S(2)}) collective-permute-start(bf16[528,128]{1,0:T(8,128)(2,1)S(1)} %shard_map.93), channel_id=1, source_target_pairs={{0,16},{4,20},{8,24},{12,28},{16,0},{20,4},{24,8},{28,12},{1,17},{... | collective-permute-start | bytes 405512 | tf_op jit(solution)/shard_map/ppermute | solution.py:324
  15.1 5.3 %collective-permute-start.7 = (bf16[528,128]{1,0:T(8,128)(2,1)S(1)}, bf16[528,128]{1,0:T(8,128)(2,1)S(1)}, u32[]{:S(2)}, u32[]{:S(2)}) collective-permute-start(bf16[528,128]{1,0:T(8,128)(2,1)S(1)} %shard_map.94), channel_id=1, source_target_pairs={{0,16},{4,20},{8,24},{12,28},{16,0},{20,4},{24,8},{28,12},{1,17},{... | collective-permute-start | bytes 405512 | tf_op jit(solution)/shard_map/ppermute | solution.py:324
  20.4 6.8 %copy-start = (bf16[2048,512]{1,0:T(8,128)(2,1)S(1)}, bf16[2048,512]{1,0:T(8,128)(2,1)}, u32[]{:S(2)}) copy-start(bf16[2048,512]{1,0:T(8,128)(2,1)} %refs_3_.3) | copy-start | bytes 6291460
  21.6 2.0 %collective-permute-start.9 = (bf16[128,1024]{1,0:T(8,128)(2,1)S(1)}, bf16[128,1024]{1,0:T(8,128)(2,1)S(1)}, u32[]{:S(2)}, u32[]{:S(2)}) collective-permute-start(bf16[128,1024]{1,0:T(8,128)(2,1)S(1)} %get-tuple-element.31), channel_id=1, source_target_pairs={{0,4},{4,0},{8,12},{12,8},{16,20},{20,16},{24,28},{28,24},{1,5},{5... | collective-permute-start | bytes 786440 | tf_op jit(solution)/shard_map/ppermute | solution.py:321
  21.6 9.2 %collective-permute-start.8 = (bf16[128,1024]{1,0:T(8,128)(2,1)S(1)}, bf16[128,1024]{1,0:T(8,128)(2,1)S(1)}, u32[]{:S(2)}, u32[]{:S(2)}) collective-permute-start(bf16[128,1024]{1,0:T(8,128)(2,1)S(1)} %get-tuple-element.30.refs_1_), channel_id=1, source_target_pairs={{0,8},{4,12},{8,0},{12,4},{16,24},{20,28},{24,16},{28,20},{1,9},{5... | collective-permute-start | bytes 786440 | tf_op jit(solution)/shard_map/ppermute | solution.py:324
  23.7 9.1 %collective-permute-start.10 = (bf16[128,1024]{1,0:T(8,128)(2,1)S(1)}, bf16[128,1024]{1,0:T(8,128)(2,1)S(1)}, u32[]{:S(2)}, u32[]{:S(2)}) collective-permute-start(bf16[128,1024]{1,0:T(8,128)(2,1)S(1)} %collective-permute-done.9.refs_2_), channel_id=1, source_target_pairs={{0,16},{4,20},{8,24},{12,28},{16,0},{20,4},{24,8},{28,12},{1,17},{... | collective-permute-start | bytes 786440 | tf_op jit(solution)/shard_map/ppermute | solution.py:324
  25.2 2.0 %collective-permute-start.11 = (f32[8,128]{1,0:T(8,128)S(1)}, f32[8,128]{1,0:T(8,128)S(1)}, u32[]{:S(2)}, u32[]{:S(2)}) collective-permute-start(f32[8,128]{1,0:T(8,128)S(1)} %get-tuple-element.33), channel_id=1, source_target_pairs={{0,4},{4,0},{8,12},{12,8},{16,20},{20,16},{24,28},{28,24},{1,5},{5... | collective-permute-start | bytes 12296 | tf_op jit(solution)/shard_map/ppermute | solution.py:321
  25.2 13.2 %collective-permute-start.12 = (bf16[128,1024]{1,0:T(8,128)(2,1)S(1)}, bf16[128,1024]{1,0:T(8,128)(2,1)S(1)}, u32[]{:S(2)}, u32[]{:S(2)}) collective-permute-start(bf16[128,1024]{1,0:T(8,128)(2,1)S(1)} %get-tuple-element.30.refs_1_), channel_id=1, source_target_pairs={{0,16},{4,20},{8,24},{12,28},{16,0},{20,4},{24,8},{28,12},{1,17},{... | collective-permute-start | bytes 786440 | tf_op jit(solution)/shard_map/ppermute | solution.py:324
  25.7 12.7 %collective-permute-start.13 = (bf16[128,1024]{1,0:T(8,128)(2,1)S(1)}, bf16[128,1024]{1,0:T(8,128)(2,1)S(1)}, u32[]{:S(2)}, u32[]{:S(2)}) collective-permute-start(bf16[128,1024]{1,0:T(8,128)(2,1)S(1)} %collective-permute-done.9.refs_2_), channel_id=1, source_target_pairs={{0,8},{4,12},{8,0},{12,4},{16,24},{20,28},{24,16},{28,20},{1,9},{5... | collective-permute-start | bytes 786440 | tf_op jit(solution)/shard_map/ppermute | solution.py:324
  32.8 11.1 %collective-permute-start.15 = (bf16[128,1024]{1,0:T(8,128)(2,1)S(1)}, bf16[128,1024]{1,0:T(8,128)(2,1)S(1)}, u32[]{:S(2)}, u32[]{:S(2)}) collective-permute-start(bf16[128,1024]{1,0:T(8,128)(2,1)S(1)} %collective-permute-done.8.refs_1_), channel_id=1, source_target_pairs={{0,16},{4,20},{8,24},{12,28},{16,0},{20,4},{24,8},{28,12},{1,17},{... | collective-permute-start | bytes 786440 | tf_op jit(solution)/shard_map/ppermute | solution.py:324
  34.3 9.6 %collective-permute-start.16 = (bf16[128,1024]{1,0:T(8,128)(2,1)S(1)}, bf16[128,1024]{1,0:T(8,128)(2,1)S(1)}, u32[]{:S(2)}, u32[]{:S(2)}) collective-permute-start(bf16[128,1024]{1,0:T(8,128)(2,1)S(1)} %collective-permute-done.10.refs_4_), channel_id=1, source_target_pairs={{0,8},{4,12},{8,0},{12,4},{16,24},{20,28},{24,16},{28,20},{1,9},{5... | collective-permute-start | bytes 786440 | tf_op jit(solution)/shard_map/ppermute | solution.py:324
  40.2 7.6 %collective-permute-start.19 = (bf16[1024,128]{1,0:T(8,128)(2,1)S(1)}, bf16[1024,128]{1,0:T(8,128)(2,1)S(1)}, u32[]{:S(2)}, u32[]{:S(2)}) collective-permute-start(bf16[1024,128]{1,0:T(8,128)(2,1)S(1)} %get-tuple-element.40), channel_id=1, source_target_pairs={{0,8},{4,12},{8,0},{12,4},{16,24},{20,28},{24,16},{28,20},{1,9},{5... | collective-permute-start | bytes 786440 | tf_op jit(solution)/shard_map/ppermute | solution.py:324
  41.8 12.7 %collective-permute-start.14 = (bf16[1024,128]{1,0:T(8,128)(2,1)S(1)}, bf16[1024,128]{1,0:T(8,128)(2,1)S(1)}, u32[]{:S(2)}, u32[]{:S(2)}) collective-permute-start(bf16[1024,128]{1,0:T(8,128)(2,1)S(1)} %get-tuple-element.37), channel_id=1, source_target_pairs={{0,16},{4,20},{8,24},{12,28},{16,0},{20,4},{24,8},{28,12},{1,17},{... | collective-permute-start | bytes 786440 | tf_op jit(solution)/shard_map/ppermute | solution.py:324
  45.2 9.3 %collective-permute-start.17 = (bf16[1024,128]{1,0:T(8,128)(2,1)S(1)}, bf16[1024,128]{1,0:T(8,128)(2,1)S(1)}, u32[]{:S(2)}, u32[]{:S(2)}) collective-permute-start(bf16[1024,128]{1,0:T(8,128)(2,1)S(1)} %shard_map.98), channel_id=1, source_target_pairs={{0,24},{4,28},{8,16},{12,20},{16,8},{20,12},{24,0},{28,4},{1,25},{... | collective-permute-start | bytes 786440 | tf_op jit(solution)/shard_map/ppermute | solution.py:324
  48.5 7.8 %collective-permute-start.20 = (bf16[1040,128]{1,0:T(8,128)(2,1)S(1)}, bf16[1040,128]{1,0:T(8,128)(2,1)S(1)}, u32[]{:S(2)}, u32[]{:S(2)}) collective-permute-start(bf16[1040,128]{1,0:T(8,128)(2,1)S(1)} %shard_map.99), channel_id=1, source_target_pairs={{0,1},{1,0},{2,3},{3,2},{4,5},{5,4},{6,7},{7,6},{8,9},{9,8},{10,11... | collective-permute-start | bytes 798728 | tf_op jit(solution)/shard_map/ppermute | solution.py:327
  54.6 7.1 %collective-permute-start.18 = (bf16[1024,128]{1,0:T(8,128)(2,1)S(1)}, bf16[1024,128]{1,0:T(8,128)(2,1)S(1)}, u32[]{:S(2)}, u32[]{:S(2)}) collective-permute-start(bf16[1024,128]{1,0:T(8,128)(2,1)S(1)} %get-tuple-element.44), channel_id=1, source_target_pairs={{0,1},{1,0},{2,3},{3,2},{4,5},{5,4},{6,7},{7,6},{8,9},{9,8},{10,11... | collective-permute-start | bytes 786440 | tf_op jit(solution)/shard_map/ppermute | solution.py:327
  62.0 12.9 %collective-permute-start.21 = (bf16[1040,128]{1,0:T(8,128)(2,1)S(1)}, bf16[1040,128]{1,0:T(8,128)(2,1)S(1)}, u32[]{:S(2)}, u32[]{:S(2)}) collective-permute-start(bf16[1040,128]{1,0:T(8,128)(2,1)S(1)} %pad_maximum_fusion), channel_id=1, source_target_pairs={{0,2},{1,3},{2,0},{3,1},{4,6},{5,7},{6,4},{7,5},{8,10},{9,11},{10,... | collective-permute-start | bytes 798728 | tf_op jit(solution)/shard_map/ppermute | solution.py:327
